TPU v7x, 32 devices: a whole 2x2x4 slice. The times are simulated.
32 devices in a mesh: dp: 8 (over y, x, core), mp: 4 (over z).
Axes of the slice: x: 2, y: 2, z: 4, core: 2. Of those that a mesh axis runs over, the one named last changes fastest.
Arguments:
- language: bfloat16 [288, 20, 768], P(('dp', 'mp')), may hold values from -6 to 6
- images: bfloat16 [72, 36, 768], P('dp'), may hold values from -6 to 6
- counts: int32 [8, 9], P('dp'), may hold values from 1 to 10, 36 in all within a row
- language_cot: bfloat16 [288, 20, 768], P(('dp', 'mp')), may hold values from -6 to 6
- vision_cot: bfloat16 [288, 36, 768], P(('dp', 'mp')), may hold values from -6 to 6
- attn_in_weight: float32 [3, 768, 3, 768], P(None, 'dp', None, 'mp')
- attn_in_moment: float32 [3, 768, 3, 768], P(None, 'dp', None, 'mp'), may hold values from -0.00015258789 to 0.00015258789
- attn_in_square: float32 [3, 768, 3, 768], P(None, 'dp', None, 'mp')
- attn_in_average: float32 [3, 768, 3, 768], P(None, 'dp', None, 'mp'), may hold values from -0.15625 to 0.15625
- attn_out_weight: float32 [3, 768, 768], P(None, 'mp', 'dp')
- attn_out_moment: float32 [3, 768, 768], P(None, 'mp', 'dp'), may hold values from -0.00015258789 to 0.00015258789
- attn_out_square: float32 [3, 768, 768], P(None, 'mp', 'dp')
- attn_out_average: float32 [3, 768, 768], P(None, 'mp', 'dp'), may hold values from -0.21875 to 0.21875
- ffn_in_weight: float32 [2, 768, 3072], P(None, 'dp', 'mp')
- ffn_in_moment: float32 [2, 768, 3072], P(None, 'dp', 'mp'), may hold values from -0.00015258789 to 0.00015258789
- ffn_in_square: float32 [2, 768, 3072], P(None, 'dp', 'mp')
- ffn_in_average: float32 [2, 768, 3072], P(None, 'dp', 'mp'), may hold values from -0.21875 to 0.21875
- ffn_out_weight: float32 [2, 3072, 768], P(None, 'mp', 'dp')
- ffn_out_moment: float32 [2, 3072, 768], P(None, 'mp', 'dp'), may hold values from -0.00015258789 to 0.00015258789
- ffn_out_square: float32 [2, 3072, 768], P(None, 'mp', 'dp')
- ffn_out_average: float32 [2, 3072, 768], P(None, 'mp', 'dp'), may hold values from -0.109375 to 0.109375
- norm_weight: float32 [2, 5, 768], replicated
- norm_moment: float32 [2, 5, 768], replicated, may hold values from -0.00061035156 to 0.00061035156
- norm_square: float32 [2, 5, 768], replicated
- norm_average: float32 [2, 5, 768], replicated, may hold values from 0.5 to 1.5
Outputs:
- language_out: bfloat16 [288, 20, 768], P(('dp', 'mp'))
- vision_out: bfloat16 [288, 36, 768], P(('dp', 'mp'))
- language_grad: float32 [288, 20, 768], P(('dp', 'mp'))
- image_grad: float32 [72, 36, 768], P('dp')
- attn_in_grad: float32 [3, 768, 3, 768], P(None, 'dp', None, 'mp')
- attn_in_new_moment: float32 [3, 768, 3, 768], P(None, 'dp', None, 'mp')
- attn_in_new_square: float32 [3, 768, 3, 768], P(None, 'dp', None, 'mp')
- attn_in_new_weight: float32 [3, 768, 3, 768], P(None, 'dp', None, 'mp')
- attn_in_copy: bfloat16 [3, 768, 3, 768], P(None, 'dp', None, 'mp')
- attn_in_new_average: float32 [3, 768, 3, 768], P(None, 'dp', None, 'mp')
- attn_out_grad: float32 [3, 768, 768], P(None, 'mp', 'dp')
- attn_out_new_moment: float32 [3, 768, 768], P(None, 'mp', 'dp')
- attn_out_new_square: float32 [3, 768, 768], P(None, 'mp', 'dp')
- attn_out_new_weight: float32 [3, 768, 768], P(None, 'mp', 'dp')
- attn_out_copy: bfloat16 [3, 768, 768], P(None, 'mp', 'dp')
- attn_out_new_average: float32 [3, 768, 768], P(None, 'mp', 'dp')
- ffn_in_grad: float32 [2, 768, 3072], P(None, 'dp', 'mp')
- ffn_in_new_moment: float32 [2, 768, 3072], P(None, 'dp', 'mp')
- ffn_in_new_square: float32 [2, 768, 3072], P(None, 'dp', 'mp')
- ffn_in_new_weight: float32 [2, 768, 3072], P(None, 'dp', 'mp')
- ffn_in_copy: bfloat16 [2, 768, 3072], P(None, 'dp', 'mp')
- ffn_in_new_average: float32 [2, 768, 3072], P(None, 'dp', 'mp')
- ffn_out_grad: float32 [2, 3072, 768], P(None, 'mp', 'dp')
- ffn_out_new_moment: float32 [2, 3072, 768], P(None, 'mp', 'dp')
- ffn_out_new_square: float32 [2, 3072, 768], P(None, 'mp', 'dp')
- ffn_out_new_weight: float32 [2, 3072, 768], P(None, 'mp', 'dp')
- ffn_out_copy: bfloat16 [2, 3072, 768], P(None, 'mp', 'dp')
- ffn_out_new_average: float32 [2, 3072, 768], P(None, 'mp', 'dp')
- norm_grad: float32 [2, 5, 768], replicated
- norm_new_moment: float32 [2, 5, 768], replicated
- norm_new_square: float32 [2, 5, 768], replicated
- norm_new_weight: float32 [2, 5, 768], replicated
- norm_new_average: float32 [2, 5, 768], replicated
- grad_norm: float32 [], replicated
Inputs may be any that keep to these rules, and one draw needn't show every extreme that they name: `counts`: row g gives the number of items of group g that show each of its 9 images, in image order; items of a group are sorted by image; each row sums to 36 and its largest entry is 10.
All inputs are finite; a program needn't handle non-finite values.
Results may differ from a plain program's by a relative error of at most 0.035.
Values may be sent and summed in bfloat16 or wider, within the bound.
No kernel may reach another device: no remote copies, remote signals or barrier semaphores. Data moves between devices by JAX's collectives and lax.ppermute only.
A program may use at most 192 MiB of HBM per device.

v0:
```python
import math

import jax
import jax.numpy as jnp
from jax import lax
from jax.sharding import PartitionSpec as P

HEAD_DIM = 64
STEP = 10


NORM_EPS = 1e-05
CLIP_NORM = 1.0
BETA_FIRST = 0.9
BETA_SECOND = 0.999
ADAM_EPS = 1e-08
WEIGHT_DECAY = 0.01
MATRIX_RATE = 0.12
NORM_RATE = 0.8
AVERAGE_CEILING = 0.999
LOW_TYPE = jnp.bfloat16
FULL_TYPE = jnp.float32
HIGHEST_PRECISION = lax.Precision.HIGHEST


def norm_forward(summed, gain, shift):
    centre = jnp.mean(summed, axis=-1, keepdims=True)
    offset = summed - centre
    spread = jnp.mean(offset * offset, axis=-1, keepdims=True)
    inverse = lax.rsqrt(spread + NORM_EPS)
    normed = offset * inverse
    return (normed * gain + shift, normed, inverse)


def norm_backward(upstream, gain, normed, inverse):
    scaled = upstream * gain
    first_mean = jnp.mean(scaled, axis=-1, keepdims=True)
    second_mean = jnp.mean(scaled * normed, axis=-1, keepdims=True)
    inward = inverse * (scaled - first_mean - normed * second_mean)
    return (inward, jnp.sum(upstream * normed, axis=(0, 1)), jnp.sum(upstream, axis=(0, 1)))


def heads_view(row_block):
    return row_block.reshape(
        row_block.shape[0], row_block.shape[1], row_block.shape[2] // HEAD_DIM, HEAD_DIM
    )


def project(row_block, weight):
    return jnp.einsum("jld,dke->kjle", row_block, weight, preferred_element_type=FULL_TYPE).astype(
        LOW_TYPE
    )


def out_product(context, weight):
    return jnp.einsum("jle,ed->jld", context, weight, preferred_element_type=FULL_TYPE).astype(
        LOW_TYPE
    )


def scaled_scores(queries, keyset):
    score_scale = 1.0 / math.sqrt(HEAD_DIM)
    return (
        jnp.einsum(
            "jqhe,jkhe->jhqk",
            heads_view(queries),
            heads_view(keyset),
            preferred_element_type=FULL_TYPE,
        )
        * score_scale
    )


def attend_forward(queries, keyset, values):
    scores = scaled_scores(queries, keyset)
    highest = jnp.max(scores, axis=-1, keepdims=True)
    powered = jnp.exp(scores - highest)
    totals = jnp.sum(powered, axis=-1, keepdims=True)
    weights = (powered / totals).astype(LOW_TYPE)
    context = jnp.einsum(
        "jhqk,jkhe->jqhe", weights, heads_view(values), preferred_element_type=FULL_TYPE
    )
    return (context.reshape(queries.shape).astype(LOW_TYPE), highest + jnp.log(totals))


def attend_backward(queries, keyset, values, logsum, grad_context):
    score_scale = 1.0 / math.sqrt(HEAD_DIM)
    softmax_out = jnp.exp(scaled_scores(queries, keyset) - logsum)
    weights = softmax_out.astype(LOW_TYPE)
    grad_heads = heads_view(grad_context)
    grad_weights = jnp.einsum(
        "jqhe,jkhe->jhqk", grad_heads, heads_view(values), preferred_element_type=FULL_TYPE
    )
    grad_values = jnp.einsum(
        "jhqk,jqhe->jkhe", weights, grad_heads, preferred_element_type=FULL_TYPE
    )
    inner_sum = jnp.sum(grad_weights * softmax_out, axis=-1, keepdims=True)
    grad_scores = (softmax_out * (grad_weights - inner_sum) * score_scale).astype(LOW_TYPE)
    grad_queries = jnp.einsum(
        "jhqk,jkhe->jqhe", grad_scores, heads_view(keyset), preferred_element_type=FULL_TYPE
    )
    grad_keys = jnp.einsum(
        "jhqk,jqhe->jkhe", grad_scores, heads_view(queries), preferred_element_type=FULL_TYPE
    )
    return (
        grad_queries.reshape(queries.shape).astype(LOW_TYPE),
        grad_keys.reshape(keyset.shape).astype(LOW_TYPE),
        grad_values.reshape(values.shape).astype(LOW_TYPE),
    )


def gelu_slope(values):
    normal_cdf = 0.5 * (1.0 + lax.erf(values * 0.7071067811865476))
    return normal_cdf + values * jnp.exp(-0.5 * values * values) * 0.3989422804014327


def adamw_step(gradient, moment, square, weight, average, rate, clip_scale):
    average_decay = min(AVERAGE_CEILING, (1.0 + STEP) / (10.0 + STEP))
    clipped = gradient * clip_scale
    moment_new = BETA_FIRST * moment + (1.0 - BETA_FIRST) * clipped
    square_new = BETA_SECOND * square + (1.0 - BETA_SECOND) * clipped * clipped
    corrected = moment_new / (1.0 - BETA_FIRST**STEP)
    denominator = jnp.sqrt(square_new / (1.0 - BETA_SECOND**STEP)) + ADAM_EPS
    weight_new = weight - rate * (corrected / denominator + WEIGHT_DECAY * weight)
    average_new = average_decay * average + (1.0 - average_decay) * weight_new
    return (clipped, moment_new, square_new, weight_new, average_new)


def local(
    language,
    images,
    counts,
    language_cot,
    vision_cot,
    attn_in_weight,
    attn_in_moment,
    attn_in_square,
    attn_in_average,
    attn_out_weight,
    attn_out_moment,
    attn_out_square,
    attn_out_average,
    ffn_in_weight,
    ffn_in_moment,
    ffn_in_square,
    ffn_in_average,
    ffn_out_weight,
    ffn_out_moment,
    ffn_out_square,
    ffn_out_average,
    norm_weight,
    norm_moment,
    norm_square,
    norm_average,
):
    attend_in, attend_out, expand_in, expand_out = (
        lax.all_gather(attn_in_weight.astype(LOW_TYPE), "dp", axis=1, tiled=True),
        lax.all_gather(attn_out_weight.astype(LOW_TYPE), "dp", axis=2, tiled=True),
        lax.all_gather(ffn_in_weight.astype(LOW_TYPE), "dp", axis=1, tiled=True),
        lax.all_gather(ffn_out_weight.astype(LOW_TYPE), "dp", axis=2, tiled=True),
    )

    def gather_rows(lang_part, vis_part):
        return (
            lax.all_gather(lang_part, "mp", axis=0, tiled=True),
            lax.all_gather(vis_part, "mp", axis=0, tiled=True),
        )

    def reduce_rows(lang_part, vis_part):
        return (
            lax.psum_scatter(lang_part, "mp", scatter_dimension=0, tiled=True).astype(jnp.float32),
            lax.psum_scatter(vis_part, "mp", scatter_dimension=0, tiled=True).astype(jnp.float32),
        )

    def gather_grads(lang_part, vis_part):
        return (
            lax.all_gather(lang_part, "mp", axis=0, tiled=True),
            lax.all_gather(vis_part, "mp", axis=0, tiled=True),
        )

    def reduce_grads(lang_part, vis_part):
        return (
            lax.psum_scatter(lang_part, "mp", scatter_dimension=0, tiled=True).astype(jnp.float32),
            lax.psum_scatter(vis_part, "mp", scatter_dimension=0, tiled=True).astype(jnp.float32),
        )

    own_items = language.shape[0]
    group_items = own_items * lax.axis_size("mp")
    first_item = lax.axis_index("mp") * own_items
    bounds = jnp.cumsum(counts[0])
    positions = jnp.arange(group_items, dtype=jnp.int32)
    item_image = jnp.sum((bounds[None, :] <= positions[:, None]).astype(jnp.int32), axis=1)
    selector = (
        item_image[:, None] == jnp.arange(images.shape[0], dtype=jnp.int32)[None, :]
    ).astype(LOW_TYPE)
    vis_all = jnp.einsum("ji,ird->jrd", selector, images, preferred_element_type=FULL_TYPE).astype(
        LOW_TYPE
    )
    own_selector = lax.dynamic_slice_in_dim(selector, first_item, own_items, 0).astype(FULL_TYPE)
    starts = [
        language.astype(FULL_TYPE),
        lax.dynamic_slice_in_dim(vis_all, first_item, own_items, 0).astype(FULL_TYPE),
    ]
    norm_gains = norm_weight[0]
    norm_shifts = norm_weight[1]
    lang_all = lax.all_gather(language, "mp", axis=0, tiled=True)
    cross_rows = [lang_all, vis_all]
    cross_triples = [project(cross_rows[stream], attend_in[0]) for stream in range(2)]
    cross_attend = [
        attend_forward(
            cross_triples[stream][0], cross_triples[1 - stream][1], cross_triples[1 - stream][2]
        )
        for stream in range(2)
    ]
    branch_sum = reduce_rows(
        out_product(cross_attend[0][0], attend_out[0]),
        out_product(cross_attend[1][0], attend_out[0]),
    )
    after_cross = [
        norm_forward(starts[stream] + branch_sum[stream], norm_gains[0], norm_shifts[0])
        for stream in range(2)
    ]
    self_rows = gather_rows(after_cross[0][0].astype(LOW_TYPE), after_cross[1][0].astype(LOW_TYPE))
    self_triples = [project(self_rows[stream], attend_in[1 + stream]) for stream in range(2)]
    self_attend = [
        attend_forward(self_triples[stream][0], self_triples[stream][1], self_triples[stream][2])
        for stream in range(2)
    ]
    branch_sum = reduce_rows(
        out_product(self_attend[0][0], attend_out[1]), out_product(self_attend[1][0], attend_out[2])
    )
    after_self = [
        norm_forward(
            after_cross[stream][0] + branch_sum[stream],
            norm_gains[1 + stream],
            norm_shifts[1 + stream],
        )
        for stream in range(2)
    ]
    feed_rows = gather_rows(after_self[0][0].astype(LOW_TYPE), after_self[1][0].astype(LOW_TYPE))
    hidden = [
        jnp.einsum(
            "jld,df->jlf", feed_rows[stream], expand_in[stream], preferred_element_type=FULL_TYPE
        )
        for stream in range(2)
    ]
    active = [
        jax.nn.gelu(hidden[stream], approximate=False).astype(LOW_TYPE) for stream in range(2)
    ]
    branch_sum = reduce_rows(
        jnp.einsum(
            "jlf,fd->jld", active[0], expand_out[0], preferred_element_type=FULL_TYPE
        ).astype(LOW_TYPE),
        jnp.einsum(
            "jlf,fd->jld", active[1], expand_out[1], preferred_element_type=FULL_TYPE
        ).astype(LOW_TYPE),
    )
    after_feed = [
        norm_forward(
            after_self[stream][0] + branch_sum[stream],
            norm_gains[3 + stream],
            norm_shifts[3 + stream],
        )
        for stream in range(2)
    ]
    gain_terms = [None] * 5
    shift_terms = [None] * 5
    upstream = [language_cot.astype(FULL_TYPE), vision_cot.astype(FULL_TYPE)]
    inward = []
    for stream in range(2):
        grad_sum, gain_term, shift_term = norm_backward(
            upstream[stream], norm_gains[3 + stream], after_feed[stream][1], after_feed[stream][2]
        )
        gain_terms[3 + stream] = gain_term
        shift_terms[3 + stream] = shift_term
        inward.append(grad_sum)
    branch = gather_grads(inward[0].astype(LOW_TYPE), inward[1].astype(LOW_TYPE))
    down_grads = []
    up_grads = []
    back_terms = []
    for stream in range(2):
        down_grads.append(
            jnp.einsum(
                "jlf,jld->fd", active[stream], branch[stream], preferred_element_type=FULL_TYPE
            )
        )
        grad_active = jnp.einsum(
            "jld,fd->jlf", branch[stream], expand_out[stream], preferred_element_type=FULL_TYPE
        )
        grad_hidden = (grad_active * gelu_slope(hidden[stream])).astype(LOW_TYPE)
        up_grads.append(
            jnp.einsum(
                "jld,jlf->df", feed_rows[stream], grad_hidden, preferred_element_type=FULL_TYPE
            )
        )
        back_terms.append(
            jnp.einsum(
                "jlf,df->jld", grad_hidden, expand_in[stream], preferred_element_type=FULL_TYPE
            ).astype(LOW_TYPE)
        )
    returned = reduce_grads(back_terms[0], back_terms[1])
    upstream = [inward[stream] + returned[stream] for stream in range(2)]
    inward = []
    for stream in range(2):
        grad_sum, gain_term, shift_term = norm_backward(
            upstream[stream], norm_gains[1 + stream], after_self[stream][1], after_self[stream][2]
        )
        gain_terms[1 + stream] = gain_term
        shift_terms[1 + stream] = shift_term
        inward.append(grad_sum)
    branch = gather_grads(inward[0].astype(LOW_TYPE), inward[1].astype(LOW_TYPE))
    in_grads = []
    out_grads = []
    back_terms = []
    for stream in range(2):
        out_grads.append(
            jnp.einsum(
                "jle,jld->ed",
                self_attend[stream][0],
                branch[stream],
                preferred_element_type=FULL_TYPE,
            )
        )
        grad_context = jnp.einsum(
            "jld,ed->jle", branch[stream], attend_out[1 + stream], preferred_element_type=FULL_TYPE
        ).astype(LOW_TYPE)
        triple = self_triples[stream]
        grad_query, grad_key, grad_value = attend_backward(
            triple[0], triple[1], triple[2], self_attend[stream][1], grad_context
        )
        stacked = jnp.stack([grad_query, grad_key, grad_value])
        in_grads.append(
            jnp.einsum(
                "jld,kjle->dke", self_rows[stream], stacked, preferred_element_type=FULL_TYPE
            )
        )
        back_terms.append(
            jnp.einsum(
                "kjle,dke->jld", stacked, attend_in[1 + stream], preferred_element_type=FULL_TYPE
            ).astype(LOW_TYPE)
        )
    returned = reduce_grads(back_terms[0], back_terms[1])
    upstream = [inward[stream] + returned[stream] for stream in range(2)]
    inward = []
    cross_gain = []
    cross_shift = []
    for stream in range(2):
        grad_sum, gain_term, shift_term = norm_backward(
            upstream[stream], norm_gains[0], after_cross[stream][1], after_cross[stream][2]
        )
        cross_gain.append(gain_term)
        cross_shift.append(shift_term)
        inward.append(grad_sum)
    gain_terms[0] = cross_gain[0] + cross_gain[1]
    shift_terms[0] = cross_shift[0] + cross_shift[1]
    branch = gather_grads(inward[0].astype(LOW_TYPE), inward[1].astype(LOW_TYPE))
    cross_out_grad = jnp.einsum(
        "jle,jld->ed", cross_attend[0][0], branch[0], preferred_element_type=FULL_TYPE
    ) + jnp.einsum("jle,jld->ed", cross_attend[1][0], branch[1], preferred_element_type=FULL_TYPE)
    pieces = []
    for stream in range(2):
        grad_context = jnp.einsum(
            "jld,ed->jle", branch[stream], attend_out[0], preferred_element_type=FULL_TYPE
        ).astype(LOW_TYPE)
        pieces.append(
            attend_backward(
                cross_triples[stream][0],
                cross_triples[1 - stream][1],
                cross_triples[1 - stream][2],
                cross_attend[stream][1],
                grad_context,
            )
        )
    stacks = [
        jnp.stack([pieces[stream][0], pieces[1 - stream][1], pieces[1 - stream][2]])
        for stream in range(2)
    ]
    cross_in_grad = jnp.einsum(
        "jld,kjle->dke", lang_all, stacks[0], preferred_element_type=FULL_TYPE
    ) + jnp.einsum("jld,kjle->dke", vis_all, stacks[1], preferred_element_type=FULL_TYPE)
    lang_term = jnp.einsum(
        "kjle,dke->jld", stacks[0], attend_in[0], preferred_element_type=FULL_TYPE
    ).astype(LOW_TYPE)
    vis_term = jnp.einsum(
        "kjle,dke->jld", stacks[1], attend_in[0], preferred_element_type=FULL_TYPE
    ).astype(LOW_TYPE)
    language_grad = (
        lax.psum_scatter(lang_term, "mp", scatter_dimension=0, tiled=True).astype(jnp.float32)
        + inward[0]
    )
    image_term = jnp.einsum(
        "ji,jrd->ird", selector, vis_term, preferred_element_type=FULL_TYPE
    ) + jnp.einsum("ji,jrd->ird", own_selector, inward[1], precision=HIGHEST_PRECISION)
    image_grad = lax.psum(image_term.astype(jnp.bfloat16), "mp").astype(jnp.float32)
    grad_attend_in = jnp.stack([cross_in_grad, in_grads[0], in_grads[1]])
    grad_attend_out = jnp.stack([cross_out_grad, out_grads[0], out_grads[1]])
    grad_expand_in = jnp.stack(up_grads)
    grad_expand_out = jnp.stack(down_grads)
    norm_partial = jnp.stack([jnp.stack(gain_terms), jnp.stack(shift_terms)])
    norm_total = lax.psum(norm_partial, ("dp", "mp"))
    summed = lax.psum((grad_attend_in, grad_attend_out, grad_expand_in, grad_expand_out), "dp")
    position = lax.axis_index("dp")
    shards = (
        lax.dynamic_slice_in_dim(
            summed[0], position * attn_in_weight.shape[1], attn_in_weight.shape[1], 1
        ),
        lax.dynamic_slice_in_dim(
            summed[1], position * attn_out_weight.shape[2], attn_out_weight.shape[2], 2
        ),
        lax.dynamic_slice_in_dim(
            summed[2], position * ffn_in_weight.shape[1], ffn_in_weight.shape[1], 1
        ),
        lax.dynamic_slice_in_dim(
            summed[3], position * ffn_out_weight.shape[2], ffn_out_weight.shape[2], 2
        ),
    )
    local_squares = (
        jnp.sum(shards[0] * shards[0])
        + jnp.sum(shards[1] * shards[1])
        + jnp.sum(shards[2] * shards[2])
        + jnp.sum(shards[3] * shards[3])
    )
    total_squares = lax.psum(local_squares, ("dp", "mp"))
    total_squares = total_squares + jnp.sum(norm_total * norm_total)
    grad_norm = jnp.sqrt(total_squares)
    clip_scale = CLIP_NORM / jnp.maximum(grad_norm, CLIP_NORM)
    attn_in_new = adamw_step(
        shards[0],
        attn_in_moment,
        attn_in_square,
        attn_in_weight,
        attn_in_average,
        MATRIX_RATE,
        clip_scale,
    )
    attn_out_new = adamw_step(
        shards[1],
        attn_out_moment,
        attn_out_square,
        attn_out_weight,
        attn_out_average,
        MATRIX_RATE,
        clip_scale,
    )
    ffn_in_new = adamw_step(
        shards[2],
        ffn_in_moment,
        ffn_in_square,
        ffn_in_weight,
        ffn_in_average,
        MATRIX_RATE,
        clip_scale,
    )
    ffn_out_new = adamw_step(
        shards[3],
        ffn_out_moment,
        ffn_out_square,
        ffn_out_weight,
        ffn_out_average,
        MATRIX_RATE,
        clip_scale,
    )
    norm_new = adamw_step(
        norm_total, norm_moment, norm_square, norm_weight, norm_average, NORM_RATE, clip_scale
    )
    return (
        after_feed[0][0].astype(LOW_TYPE),
        after_feed[1][0].astype(LOW_TYPE),
        language_grad,
        image_grad,
        attn_in_new[0],
        attn_in_new[1],
        attn_in_new[2],
        attn_in_new[3],
        attn_in_new[3].astype(LOW_TYPE),
        attn_in_new[4],
        attn_out_new[0],
        attn_out_new[1],
        attn_out_new[2],
        attn_out_new[3],
        attn_out_new[3].astype(LOW_TYPE),
        attn_out_new[4],
        ffn_in_new[0],
        ffn_in_new[1],
        ffn_in_new[2],
        ffn_in_new[3],
        ffn_in_new[3].astype(LOW_TYPE),
        ffn_in_new[4],
        ffn_out_new[0],
        ffn_out_new[1],
        ffn_out_new[2],
        ffn_out_new[3],
        ffn_out_new[3].astype(LOW_TYPE),
        ffn_out_new[4],
        norm_new[0],
        norm_new[1],
        norm_new[2],
        norm_new[3],
        norm_new[4],
        grad_norm,
    )


def solution(mesh):
    in_specs = (
        P(("dp", "mp"), None, None),
        P("dp", None, None),
        P("dp", None),
        P(("dp", "mp"), None, None),
        P(("dp", "mp"), None, None),
        P(None, "dp", None, "mp"),
        P(None, "dp", None, "mp"),
        P(None, "dp", None, "mp"),
        P(None, "dp", None, "mp"),
        P(None, "mp", "dp"),
        P(None, "mp", "dp"),
        P(None, "mp", "dp"),
        P(None, "mp", "dp"),
        P(None, "dp", "mp"),
        P(None, "dp", "mp"),
        P(None, "dp", "mp"),
        P(None, "dp", "mp"),
        P(None, "mp", "dp"),
        P(None, "mp", "dp"),
        P(None, "mp", "dp"),
        P(None, "mp", "dp"),
        P(),
        P(),
        P(),
        P(),
    )
    out_specs = (
        P(("dp", "mp"), None, None),
        P(("dp", "mp"), None, None),
        P(("dp", "mp"), None, None),
        P("dp", None, None),
        P(None, "dp", None, "mp"),
        P(None, "dp", None, "mp"),
        P(None, "dp", None, "mp"),
        P(None, "dp", None, "mp"),
        P(None, "dp", None, "mp"),
        P(None, "dp", None, "mp"),
        P(None, "mp", "dp"),
        P(None, "mp", "dp"),
        P(None, "mp", "dp"),
        P(None, "mp", "dp"),
        P(None, "mp", "dp"),
        P(None, "mp", "dp"),
        P(None, "dp", "mp"),
        P(None, "dp", "mp"),
        P(None, "dp", "mp"),
        P(None, "dp", "mp"),
        P(None, "dp", "mp"),
        P(None, "dp", "mp"),
        P(None, "mp", "dp"),
        P(None, "mp", "dp"),
        P(None, "mp", "dp"),
        P(None, "mp", "dp"),
        P(None, "mp", "dp"),
        P(None, "mp", "dp"),
        P(),
        P(),
        P(),
        P(),
        P(),
        P(),
    )
    return jax.shard_map(local, mesh=mesh, in_specs=in_specs, out_specs=out_specs, check_vma=False)
```

profile of v0, /device:TPU:0, one launch (start us, length us, event | category | flops | bytes accessed | tf_op | source)
XLA Modules:
  0.0 1477.5 jit_solution(9022954642787239009)
XLA Ops:
  10.8 16.6 %all_gather.47 = bf16[3,192,768]{1,0,2:T(4,128)(2,1)S(1)} all-gather(bf16[3,192,96]{1,0,2:T(4,128)(2,1)S(1)} %copy.569), channel_id=1, replica_groups=mesh['dp'=8,'mp'=4] {'dp'}, dimensions={2}, use_global_device_ids=true | all-gather | bytes 995328 | tf_op jit(solution)/shard_map/all_gather | solution.py:158
  34.4 18.8 %all-gather.15.cloned.1.call-done = bf16[3,768,3,192]{3,2,0,1:T(4,128)(2,1)} async-done(((bf16[3,96,3,192]{3,2,0,1:T(4,128)(2,1)}), bf16[3,768,3,192]{3,2,0,1:T(4,128)(2,1)}) %all-gather.15.cloned.1.call-update) | async-done | bytes 2654224 | tf_op jit(solution)/shard_map/all_gather | solution.py:157
  61.1 26.7 %all-gather.17.cloned.1.call-done = bf16[36,20,768]{2,1,0:T(8,128)(2,1)} async-done(((bf16[9,20,768]{2,1,0:T(8,128)(2,1)}), bf16[36,20,768]{2,1,0:T(8,128)(2,1)}) %all-gather.17.cloned.1.call-update) | async-done | bytes 1105936 | tf_op jit(solution)/shard_map/all_gather | solution.py:206
  116.0 29.9 %reduce-scatter.12.cloned.1.call-done = bf16[9,20,768]{2,1,0:T(8,128)(2,1)} async-done(((bf16[36,20,768]{2,1,0:T(8,128)(2,1)}), bf16[9,20,768]{2,1,0:T(8,128)(2,1)}) %reduce-scatter.12.cloned.1.call-update) | async-done | bytes 276496 | tf_op jit(solution)/shard_map/reduce_scatter | solution.py:171
  200.8 28.4 %reduce-scatter.18.cloned.1.call-done = bf16[9,36,768]{2,1,0:T(8,128)(2,1)} async-done(((bf16[36,36,768]{2,1,0:T(8,128)(2,1)}), bf16[9,36,768]{2,1,0:T(8,128)(2,1)}) %reduce-scatter.18.cloned.1.call-update) | async-done | bytes 497680 | tf_op jit(solution)/shard_map/reduce_scatter | solution.py:172
  243.7 18.8 %reduce-scatter.14.cloned.1.call-done = bf16[9,20,768]{2,1,0:T(8,128)(2,1)} async-done(((bf16[36,20,768]{2,1,0:T(8,128)(2,1)}), bf16[9,20,768]{2,1,0:T(8,128)(2,1)}) %reduce-scatter.14.cloned.1.call-update) | async-done | bytes 276496 | tf_op jit(solution)/shard_map/reduce_scatter | solution.py:171
  265.2 46.2 %all-gather.27.cloned.1.call-done = bf16[36,36,768]{2,1,0:T(8,128)(2,1)} async-done(((bf16[9,36,768]{2,1,0:T(8,128)(2,1)}), bf16[36,36,768]{2,1,0:T(8,128)(2,1)}) %all-gather.27.cloned.1.call-update) | async-done | bytes 1990672 | tf_op jit(solution)/shard_map/all_gather | solution.py:166
  341.8 8.6 fusion.319
  350.4 6.5 copy.729
  356.9 16.4 %all-gather.23.cloned.1.call-done = bf16[2,768,768]{2,1,0:T(8,128)(2,1)} async-done(((bf16[2,96,768]{2,1,0:T(8,128)(2,1)}), bf16[2,768,768]{2,1,0:T(8,128)(2,1)}) %all-gather.23.cloned.1.call-update) | async-done | bytes 2359312 | tf_op jit(solution)/shard_map/all_gather | solution.py:159
  373.3 35.0 %all-gather.21.cloned.1.call-done = bf16[36,20,768]{2,1,0:T(8,128)(2,1)} async-done(((bf16[9,20,768]{2,1,0:T(8,128)(2,1)}), bf16[36,20,768]{2,1,0:T(8,128)(2,1)}) %all-gather.21.cloned.1.call-update) | async-done | bytes 1105936 | tf_op jit(solution)/shard_map/all_gather | solution.py:165
  419.8 35.7 %reduce-scatter.20.cloned.1.call-done = bf16[9,36,768]{2,1,0:T(8,128)(2,1)} async-done(((bf16[36,36,768]{2,1,0:T(8,128)(2,1)}), bf16[9,36,768]{2,1,0:T(8,128)(2,1)}) %reduce-scatter.20.cloned.1.call-update) | async-done | bytes 497680 | tf_op jit(solution)/shard_map/reduce_scatter | solution.py:172
  461.1 6.5 copy.732
  467.5 21.3 %reduce-scatter.16.cloned.1.call-done = bf16[9,20,768]{2,1,0:T(8,128)(2,1)} async-done(((bf16[36,20,768]{2,1,0:T(8,128)(2,1)}), bf16[9,20,768]{2,1,0:T(8,128)(2,1)}) %reduce-scatter.16.cloned.1.call-update) | async-done | bytes 276496 | tf_op jit(solution)/shard_map/reduce_scatter | solution.py:171
  493.1 44.7 %all-gather.29.cloned.1.call-done = bf16[36,36,768]{2,1,0:T(8,128)(2,1)} async-done(((bf16[9,36,768]{2,1,0:T(8,128)(2,1)}), bf16[36,36,768]{2,1,0:T(8,128)(2,1)}) %all-gather.29.cloned.1.call-update) | async-done | bytes 1990672 | tf_op jit(solution)/shard_map/all_gather | solution.py:166
  537.8 13.9 fusion.6
  556.5 15.2 %all-gather.31.cloned.1.call-done = bf16[36,20,768]{2,1,0:T(8,128)(2,1)} async-done(((bf16[9,20,768]{2,1,0:T(8,128)(2,1)}), bf16[36,20,768]{2,1,0:T(8,128)(2,1)}) %all-gather.31.cloned.1.call-update) | async-done | bytes 1105936 | tf_op jit(solution)/shard_map/all_gather | solution.py:177
  578.8 39.9 %reduce-scatter.22.cloned.1.call-done = bf16[9,36,768]{2,1,0:T(8,128)(2,1)} async-done(((bf16[36,36,768]{2,1,0:T(8,128)(2,1)}), bf16[9,36,768]{2,1,0:T(8,128)(2,1)}) %reduce-scatter.22.cloned.1.call-update) | async-done | bytes 497680 | tf_op jit(solution)/shard_map/reduce_scatter | solution.py:172
  627.0 25.0 %reduce-scatter.24.cloned.1.call-done = bf16[9,20,768]{2,1,0:T(8,128)(2,1)} async-done(((bf16[36,20,768]{2,1,0:T(8,128)(2,1)}), bf16[9,20,768]{2,1,0:T(8,128)(2,1)}) %reduce-scatter.24.cloned.1.call-update) | async-done | bytes 276496 | tf_op jit(solution)/shard_map/reduce_scatter | solution.py:183
  657.7 43.2 %all-gather.37.cloned.1.call-done = bf16[36,36,768]{2,1,0:T(8,128)(2,1)} async-done(((bf16[9,36,768]{2,1,0:T(8,128)(2,1)}), bf16[36,36,768]{2,1,0:T(8,128)(2,1)}) %all-gather.37.cloned.1.call-update) | async-done | bytes 1990672 | tf_op jit(solution)/shard_map/all_gather | solution.py:178
  713.0 21.7 %all-gather.33.cloned.1.call-done = bf16[36,20,768]{2,1,0:T(8,128)(2,1)} async-done(((bf16[9,20,768]{2,1,0:T(8,128)(2,1)}), bf16[36,20,768]{2,1,0:T(8,128)(2,1)}) %all-gather.33.cloned.1.call-update) | async-done | bytes 1105936 | tf_op jit(solution)/shard_map/all_gather | solution.py:177
  770.5 11.5 reduce-scatter.28.cloned.1.call-done
  794.1 21.1 %reduce-scatter.26.cloned.1.call-done = bf16[9,20,768]{2,1,0:T(8,128)(2,1)} async-done(((bf16[36,20,768]{2,1,0:T(8,128)(2,1)}), bf16[9,20,768]{2,1,0:T(8,128)(2,1)}) %reduce-scatter.26.cloned.1.call-update) | async-done | bytes 276496 | tf_op jit(solution)/shard_map/reduce_scatter | solution.py:183
  820.1 44.1 %all-gather.39.cloned.1.call-done = bf16[36,36,768]{2,1,0:T(8,128)(2,1)} async-done(((bf16[9,36,768]{2,1,0:T(8,128)(2,1)}), bf16[36,36,768]{2,1,0:T(8,128)(2,1)}) %all-gather.39.cloned.1.call-update) | async-done | bytes 1990672 | tf_op jit(solution)/shard_map/all_gather | solution.py:178
  886.7 6.8 fusion.102
  935.4 18.3 %fusion.117 = bf16[36,20,3,64]{3,1,2,0:T(8,128)(2,1)} fusion(f32[36,3,20,36]{3,2,1,0:T(8,128)} %fusion.190, bf16[36,36,3,64]{3,2,1,0:T(4,128)(2,1)} %reshape_squeeze.26, f32[36,3,20,36]{3,2,1,0:T(8,128)} %copy-done.19, f32[36,3,20]{2,1,0:T(4,128)} %log_add_fusion.3), kind=kOutput, calls=%fused_computation.206 | convolution fusion | flops 10638035 | bytes 1404864 | tf_op jit(solution)/shard_map/jhqk,jkhe->jqhe/dot_general | solution.py:99
  966.3 18.5 %fusion.97 = bf16[36,36,3,64]{3,1,2,0:T(8,128)(2,1)} fusion(f32[36,3,20,36]{3,2,1,0:T(8,128)} %fusion.190, f32[36,3,20,36]{3,2,1,0:T(8,128)} %copy-done.19, f32[36,3,20]{2,1,0:T(4,128)} %log_add_fusion.3, bf16[36,20,3,64]{3,2,0,1:T(4,128)(2,1)S(1)} %copy-done.43), kind=kOutput, calls=%fused_computation.170 | convolution fusion | flops 10748627 | bytes 1404864 | tf_op jit(solution)/shard_map/jhqk,jqhe->jkhe/dot_general | solution.py:102
  1018.7 27.0 %all-gather.41.cloned.1.call-done = bf16[36,36,768]{2,1,0:T(8,128)(2,1)} async-done(((bf16[9,36,768]{2,1,0:T(8,128)(2,1)}), bf16[36,36,768]{2,1,0:T(8,128)(2,1)}) %all-gather.41.cloned.1.call-update) | async-done | bytes 1990672 | tf_op jit(solution)/shard_map/all_gather | solution.py:178
  1122.5 22.3 %all-reduce.5.cloned.1.call-done = bf16[9,36,768]{2,0,1:T(8,128)(2,1)} async-done(((bf16[9,36,768]{2,0,1:T(8,128)(2,1)}), bf16[9,36,768]{2,0,1:T(8,128)(2,1)}) %all-reduce.5.cloned.1.call-update) | async-done | bytes 497680 | tf_op jit(solution)/shard_map/psum | solution.py:394
  1147.1 216.5 %all-reduce.7.cloned.1.call-done = (f32[3,768,3,192]{1,3,2,0:T(8,128)}, f32[3,192,768]{2,1,0:T(8,128)}, f32[2,768,768]{2,1,0:T(8,128)}, f32[2,768,768]{1,2,0:T(8,128)}) async-done(((f32[3,768,3,192]{1,3,2,0:T(8,128)}, f32[3,192,768]{2,1,0:T(8,128)}, f32[2,768,768]{2,1,0:T(8,128)}, f32[2,768,768]{1,2,0:T(8,128)}), (f32[3,768,3,192]{1,3,2,0:T(8,128)}, f32[3,192,768]{2,1,0:T(8,128)}, f32[2,768,768]{2,1,0:T(8,128)}, ...) | async-done | bytes 16515088 | tf_op jit(solution)/shard_map/psum | solution.py:401
  1374.1 23.5 %reduce-scatter.32.cloned.1.call-done = bf16[9,20,768]{2,1,0:T(8,128)(2,1)} async-done(((bf16[36,20,768]{2,1,0:T(8,128)(2,1)}), bf16[9,20,768]{2,1,0:T(8,128)(2,1)}) %reduce-scatter.32.cloned.1.call-update) | async-done | bytes 276496 | tf_op jit(solution)/shard_map/reduce_scatter | solution.py:388
  1399.8 39.8 %all-reduce = (f32[]{:T(128)}, f32[2,5,768]{2,1,0:T(8,128)S(1)}) all-reduce(f32[]{:T(128)S(6)} %add.415, f32[2,5,768]{2,1,0:T(8,128)S(1)} %pad_maximum_fusion.11), channel_id=1, replica_groups=mesh['dp'=8,'mp'=4] {'dp','mp'}, use_global_device_ids=true, to_apply=%region_58.59 | all-reduce | flops 7681 | bytes 61448 | tf_op jit(solution)/shard_map/psum | solution.py:423
  (697 shorter events, 486.8 us)
Async XLA Ops:
  7.2 46.0 %all-gather.15.cloned.1.call-start = ((), (), s32[]{:S(2)}) async-start(), calls=%async_computation.11 | async-start | bytes 5308416 | tf_op jit(solution)/shard_map/all_gather | solution.py:157
  9.8 78.0 %all-gather.17.cloned.1.call-start = ((), (), s32[]{:S(2)}) async-start(), calls=%async_computation.12 | async-start | bytes 1658880 | tf_op jit(solution)/shard_map/all_gather | solution.py:206
  10.6 135.3 %reduce-scatter.12.cloned.1.call-start = ((), (), s32[]{:S(2)}) async-start(), calls=%async_computation.13 | async-start | bytes 1658880 | tf_op jit(solution)/shard_map/reduce_scatter | solution.py:171
  115.1 67.0 %all-gather.19.cloned.1.call-start = ((), (), s32[]{:S(2)}) async-start(), calls=%async_computation.14 | async-start | bytes 1658880 | tf_op jit(solution)/shard_map/all_gather | solution.py:165
  150.2 79.0 %reduce-scatter.18.cloned.1.call-start = ((), (), s32[]{:S(2)}) async-start(), calls=%async_computation.20 | async-start | bytes 2764800 | tf_op jit(solution)/shard_map/reduce_scatter | solution.py:172
  170.9 91.6 %reduce-scatter.14.cloned.1.call-start = ((), (), s32[]{:S(2)}) async-start(), calls=%async_computation.15 | async-start | bytes 1658880 | tf_op jit(solution)/shard_map/reduce_scatter | solution.py:171
  200.5 111.0 %all-gather.27.cloned.1.call-start = ((), (), s32[]{:S(2)}) async-start(), calls=%async_computation.21 | async-start | bytes 2764800 | tf_op jit(solution)/shard_map/all_gather | solution.py:166
  234.4 107.4 %all-gather.25.cloned.1.call-start = ((), (), s32[]{:S(2)}) async-start(), calls=%async_computation.18 | async-start | bytes 2654208 | tf_op jit(solution)/shard_map/all_gather | solution.py:160
  236.7 136.6 %all-gather.23.cloned.1.call-start = ((), (), s32[]{:S(2)}) async-start(), calls=%async_computation.17 | async-start | bytes 2654208 | tf_op jit(solution)/shard_map/all_gather | solution.py:159
  238.6 169.8 %all-gather.21.cloned.1.call-start = ((), (), s32[]{:S(2)}) async-start(), calls=%async_computation.16 | async-start | bytes 1658880 | tf_op jit(solution)/shard_map/all_gather | solution.py:165
  265.2 190.4 %reduce-scatter.20.cloned.1.call-start = ((), (), s32[]{:S(2)}) async-start(), calls=%async_computation.22 | async-start | bytes 2764800 | tf_op jit(solution)/shard_map/reduce_scatter | solution.py:172
  340.6 148.2 %reduce-scatter.16.cloned.1.call-start = ((), (), s32[]{:S(2)}) async-start(), calls=%async_computation.19 | async-start | bytes 1658880 | tf_op jit(solution)/shard_map/reduce_scatter | solution.py:171
  419.8 118.1 %all-gather.29.cloned.1.call-start = ((), (), s32[]{:S(2)}) async-start(), calls=%async_computation.23 | async-start | bytes 2764800 | tf_op jit(solution)/shard_map/all_gather | solution.py:166
  457.7 330.3 %copy-start.76 = (f32[9,36]{0,1:T(8,128)}, f32[9,36]{0,1:T(8,128)S(1)}, u32[]{:S(2)}) copy-start(f32[9,36]{0,1:T(8,128)S(1)} %broadcast_multiply_fusion.8) | copy-start | bytes 3892
  458.8 329.2 %copy-start.83 = (f32[9,36]{0,1:T(8,128)}, f32[9,36]{0,1:T(8,128)S(1)}, u32[]{:S(2)}) copy-start(f32[9,36]{0,1:T(8,128)S(1)} %add_rsqrt_fusion.1) | copy-start | bytes 3892
  460.8 110.9 %all-gather.31.cloned.1.call-start = ((), (), s32[]{:S(2)}) async-start(), calls=%async_computation.25 | async-start | bytes 1658880 | tf_op jit(solution)/shard_map/all_gather | solution.py:177
  493.1 125.7 %reduce-scatter.22.cloned.1.call-start = ((), (), s32[]{:S(2)}) async-start(), calls=%async_computation.24 | async-start | bytes 2764800 | tf_op jit(solution)/shard_map/reduce_scatter | solution.py:172
  556.4 95.6 %reduce-scatter.24.cloned.1.call-start = ((), (), s32[]{:S(2)}) async-start(), calls=%async_computation.26 | async-start | bytes 1658880 | tf_op jit(solution)/shard_map/reduce_scatter | solution.py:183
  578.6 122.3 %all-gather.37.cloned.1.call-start = ((), (), s32[]{:S(2)}) async-start(), calls=%async_computation.30 | async-start | bytes 2764800 | tf_op jit(solution)/shard_map/all_gather | solution.py:178
  627.0 107.7 %all-gather.33.cloned.1.call-start = ((), (), s32[]{:S(2)}) async-start(), calls=%async_computation.27 | async-start | bytes 1658880 | tf_op jit(solution)/shard_map/all_gather | solution.py:177
  657.6 124.3 %reduce-scatter.28.cloned.1.call-start = ((), (), s32[]{:S(2)}) async-start(), calls=%async_computation.31 | async-start | bytes 2764800 | tf_op jit(solution)/shard_map/reduce_scatter | solution.py:184
  711.0 104.2 %reduce-scatter.26.cloned.1.call-start = ((), (), s32[]{:S(2)}) async-start(), calls=%async_computation.28 | async-start | bytes 1658880 | tf_op jit(solution)/shard_map/reduce_scatter | solution.py:183
  770.4 93.8 %all-gather.39.cloned.1.call-start = ((), (), s32[]{:S(2)}) async-start(), calls=%async_computation.32 | async-start | bytes 2764800 | tf_op jit(solution)/shard_map/all_gather | solution.py:178
  791.3 136.6 %all-gather.35.cloned.1.call-start = ((), (), s32[]{:S(2)}) async-start(), calls=%async_computation.29 | async-start | bytes 1658880 | tf_op jit(solution)/shard_map/all_gather | solution.py:177
  819.9 171.3 %reduce-scatter.30.cloned.1.call-start = ((), (), s32[]{:S(2)}) async-start(), calls=%async_computation.33 | async-start | bytes 2764800 | tf_op jit(solution)/shard_map/reduce_scatter | solution.py:184
  912.8 133.0 %all-gather.41.cloned.1.call-start = ((), (), s32[]{:S(2)}) async-start(), calls=%async_computation.34 | async-start | bytes 2764800 | tf_op jit(solution)/shard_map/all_gather | solution.py:178
  998.8 146.0 %all-reduce.5.cloned.1.call-start = ((), (), s32[]{:S(2)}) async-start(), calls=%async_computation.36 | async-start | bytes 1769472 | tf_op jit(solution)/shard_map/psum | solution.py:394
  1099.1 264.5 %all-reduce.7.cloned.1.call-start = ((), (), s32[]{:S(2)}) async-start(), calls=%async_computation.37 | async-start | bytes 33030144 | tf_op jit(solution)/shard_map/psum | solution.py:401
  1108.3 289.3 %reduce-scatter.32.cloned.1.call-start = ((), (), s32[]{:S(2)}) async-start(), calls=%async_computation.35 | async-start | bytes 1658880 | tf_op jit(solution)/shard_map/reduce_scatter | solution.py:388
  1122.4 275.2 %copy-start.9 = (bf16[9,20,768]{2,1,0:T(8,128)(2,1)S(1)}, bf16[9,20,768]{2,1,0:T(8,128)(2,1)}, u32[]{:S(2)}) copy-start(bf16[9,20,768]{2,1,0:T(8,128)(2,1)} %param.25) | copy-start | bytes 829444
  1122.4 275.2 %copy-start.13 = (bf16[9,20,768]{2,1,0:T(8,128)(2,1)S(1)}, bf16[9,20,768]{2,1,0:T(8,128)(2,1)}, u32[]{:S(2)}) copy-start(bf16[9,20,768]{2,1,0:T(8,128)(2,1)} %reduce-scatter.12.cloned.1.call-done) | copy-start | bytes 829444
  1122.4 275.2 %copy-start.23 = (f32[9,20,768]{2,1,0:T(8,128)S(1)}, f32[9,20,768]{2,1,0:T(8,128)}, u32[]{:S(2)}) copy-start(f32[9,20,768]{2,1,0:T(8,128)} %copy-done.22) | copy-start | bytes 1658884
  (188 other events, 2577.5 us)
Sparse Core Ops, SparseCore 0:
  10.5 42.6 all-gather.14
  54.8 32.9 all-gather.16
  115.2 30.6 reduce-scatter.11
  150.3 31.7 all-gather.18
  184.3 44.8 reduce-scatter.17
  231.4 31.0 reduce-scatter.13
  264.6 46.8 all-gather.26
  313.9 27.8 all-gather.24
  344.3 29.0 all-gather.22
  375.3 32.9 all-gather.20
  410.7 44.8 reduce-scatter.19
  457.7 31.0 reduce-scatter.15
  490.9 46.8 all-gather.28
  539.8 31.8 all-gather.30
  573.9 44.8 reduce-scatter.21
  620.9 31.0 reduce-scatter.23
  654.0 46.8 all-gather.36
  702.9 31.7 all-gather.32
  737.0 44.8 reduce-scatter.27
  784.1 31.0 reduce-scatter.25
  817.3 46.8 all-gather.38
  866.3 31.7 all-gather.34
  912.9 44.6 reduce-scatter.29
  998.9 46.7 all-gather.40
  1099.2 45.5 all-reduce.4
  1149.0 214.5 all-reduce.6
  1365.9 31.7 reduce-scatter.31
where the time goes:
time: 1490 us; the launch traced here: 1480 us
  waiting for transfers between devices  840 us (56%)
  local copies, waits for them, and re-layouts  230 us (15%)
  matrix products  226 us (15%)
  other arithmetic  99.4 us (7%)
  blocking collectives  56.4 us (4%)
  between operations  22.2 us (1%)
    psum x1, waiting for transfers between devices, local(): lax.psum((grad_attend_in, grad_attend_out, grad_expand_in, grad_expand_ou...  216 us
    all_gather x3, waiting for transfers between devices, gather_grads(): lax.all_gather(vis_part, 'mp', axis=0, tiled=True)  114 us
    reduce_scatter x3, waiting for transfers between devices, reduce_rows(): lax.psum_scatter(vis_part, 'mp', scatter_dimension=0, tiled=True)  104 us
    all_gather x2, waiting for transfers between devices, gather_rows(): lax.all_gather(vis_part, 'mp', axis=0, tiled=True)  91 us
    unnamed x414, local copies, waits for them, and re-layouts  78.7 us
    reduce_scatter x3, waiting for transfers between devices, reduce_rows(): lax.psum_scatter(lang_part, 'mp', scatter_dimension=0, tiled=True)  69.9 us
    reduce_scatter x2, waiting for transfers between devices, reduce_grads(): lax.psum_scatter(lang_part, 'mp', scatter_dimension=0, tiled=True)  46.1 us
    all_gather x2, waiting for transfers between devices, gather_rows(): lax.all_gather(lang_part, 'mp', axis=0, tiled=True)  40 us
  transfers between devices with their start and end apart: 27, of which 25 were waited for; matrix products, arithmetic and copies ran while one was open for 28% of the time, Pallas kernels for 0%

commit v1 on v0

v1 whole, which is shorter than its diff:
```python
import functools
import math

import jax
import jax.numpy as jnp
from jax import lax
from jax.experimental import pallas as pl
from jax.experimental.pallas import tpu as pltpu
from jax.sharding import PartitionSpec as P

HEAD_DIM = 64
STEP = 10

NORM_EPS = 1e-05
CLIP_NORM = 1.0
BETA_FIRST = 0.9
BETA_SECOND = 0.999
ADAM_EPS = 1e-08
WEIGHT_DECAY = 0.01
MATRIX_RATE = 0.12
NORM_RATE = 0.8
AVERAGE_CEILING = 0.999
BF = jnp.bfloat16
F32 = jnp.float32
HIGHEST = lax.Precision.HIGHEST
SCALE = 1.0 / math.sqrt(HEAD_DIM)
VMEM_LIMIT = 56 * 1024 * 1024


def dot_nn(a, b):
    return lax.dot_general(a, b, (((1,), (0,)), ((), ())), preferred_element_type=F32)


def dot_nt(a, b):
    return lax.dot_general(a, b, (((1,), (1,)), ((), ())), preferred_element_type=F32)


def dot_tn(a, b):
    return lax.dot_general(a, b, (((0,), (0,)), ((), ())), preferred_element_type=F32)


def norm_forward(summed, gain, shift):
    centre = jnp.mean(summed, axis=-1, keepdims=True)
    offset = summed - centre
    spread = jnp.mean(offset * offset, axis=-1, keepdims=True)
    inverse = lax.rsqrt(spread + NORM_EPS)
    normed = offset * inverse
    return normed * gain + shift, normed, inverse


def norm_backward(upstream, gain, normed, inverse):
    scaled = upstream * gain
    first_mean = jnp.mean(scaled, axis=-1, keepdims=True)
    second_mean = jnp.mean(scaled * normed, axis=-1, keepdims=True)
    inward = inverse * (scaled - first_mean - normed * second_mean)
    gain_term = jnp.sum(upstream * normed, axis=0, keepdims=True)
    shift_term = jnp.sum(upstream, axis=0, keepdims=True)
    return inward, gain_term, shift_term


def head(block, kind, index, width):
    start = kind * width + index * HEAD_DIM
    return block[:, start : start + HEAD_DIM]


def attend(query, key, value, mask):
    scores = jnp.where(mask, dot_nt(query, key) * SCALE, -1e30)
    powered = jnp.exp(scores - jnp.max(scores, axis=-1, keepdims=True))
    probs = (powered * (1.0 / jnp.sum(powered, axis=-1, keepdims=True))).astype(BF)
    return probs, dot_nn(probs, value).astype(BF)


def attend_back(query, key, value, probs, grad_context):
    grad_probs = dot_nt(grad_context, value)
    grad_value = dot_tn(probs, grad_context).astype(BF)
    wide = probs.astype(F32)
    inner = jnp.sum(grad_probs * wide, axis=-1, keepdims=True)
    grad_scores = (wide * (grad_probs - inner) * SCALE).astype(BF)
    grad_query = dot_nn(grad_scores, key).astype(BF)
    grad_key = dot_tn(grad_scores, query).astype(BF)
    return grad_query, grad_key, grad_value


def load_weight(pieces, weight):
    row = 0
    for piece in pieces:
        for part in range(piece.shape[0]):
            block = piece[part, 0]
            weight[row : row + block.shape[0], :] = block
            row += block.shape[0]


def store_weight(value, pieces):
    row = 0
    for piece in pieces:
        for part in range(piece.shape[0]):
            rows = piece.shape[2]
            piece[part, 0] = value[row : row + rows, :].astype(piece.dtype)
            row += rows


def cross_forward_kernel(width, lang, vis, norm, lang_col, lang_row, vis_col, vis_row, *refs):
    pieces, refs = refs[:8], refs[8:]
    lang_one, lang_n, lang_r, vis_one, vis_n, vis_r = refs[:6]
    lang_qkv, vis_qkv, lang_ctx, vis_ctx, lang_p, vis_p = refs[6:12]
    weight, lang_acc, vis_acc = refs[12:]
    load_weight(pieces, weight)
    step = pl.program_id(0)

    @pl.when(step == 0)
    def _():
        lang_acc[...] = lang[...].astype(F32)
        vis_acc[...] = vis[...].astype(F32)

    full = weight[...]
    in_part, out_part = full[:, : 3 * width], full[:, 3 * width :]
    lang_triple = dot_nn(lang[...], in_part).astype(BF)
    vis_triple = dot_nn(vis[...], in_part).astype(BF)
    lang_qkv[0] = lang_triple
    vis_qkv[0] = vis_triple
    for source, target, probs_ref, ctx_ref, acc, mask in (
        (lang_triple, vis_triple, lang_p, lang_ctx, lang_acc, lang_col[...] == vis_row[...]),
        (vis_triple, lang_triple, vis_p, vis_ctx, vis_acc, vis_col[...] == lang_row[...]),
    ):
        contexts = []
        for index in range(width // HEAD_DIM):
            probs, context = attend(
                head(source, 0, index, width),
                head(target, 1, index, width),
                head(target, 2, index, width),
                mask,
            )
            probs_ref[0, index] = probs
            contexts.append(context)
        context = jnp.concatenate(contexts, axis=1)
        ctx_ref[0] = context
        acc[...] += dot_nt(context, out_part)

    @pl.when(step == pl.num_programs(0) - 1)
    def _():
        for acc, one, n_ref, r_ref in (
            (lang_acc, lang_one, lang_n, lang_r),
            (vis_acc, vis_one, vis_n, vis_r),
        ):
            out, normed, inverse = norm_forward(acc[...], norm[0:1, :], norm[1:2, :])
            one[...] = out.astype(BF)
            n_ref[...] = normed
            r_ref[...] = inverse


def self_forward_kernel(width, slot, rows, norm, col, row, *refs):
    pieces, refs = refs[:4], refs[4:]
    two, n_ref, r_ref, qkv, ctx, probs_ref, weight, acc = refs
    load_weight(pieces, weight)
    step = pl.program_id(0)

    @pl.when(step == 0)
    def _():
        acc[...] = rows[...].astype(F32)

    full = weight[...]
    in_part, out_part = full[:, : 3 * width], full[:, 3 * width :]
    triple = dot_nn(rows[...], in_part).astype(BF)
    qkv[0] = triple
    mask = col[...] == row[...]
    slots = []
    for place in range(rows.shape[0] // slot):
        part = triple[place * slot : (place + 1) * slot]
        contexts = []
        for index in range(width // HEAD_DIM):
            probs, context = attend(
                head(part, 0, index, width),
                head(part, 1, index, width),
                head(part, 2, index, width),
                mask,
            )
            probs_ref[0, place, index] = probs
            contexts.append(context)
        slots.append(jnp.concatenate(contexts, axis=1))
    context = jnp.concatenate(slots, axis=0)
    ctx[0] = context
    acc[...] += dot_nt(context, out_part)

    @pl.when(step == pl.num_programs(0) - 1)
    def _():
        out, normed, inverse = norm_forward(acc[...], norm[0:1, :], norm[1:2, :])
        two[...] = out.astype(BF)
        n_ref[...] = normed
        r_ref[...] = inverse


def feed_forward_kernel(rows, normed_two, cot, norm, *refs):
    in_pieces, out_pieces, refs = refs[:4], refs[4:8], refs[8:]
    three, inward_ref, gain_ref, shift_ref, active_ref, slope_ref = refs[:6]
    weight_in, weight_out, acc = refs[6:]
    load_weight(in_pieces, weight_in)
    load_weight(out_pieces, weight_out)
    step = pl.program_id(0)

    @pl.when(step == 0)
    def _():
        acc[...] = normed_two[...] * norm[0:1, :] + norm[1:2, :]

    hidden = dot_nn(rows[...], weight_in[...])
    normal = 0.5 * (1.0 + lax.erf(hidden * 0.7071067811865476))
    active = (hidden * normal).astype(BF)
    slope = normal + hidden * jnp.exp(-0.5 * hidden * hidden) * 0.3989422804014327
    active_ref[0] = active
    slope_ref[0] = slope.astype(slope_ref.dtype)
    acc[...] += dot_nt(active, weight_out[...])

    @pl.when(step == pl.num_programs(0) - 1)
    def _():
        gain = norm[2:3, :]
        out, normed, inverse = norm_forward(acc[...], gain, norm[3:4, :])
        three[...] = out.astype(BF)
        inward, gain_term, shift_term = norm_backward(cot[...].astype(F32), gain, normed, inverse)
        inward_ref[...] = inward
        gain_ref[...] = gain_term
        shift_ref[...] = shift_term


def feed_backward_kernel(inward, rows, active, slope, normed, inverse, norm, *refs):
    in_pieces, out_pieces, refs = refs[:4], refs[4:8], refs[8:]
    grad_in, grad_out, refs = refs[:4], refs[4:8], refs[8:]
    down_ref, gain_ref, shift_ref, weight_in, weight_out, acc, branch = refs
    load_weight(in_pieces, weight_in)
    load_weight(out_pieces, weight_out)
    step = pl.program_id(0)

    @pl.when(step == 0)
    def _():
        acc[...] = inward[...]
        branch[...] = inward[...].astype(BF)

    store_weight(dot_tn(branch[...], active[0]), grad_out)
    grad_active = dot_nn(branch[...], weight_out[...])
    grad_hidden = (grad_active * slope[0].astype(F32)).astype(BF)
    store_weight(dot_tn(rows[...], grad_hidden), grad_in)
    acc[...] += dot_nt(grad_hidden, weight_in[...])

    @pl.when(step == pl.num_programs(0) - 1)
    def _():
        down, gain_term, shift_term = norm_backward(
            acc[...], norm[0:1, :], normed[...], inverse[...]
        )
        down_ref[...] = down
        gain_ref[...] = gain_term
        shift_ref[...] = shift_term


def self_backward_kernel(width, slot, inward, rows, qkv, ctx, probs, *refs):
    pieces, grads, refs = refs[:4], refs[4:8], refs[8:]
    down_ref, weight, acc, branch = refs
    load_weight(pieces, weight)
    step = pl.program_id(0)

    @pl.when(step == 0)
    def _():
        acc[...] = inward[...]
        branch[...] = inward[...].astype(BF)

    full = weight[...]
    in_part, out_part = full[:, : 3 * width], full[:, 3 * width :]
    grad_context = dot_nn(branch[...], out_part).astype(BF)
    slots = []
    for place in range(rows.shape[0] // slot):
        span = slice(place * slot, (place + 1) * slot)
        part, grad_part = qkv[0, span], grad_context[span]
        found = [
            attend_back(
                head(part, 0, index, width),
                head(part, 1, index, width),
                head(part, 2, index, width),
                probs[0, place, index],
                head(grad_part, 0, index, width),
            )
            for index in range(width // HEAD_DIM)
        ]
        slots.append(
            jnp.concatenate([entry[kind] for kind in range(3) for entry in found], axis=1)
        )
    grad_triple = jnp.concatenate(slots, axis=0)
    store_weight(
        jnp.concatenate(
            [dot_tn(rows[...], grad_triple).astype(BF), dot_tn(branch[...], ctx[0]).astype(BF)],
            axis=1,
        ),
        grads,
    )
    acc[...] += dot_nt(grad_triple, in_part)

    @pl.when(step == pl.num_programs(0) - 1)
    def _():
        down_ref[...] = acc[...]


def cross_backward_kernel(width, lang_up, vis_up, lang, vis, lang_n, lang_r, vis_n, vis_r, norm, *refs):
    lang_qkv, vis_qkv, lang_ctx, vis_ctx, lang_p, vis_p = refs[:6]
    pieces, grads, refs = refs[6:14], refs[14:22], refs[22:]
    lang_out, vis_out, gain_ref, shift_ref = refs[:4]
    weight, lang_acc, vis_acc, lang_branch, vis_branch = refs[4:]
    load_weight(pieces, weight)
    step = pl.program_id(0)

    @pl.when(step == 0)
    def _():
        gain_total, shift_total = 0.0, 0.0
        for up, n_ref, r_ref, acc, branch in (
            (lang_up, lang_n, lang_r, lang_acc, lang_branch),
            (vis_up, vis_n, vis_r, vis_acc, vis_branch),
        ):
            inward, gain_term, shift_term = norm_backward(
                up[...], norm[0:1, :], n_ref[...], r_ref[...]
            )
            acc[...] = inward
            branch[...] = inward.astype(BF)
            gain_total += gain_term
            shift_total += shift_term
        gain_ref[...] = gain_total
        shift_ref[...] = shift_total

    full = weight[...]
    in_part, out_part = full[:, : 3 * width], full[:, 3 * width :]
    lang_gc = dot_nn(lang_branch[...], out_part).astype(BF)
    vis_gc = dot_nn(vis_branch[...], out_part).astype(BF)
    lang_triple, vis_triple = lang_qkv[0], vis_qkv[0]
    found = []
    for source, target, probs, grad_context in (
        (lang_triple, vis_triple, lang_p, lang_gc),
        (vis_triple, lang_triple, vis_p, vis_gc),
    ):
        found.append(
            [
                attend_back(
                    head(source, 0, index, width),
                    head(target, 1, index, width),
                    head(target, 2, index, width),
                    probs[0, index],
                    head(grad_context, 0, index, width),
                )
                for index in range(width // HEAD_DIM)
            ]
        )
    lang_grad = jnp.concatenate(
        [e[0] for e in found[0]] + [e[1] for e in found[1]] + [e[2] for e in found[1]], axis=1
    )
    vis_grad = jnp.concatenate(
        [e[0] for e in found[1]] + [e[1] for e in found[0]] + [e[2] for e in found[0]], axis=1
    )
    in_grad = dot_tn(lang[...], lang_grad) + dot_tn(vis[...], vis_grad)
    out_grad = dot_tn(lang_branch[...], lang_ctx[0]) + dot_tn(vis_branch[...], vis_ctx[0])
    store_weight(jnp.concatenate([in_grad.astype(BF), out_grad.astype(BF)], axis=1), grads)
    lang_acc[...] += dot_nt(lang_grad, in_part)
    vis_acc[...] += dot_nt(vis_grad, in_part)

    @pl.when(step == pl.num_programs(0) - 1)
    def _():
        lang_out[...] = lang_acc[...].astype(lang_out.dtype)
        vis_out[...] = vis_acc[...].astype(vis_out.dtype)


def whole(shape):
    return pl.BlockSpec(shape, lambda m: (0,) * len(shape))


def per_step(shape):
    rest = (0,) * (len(shape) - 1)
    return pl.BlockSpec((1,) + tuple(shape[1:]), lambda m: (m,) + rest)


def piece_spec(shape):
    return pl.BlockSpec((shape[0], 1) + tuple(shape[2:]), lambda m: (0, m, 0, 0))


def call(kernel, steps, ins, outs, scratch, name, flops):
    spec = {"whole": whole, "step": per_step, "piece": piece_spec}
    moved = sum(a.size * a.dtype.itemsize for _, a in ins)
    moved += sum(math.prod(s) * jnp.dtype(t).itemsize for _, s, t in outs)
    return pl.pallas_call(
        kernel,
        grid=(steps,),
        in_specs=[spec[kind](a.shape) for kind, a in ins],
        out_specs=[spec[kind](s) for kind, s, _ in outs],
        out_shape=[jax.ShapeDtypeStruct(s, t) for _, s, t in outs],
        scratch_shapes=[pltpu.VMEM(s, t) for s, t in scratch],
        compiler_params=pltpu.CompilerParams(
            vmem_limit_bytes=VMEM_LIMIT, dimension_semantics=("arbitrary",)
        ),
        cost_estimate=pl.CostEstimate(flops=flops, bytes_accessed=moved, transcendentals=0),
        name=name,
    )(*[a for _, a in ins])


def swap_dp(value, bit):
    count = lax.axis_size("dp")
    return lax.ppermute(value, "dp", [(i, i ^ (1 << bit)) for i in range(count)])


def swap_mp(value, mask):
    count = lax.axis_size("mp")
    return lax.ppermute(value, "mp", [(i, i ^ mask) for i in range(count)])


def extra_bits():
    return range(3, int(math.log2(lax.axis_size("dp"))))


def gather_home(shard):
    current = jnp.stack([shard] + [swap_mp(shard, j) for j in range(1, lax.axis_size("mp"))])
    for bit in extra_bits():
        current = jnp.concatenate([current, swap_dp(current, bit)], axis=1)
    found = {(0, 0, 0): current[None]}
    for place, bit in ((0, 2), (1, 1), (2, 0)):
        for key in list(found):
            new = list(key)
            new[place] = 1
            found[tuple(new)] = swap_dp(found[key], bit)
    return [found[(hi, mid, lo)] for hi in (0, 1) for lo in (0, 1) for mid in (0, 1)]


def gather_stream(own, other):
    pair = jnp.stack([own, swap_dp(other, 1)])
    current = jnp.stack(
        [pair] + [swap_mp(pair, j) for j in range(1, lax.axis_size("mp"))], axis=1
    )
    for bit in extra_bits():
        current = jnp.concatenate([current, swap_dp(current, bit)], axis=2)
    found = {(0, 0): current}
    for place, bit in ((0, 2), (1, 0)):
        for key in list(found):
            new = list(key)
            new[place] = 1
            found[tuple(new)] = swap_dp(found[key], bit)
    return [found[(hi, lo)] for hi in (0, 1) for lo in (0, 1)]


def added(mine, theirs):
    return (mine.astype(F32) + theirs.astype(F32)).astype(BF)


def scatter_rows(current, axis):
    for bit in reversed(extra_bits()):
        low, high = jnp.split(current, 2, axis=axis)
        current = added(low, swap_dp(high, bit))
    return current


def scatter_home(grads):
    found = {}
    for index, grad in enumerate(grads):
        found[(index >> 2, index & 1, (index >> 1) & 1)] = grad[0]
    for place, bit in ((2, 0), (1, 1), (0, 2)):
        for key in [k for k in found if k[place] == 0]:
            far = list(key)
            far[place] = 1
            found[key] = added(found[key], swap_dp(found.pop(tuple(far)), bit))
    current = scatter_rows(found[(0, 0, 0)], 1)
    total = current[0].astype(F32)
    for j in range(1, current.shape[0]):
        total += swap_mp(current[j], j).astype(F32)
    return total


def scatter_stream(grads):
    found = {(index >> 1, index & 1): grad for index, grad in enumerate(grads)}
    for place, bit in ((1, 0), (0, 2)):
        for key in [k for k in found if k[place] == 0]:
            far = list(key)
            far[place] = 1
            found[key] = added(found[key], swap_dp(found.pop(tuple(far)), bit))
    current = scatter_rows(found[(0, 0)], 2)
    total = current[:, 0].astype(F32)
    for j in range(1, current.shape[1]):
        total += swap_mp(current[:, j], j).astype(F32)
    return total[0], swap_dp(total[1].astype(BF), 1).astype(F32)


def adamw_step(gradient, moment, square, weight, average, rate, clip_scale):
    average_decay = min(AVERAGE_CEILING, (1.0 + STEP) / (10.0 + STEP))
    clipped = gradient * clip_scale
    moment_new = BETA_FIRST * moment + (1.0 - BETA_FIRST) * clipped
    square_new = BETA_SECOND * square + (1.0 - BETA_SECOND) * clipped * clipped
    corrected = moment_new / (1.0 - BETA_FIRST**STEP)
    denominator = jnp.sqrt(square_new / (1.0 - BETA_SECOND**STEP)) + ADAM_EPS
    weight_new = weight - rate * (corrected / denominator + WEIGHT_DECAY * weight)
    average_new = average_decay * average + (1.0 - average_decay) * weight_new
    return (clipped, moment_new, square_new, weight_new, average_new)


def pad_rows(block, rows):
    return jnp.pad(block, ((0, rows - block.shape[0]), (0, 0)))


def local(
    language,
    images,
    counts,
    language_cot,
    vision_cot,
    attn_in_weight,
    attn_in_moment,
    attn_in_square,
    attn_in_average,
    attn_out_weight,
    attn_out_moment,
    attn_out_square,
    attn_out_average,
    ffn_in_weight,
    ffn_in_moment,
    ffn_in_square,
    ffn_in_average,
    ffn_out_weight,
    ffn_out_moment,
    ffn_out_square,
    ffn_out_average,
    norm_weight,
    norm_moment,
    norm_square,
    norm_average,
):
    n_dp, n_mp = lax.axis_size("dp"), lax.axis_size("mp")
    me = lax.axis_index("dp")
    stream = (me >> 1) & 1
    is_vis = stream == 1
    own_items, words, dim = language.shape
    regions = images.shape[1]
    lang_rows, vis_rows = own_items * words, own_items * regions
    lang_pad, slot = -(-lang_rows // 16) * 16, -(-vis_rows // 16) * 16
    total = 2 * slot
    shard_rows = attn_in_weight.shape[1]
    width = attn_in_weight.shape[3]
    units = ffn_in_weight.shape[2]
    heads = width // HEAD_DIM

    attn_shards = [
        jnp.concatenate(
            [attn_in_weight[b].reshape(shard_rows, 3 * width), attn_out_weight[b].T], axis=1
        ).astype(BF)
        for b in range(3)
    ]
    up_shards = [ffn_in_weight[s].astype(BF) for s in range(2)]
    down_shards = [ffn_out_weight[s].T.astype(BF) for s in range(2)]

    def mine_first(pair):
        return jnp.where(is_vis, pair[1], pair[0]), jnp.where(is_vis, pair[0], pair[1])

    cross_w = gather_home(attn_shards[0])
    self_w = gather_stream(*mine_first(attn_shards[1:]))
    up_w = gather_stream(*mine_first(up_shards))
    down_w = gather_stream(*mine_first(down_shards))

    place = jnp.arange(dim, dtype=jnp.int32)
    block = place // shard_rows
    sub, eighth = block % (n_dp // 8), block // (n_dp // 8)
    relative = 8 * sub + 4 * (eighth >> 2) + ((eighth >> 1) & 1) + 2 * (eighth & 1)
    origin = (relative ^ me) * shard_rows + place % shard_rows
    order = (place[:, None] == origin[None, :]).astype(BF)

    def to_order(value):
        return lax.dot_general(
            value, order, (((1,), (0,)), ((), ())), preferred_element_type=F32
        ).astype(BF)

    def from_order(value, precision=None):
        return lax.dot_general(
            value, order, (((1,), (1,)), ((), ())), preferred_element_type=F32, precision=precision
        )

    def flip(value):
        parts = value.reshape(value.shape[0], 4, 2, dim // 8)
        return parts[:, :, ::-1, :].reshape(value.shape)

    norm_ordered = lax.dot_general(
        norm_weight.reshape(-1, dim),
        order.astype(F32),
        (((1,), (0,)), ((), ())),
        precision=HIGHEST,
        preferred_element_type=F32,
    ).reshape(norm_weight.shape)
    norm_cross = norm_ordered[:, 0]
    norm_self = jnp.where(is_vis, norm_ordered[:, 2], norm_ordered[:, 1])
    norm_feed = jnp.where(is_vis, norm_ordered[:, 4], norm_ordered[:, 3])

    first_item = lax.axis_index("mp") * own_items
    bounds = jnp.cumsum(counts[0])
    positions = first_item + jnp.arange(own_items, dtype=jnp.int32)
    item_image = jnp.sum((bounds[None, :] <= positions[:, None]).astype(jnp.int32), axis=1)
    region = jnp.arange(regions, dtype=jnp.int32)
    row_source = pad_rows((item_image[:, None] * regions + region[None, :]).reshape(-1, 1) + 1, slot)
    picker = (
        row_source == 1 + jnp.arange(images.shape[0] * regions, dtype=jnp.int32)[None, :]
    ).astype(BF)
    lang = to_order(pad_rows(language.reshape(lang_rows, dim), lang_pad))
    image_rows = to_order(images.reshape(-1, dim))
    vis = dot_nn(picker, image_rows).astype(BF)

    lang_cot = pad_rows(language_cot.reshape(lang_rows, dim), slot)
    vis_cot = pad_rows(vision_cot.reshape(vis_rows, dim), slot)
    cot_own, cot_other = mine_first((lang_cot, vis_cot))
    cot = to_order(jnp.concatenate([cot_own, swap_dp(cot_other, 1)], axis=0))

    lang_ids = jnp.arange(lang_pad, dtype=jnp.int32) // words
    vis_ids = jnp.arange(slot, dtype=jnp.int32) // regions
    slot_ids = jnp.where(is_vis, vis_ids, jnp.arange(slot, dtype=jnp.int32) // words)

    pieces = lambda arrays: [("piece", a) for a in arrays]
    ins = [("whole", a) for a in (lang, vis, norm_cross)]
    ins += [("whole", a) for a in (lang_ids[:, None], lang_ids[None, :], vis_ids[:, None], vis_ids[None, :])]
    outs = []
    for rows in (lang_pad, slot):
        outs += [
            ("whole", (rows, dim), BF),
            ("whole", (rows, dim), F32),
            ("whole", (rows, 1), F32),
        ]
    outs += [("step", (n_mp, rows, 3 * width), BF) for rows in (lang_pad, slot)]
    outs += [("step", (n_mp, rows, width), BF) for rows in (lang_pad, slot)]
    outs += [
        ("step", (n_mp, heads, lang_pad, slot), BF),
        ("step", (n_mp, heads, slot, lang_pad), BF),
    ]
    both = lang_pad + slot
    found = call(
        functools.partial(cross_forward_kernel, width),
        n_mp,
        ins + pieces(cross_w),
        outs,
        [((dim, 4 * width), BF), ((lang_pad, dim), F32), ((slot, dim), F32)],
        "cross_forward",
        2 * both * dim * 4 * width * n_mp,
    )
    lang_one, lang_n, lang_r, vis_one, vis_n, vis_r = found[:6]
    cross_saved = found[6:]

    own_one, other_one = mine_first((pad_rows(lang_one, slot), vis_one))
    rows_one = jnp.concatenate([own_one, flip(swap_dp(other_one, 1))], axis=0)
    rows_two, normed_two, inverse_two, self_qkv, self_ctx, self_probs = call(
        functools.partial(self_forward_kernel, width, slot),
        n_mp,
        [("whole", a) for a in (rows_one, norm_self, slot_ids[:, None], slot_ids[None, :])]
        + pieces(self_w),
        [
            ("whole", (total, dim), BF),
            ("whole", (total, dim), F32),
            ("whole", (total, 1), F32),
            ("step", (n_mp, total, 3 * width), BF),
            ("step", (n_mp, total, width), BF),
            ("step", (n_mp, 2, heads, slot, slot), BF),
        ],
        [((dim, 4 * width), BF), ((total, dim), F32)],
        "self_forward",
        2 * total * dim * 4 * width * n_mp,
    )
    norm_pair = jnp.concatenate([norm_self, norm_feed], axis=0)
    rows_three, inward, feed_gain, feed_shift, active, slope = call(
        feed_forward_kernel,
        n_mp,
        [("whole", a) for a in (rows_two, normed_two, cot, norm_pair)]
        + pieces(up_w)
        + pieces(down_w),
        [
            ("whole", (total, dim), BF),
            ("whole", (total, dim), F32),
            ("whole", (1, dim), F32),
            ("whole", (1, dim), F32),
            ("step", (n_mp, total, units), BF),
            ("step", (n_mp, total, units), BF),
        ],
        [((dim, units), BF), ((dim, units), BF), ((total, dim), F32)],
        "feed_forward",
        4 * total * dim * units * n_mp,
    )

    final = from_order(rows_three).astype(BF)
    final_other = swap_dp(final[slot:], 1)
    language_out = jnp.where(is_vis, final_other[:lang_rows], final[:lang_rows])
    vision_out = jnp.where(is_vis, final[:vis_rows], final_other[:vis_rows])

    stream_grad = [("piece", (2, n_mp, dim // 8, units), BF)] * 4
    found = call(
        feed_backward_kernel,
        n_mp,
        [("whole", inward), ("whole", rows_two), ("step", active), ("step", slope)]
        + [("whole", a) for a in (normed_two, inverse_two, norm_self)]
        + pieces(up_w)
        + pieces(down_w),
        stream_grad
        + stream_grad
        + [("whole", (total, dim), F32), ("whole", (1, dim), F32), ("whole", (1, dim), F32)],
        [
            ((dim, units), BF),
            ((dim, units), BF),
            ((total, dim), F32),
            ((total, dim), BF),
        ],
        "feed_backward",
        8 * total * dim * units * n_mp,
    )
    up_grads = scatter_stream(found[:4])
    down_grads = scatter_stream(found[4:8])
    inward, self_gain, self_shift = found[8:]
    found = call(
        functools.partial(self_backward_kernel, width, slot),
        n_mp,
        [("whole", inward), ("whole", rows_one)]
        + [("step", a) for a in (self_qkv, self_ctx, self_probs)]
        + pieces(self_w),
        [("piece", (2, n_mp, dim // 8, 4 * width), BF)] * 4 + [("whole", (total, dim), F32)],
        [((dim, 4 * width), BF), ((total, dim), F32), ((total, dim), BF)],
        "self_backward",
        4 * total * dim * 4 * width * n_mp,
    )
    self_grads = scatter_stream(found[:4])
    back = found[4]
    back_other = swap_dp(flip(back[slot:].astype(BF)), 1).astype(F32)
    lang_up = jnp.where(is_vis, back_other[:lang_pad], back[:lang_pad])
    vis_up = jnp.where(is_vis, back[:slot], back_other)
    found = call(
        functools.partial(cross_backward_kernel, width),
        n_mp,
        [("whole", a) for a in (lang_up, vis_up, lang, vis, lang_n, lang_r, vis_n, vis_r, norm_cross)]
        + [("step", a) for a in cross_saved]
        + pieces(cross_w),
        [("piece", (1, n_mp, dim // 8, 4 * width), BF)] * 8
        + [
            ("whole", (lang_pad, dim), BF),
            ("whole", (slot, dim), BF),
            ("whole", (1, dim), F32),
            ("whole", (1, dim), F32),
        ],
        [
            ((dim, 4 * width), BF),
            ((lang_pad, dim), F32),
            ((slot, dim), F32),
            ((lang_pad, dim), BF),
            ((slot, dim), BF),
        ],
        "cross_backward",
        4 * both * dim * 4 * width * n_mp,
    )
    cross_grad = scatter_home(found[:8])
    lang_back, vis_back, cross_gain, cross_shift = found[8:]

    language_grad = from_order(lang_back[:lang_rows]).reshape(language.shape)
    image_term = lax.dot_general(
        picker, vis_back, (((0,), (0,)), ((), ())), preferred_element_type=F32
    ).astype(BF)
    image_term = from_order(image_term).astype(BF)
    image_grad = lax.psum(image_term, "mp").astype(F32).reshape(images.shape)

    here = (jnp.arange(2, dtype=jnp.int32) == stream).astype(F32)[None, :, None]
    norm_partial = jnp.concatenate(
        [
            jnp.stack([cross_gain, cross_shift]),
            here * jnp.stack([self_gain, self_shift]),
            here * jnp.stack([feed_gain, feed_shift]),
        ],
        axis=1,
    )
    norm_partial = from_order(norm_partial.reshape(-1, dim).astype(F32), HIGHEST)
    norm_total = lax.psum(norm_partial.reshape(norm_weight.shape), ("dp", "mp"))

    def by_stream(pair):
        return [jnp.where(is_vis, pair[1], pair[0]), jnp.where(is_vis, pair[0], pair[1])]

    attn_total = [cross_grad] + by_stream(self_grads)
    up_total, down_total = by_stream(up_grads), by_stream(down_grads)
    local_squares = sum(jnp.sum(g * g) for g in attn_total + up_total + down_total)
    total_squares = lax.psum(local_squares, ("dp", "mp")) + jnp.sum(norm_total * norm_total)
    grad_norm = jnp.sqrt(total_squares)
    clip_scale = CLIP_NORM / jnp.maximum(grad_norm, CLIP_NORM)

    shards = (
        jnp.stack([g[:, : 3 * width].reshape(shard_rows, 3, width) for g in attn_total]),
        jnp.stack([g[:, 3 * width :].T for g in attn_total]),
        jnp.stack(up_total),
        jnp.stack([g.T for g in down_total]),
    )
    states = (
        (attn_in_moment, attn_in_square, attn_in_weight, attn_in_average),
        (attn_out_moment, attn_out_square, attn_out_weight, attn_out_average),
        (ffn_in_moment, ffn_in_square, ffn_in_weight, ffn_in_average),
        (ffn_out_moment, ffn_out_square, ffn_out_weight, ffn_out_average),
    )
    results = [
        language_out.reshape(language.shape),
        vision_out.reshape(vision_cot.shape),
        language_grad,
        image_grad,
    ]
    for shard, state in zip(shards, states):
        new = adamw_step(shard, *state, MATRIX_RATE, clip_scale)
        results += [new[0], new[1], new[2], new[3], new[3].astype(BF), new[4]]
    results += adamw_step(
        norm_total, norm_moment, norm_square, norm_weight, norm_average, NORM_RATE, clip_scale
    )
    return tuple(results) + (grad_norm,)


def solution(mesh):
    rows = P(("dp", "mp"), None, None)
    attn_in, attn_out = P(None, "dp", None, "mp"), P(None, "mp", "dp")
    ffn_in, ffn_out = P(None, "dp", "mp"), P(None, "mp", "dp")
    in_specs = (rows, P("dp", None, None), P("dp", None), rows, rows)
    in_specs += (attn_in,) * 4 + (attn_out,) * 4 + (ffn_in,) * 4 + (ffn_out,) * 4 + (P(),) * 4
    out_specs = (rows, rows, rows, P("dp", None, None))
    out_specs += (attn_in,) * 6 + (attn_out,) * 6 + (ffn_in,) * 6 + (ffn_out,) * 6 + (P(),) * 6
    return jax.shard_map(local, mesh=mesh, in_specs=in_specs, out_specs=out_specs, check_vma=False)
```

time: 1490 us -> 665 us (0.45)
  waiting for transfers between devices: 840 us -> 222 us
  matrix products: 226 us -> 15.3 us
  local copies, waits for them, and re-layouts: 230 us -> 79.4 us
  Pallas kernels: 0 us -> 132 us
  starting transfers between devices: 3.05 us -> 95 us
  other arithmetic: 99.4 us -> 51.6 us
  blocking collectives: 56.4 us -> 39.4 us
    all_gather x14 -> x0, waiting for transfers between devices: 345 us -> none  [the longest x3 114 us: gather_grads(): lax.all_gather(vis_part, 'mp', axis=0, tiled=True)]
    reduce_scatter x11 -> x0, waiting for transfers between devices: 255 us -> none  [the longest x3 104 us: reduce_rows(): lax.psum_scatter(vis_part, 'mp', scatter_dimension=0, tiled=True)]
    dot_general x62 -> x8, matrix products: 226 us -> 15.3 us  [the longest x4 8.73 us: from_order(): lax.dot_general(value, order, (((1,), (1,)), ((), ())), preferred_element...]
    psum x2 -> x1, waiting for transfers between devices: 239 us -> 29.3 us  [local(): image_grad = lax.psum(image_term, 'mp').astype(F32).reshape(images.shape)]
    ppermute x0 -> x66, waiting for transfers between devices: none -> 192 us  [the longest x42 120 us: swap_dp(): return lax.ppermute(value, 'dp', [(i, i ^ 1 << bit) for i in range(count)])]
    pallas_call x0 -> x6, Pallas kernels: none -> 132 us  [call(): pl.pallas_call(kernel, grid=(steps,), in_specs=[spec[kind](a.shape) for k...]
    ppermute x0 -> x66, starting transfers between devices: none -> 95 us  [the longest x24 66.9 us: swap_mp(): return lax.ppermute(value, 'mp', [(i, i ^ mask) for i in range(count)])]
    convert_element_type x45 -> x3, local copies, waits for them, and re-layouts: 87.4 us -> 0.71 us  [scatter_stream(): return (total[0], swap_dp(total[1].astype(BF), 1).astype(F32))]
  transfers between devices with their start and end apart: 27 -> 67, of which waited for: 25 -> 19; matrix products, arithmetic and copies ran while one was open for 28% -> 15% of each run, Pallas kernels for 0% -> 9%
where the time goes in v1:
time: 665 us; the launch traced here: 657 us
  waiting for transfers between devices  222 us (33%)
  Pallas kernels  132 us (20%)
  starting transfers between devices  95 us (14%)
  local copies, waits for them, and re-layouts  79.4 us (12%)
  other arithmetic  51.6 us (8%)
  blocking collectives  39.4 us (6%)
  between operations  22.8 us (3%)
  matrix products  15.3 us (2%)
    pallas_call x6, Pallas kernels, call(): pl.pallas_call(kernel, grid=(steps,), in_specs=[spec[kind](a.shape) for k...  132 us
    ppermute x42, waiting for transfers between devices, swap_dp(): return lax.ppermute(value, 'dp', [(i, i ^ 1 << bit) for i in range(count)])  120 us
    ppermute x24, waiting for transfers between devices, swap_mp(): return lax.ppermute(value, 'mp', [(i, i ^ mask) for i in range(count)])  71.9 us
    ppermute x24, starting transfers between devices, swap_mp(): return lax.ppermute(value, 'mp', [(i, i ^ mask) for i in range(count)])  66.9 us
    psum x1, blocking collectives, local(): lax.psum(local_squares, ('dp', 'mp')) + jnp.sum(norm_total * norm_total)  39.4 us
    unnamed x213, local copies, waits for them, and re-layouts  38.1 us
    psum x1, waiting for transfers between devices, local(): image_grad = lax.psum(image_term, 'mp').astype(F32).reshape(images.shape)  29.3 us
    ppermute x42, starting transfers between devices, swap_dp(): return lax.ppermute(value, 'dp', [(i, i ^ 1 << bit) for i in range(count)])  28 us
  transfers between devices with their start and end apart: 67, of which 19 were waited for; matrix products, arithmetic and copies ran while one was open for 15% of the time, Pallas kernels for 9%

profile of v1, /device:TPU:0, one launch (start us, length us, event | category | flops | bytes accessed | tf_op | source)
XLA Modules:
  0.0 657.0 jit_solution(2709425024337240109)
XLA Ops:
  9.0 5.1 collective-permute-start.2
  25.2 3.5 collective-permute-start.14
  29.4 7.2 %collective-permute-done.1 = bf16[96,768]{1,0:T(8,128)(2,1)S(1)} collective-permute-done((bf16[96,768]{1,0:T(8,128)(2,1)S(1)}, bf16[96,768]{1,0:T(8,128)(2,1)S(1)}, u32[]{:S(2)}, u32[]{:S(2)}) %collective-permute-start.1) | collective-permute-done | bytes 147488 | tf_op jit(solution)/shard_map/ppermute | solution.py:402
  41.2 15.0 %collective-permute-start.20 = (bf16[2,96,768]{2,1,0:T(8,128)(2,1)}, bf16[2,96,768]{2,1,0:T(8,128)(2,1)S(1)}, u32[]{:S(2)}, u32[]{:S(2)}) collective-permute-start(bf16[2,96,768]{2,1,0:T(8,128)(2,1)} %get-tuple-element.309), channel_id=1, source_target_pairs={{0,1},{1,0},{2,3},{3,2},{4,5},{5,4},{6,7},{7,6},{8,9},{9,8},{10,11... | collective-permute-start | bytes 884744 | tf_op jit(solution)/shard_map/ppermute | solution.py:402
  57.8 7.7 %collective-permute-done.13 = bf16[2,96,768]{2,1,0:T(8,128)(2,1)} collective-permute-done((bf16[2,96,768]{2,1,0:T(8,128)(2,1)}, bf16[2,96,768]{2,1,0:T(8,128)(2,1)}, u32[]{:S(2)}, u32[]{:S(2)}) %collective-permute-start.13) | collective-permute-done | bytes 294944 | tf_op jit(solution)/shard_map/ppermute | solution.py:402
  68.5 2.7 collective-permute-start.29
  71.3 13.0 %collective-permute-done.21 = bf16[2,96,768]{2,1,0:T(8,128)(2,1)S(1)} collective-permute-done((bf16[2,96,768]{2,1,0:T(8,128)(2,1)}, bf16[2,96,768]{2,1,0:T(8,128)(2,1)S(1)}, u32[]{:S(2)}, u32[]{:S(2)}) %collective-permute-start.21) | collective-permute-done | bytes 294944 | tf_op jit(solution)/shard_map/ppermute | solution.py:402
  84.3 3.3 collective-permute-start.27
  93.2 9.4 %collective-permute-done.28 = bf16[2,96,768]{2,1,0:T(8,128)(2,1)} collective-permute-done((bf16[2,96,768]{2,1,0:T(8,128)(2,1)}, bf16[2,96,768]{2,1,0:T(8,128)(2,1)}, u32[]{:S(2)}, u32[]{:S(2)}) %collective-permute-start.28) | collective-permute-done | bytes 294944 | tf_op jit(solution)/shard_map/ppermute | solution.py:402
  110.3 10.4 %collective-permute-done.7.refs_5_.refs_11_ = bf16[1,4,96,768]{3,2,1,0:T(8,128)(2,1)S(1)} collective-permute-done((bf16[1,4,96,768]{3,2,1,0:T(8,128)(2,1)}, bf16[1,4,96,768]{3,2,1,0:T(8,128)(2,1)S(1)}, u32[]{:S(2)}, u32[]{:S(2)}) %collective-permute-start.7) | collective-permute-done | bytes 589856 | tf_op jit(solution)/shard_map/ppermute | solution.py:397
  124.7 6.7 %collective-permute-done.16 = bf16[2,4,96,768]{3,2,0,1:T(8,128)(2,1)} collective-permute-done((bf16[2,4,96,768]{3,2,0,1:T(8,128)(2,1)S(1)}, bf16[2,4,96,768]{3,2,0,1:T(8,128)(2,1)}, u32[]{:S(2)}, u32[]{:S(2)}) %collective-permute-start.16) | collective-permute-done | bytes 1179680 | tf_op jit(solution)/shard_map/ppermute | solution.py:397
  135.2 21.5 %collective-permute-done.24 = bf16[2,4,96,768]{3,2,0,1:T(8,128)(2,1)} collective-permute-done((bf16[2,4,96,768]{3,2,0,1:T(8,128)(2,1)S(1)}, bf16[2,4,96,768]{3,2,0,1:T(8,128)(2,1)}, u32[]{:S(2)}, u32[]{:S(2)}) %collective-permute-start.24) | collective-permute-done | bytes 1179680 | tf_op jit(solution)/shard_map/ppermute | solution.py:397
  157.3 17.9 %cross_forward.1 = (bf16[192,768]{1,0:T(8,128)(2,1)}, f32[192,768]{1,0:T(8,128)}, f32[192,1]{1,0:T(8,128)}, bf16[336,768]{1,0:T(8,128)(2,1)}, f32[336,768]{1,0:T...) custom-call(bf16[192,768]{1,0:T(8,128)(2,1)} %fusion.14.lang, ...), custom_call_target="tpu_custom_call" | custom-call | flops 2491416576 | bytes 14315712 | tf_op jit(solution)/shard_map/cross_forward/pallas_call | solution.py:380
  175.3 6.4 collective-permute-done.31.refs_6_
  192.2 2.5 copy.273
  223.1 19.2 %self_forward.1 = (bf16[672,768]{1,0:T(8,128)(2,1)}, f32[672,768]{1,0:T(8,128)}, f32[672,1]{1,0:T(8,128)}, bf16[4,672,576]{2,1,0:T(8,128)(2,1)}, bf16[4,672,192]...) custom-call(bf16[672,768]{1,0:T(8,128)(2,1)} %pad_maximum_fusion.3.rows, f32[2,768]{1,0:T(2,128)} %copy-done.72, ...), custom_call_target="tpu_custom_call" | custom-call | flops 3170893824 | bytes 18406656 | tf_op jit(solution)/shard_map/self_forward/pallas_call | solution.py:380
  242.3 17.1 %feed_forward.1 = (bf16[672,768]{1,0:T(8,128)(2,1)}, f32[672,768]{1,0:T(8,128)}, f32[1,768]{1,0:T(1,128)}, f32[1,768]{1,0:T(1,128)}, bf16[4,672,768]{2,1,0:T(8,128)(2,1)}, /*index=5*/bf16[4,672,768]{2,1,0:T(8,128)(2,1)}) custom-call(bf16[672,768]{1,0:T(8,128)(2,1)} %get-tuple-element.88.rows, f32[672,768]{1,0:T(8,128)} %get-tuple-element.89.normed_two.normed, ...), custom_call_target="tpu_custom_call" | custom-call | flops 6341787648 | bytes 24938496 | tf_op jit(solution)/shard_map/feed_forward/pallas_call | solution.py:380
  259.4 22.9 %feed_backward.1 = (bf16[2,4,96,768]{3,2,1,0:T(8,128)(2,1)}, bf16[2,4,96,768]{3,2,1,0:T(8,128)(2,1)}, bf16[2,4,96,768]{3,2,1,0:T(8,128)(2,1)}, bf16[2,4,96,768]{...) custom-call(f32[672,768]{1,0:T(8,128)} %get-tuple-element.91.inward,, ...), custom_call_target="tpu_custom_call" | custom-call | flops 12683575296 | bytes 34372224 | tf_op jit(solution)/shard_map/feed_backward/pallas_call | solution.py:380
  282.3 30.1 %self_backward.1 = (bf16[2,4,96,768]{3,2,1,0:T(8,128)(2,1)}, bf16[2,4,96,768]{3,2,1,0:T(8,128)(2,1)}, bf16[2,4,96,768]{3,2,1,0:T(8,128)(2,1)}, bf16[2,4,96,768]{3,2,1,0:T(8,128)(2,1)}, f32[672,768]{1,0:T(8,128)}) custom-call(f32[672,768]{1,0:T(8,128)} %get-tuple-element.95.inward, bf16[672,768]{1,0:T(8,128)(2,1)} %pad_maximum_fusion.3.rows, ...), custom_call_target="tpu_custom_call" | custom-call | flops 6341787648 | bytes 24145920 | tf_op jit(solution)/shard_map/self_backward/pallas_call | solution.py:380
  331.4 24.5 %cross_backward.1 = (bf16[1,4,96,768]{3,2,1,0:T(8,128)(2,1)}, bf16[1,4,96,768]{3,2,1,0:T(8,128)(2,1)}, bf16[1,4,96,768]{3,2,1,0:T(8,128)(2,1)}, bf16[1,4,96,768]...) custom-call(f32[192,768]{1,0:T(8,128)} %slice_select_fusion.1.lang_u, ...), custom_call_target="tpu_custom_call" | custom-call | flops 4982833152 | bytes 20658240 | tf_op jit(solution)/shard_map/cross_backward/pallas_call | solution.py:380
  371.2 29.3 %all-reduce.8.cloned.1.call-done = bf16[9,36,768]{2,1,0:T(8,128)(2,1)} async-done(((bf16[9,36,768]{2,1,0:T(8,128)(2,1)}), bf16[9,36,768]{2,1,0:T(8,128)(2,1)}) %all-reduce.8.cloned.1.call-update) | async-done | bytes 497680 | tf_op jit(solution)/shard_map/psum | solution.py:750
  413.2 8.4 %collective-permute-done.37 = bf16[4,96,768]{2,1,0:T(8,128)(2,1)S(1)} collective-permute-done((bf16[4,96,768]{2,1,0:T(8,128)(2,1)S(1)}, bf16[4,96,768]{2,1,0:T(8,128)(2,1)S(1)}, u32[]{:S(2)}, u32[]{:S(2)}) %collective-permute-start.37) | collective-permute-done | bytes 589856 | tf_op jit(solution)/shard_map/ppermute | solution.py:397
  423.4 25.8 %collective-permute-done.41 = bf16[4,96,768]{2,1,0:T(8,128)(2,1)S(1)} collective-permute-done((bf16[4,96,768]{2,1,0:T(8,128)(2,1)S(1)}, bf16[4,96,768]{2,1,0:T(8,128)(2,1)S(1)}, u32[]{:S(2)}, u32[]{:S(2)}) %collective-permute-start.41) | collective-permute-done | bytes 589856 | tf_op jit(solution)/shard_map/ppermute | solution.py:397
  455.8 18.7 %collective-permute-done.54 = bf16[2,4,96,768]{3,2,0,1:T(8,128)(2,1)S(1)} collective-permute-done((bf16[2,4,96,768]{3,2,0,1:T(8,128)(2,1)S(1)}, bf16[2,4,96,768]{3,2,0,1:T(8,128)(2,1)S(1)}, u32[]{:S(2)}, u32[]{:S(2)}) %collective-permute-start.54) | collective-permute-done | bytes 1179680 | tf_op jit(solution)/shard_map/ppermute | solution.py:397
  478.7 20.0 %collective-permute-done.61 = bf16[2,4,96,768]{3,2,0,1:T(8,128)(2,1)S(1)} collective-permute-done((bf16[2,4,96,768]{3,2,0,1:T(8,128)(2,1)S(1)}, bf16[2,4,96,768]{3,2,0,1:T(8,128)(2,1)S(1)}, u32[]{:S(2)}, u32[]{:S(2)}) %collective-permute-start.61) | collective-permute-done | bytes 1179680 | tf_op jit(solution)/shard_map/ppermute | solution.py:397
  508.1 17.4 %collective-permute-done.49 = bf16[2,96,768]{2,1,0:T(8,128)(2,1)S(1)} collective-permute-done((bf16[2,96,768]{2,1,0:T(8,128)(2,1)S(1)}, bf16[2,96,768]{2,1,0:T(8,128)(2,1)S(1)}, u32[]{:S(2)}, u32[]{:S(2)}) %collective-permute-start.49) | collective-permute-done | bytes 294944 | tf_op jit(solution)/shard_map/ppermute | solution.py:402
  527.9 17.1 %collective-permute-start.62 = (bf16[2,96,768]{2,1,0:T(8,128)(2,1)S(1)}, bf16[2,96,768]{2,1,0:T(8,128)(2,1)S(1)}, u32[]{:S(2)}, u32[]{:S(2)}) collective-permute-start(bf16[2,96,768]{2,1,0:T(8,128)(2,1)S(1)} %get-tuple-element.277), channel_id=1, source_target_pairs={{0,1},{1,0},{2,3},{3,2},{4,5},{5,4},{6,7},{7,6},{8,9},{9,8},{10,11... | collective-permute-start | bytes 884744 | tf_op jit(solution)/shard_map/ppermute | solution.py:402
  545.0 7.7 %collective-permute-done.56 = bf16[2,96,768]{2,1,0:T(8,128)(2,1)S(1)} collective-permute-done((bf16[2,96,768]{2,1,0:T(8,128)(2,1)S(1)}, bf16[2,96,768]{2,1,0:T(8,128)(2,1)S(1)}, u32[]{:S(2)}, u32[]{:S(2)}) %collective-permute-start.56) | collective-permute-done | bytes 294944 | tf_op jit(solution)/shard_map/ppermute | solution.py:402
  555.0 9.4 %collective-permute-done.63 = bf16[2,96,768]{2,1,0:T(8,128)(2,1)S(1)} collective-permute-done((bf16[2,96,768]{2,1,0:T(8,128)(2,1)S(1)}, bf16[2,96,768]{2,1,0:T(8,128)(2,1)S(1)}, u32[]{:S(2)}, u32[]{:S(2)}) %collective-permute-start.63) | collective-permute-done | bytes 294944 | tf_op jit(solution)/shard_map/ppermute | solution.py:402
  574.9 39.4 %all-reduce.5 = (f32[]{:T(128)}, f32[2,5,768]{2,1,0:T(8,128)S(1)}) all-reduce(f32[]{:T(128)S(6)} %add.417, f32[2,5,768]{2,1,0:T(8,128)S(1)} %copy-done.68), channel_id=1, replica_groups=mesh['dp'=8,'mp'=4] {'dp','mp'}, use_global_device_ids=true, to_apply=%region_10.11 | all-reduce | flops 7681 | bytes 61448 | tf_op jit(solution)/shard_map/psum | solution.py:770
  618.2 3.5 multiply_add_fusion
  638.6 3.0 multiply_add_fusion.4
  (461 shorter events, 188.4 us)
Async XLA Ops:
  7.2 393.3 %all-reduce.8.cloned.1.call-start = ((), (), s32[]{:S(2)}) async-start(), calls=%async_computation | async-start | bytes 1105920 | tf_op jit(solution)/shard_map/psum | solution.py:750
  29.4 36.1 %collective-permute-start.13 = (bf16[2,96,768]{2,1,0:T(8,128)(2,1)}, bf16[2,96,768]{2,1,0:T(8,128)(2,1)}, u32[]{:S(2)}, u32[]{:S(2)}) collective-permute-start(bf16[2,96,768]{2,1,0:T(8,128)(2,1)} %get-tuple-element.311), channel_id=1, source_target_pairs={{0,2},{1,3},{2,0},{3,1},{4,6},{5,7},{6,4},{7,5},{8,10},{9,11},{10,... | collective-permute-start | bytes 884744 | tf_op jit(solution)/shard_map/ppermute | solution.py:402
  39.6 44.7 %collective-permute-start.21 = (bf16[2,96,768]{2,1,0:T(8,128)(2,1)}, bf16[2,96,768]{2,1,0:T(8,128)(2,1)S(1)}, u32[]{:S(2)}, u32[]{:S(2)}) collective-permute-start(bf16[2,96,768]{2,1,0:T(8,128)(2,1)} %get-tuple-element.309), channel_id=1, source_target_pairs={{0,2},{1,3},{2,0},{3,1},{4,6},{5,7},{6,4},{7,5},{8,10},{9,11},{10,... | collective-permute-start | bytes 884744 | tf_op jit(solution)/shard_map/ppermute | solution.py:402
  41.2 43.2 %collective-permute-start.20 = (bf16[2,96,768]{2,1,0:T(8,128)(2,1)}, bf16[2,96,768]{2,1,0:T(8,128)(2,1)S(1)}, u32[]{:S(2)}, u32[]{:S(2)}) collective-permute-start(bf16[2,96,768]{2,1,0:T(8,128)(2,1)} %get-tuple-element.309), channel_id=1, source_target_pairs={{0,1},{1,0},{2,3},{3,2},{4,5},{5,4},{6,7},{7,6},{8,9},{9,8},{10,11... | collective-permute-start | bytes 884744 | tf_op jit(solution)/shard_map/ppermute | solution.py:402
  65.4 39.3 %collective-permute-start.3 = (bf16[1,4,96,768]{3,2,1,0:T(8,128)(2,1)}, bf16[1,4,96,768]{3,2,1,0:T(8,128)(2,1)}, u32[]{:S(2)}, u32[]{:S(2)}) collective-permute-start(bf16[1,4,96,768]{3,2,1,0:T(8,128)(2,1)} %maximum_bitcast_fusion.refs_0_.refs_6_), channel_id=1, source_target_pairs={{0,8},{4,12},{8,0},{12,4},{16,24},{20,28},{24,16},{28,20},{1,9},{5... | collective-permute-start | bytes 1769480 | tf_op jit(solution)/shard_map/ppermute | solution.py:397
  66.9 38.1 %collective-permute-start.6 = (bf16[1,4,96,768]{3,2,1,0:T(8,128)(2,1)}, bf16[1,4,96,768]{3,2,1,0:T(8,128)(2,1)}, u32[]{:S(2)}, u32[]{:S(2)}) collective-permute-start(bf16[1,4,96,768]{3,2,1,0:T(8,128)(2,1)} %maximum_bitcast_fusion.refs_0_.refs_6_), channel_id=1, source_target_pairs={{0,16},{4,20},{8,24},{12,28},{16,0},{20,4},{24,8},{28,12},{1,17},{... | collective-permute-start | bytes 1769480 | tf_op jit(solution)/shard_map/ppermute | solution.py:397
  107.3 49.4 %collective-permute-start.24 = (bf16[2,4,96,768]{3,2,0,1:T(8,128)(2,1)S(1)}, bf16[2,4,96,768]{3,2,0,1:T(8,128)(2,1)}, u32[]{:S(2)}, u32[]{:S(2)}) collective-permute-start(bf16[2,4,96,768]{3,2,0,1:T(8,128)(2,1)S(1)} %pad_maximum_fusion.1), channel_id=1, source_target_pairs={{0,16},{4,20},{8,24},{12,28},{16,0},{20,4},{24,8},{28,12},{1,17},{... | collective-permute-start | bytes 3538952 | tf_op jit(solution)/shard_map/ppermute | solution.py:397
  110.2 65.0 %collective-permute-start.15 = (bf16[2,4,96,768]{3,2,0,1:T(8,128)(2,1)S(1)}, bf16[2,4,96,768]{3,2,0,1:T(8,128)(2,1)}, u32[]{:S(2)}, u32[]{:S(2)}) collective-permute-start(bf16[2,4,96,768]{3,2,0,1:T(8,128)(2,1)S(1)} %pad_maximum_fusion), channel_id=1, source_target_pairs={{0,4},{4,0},{8,12},{12,8},{16,20},{20,16},{24,28},{28,24},{1,5},{5... | collective-permute-start | bytes 3538952 | tf_op jit(solution)/shard_map/ppermute | solution.py:397
  120.7 60.9 %collective-permute-start.31 = (bf16[2,4,96,768]{3,2,1,0:T(8,128)(2,1)}, bf16[2,4,96,768]{3,2,1,0:T(8,128)(2,1)}, u32[]{:S(2)}, u32[]{:S(2)}) collective-permute-start(bf16[2,4,96,768]{3,2,1,0:T(8,128)(2,1)} %pad_maximum_fusion.2.refs_4_), channel_id=1, source_target_pairs={{0,16},{4,20},{8,24},{12,28},{16,0},{20,4},{24,8},{28,12},{1,17},{... | collective-permute-start | bytes 3538952 | tf_op jit(solution)/shard_map/ppermute | solution.py:397
  124.1 59.8 %collective-permute-start.23 = (bf16[2,4,96,768]{3,2,0,1:T(8,128)(2,1)S(1)}, bf16[2,4,96,768]{3,2,0,1:T(8,128)(2,1)}, u32[]{:S(2)}, u32[]{:S(2)}) collective-permute-start(bf16[2,4,96,768]{3,2,0,1:T(8,128)(2,1)S(1)} %pad_maximum_fusion.1), channel_id=1, source_target_pairs={{0,4},{4,0},{8,12},{12,8},{16,20},{20,16},{24,28},{28,24},{1,5},{5... | collective-permute-start | bytes 3538952 | tf_op jit(solution)/shard_map/ppermute | solution.py:397
  156.7 61.6 %collective-permute-start.17 = (bf16[2,4,96,768]{3,2,0,1:T(8,128)(2,1)}, bf16[2,4,96,768]{3,2,0,1:T(8,128)(2,1)}, u32[]{:S(2)}, u32[]{:S(2)}) collective-permute-start(bf16[2,4,96,768]{3,2,0,1:T(8,128)(2,1)} %collective-permute-done.16), channel_id=1, source_target_pairs={{0,4},{4,0},{8,12},{12,8},{16,20},{20,16},{24,28},{28,24},{1,5},{5... | collective-permute-start | bytes 3538952 | tf_op jit(solution)/shard_map/ppermute | solution.py:397
  156.8 63.9 %collective-permute-start.25 = (bf16[2,4,96,768]{3,2,0,1:T(8,128)(2,1)}, bf16[2,4,96,768]{3,2,0,1:T(8,128)(2,1)}, u32[]{:S(2)}, u32[]{:S(2)}) collective-permute-start(bf16[2,4,96,768]{3,2,0,1:T(8,128)(2,1)} %collective-permute-done.24), channel_id=1, source_target_pairs={{0,4},{4,0},{8,12},{12,8},{16,20},{20,16},{24,28},{28,24},{1,5},{5... | collective-permute-start | bytes 3538952 | tf_op jit(solution)/shard_map/ppermute | solution.py:397
  175.2 67.1 %collective-permute-start.30 = (bf16[2,4,96,768]{3,2,1,0:T(8,128)(2,1)}, bf16[2,4,96,768]{3,2,1,0:T(8,128)(2,1)}, u32[]{:S(2)}, u32[]{:S(2)}) collective-permute-start(bf16[2,4,96,768]{3,2,1,0:T(8,128)(2,1)} %pad_maximum_fusion.2.refs_4_), channel_id=1, source_target_pairs={{0,4},{4,0},{8,12},{12,8},{16,20},{20,16},{24,28},{28,24},{1,5},{5... | collective-permute-start | bytes 3538952 | tf_op jit(solution)/shard_map/ppermute | solution.py:397
  181.6 60.6 %collective-permute-start.32 = (bf16[2,4,96,768]{3,2,1,0:T(8,128)(2,1)}, bf16[2,4,96,768]{3,2,1,0:T(8,128)(2,1)}, u32[]{:S(2)}, u32[]{:S(2)}) collective-permute-start(bf16[2,4,96,768]{3,2,1,0:T(8,128)(2,1)} %collective-permute-done.31.refs_6_), channel_id=1, source_target_pairs={{0,4},{4,0},{8,12},{12,8},{16,20},{20,16},{24,28},{28,24},{1,5},{5... | collective-permute-start | bytes 3538952 | tf_op jit(solution)/shard_map/ppermute | solution.py:397
  317.3 38.8 %collective-permute-start.33 = (bf16[336,768]{1,0:T(8,128)(2,1)S(1)}, bf16[336,768]{1,0:T(8,128)(2,1)S(1)}, u32[]{:S(2)}, u32[]{:S(2)}) collective-permute-start(bf16[336,768]{1,0:T(8,128)(2,1)S(1)} %slice.228), channel_id=1, source_target_pairs={{0,8},{4,12},{8,0},{12,4},{16,24},{20,28},{24,16},{28,20},{1,9},{5... | collective-permute-start | bytes 1548296 | tf_op jit(solution)/shard_map/ppermute | solution.py:397
  320.0 82.7 %collective-permute-start.46 = (bf16[2,4,96,768]{3,2,0,1:T(8,128)(2,1)}, bf16[2,4,96,768]{3,2,0,1:T(8,128)(2,1)}, u32[]{:S(2)}, u32[]{:S(2)}) collective-permute-start(bf16[2,4,96,768]{3,2,0,1:T(8,128)(2,1)} %copy.262), channel_id=1, source_target_pairs={{0,4},{4,0},{8,12},{12,8},{16,20},{20,16},{24,28},{28,24},{1,5},{5... | collective-permute-start | bytes 3538952 | tf_op jit(solution)/shard_map/ppermute | solution.py:397
  323.3 87.4 %collective-permute-start.53 = (bf16[2,4,96,768]{3,2,0,1:T(8,128)(2,1)}, bf16[2,4,96,768]{3,2,0,1:T(8,128)(2,1)}, u32[]{:S(2)}, u32[]{:S(2)}) collective-permute-start(bf16[2,4,96,768]{3,2,0,1:T(8,128)(2,1)} %copy.268), channel_id=1, source_target_pairs={{0,4},{4,0},{8,12},{12,8},{16,20},{20,16},{24,28},{28,24},{1,5},{5... | collective-permute-start | bytes 3538952 | tf_op jit(solution)/shard_map/ppermute | solution.py:397
  362.2 43.6 %collective-permute-start.38 = (bf16[4,96,768]{2,1,0:T(8,128)(2,1)}, bf16[4,96,768]{2,1,0:T(8,128)(2,1)}, u32[]{:S(2)}, u32[]{:S(2)}) collective-permute-start(bf16[4,96,768]{2,1,0:T(8,128)(2,1)} %bitcast.259), channel_id=1, source_target_pairs={{0,4},{4,0},{8,12},{12,8},{16,20},{20,16},{24,28},{28,24},{1,5},{5... | collective-permute-start | bytes 1769480 | tf_op jit(solution)/shard_map/ppermute | solution.py:397
  362.8 43.4 %collective-permute-start.35 = (bf16[4,96,768]{2,1,0:T(8,128)(2,1)}, bf16[4,96,768]{2,1,0:T(8,128)(2,1)}, u32[]{:S(2)}, u32[]{:S(2)}) collective-permute-start(bf16[4,96,768]{2,1,0:T(8,128)(2,1)} %bitcast.258), channel_id=1, source_target_pairs={{0,4},{4,0},{8,12},{12,8},{16,20},{20,16},{24,28},{28,24},{1,5},{5... | collective-permute-start | bytes 1769480 | tf_op jit(solution)/shard_map/ppermute | solution.py:397
  365.1 42.6 %collective-permute-start.40 = (bf16[4,96,768]{2,1,0:T(8,128)(2,1)}, bf16[4,96,768]{2,1,0:T(8,128)(2,1)}, u32[]{:S(2)}, u32[]{:S(2)}) collective-permute-start(bf16[4,96,768]{2,1,0:T(8,128)(2,1)} %fusion.15), channel_id=1, source_target_pairs={{0,8},{4,12},{8,0},{12,4},{16,24},{20,28},{24,16},{28,20},{1,9},{5... | collective-permute-start | bytes 1769480 | tf_op jit(solution)/shard_map/ppermute | solution.py:397
  405.8 44.9 %collective-permute-start.45 = (bf16[2,4,96,768]{3,2,0,1:T(8,128)(2,1)S(1)}, bf16[2,4,96,768]{3,2,0,1:T(8,128)(2,1)S(1)}, u32[]{:S(2)}, u32[]{:S(2)}) collective-permute-start(bf16[2,4,96,768]{3,2,0,1:T(8,128)(2,1)S(1)} %copy-done.33), channel_id=1, source_target_pairs={{0,4},{4,0},{8,12},{12,8},{16,20},{20,16},{24,28},{28,24},{1,5},{5... | collective-permute-start | bytes 3538952 | tf_op jit(solution)/shard_map/ppermute | solution.py:397
  407.7 44.6 %collective-permute-start.47 = (bf16[2,4,96,768]{3,2,0,1:T(8,128)(2,1)S(1)}, bf16[2,4,96,768]{3,2,0,1:T(8,128)(2,1)S(1)}, u32[]{:S(2)}, u32[]{:S(2)}) collective-permute-start(bf16[2,4,96,768]{3,2,0,1:T(8,128)(2,1)S(1)} %add_convert_fusion.7), channel_id=1, source_target_pairs={{0,16},{4,20},{8,24},{12,28},{16,0},{20,4},{24,8},{28,12},{1,17},{... | collective-permute-start | bytes 3538952 | tf_op jit(solution)/shard_map/ppermute | solution.py:397
  410.8 38.4 %collective-permute-start.41 = (bf16[4,96,768]{2,1,0:T(8,128)(2,1)S(1)}, bf16[4,96,768]{2,1,0:T(8,128)(2,1)S(1)}, u32[]{:S(2)}, u32[]{:S(2)}) collective-permute-start(bf16[4,96,768]{2,1,0:T(8,128)(2,1)S(1)} %add_convert_fusion.10), channel_id=1, source_target_pairs={{0,16},{4,20},{8,24},{12,28},{16,0},{20,4},{24,8},{28,12},{1,17},{... | collective-permute-start | bytes 1769480 | tf_op jit(solution)/shard_map/ppermute | solution.py:397
  413.1 42.2 %collective-permute-start.52 = (bf16[2,4,96,768]{3,2,0,1:T(8,128)(2,1)S(1)}, bf16[2,4,96,768]{3,2,0,1:T(8,128)(2,1)S(1)}, u32[]{:S(2)}, u32[]{:S(2)}) collective-permute-start(bf16[2,4,96,768]{3,2,0,1:T(8,128)(2,1)S(1)} %copy-done.32), channel_id=1, source_target_pairs={{0,4},{4,0},{8,12},{12,8},{16,20},{20,16},{24,28},{28,24},{1,5},{5... | collective-permute-start | bytes 3538952 | tf_op jit(solution)/shard_map/ppermute | solution.py:397
  421.6 52.9 %collective-permute-start.54 = (bf16[2,4,96,768]{3,2,0,1:T(8,128)(2,1)S(1)}, bf16[2,4,96,768]{3,2,0,1:T(8,128)(2,1)S(1)}, u32[]{:S(2)}, u32[]{:S(2)}) collective-permute-start(bf16[2,4,96,768]{3,2,0,1:T(8,128)(2,1)S(1)} %add_convert_fusion.4), channel_id=1, source_target_pairs={{0,16},{4,20},{8,24},{12,28},{16,0},{20,4},{24,8},{28,12},{1,17},{... | collective-permute-start | bytes 3538952 | tf_op jit(solution)/shard_map/ppermute | solution.py:397
  450.8 47.9 %collective-permute-start.61 = (bf16[2,4,96,768]{3,2,0,1:T(8,128)(2,1)S(1)}, bf16[2,4,96,768]{3,2,0,1:T(8,128)(2,1)S(1)}, u32[]{:S(2)}, u32[]{:S(2)}) collective-permute-start(bf16[2,4,96,768]{3,2,0,1:T(8,128)(2,1)S(1)} %add_convert_fusion.1), channel_id=1, source_target_pairs={{0,16},{4,20},{8,24},{12,28},{16,0},{20,4},{24,8},{28,12},{1,17},{... | collective-permute-start | bytes 3538952 | tf_op jit(solution)/shard_map/ppermute | solution.py:397
  452.3 49.0 %collective-permute-start.44 = (bf16[96,768]{1,0:T(8,128)(2,1)S(1)}, bf16[96,768]{1,0:T(8,128)(2,1)S(1)}, u32[]{:S(2)}, u32[]{:S(2)}) collective-permute-start(bf16[96,768]{1,0:T(8,128)(2,1)S(1)} %get-tuple-element.300), channel_id=1, source_target_pairs={{0,3},{1,2},{2,1},{3,0},{4,7},{5,6},{6,5},{7,4},{8,11},{9,10},{10,... | collective-permute-start | bytes 442376 | tf_op jit(solution)/shard_map/ppermute | solution.py:402
  455.3 47.0 %collective-permute-start.43 = (bf16[96,768]{1,0:T(8,128)(2,1)S(1)}, bf16[96,768]{1,0:T(8,128)(2,1)S(1)}, u32[]{:S(2)}, u32[]{:S(2)}) collective-permute-start(bf16[96,768]{1,0:T(8,128)(2,1)S(1)} %get-tuple-element.301), channel_id=1, source_target_pairs={{0,2},{1,3},{2,0},{3,1},{4,6},{5,7},{6,4},{7,5},{8,10},{9,11},{10,... | collective-permute-start | bytes 442376 | tf_op jit(solution)/shard_map/ppermute | solution.py:402
  503.7 49.1 %collective-permute-start.56 = (bf16[2,96,768]{2,1,0:T(8,128)(2,1)S(1)}, bf16[2,96,768]{2,1,0:T(8,128)(2,1)S(1)}, u32[]{:S(2)}, u32[]{:S(2)}) collective-permute-start(bf16[2,96,768]{2,1,0:T(8,128)(2,1)S(1)} %get-tuple-element.282), channel_id=1, source_target_pairs={{0,2},{1,3},{2,0},{3,1},{4,6},{5,7},{6,4},{7,5},{8,10},{9,11},{10,... | collective-permute-start | bytes 884744 | tf_op jit(solution)/shard_map/ppermute | solution.py:402
  506.3 47.0 %collective-permute-start.55 = (bf16[2,96,768]{2,1,0:T(8,128)(2,1)S(1)}, bf16[2,96,768]{2,1,0:T(8,128)(2,1)S(1)}, u32[]{:S(2)}, u32[]{:S(2)}) collective-permute-start(bf16[2,96,768]{2,1,0:T(8,128)(2,1)S(1)} %get-tuple-element.280), channel_id=1, source_target_pairs={{0,1},{1,0},{2,3},{3,2},{4,5},{5,4},{6,7},{7,6},{8,9},{9,8},{10,11... | collective-permute-start | bytes 884744 | tf_op jit(solution)/shard_map/ppermute | solution.py:402
  527.7 36.7 %collective-permute-start.63 = (bf16[2,96,768]{2,1,0:T(8,128)(2,1)S(1)}, bf16[2,96,768]{2,1,0:T(8,128)(2,1)S(1)}, u32[]{:S(2)}, u32[]{:S(2)}) collective-permute-start(bf16[2,96,768]{2,1,0:T(8,128)(2,1)S(1)} %get-tuple-element.279), channel_id=1, source_target_pairs={{0,2},{1,3},{2,0},{3,1},{4,6},{5,7},{6,4},{7,5},{8,10},{9,11},{10,... | collective-permute-start | bytes 884744 | tf_op jit(solution)/shard_map/ppermute | solution.py:402
  527.9 36.5 %collective-permute-start.62 = (bf16[2,96,768]{2,1,0:T(8,128)(2,1)S(1)}, bf16[2,96,768]{2,1,0:T(8,128)(2,1)S(1)}, u32[]{:S(2)}, u32[]{:S(2)}) collective-permute-start(bf16[2,96,768]{2,1,0:T(8,128)(2,1)S(1)} %get-tuple-element.277), channel_id=1, source_target_pairs={{0,1},{1,0},{2,3},{3,2},{4,5},{5,4},{6,7},{7,6},{8,9},{9,8},{10,11... | collective-permute-start | bytes 884744 | tf_op jit(solution)/shard_map/ppermute | solution.py:402
  (128 other events, 1587.8 us)
Sparse Core Ops, SparseCore 0:
  362.3 38.1 all-reduce.7

commit v2 on v1

v2 whole, which is shorter than its diff:
```python
import functools
import math

import jax
import jax.numpy as jnp
from jax import lax
from jax.experimental import pallas as pl
from jax.experimental.pallas import tpu as pltpu
from jax.sharding import PartitionSpec as P

HEAD_DIM = 64
STEP = 10

NORM_EPS = 1e-05
CLIP_NORM = 1.0
BETA_FIRST = 0.9
BETA_SECOND = 0.999
ADAM_EPS = 1e-08
WEIGHT_DECAY = 0.01
MATRIX_RATE = 0.12
NORM_RATE = 0.8
AVERAGE_CEILING = 0.999
BF = jnp.bfloat16
F32 = jnp.float32
HIGHEST = lax.Precision.HIGHEST
SCALE = 1.0 / math.sqrt(HEAD_DIM)
VMEM_LIMIT = 56 * 1024 * 1024
GROUP = 3


def dot_nn(a, b):
    return lax.dot_general(a, b, (((1,), (0,)), ((), ())), preferred_element_type=F32)


def dot_nt(a, b):
    return lax.dot_general(a, b, (((1,), (1,)), ((), ())), preferred_element_type=F32)


def dot_tn(a, b):
    return lax.dot_general(a, b, (((0,), (0,)), ((), ())), preferred_element_type=F32)


def norm_forward(summed, gain, shift):
    centre = jnp.mean(summed, axis=-1, keepdims=True)
    offset = summed - centre
    spread = jnp.mean(offset * offset, axis=-1, keepdims=True)
    inverse = lax.rsqrt(spread + NORM_EPS)
    normed = offset * inverse
    return normed * gain + shift, normed, inverse


def norm_backward(upstream, gain, normed, inverse):
    scaled = upstream * gain
    first_mean = jnp.mean(scaled, axis=-1, keepdims=True)
    second_mean = jnp.mean(scaled * normed, axis=-1, keepdims=True)
    inward = inverse * (scaled - first_mean - normed * second_mean)
    gain_term = jnp.sum(upstream * normed, axis=0, keepdims=True)
    shift_term = jnp.sum(upstream, axis=0, keepdims=True)
    return inward, gain_term, shift_term


def cut(block, blocks):
    rows = block.shape[0] // blocks
    return [block[i * rows : (i + 1) * rows] for i in range(blocks)]


def stack_rows(parts):
    return jnp.concatenate(parts, axis=0)


def thirds(triple, width):
    return [triple[:, i * width : (i + 1) * width] for i in range(triple.shape[1] // width)]


def lane_head(block):
    return lax.broadcasted_iota(jnp.int32, block.shape, 1) // HEAD_DIM


def spread(block):
    lanes = lane_head(block)
    zero = jnp.zeros_like(block)
    heads = block.shape[1] // HEAD_DIM
    return stack_rows([jnp.where(lanes == h, block, zero) for h in range(heads)])


def gathered(block):
    parts = cut(block, block.shape[1] // HEAD_DIM)
    lanes = lane_head(parts[0])
    out = parts[0]
    for h in range(1, len(parts)):
        out = jnp.where(lanes == h, parts[h], out)
    return out


def attend(query, key, value, mask, blocks):
    pairs = zip(cut(query, blocks), cut(key, blocks))
    scores = stack_rows([jnp.where(mask, dot_nt(spread(q), k) * SCALE, -1e30) for q, k in pairs])
    powered = jnp.exp(scores - jnp.max(scores, axis=-1, keepdims=True))
    probs = (powered * (1.0 / jnp.sum(powered, axis=-1, keepdims=True))).astype(BF)
    mixed = [gathered(dot_nn(p, v)) for p, v in zip(cut(probs, blocks), cut(value, blocks))]
    return probs, stack_rows(mixed).astype(BF)


def attend_back(query, key, value, probs, grad_context, blocks):
    queries, keys, values = cut(query, blocks), cut(key, blocks), cut(value, blocks)
    contexts, weights = [spread(g) for g in cut(grad_context, blocks)], cut(probs, blocks)
    grad_probs = stack_rows([dot_nt(g, v) for g, v in zip(contexts, values)])
    grad_value = stack_rows([dot_tn(p, g) for p, g in zip(weights, contexts)]).astype(BF)
    wide = probs.astype(F32)
    inner = jnp.sum(grad_probs * wide, axis=-1, keepdims=True)
    grad_scores = cut((wide * (grad_probs - inner) * SCALE).astype(BF), blocks)
    grad_query = stack_rows([gathered(dot_nn(s, k)) for s, k in zip(grad_scores, keys)])
    grad_key = stack_rows([dot_tn(s, spread(q)) for s, q in zip(grad_scores, queries)])
    return grad_query.astype(BF), grad_key.astype(BF), grad_value


def load_weight(pieces, weight, column=0):
    row = 0
    for piece in pieces:
        for part in range(piece.shape[1]):
            rows, columns = piece.shape[2:]
            weight[row : row + rows, column : column + columns] = piece[0, part]
            row += rows


def store_weight(value, pieces):
    row = 0
    for piece in pieces:
        for part in range(piece.shape[1]):
            rows = piece.shape[2]
            piece[0, part] = value[row : row + rows, :].astype(piece.dtype)
            row += rows


def cross_forward_kernel(width, blocks, lang, vis, norm, lang_col, lang_row, vis_col, vis_row, *refs):
    first, second, refs = refs[:8], refs[8:16], refs[16:]
    lang_one, lang_n, lang_r, vis_one, vis_n, vis_r = refs[:6]
    lang_qkv, vis_qkv, lang_ctx, vis_ctx, lang_p, vis_p = refs[6:12]
    weight, lang_acc, vis_acc = refs[12:]
    load_weight(first, weight)
    load_weight(second, weight, first[0].shape[3])
    step = pl.program_id(0)

    @pl.when(step == 0)
    def _():
        lang_acc[...] = lang[...].astype(F32)
        vis_acc[...] = vis[...].astype(F32)

    full = weight[...]
    in_part, out_part = full[:, : 3 * width], full[:, 3 * width :]
    lang_triple = dot_nn(lang[...], in_part).astype(BF)
    vis_triple = dot_nn(vis[...], in_part).astype(BF)
    lang_qkv[0] = lang_triple
    vis_qkv[0] = vis_triple
    lang_query, lang_key, lang_value = thirds(lang_triple, width)
    vis_query, vis_key, vis_value = thirds(vis_triple, width)
    for query, key, value, probs_ref, ctx_ref, acc, mask in (
        (lang_query, vis_key, vis_value, lang_p, lang_ctx, lang_acc, lang_col[...] == vis_row[...]),
        (vis_query, lang_key, lang_value, vis_p, vis_ctx, vis_acc, vis_col[...] == lang_row[...]),
    ):
        probs, context = attend(query, key, value, mask, blocks)
        probs_ref[0] = probs
        ctx_ref[0] = context
        acc[...] += dot_nt(context, out_part)

    @pl.when(step == pl.num_programs(0) - 1)
    def _():
        for acc, one, n_ref, r_ref in (
            (lang_acc, lang_one, lang_n, lang_r),
            (vis_acc, vis_one, vis_n, vis_r),
        ):
            out, normed, inverse = norm_forward(acc[...], norm[0:1, :], norm[1:2, :])
            one[...] = out.astype(BF)
            n_ref[...] = normed
            r_ref[...] = inverse


def self_forward_kernel(width, blocks, rows, norm, col, row, *refs):
    pieces, refs = refs[:4], refs[4:]
    two, n_ref, r_ref, qkv, ctx, probs_ref, weight, acc = refs
    load_weight(pieces, weight)
    step = pl.program_id(0)

    @pl.when(step == 0)
    def _():
        acc[...] = rows[...].astype(F32)

    full = weight[...]
    in_part, out_part = full[:, : 3 * width], full[:, 3 * width :]
    triple = dot_nn(rows[...], in_part).astype(BF)
    qkv[0] = triple
    probs, context = attend(*thirds(triple, width), col[...] == row[...], blocks)
    probs_ref[0] = probs
    ctx[0] = context
    acc[...] += dot_nt(context, out_part)

    @pl.when(step == pl.num_programs(0) - 1)
    def _():
        out, normed, inverse = norm_forward(acc[...], norm[0:1, :], norm[1:2, :])
        two[...] = out.astype(BF)
        n_ref[...] = normed
        r_ref[...] = inverse


def feed_up_kernel(rows, *refs):
    pieces, refs = refs[:4], refs[4:]
    active_ref, slope_ref, weight = refs
    load_weight(pieces, weight)
    hidden = dot_nn(rows[...], weight[...])
    normal = 0.5 * (1.0 + lax.erf(hidden * 0.7071067811865476))
    slope = normal + hidden * jnp.exp(-0.5 * hidden * hidden) * 0.3989422804014327
    active_ref[0] = (hidden * normal).astype(BF)
    slope_ref[0] = slope.astype(slope_ref.dtype)


def feed_down_kernel(active, normed_two, cot, norm, *refs):
    pieces, grads, refs = refs[:4], refs[4:8], refs[8:]
    three, inward_ref, gain_ref, shift_ref, weight, acc, turned = refs
    step, groups = pl.program_id(0), pl.num_programs(0) // 2

    @pl.when(step == 0)
    def _():
        acc[...] = normed_two[...] * norm[0:1, :] + norm[1:2, :]

    @pl.when(step < groups)
    def _():
        load_weight(pieces, weight)
        acc[...] += dot_nt(active[0], weight[...])

    @pl.when(step == groups - 1)
    def _():
        gain = norm[2:3, :]
        out, normed, inverse = norm_forward(acc[...], gain, norm[3:4, :])
        three[...] = out.astype(BF)
        inward, gain_term, shift_term = norm_backward(cot[...].astype(F32), gain, normed, inverse)
        inward_ref[...] = inward
        turned[...] = inward.astype(BF).T
        gain_ref[...] = gain_term
        shift_ref[...] = shift_term

    @pl.when(step >= groups)
    def _():
        store_weight(dot_nn(turned[...], active[0]), grads)


def feed_back_kernel(inward, rows, slope, normed, inverse, norm, *refs):
    in_pieces, out_pieces, grads, refs = refs[:4], refs[4:8], refs[8:12], refs[12:]
    down_ref, gain_ref, shift_ref, weight_in, weight_out, acc, branch, turned = refs
    load_weight(in_pieces, weight_in)
    load_weight(out_pieces, weight_out)
    step = pl.program_id(0)

    @pl.when(step == 0)
    def _():
        acc[...] = inward[...]
        branch[...] = inward[...].astype(BF)
        turned[...] = rows[...].T

    grad_active = dot_nn(branch[...], weight_out[...])
    grad_hidden = (grad_active * slope[0].astype(F32)).astype(BF)
    store_weight(dot_nn(turned[...], grad_hidden), grads)
    acc[...] += dot_nt(grad_hidden, weight_in[...])

    @pl.when(step == pl.num_programs(0) - 1)
    def _():
        down, gain_term, shift_term = norm_backward(
            acc[...], norm[0:1, :], normed[...], inverse[...]
        )
        down_ref[...] = down
        gain_ref[...] = gain_term
        shift_ref[...] = shift_term


def self_backward_kernel(width, blocks, inward, rows, qkv, ctx, probs, *refs):
    pieces, grads, refs = refs[:4], refs[4:8], refs[8:]
    down_ref, weight, acc, branch, turned, branch_turned = refs
    load_weight(pieces, weight)
    step = pl.program_id(0)

    @pl.when(step == 0)
    def _():
        acc[...] = inward[...]
        gradient = inward[...].astype(BF)
        branch[...] = gradient
        branch_turned[...] = gradient.T
        turned[...] = rows[...].T

    full = weight[...]
    in_part, out_part = full[:, : 3 * width], full[:, 3 * width :]
    grad_context = dot_nn(branch[...], out_part).astype(BF)
    grads_of = attend_back(*thirds(qkv[0], width), probs[0], grad_context, blocks)
    grad_triple = jnp.concatenate(grads_of, axis=1)
    in_grad = dot_nn(turned[...], grad_triple).astype(BF)
    out_grad = dot_nn(branch_turned[...], ctx[0]).astype(BF)
    store_weight(jnp.concatenate([in_grad, out_grad], axis=1), grads)
    acc[...] += dot_nt(grad_triple, in_part)

    @pl.when(step == pl.num_programs(0) - 1)
    def _():
        down_ref[...] = acc[...].astype(down_ref.dtype)


def cross_backward_kernel(
    width, blocks, lang_up, vis_up, lang, vis, lang_n, lang_r, vis_n, vis_r, norm, *refs
):
    lang_qkv, vis_qkv, lang_ctx, vis_ctx, lang_p, vis_p = refs[:6]
    first, second, refs = refs[6:14], refs[14:22], refs[22:]
    first_grads, second_grads, refs = refs[:8], refs[8:16], refs[16:]
    lang_out, vis_out, gain_ref, shift_ref = refs[:4]
    weight, lang_acc, vis_acc, lang_branch, vis_branch, turned, branch_turned = refs[4:]
    load_weight(first, weight)
    load_weight(second, weight, first[0].shape[3])
    step = pl.program_id(0)

    @pl.when(step == 0)
    def _():
        gain_total, shift_total = 0.0, 0.0
        for up, n_ref, r_ref, acc, branch in (
            (lang_up, lang_n, lang_r, lang_acc, lang_branch),
            (vis_up, vis_n, vis_r, vis_acc, vis_branch),
        ):
            inward, gain_term, shift_term = norm_backward(
                up[...].astype(F32), norm[0:1, :], n_ref[...], r_ref[...]
            )
            acc[...] = inward
            branch[...] = inward.astype(BF)
            gain_total += gain_term
            shift_total += shift_term
        gain_ref[...] = gain_total
        shift_ref[...] = shift_total
        turned[...] = stack_rows([lang[...], vis[...]]).T
        branch_turned[...] = stack_rows([lang_branch[...], vis_branch[...]]).T

    full = weight[...]
    in_part, out_part = full[:, : 3 * width], full[:, 3 * width :]
    lang_gc = dot_nn(lang_branch[...], out_part).astype(BF)
    vis_gc = dot_nn(vis_branch[...], out_part).astype(BF)
    lang_query, lang_key, lang_value = thirds(lang_qkv[0], width)
    vis_query, vis_key, vis_value = thirds(vis_qkv[0], width)
    lang_dq, vis_dk, vis_dv = attend_back(
        lang_query, vis_key, vis_value, lang_p[0], lang_gc, blocks
    )
    vis_dq, lang_dk, lang_dv = attend_back(
        vis_query, lang_key, lang_value, vis_p[0], vis_gc, blocks
    )
    lang_grad = jnp.concatenate([lang_dq, lang_dk, lang_dv], axis=1)
    vis_grad = jnp.concatenate([vis_dq, vis_dk, vis_dv], axis=1)
    in_grad = dot_nn(turned[...], stack_rows([lang_grad, vis_grad]))
    out_grad = dot_nn(branch_turned[...], stack_rows([lang_ctx[0], vis_ctx[0]]))
    grad = jnp.concatenate([in_grad.astype(BF), out_grad.astype(BF)], axis=1)
    middle = first[0].shape[3]
    store_weight(grad[:, :middle], first_grads)
    store_weight(grad[:, middle:], second_grads)
    lang_acc[...] += dot_nt(lang_grad, in_part)
    vis_acc[...] += dot_nt(vis_grad, in_part)

    @pl.when(step == pl.num_programs(0) - 1)
    def _():
        lang_out[...] = lang_acc[...].astype(lang_out.dtype)
        vis_out[...] = vis_acc[...].astype(vis_out.dtype)


def store_step(state, clip, outs):
    new = adamw_step(*state, MATRIX_RATE, clip[0, 0])
    for (ref, place), value in zip(outs, new[:4] + (new[3], new[4])):
        ref[place] = value.astype(ref.dtype)


def attn_step_kernel(width, clip, grad, *refs):
    ins, outs, refs = refs[:4], refs[4:8], refs[8:]
    for kind in range(3):
        part = grad[0, :, kind * width : (kind + 1) * width]
        store_step([part] + [ref[0, kind] for ref in ins], clip, [(r, (0, kind)) for r in refs[:6]])
    part = grad[0, :, 3 * width :].T
    store_step([part] + [ref[0] for ref in outs], clip, [(r, 0) for r in refs[6:]])


def feed_step_kernel(clip, up, down, *refs):
    ins, outs, refs = refs[:4], refs[4:8], refs[8:]
    store_step([up[0]] + [ref[0] for ref in ins], clip, [(r, 0) for r in refs[:6]])
    store_step([down[0]] + [ref[0] for ref in outs], clip, [(r, 0) for r in refs[6:]])


def whole(shape):
    return pl.BlockSpec(shape, lambda m: (0,) * len(shape))


def per_step(shape):
    rest = (0,) * (len(shape) - 1)
    return pl.BlockSpec((1,) + tuple(shape[1:]), lambda m: (m,) + rest)


def held(shape, steps):
    rest = (0,) * (len(shape) - 1)
    last = shape[0] - 1
    return pl.BlockSpec((1,) + tuple(shape[1:]), lambda m: (jnp.minimum(m, last),) + rest)


def again(shape, steps):
    rest = (0,) * (len(shape) - 1)
    groups = shape[0]
    return pl.BlockSpec((1,) + tuple(shape[1:]), lambda m: (lax.rem(m, groups),) + rest)


def late(shape, steps):
    rest = (0,) * (len(shape) - 1)
    skip = steps - shape[0]
    return pl.BlockSpec((1,) + tuple(shape[1:]), lambda m: (jnp.maximum(m - skip, 0),) + rest)


def call(kernel, steps, ins, outs, scratch, name, flops):
    spec = {
        "whole": lambda s: whole(s),
        "step": lambda s: per_step(s),
        "held": lambda s: held(s, steps),
        "again": lambda s: again(s, steps),
        "late": lambda s: late(s, steps),
        "scalar": lambda s: pl.BlockSpec(memory_space=pltpu.SMEM),
    }
    moved = sum(a.size * a.dtype.itemsize for _, a in ins)
    moved += sum(math.prod(s) * jnp.dtype(t).itemsize for _, s, t in outs)
    return pl.pallas_call(
        kernel,
        grid=(steps,),
        in_specs=[spec[kind](a.shape) for kind, a in ins],
        out_specs=[spec[kind](s) for kind, s, _ in outs],
        out_shape=[jax.ShapeDtypeStruct(s, t) for _, s, t in outs],
        scratch_shapes=[pltpu.VMEM(s, t) for s, t in scratch],
        compiler_params=pltpu.CompilerParams(
            vmem_limit_bytes=VMEM_LIMIT, dimension_semantics=("arbitrary",)
        ),
        cost_estimate=pl.CostEstimate(flops=flops, bytes_accessed=moved, transcendentals=0),
        name=name,
    )(*[a for _, a in ins])


def swap_dp(value, bit):
    count = lax.axis_size("dp")
    return lax.ppermute(value, "dp", [(i, i ^ (1 << bit)) for i in range(count)])


def swap_mp(value, bit):
    count = lax.axis_size("mp")
    return lax.ppermute(value, "mp", [(i, i ^ (1 << bit)) for i in range(count)])


def after(value, *others):
    flat, tree = jax.tree.flatten(value)
    kept = lax.optimization_barrier((flat, jax.tree.leaves(others)))[0]
    return jax.tree.unflatten(tree, kept)


def extra_bits():
    return range(3, int(math.log2(lax.axis_size("dp"))))


def mp_bits():
    return range(int(math.log2(lax.axis_size("mp"))))


def gather_mp(current):
    for bit in reversed(mp_bits()):
        current = jnp.concatenate([current, swap_mp(current, bit)], axis=0)
    return current


def gather_extra(current):
    for bit in extra_bits():
        current = jnp.concatenate([current, swap_dp(current, bit)], axis=2)
    return current


def scatter_mp(current):
    for bit in mp_bits():
        half = current.shape[0] // 2
        current = added(current[:half], swap_mp(current[half:], bit))
    return current


def scatter_extra(current):
    for bit in reversed(extra_bits()):
        half = current.shape[2] // 2
        current = added(current[:, :, :half], swap_dp(current[:, :, half:], bit))
    return current


def added(mine, theirs):
    return (mine.astype(F32) + theirs.astype(F32)).astype(BF)


def grow(found, place, bit):
    for key in list(found):
        new = list(key)
        new[place] = 1
        found[tuple(new)] = swap_dp(found[key], bit)


def shrink(found, place, bit):
    for key in [k for k in found if k[place] == 0]:
        far = list(key)
        far[place] = 1
        found[key] = added(found[key], swap_dp(found.pop(tuple(far)), bit))


def home_list(found):
    return [found[(hi, mid, lo)] for hi in (0, 1) for lo in (0, 1) for mid in (0, 1)]


def stream_list(found):
    return [found[(hi, lo)] for hi in (0, 1) for lo in (0, 1)]


def home_keys(arrays):
    return {(i >> 2, i & 1, (i >> 1) & 1): a for i, a in enumerate(arrays)}


def stream_keys(arrays):
    return {(i >> 1, i & 1): a for i, a in enumerate(arrays)}


def adamw_step(gradient, moment, square, weight, average, rate, clip_scale):
    average_decay = min(AVERAGE_CEILING, (1.0 + STEP) / (10.0 + STEP))
    clipped = gradient * clip_scale
    moment_new = BETA_FIRST * moment + (1.0 - BETA_FIRST) * clipped
    square_new = BETA_SECOND * square + (1.0 - BETA_SECOND) * clipped * clipped
    corrected = moment_new / (1.0 - BETA_FIRST**STEP)
    denominator = jnp.sqrt(square_new / (1.0 - BETA_SECOND**STEP)) + ADAM_EPS
    weight_new = weight - rate * (corrected / denominator + WEIGHT_DECAY * weight)
    average_new = average_decay * average + (1.0 - average_decay) * weight_new
    return (clipped, moment_new, square_new, weight_new, average_new)


def pad_rows(block, rows):
    return jnp.pad(block, ((0, rows - block.shape[0]), (0, 0)))


def local(
    language,
    images,
    counts,
    language_cot,
    vision_cot,
    attn_in_weight,
    attn_in_moment,
    attn_in_square,
    attn_in_average,
    attn_out_weight,
    attn_out_moment,
    attn_out_square,
    attn_out_average,
    ffn_in_weight,
    ffn_in_moment,
    ffn_in_square,
    ffn_in_average,
    ffn_out_weight,
    ffn_out_moment,
    ffn_out_square,
    ffn_out_average,
    norm_weight,
    norm_moment,
    norm_square,
    norm_average,
):
    n_dp, n_mp = lax.axis_size("dp"), lax.axis_size("mp")
    me = lax.axis_index("dp")
    stream = (me >> 1) & 1
    is_vis = stream == 1
    own_items, words, dim = language.shape
    regions = images.shape[1]
    blocks = own_items // GROUP
    lang_block, vis_block = (-(-GROUP * rows // 16) * 16 for rows in (words, regions))
    lang_pad, slot = blocks * lang_block, blocks * vis_block
    total = 2 * slot
    shard_rows = attn_in_weight.shape[1]
    width = attn_in_weight.shape[3]
    units = ffn_in_weight.shape[2]
    heads = width // HEAD_DIM
    half = 2 * width
    eighth = dim // 8

    def mine_first(pair):
        return jnp.where(is_vis, pair[1], pair[0]), jnp.where(is_vis, pair[0], pair[1])

    attn_shards = [
        jnp.concatenate(
            [attn_in_weight[b].reshape(shard_rows, 3 * width), attn_out_weight[b].T], axis=1
        ).astype(BF)[None, None]
        for b in range(3)
    ]
    up_shards = [ffn_in_weight[s].astype(BF)[None, None] for s in range(2)]
    down_shards = [ffn_out_weight[s].T.astype(BF)[None, None] for s in range(2)]

    def pair_up(shards):
        own, other = mine_first(shards)
        return jnp.concatenate([own, swap_dp(other, 1)], axis=1)

    first, second = (gather_extra(gather_mp(attn_shards[0][..., c : c + half])) for c in (0, half))
    first, second = {(0, 0, 0): first}, {(0, 0, 0): second}
    down_pair = pair_up(down_shards)
    self_pair = pair_up(attn_shards[1:])
    up_pair = pair_up(up_shards)
    down_pair = jnp.stack([down_pair, swap_dp(down_pair, 2)], axis=1)
    grow(first, 0, 2)
    grow(second, 1, 1)
    self_w = {(0, 0): gather_extra(gather_mp(self_pair))}
    grow(first, 1, 1)
    grow(second, 0, 2)
    grow(first, 2, 0)
    grow(second, 2, 0)

    place = jnp.arange(dim, dtype=jnp.int32)
    block = place // shard_rows
    sub, high = block % (n_dp // 8), block // (n_dp // 8)
    relative = 8 * sub + 4 * (high >> 2) + ((high >> 1) & 1) + 2 * (high & 1)
    origin = (relative ^ me) * shard_rows + place % shard_rows
    order = (place[:, None] == origin[None, :]).astype(BF)

    def to_order(value):
        return dot_nn(value, order).astype(BF)

    def from_order(value, precision=None):
        return lax.dot_general(
            value, order, (((1,), (1,)), ((), ())), preferred_element_type=F32, precision=precision
        )

    def flip(value):
        parts = value.reshape(value.shape[0], 4, 2, eighth)
        return parts[:, :, ::-1, :].reshape(value.shape)

    norm_ordered = lax.dot_general(
        norm_weight.reshape(-1, dim),
        order.astype(F32),
        (((1,), (0,)), ((), ())),
        precision=HIGHEST,
        preferred_element_type=F32,
    ).reshape(norm_weight.shape)
    norm_cross = norm_ordered[:, 0]
    norm_self = jnp.where(is_vis, norm_ordered[:, 2], norm_ordered[:, 1])
    norm_feed = jnp.where(is_vis, norm_ordered[:, 4], norm_ordered[:, 3])
    norm_pair = jnp.concatenate([norm_self, norm_feed], axis=0)

    def in_blocks(value, rows, target):
        value = value.reshape(blocks, rows, dim)
        value = jnp.pad(value, ((0, 0), (0, target - rows), (0, 0)))
        return value.reshape(blocks * target, dim)

    def out_of_blocks(value, rows):
        return value.reshape(blocks, -1, dim)[:, :rows].reshape(blocks * rows, dim)

    lang_rows, vis_rows = GROUP * words, GROUP * regions
    first_item = lax.axis_index("mp") * own_items
    bounds = jnp.cumsum(counts[0])
    positions = first_item + jnp.arange(own_items, dtype=jnp.int32)
    item_image = jnp.sum((bounds[None, :] <= positions[:, None]).astype(jnp.int32), axis=1)
    region = jnp.arange(regions, dtype=jnp.int32)
    row_source = (item_image[:, None] * regions + region[None, :]).reshape(blocks, vis_rows) + 1
    row_source = jnp.pad(row_source, ((0, 0), (0, vis_block - vis_rows))).reshape(slot, 1)
    picker = (
        row_source == 1 + jnp.arange(images.shape[0] * regions, dtype=jnp.int32)[None, :]
    ).astype(BF)
    lang = to_order(in_blocks(language, lang_rows, lang_block))
    image_rows = to_order(images.reshape(-1, dim))
    vis = dot_nn(picker, image_rows).astype(BF)

    lang_cot = in_blocks(language_cot, lang_rows, vis_block)
    vis_cot = in_blocks(vision_cot, vis_rows, vis_block)
    cot_own, cot_other = mine_first((lang_cot, vis_cot))

    lang_ids = jnp.arange(lang_block, dtype=jnp.int32) // words
    vis_ids = jnp.arange(vis_block, dtype=jnp.int32) // regions
    slot_ids = jnp.where(is_vis, vis_ids, jnp.arange(vis_block, dtype=jnp.int32) // words)

    def tall(ids):
        return jnp.tile(ids, heads)[:, None]

    pieces = lambda arrays: [("step", a) for a in arrays]
    ins = [("whole", a) for a in (lang, vis, norm_cross)]
    ins += [
        ("whole", a)
        for a in (tall(lang_ids), lang_ids[None, :], tall(vis_ids), vis_ids[None, :])
    ]
    outs = []
    for rows in (lang_pad, slot):
        outs += [
            ("whole", (rows, dim), BF),
            ("whole", (rows, dim), F32),
            ("whole", (rows, 1), F32),
        ]
    outs += [("step", (n_mp, rows, 3 * width), BF) for rows in (lang_pad, slot)]
    outs += [("step", (n_mp, rows, width), BF) for rows in (lang_pad, slot)]
    outs += [
        ("step", (n_mp, heads * lang_pad, vis_block), BF),
        ("step", (n_mp, heads * slot, lang_block), BF),
    ]
    both = lang_pad + slot
    cross_w = home_list(first) + home_list(second)
    cross_w = after(cross_w, down_pair, self_w, up_pair)
    found = call(
        functools.partial(cross_forward_kernel, width, blocks),
        n_mp,
        ins + pieces(cross_w),
        outs,
        [((dim, 4 * width), BF), ((lang_pad, dim), F32), ((slot, dim), F32)],
        "cross_forward",
        12 * both * dim * 4 * width * n_mp,
    )
    lang_one, lang_n, lang_r, vis_one, vis_n, vis_r = found[:6]
    cross_saved = found[6:]

    grow(self_w, 0, 2)
    up_pair = gather_mp(up_pair)
    lang_wide = lang_one.reshape(blocks, lang_block, dim)
    lang_wide = jnp.pad(lang_wide, ((0, 0), (0, vis_block - lang_block), (0, 0)))
    own_one, other_one = mine_first((lang_wide.reshape(slot, dim), vis_one))
    rows_one = jnp.concatenate([own_one, flip(swap_dp(other_one, 1))], axis=0)
    grow(self_w, 1, 0)
    self_pieces = after(stream_list(self_w), up_pair)
    rows_two, normed_two, inverse_two, self_qkv, self_ctx, self_probs = call(
        functools.partial(self_forward_kernel, width, 2 * blocks),
        n_mp,
        [("whole", a) for a in (rows_one, norm_self, tall(slot_ids), slot_ids[None, :])]
        + pieces(self_pieces),
        [
            ("whole", (total, dim), BF),
            ("whole", (total, dim), F32),
            ("whole", (total, 1), F32),
            ("step", (n_mp, total, 3 * width), BF),
            ("step", (n_mp, total, width), BF),
            ("step", (n_mp, heads * total, vis_block), BF),
        ],
        [((dim, 4 * width), BF), ((total, dim), F32)],
        "self_forward",
        12 * total * dim * 4 * width * n_mp,
    )
    up_w = {(0, 0): gather_extra(up_pair)}
    grow(up_w, 0, 2)
    grow(up_w, 1, 0)
    up_w = stream_list(up_w)
    down_all = gather_mp(down_pair)
    down_w = {(h, 0): gather_extra(down_all[:, h]) for h in range(2)}
    grow(down_w, 1, 0)
    cot = to_order(jnp.concatenate([cot_own, swap_dp(cot_other, 1)], axis=0))

    active, slope = call(
        feed_up_kernel,
        n_mp,
        [("whole", rows_two)] + pieces(up_w),
        [("step", (n_mp, total, units), BF), ("step", (n_mp, total, units), BF)],
        [((dim, units), BF)],
        "feed_up",
        10 * total * dim * units * n_mp,
    )
    down_w = stream_list(down_w)
    stream_grad = [("step", (n_mp, 2, eighth, units), BF)] * 4
    found = call(
        feed_down_kernel,
        2 * n_mp,
        [("again", active)]
        + [("whole", a) for a in (normed_two, cot, norm_pair)]
        + [("held", a) for a in down_w],
        [("late", s, t) for _, s, t in stream_grad]
        + [
            ("whole", (total, dim), BF),
            ("whole", (total, dim), F32),
            ("whole", (1, dim), F32),
            ("whole", (1, dim), F32),
        ],
        [((dim, units), BF), ((total, dim), F32), ((dim, total), BF)],
        "feed_down",
        8 * total * dim * units * n_mp,
    )
    down_g = stream_keys(found[:4])
    rows_three, inward, feed_gain, feed_shift = found[4:]

    found = call(
        feed_back_kernel,
        n_mp,
        [("whole", inward), ("whole", rows_two), ("step", slope)]
        + [("whole", a) for a in (normed_two, inverse_two, norm_self)]
        + pieces(up_w)
        + pieces(down_w),
        stream_grad
        + [("whole", (total, dim), F32), ("whole", (1, dim), F32), ("whole", (1, dim), F32)],
        [
            ((dim, units), BF),
            ((dim, units), BF),
            ((total, dim), F32),
            ((total, dim), BF),
            ((dim, total), BF),
        ],
        "feed_back",
        12 * total * dim * units * n_mp,
    )
    up_g = stream_keys(found[:4])
    inward, self_gain, self_shift = found[4:]
    shrink(down_g, 1, 0)
    found = call(
        functools.partial(self_backward_kernel, width, 2 * blocks),
        n_mp,
        [("whole", after(inward, down_g)), ("whole", rows_one)]
        + [("step", a) for a in (self_qkv, self_ctx, self_probs)]
        + pieces(self_pieces),
        [("step", (n_mp, 2, eighth, 4 * width), BF)] * 4 + [("whole", (total, dim), BF)],
        [((dim, 4 * width), BF), ((total, dim), F32), ((total, dim), BF)] + [((dim, total), BF)] * 2,
        "self_backward",
        20 * total * dim * 4 * width * n_mp,
    )
    self_g = stream_keys(found[:4])
    back = found[4]
    shrink(up_g, 1, 0)
    down_g = {k: scatter_mp(scatter_extra(v)) for k, v in down_g.items()}
    back_other = swap_dp(flip(back[slot:]), 1)
    lang_up = jnp.where(is_vis, back_other, back[:slot])
    lang_up = lang_up.reshape(blocks, vis_block, dim)[:, :lang_block].reshape(lang_pad, dim)
    vis_up = jnp.where(is_vis, back[:slot], back_other)
    lang_up = after(lang_up, up_g)
    found = call(
        functools.partial(cross_backward_kernel, width, blocks),
        n_mp,
        [("whole", a) for a in (lang_up, vis_up, lang, vis, lang_n, lang_r, vis_n, vis_r, norm_cross)]
        + [("step", a) for a in cross_saved]
        + pieces(cross_w),
        [("step", (n_mp, 1, eighth, half), BF)] * 16
        + [
            ("whole", (lang_pad, dim), BF),
            ("whole", (slot, dim), BF),
            ("whole", (1, dim), F32),
            ("whole", (1, dim), F32),
        ],
        [
            ((dim, 4 * width), BF),
            ((lang_pad, dim), F32),
            ((slot, dim), F32),
            ((lang_pad, dim), BF),
            ((slot, dim), BF),
            ((dim, both), BF),
            ((dim, both), BF),
        ],
        "cross_backward",
        20 * both * dim * 4 * width * n_mp,
    )
    first_g, second_g = home_keys(found[:8]), home_keys(found[8:16])
    lang_back, vis_back, cross_gain, cross_shift = found[16:]
    shrink(self_g, 1, 0)
    shrink(up_g, 0, 2)
    shrink(first_g, 2, 0)
    shrink(second_g, 2, 0)
    shrink(first_g, 1, 1)
    shrink(second_g, 0, 2)
    shrink(down_g, 0, 2)
    shrink(self_g, 0, 2)
    shrink(first_g, 0, 2)
    shrink(second_g, 1, 1)

    def finish_home(found):
        return scatter_mp(scatter_extra(found[(0, 0, 0)]))[0, 0].astype(F32)

    def finish_stream(pair):
        mine, theirs = pair[0, 0].astype(F32), swap_dp(pair[0, 1], 1).astype(F32)
        return [jnp.where(is_vis, theirs, mine), jnp.where(is_vis, mine, theirs)]

    up_total = finish_stream(scatter_mp(scatter_extra(up_g[(0, 0)])))
    down_total = finish_stream(down_g[(0, 0)])
    self_total = finish_stream(scatter_mp(scatter_extra(self_g[(0, 0)])))
    attn_total = [jnp.concatenate([finish_home(first_g), finish_home(second_g)], axis=1)]
    attn_total += self_total

    final = from_order(rows_three).astype(BF)
    final_other = swap_dp(final[slot:], 1)
    language_out = out_of_blocks(jnp.where(is_vis, final_other, final[:slot]), lang_rows)
    vision_out = out_of_blocks(jnp.where(is_vis, final[:slot], final_other), vis_rows)
    language_grad = from_order(out_of_blocks(lang_back, lang_rows)).reshape(language.shape)
    image_term = lax.dot_general(
        picker, vis_back, (((0,), (0,)), ((), ())), preferred_element_type=F32
    ).astype(BF)
    image_term = from_order(image_term).astype(BF)
    image_grad = lax.psum(image_term, "mp")

    here = (jnp.arange(2, dtype=jnp.int32) == stream).astype(F32)[None, :, None]
    norm_partial = jnp.concatenate(
        [
            jnp.stack([cross_gain, cross_shift]),
            here * jnp.stack([self_gain, self_shift]),
            here * jnp.stack([feed_gain, feed_shift]),
        ],
        axis=1,
    )
    norm_partial = from_order(norm_partial.reshape(-1, dim).astype(F32), HIGHEST)

    squares = sum(jnp.sum(g * g) for g in attn_total + up_total + down_total)
    sums = jnp.concatenate([norm_partial, jnp.full((1, dim), squares)], axis=0)
    for bit in reversed(mp_bits()):
        sums += swap_mp(sums, bit)
    for bit in reversed(range(int(math.log2(n_dp)))):
        sums += swap_dp(sums, bit)
    norm_total = sums[:-1].reshape(norm_weight.shape)
    total_squares = sums[-1, 0] + jnp.sum(norm_total * norm_total)
    grad_norm = jnp.sqrt(total_squares)
    clip_scale = CLIP_NORM / jnp.maximum(grad_norm, CLIP_NORM)
    image_grad = after(image_grad, clip_scale).astype(F32).reshape(images.shape)

    clip = clip_scale.reshape(1, 1)
    kinds = [("step", t) for t in (F32, F32, F32, F32, BF, F32)]
    wide_in = [jnp.swapaxes(a, 1, 2) for a in (attn_in_moment, attn_in_square, attn_in_weight, attn_in_average)]
    wide_out = [attn_out_moment, attn_out_square, attn_out_weight, attn_out_average]
    attn_new = call(
        functools.partial(attn_step_kernel, width),
        3,
        [("scalar", clip), ("step", jnp.stack(attn_total))] + [("step", a) for a in wide_in + wide_out],
        [(k, wide_in[0].shape, t) for k, t in kinds] + [(k, wide_out[0].shape, t) for k, t in kinds],
        [],
        "attn_step",
        20 * 4 * dim * width,
    )
    attn_new = [jnp.swapaxes(a, 1, 2) for a in attn_new[:6]] + list(attn_new[6:])
    feed_in = [ffn_in_moment, ffn_in_square, ffn_in_weight, ffn_in_average]
    feed_out = [jnp.swapaxes(a, 1, 2) for a in (ffn_out_moment, ffn_out_square, ffn_out_weight, ffn_out_average)]
    feed_new = call(
        feed_step_kernel,
        2,
        [("scalar", clip), ("step", jnp.stack(up_total)), ("step", jnp.stack(down_total))]
        + [("step", a) for a in feed_in + feed_out],
        [(k, feed_in[0].shape, t) for k, t in kinds * 2],
        [],
        "feed_step",
        20 * 4 * dim * units,
    )
    feed_new = list(feed_new[:6]) + [jnp.swapaxes(a, 1, 2) for a in feed_new[6:]]

    results = [
        language_out.reshape(language.shape),
        vision_out.reshape(vision_cot.shape),
        language_grad,
        image_grad,
    ]
    results += attn_new + feed_new
    results += adamw_step(
        norm_total, norm_moment, norm_square, norm_weight, norm_average, NORM_RATE, clip_scale
    )
    return tuple(results) + (grad_norm,)


def solution(mesh):
    rows = P(("dp", "mp"), None, None)
    attn_in, attn_out = P(None, "dp", None, "mp"), P(None, "mp", "dp")
    ffn_in, ffn_out = P(None, "dp", "mp"), P(None, "mp", "dp")
    in_specs = (rows, P("dp", None, None), P("dp", None), rows, rows)
    in_specs += (attn_in,) * 4 + (attn_out,) * 4 + (ffn_in,) * 4 + (ffn_out,) * 4 + (P(),) * 4
    out_specs = (rows, rows, rows, P("dp", None, None))
    out_specs += (attn_in,) * 6 + (attn_out,) * 6 + (ffn_in,) * 6 + (ffn_out,) * 6 + (P(),) * 6
    return jax.shard_map(local, mesh=mesh, in_specs=in_specs, out_specs=out_specs, check_vma=False)
```

time: 665 us -> 485 us (0.73)
  waiting for transfers between devices: 222 us -> 158 us
  local copies, waits for them, and re-layouts: 79.4 us -> 37.4 us
  blocking collectives: 39.4 us -> 0 us
  starting transfers between devices: 95 us -> 71.2 us
  other arithmetic: 51.6 us -> 42.2 us
    psum x1 -> x0, blocking collectives: 39.4 us -> none  [local(): lax.psum(local_squares, ('dp', 'mp')) + jnp.sum(norm_total * norm_total)]
    ppermute x24, starting transfers between devices: 66.9 us -> 28.1 us  [swap_mp(): return lax.ppermute(value, 'mp', [(i, i ^ 1 << bit) for i in range(count)])]
    ppermute x42 -> x59, waiting for transfers between devices: 120 us -> 85 us  [swap_dp(): return lax.ppermute(value, 'dp', [(i, i ^ 1 << bit) for i in range(count)])]
    unnamed x213 -> x154, local copies, waits for them, and re-layouts: 38.1 us -> 7.37 us
    psum x1, waiting for transfers between devices: 29.3 us -> 0.01 us  [local(): image_grad = lax.psum(image_term, 'mp')]
    ppermute x42 -> x59, starting transfers between devices: 28 us -> 43 us  [swap_dp(): return lax.ppermute(value, 'dp', [(i, i ^ 1 << bit) for i in range(count)])]
    ppermute x7 -> x1, local copies, waits for them, and re-layouts: 15.6 us -> 1.34 us  [swap_dp(): return lax.ppermute(value, 'dp', [(i, i ^ 1 << bit) for i in range(count)])]
    add x5 -> x1, other arithmetic: 9.16 us -> 0.07 us  [adamw_step(): average_new = average_decay * average + (1.0 - average_decay) * weight_new]
  transfers between devices with their start and end apart: 67 -> 84, of which waited for: 19 -> 27; matrix products, arithmetic and copies ran while one was open for 15% -> 18% of each run, Pallas kernels for 9% -> 21%
where the time goes in v2:
time: 485 us; the launch traced here: 477 us
  waiting for transfers between devices  158 us (33%)
  Pallas kernels  131 us (27%)
  starting transfers between devices  71.2 us (15%)
  other arithmetic  42.2 us (9%)
  local copies, waits for them, and re-layouts  37.4 us (8%)
  between operations  22.9 us (5%)
  matrix products  14.7 us (3%)
    pallas_call x9, Pallas kernels, call(): pl.pallas_call(kernel, grid=(steps,), in_specs=[spec[kind](a.shape) for k...  131 us
    ppermute x59, waiting for transfers between devices, swap_dp(): return lax.ppermute(value, 'dp', [(i, i ^ 1 << bit) for i in range(count)])  85 us
    ppermute x24, waiting for transfers between devices, swap_mp(): return lax.ppermute(value, 'mp', [(i, i ^ 1 << bit) for i in range(count)])  73.1 us
    ppermute x59, starting transfers between devices, swap_dp(): return lax.ppermute(value, 'dp', [(i, i ^ 1 << bit) for i in range(count)])  43 us
    ppermute x24, starting transfers between devices, swap_mp(): return lax.ppermute(value, 'mp', [(i, i ^ 1 << bit) for i in range(count)])  28.1 us
    convert_element_type x24, other arithmetic, added(): return (mine.astype(F32) + theirs.astype(F32)).astype(BF)  12.4 us
  transfers between devices with their start and end apart: 84, of which 27 were waited for; matrix products, arithmetic and copies ran while one was open for 18% of the time, Pallas kernels for 21%

profile of v2, /device:TPU:0, one launch (start us, length us, event | category | flops | bytes accessed | tf_op | source)
XLA Modules:
  0.0 477.2 jit_solution(11273979677954124237)
XLA Ops:
  9.7 3.0 collective-permute-start.20
  27.3 2.7 collective-permute-start.21
  32.5 3.5 collective-permute-done.10
  39.8 11.0 %collective-permute-done.21 = bf16[1,2,96,768]{3,2,1,0:T(8,128)(2,1)S(1)} collective-permute-done((bf16[1,2,96,768]{3,2,1,0:T(8,128)(2,1)S(1)}, bf16[1,2,96,768]{3,2,1,0:T(8,128)(2,1)S(1)}, u32[]{:S(2)}, u32[]{:S(2)}) %collective-permute-start.21) | collective-permute-done | bytes 294944 | tf_op jit(solution)/shard_map/ppermute | solution.py:444
  63.2 5.9 %collective-permute-done.15.refs_13_.refs_19_ = bf16[4,1,96,384]{3,2,1,0:T(8,128)(2,1)S(1)} collective-permute-done((bf16[4,1,96,384]{3,2,1,0:T(8,128)(2,1)}, bf16[4,1,96,384]{3,2,1,0:T(8,128)(2,1)S(1)}, u32[]{:S(2)}, u32[]{:S(2)}) %collective-permute-start.15) | collective-permute-done | bytes 294944 | tf_op jit(solution)/shard_map/ppermute | solution.py:439
  81.1 2.9 convolution_convert_fusion.vis
  86.9 10.4 %collective-permute-done.29 = bf16[2,2,96,768]{3,2,1,0:T(8,128)(2,1)} collective-permute-done((bf16[2,2,96,768]{3,2,1,0:T(8,128)(2,1)S(1)}, bf16[2,2,96,768]{3,2,1,0:T(8,128)(2,1)}, u32[]{:S(2)}, u32[]{:S(2)}) %collective-permute-start.29) | collective-permute-done | bytes 589856 | tf_op jit(solution)/shard_map/ppermute | solution.py:444
  108.8 14.4 %cross_forward.1 = (bf16[192,768]{1,0:T(8,128)(2,1)}, f32[192,768]{1,0:T(8,128)}, f32[192,1]{1,0:T(8,128)}, bf16[336,768]{1,0:T(8,128)(2,1)}, f32[336,768]{1,0:T...) custom-call(bf16[192,768]{1,0:T(8,128)(2,1)} %fusion.14.lang, ...), custom_call_target="tpu_custom_call" | custom-call | flops 14948499456 | bytes 12249920 | tf_op jit(solution)/shard_map/cross_forward/pallas_call | solution.py:422
  126.0 8.1 %collective-permute-done.26.refs_2_ = bf16[4,2,96,768]{3,2,1,0:T(8,128)(2,1)} collective-permute-done((bf16[4,2,96,768]{3,2,1,0:T(8,128)(2,1)}, bf16[4,2,96,768]{3,2,1,0:T(8,128)(2,1)}, u32[]{:S(2)}, u32[]{:S(2)}) %collective-permute-start.26) | collective-permute-done | bytes 1179680 | tf_op jit(solution)/shard_map/ppermute | solution.py:439
  136.1 3.0 fusion.10.cot
  144.8 13.4 %collective-permute-done.31.refs_2_ = bf16[4,2,96,768]{3,2,1,0:T(8,128)(2,1)} collective-permute-done((bf16[4,2,96,768]{3,2,1,0:T(8,128)(2,1)}, bf16[4,2,96,768]{3,2,1,0:T(8,128)(2,1)}, u32[]{:S(2)}, u32[]{:S(2)}) %collective-permute-start.31) | collective-permute-done | bytes 1179680 | tf_op jit(solution)/shard_map/ppermute | solution.py:439
  158.1 13.7 %self_forward.1 = (bf16[672,768]{1,0:T(8,128)(2,1)}, f32[672,768]{1,0:T(8,128)}, f32[672,1]{1,0:T(8,128)}, bf16[4,672,576]{2,1,0:T(8,128)(2,1)}, bf16[4,672,192]...) custom-call(bf16[672,768]{1,0:T(8,128)(2,1)} %pad_maximum_fusion.4.rows, f32[2,768]{1,0:T(2,128)} %copy-done.38, ...), custom_call_target="tpu_custom_call" | custom-call | flops 19025362944 | bytes 14793088 | tf_op jit(solution)/shard_map/self_forward/pallas_call | solution.py:422
  172.9 9.5 %feed_up.1 = (bf16[4,672,768]{2,1,0:T(8,128)(2,1)}, bf16[4,672,768]{2,1,0:T(8,128)(2,1)}) custom-call(bf16[672,768]{1,0:T(8,128)(2,1)} %get-tuple-element.163.rows, bf16[4,2,96,768]{3,2,1,0:T(8,128)(2,1)} %pad_maximum_fusion.2.refs_0_, bf16[4,2,96,768]{3,2,1,0:T(8,128)(2,1)} %collective-permute-done.30.refs_1_, ...), custom_call_target="tpu_custom_call" | custom-call | flops 15854469120 | bytes 14008320 | tf_op jit(solution)/shard_map/feed_up/pallas_call | solution.py:422
  183.8 17.0 %feed_down.1 = (bf16[4,2,96,768]{3,2,1,0:T(8,128)(2,1)}, bf16[4,2,96,768]{3,2,1,0:T(8,128)(2,1)}, bf16[4,2,96,768]{3,2,1,0:T(8,128)(2,1)}, bf16[4,2,96,768]{3,2,...) custom-call(bf16[4,672,768]{2,1,0:T(8,128)(2,1)} %get-tuple-element.164., ...), custom_call_target="tpu_custom_call" | custom-call | flops 12683575296 | bytes 19777536 | tf_op jit(solution)/shard_map/feed_down/pallas_call | solution.py:422
  201.5 18.9 %feed_back.1 = (bf16[4,2,96,768]{3,2,1,0:T(8,128)(2,1)}, bf16[4,2,96,768]{3,2,1,0:T(8,128)(2,1)}, bf16[4,2,96,768]{3,2,1,0:T(8,128)(2,1)}, bf16[4,2,96,768]{3,2,...) custom-call(f32[672,768]{1,0:T(8,128)} %get-tuple-element.167.inward, ...), custom_call_target="tpu_custom_call" | custom-call | flops 19025362944 | bytes 25524864 | tf_op jit(solution)/shard_map/feed_back/pallas_call | solution.py:422
  232.0 8.9 %collective-permute-done.74 = bf16[2,2,96,768]{3,2,1,0:T(8,128)(2,1)S(1)} collective-permute-done((bf16[2,2,96,768]{3,2,1,0:T(8,128)(2,1)S(1)}, bf16[2,2,96,768]{3,2,1,0:T(8,128)(2,1)S(1)}, u32[]{:S(2)}, u32[]{:S(2)}) %collective-permute-start.74) | collective-permute-done | bytes 589856 | tf_op jit(solution)/shard_map/ppermute | solution.py:444
  243.7 23.7 %self_backward.1 = (bf16[4,2,96,768]{3,2,1,0:T(8,128)(2,1)}, bf16[4,2,96,768]{3,2,1,0:T(8,128)(2,1)}, bf16[4,2,96,768]{3,2,1,0:T(8,128)(2,1)}, bf16[4,2,96,768]{3,2,1,0:T(8,128)(2,1)}, bf16[672,768]{1,0:T(8,128)(2,1)}) custom-call(f32[672,768]{1,0:T(8,128)} %get-tuple-element.175.inward, bf16[672,768]{1,0:T(8,128)(2,1)} %pad_maximum_fusion.4.rows, ...), custom_call_target="tpu_custom_call" | custom-call | flops 31708938240 | bytes 19501056 | tf_op jit(solution)/shard_map/self_backward/pallas_call | solution.py:422
  279.4 3.5 collective-permute-done.41
  293.4 21.6 %cross_backward.1 = (bf16[4,1,96,384]{3,2,1,0:T(8,128)(2,1)}, bf16[4,1,96,384]{3,2,1,0:T(8,128)(2,1)}, bf16[4,1,96,384]{3,2,1,0:T(8,128)(2,1)}, bf16[4,1,96,384]...) custom-call(bf16[192,768]{1,0:T(8,128)(2,1)} %bitcast.198, ...), custom_call_target="tpu_custom_call" | custom-call | flops 24914165760 | bytes 17782848 | tf_op jit(solution)/shard_map/cross_backward/pallas_call | solution.py:422
  316.9 3.1 fusion.13
  330.6 7.3 %collective-permute-done.49 = bf16[4,1,96,384]{3,2,1,0:T(8,128)(2,1)S(1)} collective-permute-done((bf16[4,1,96,384]{3,2,1,0:T(8,128)(2,1)S(1)}, bf16[4,1,96,384]{3,2,1,0:T(8,128)(2,1)S(1)}, u32[]{:S(2)}, u32[]{:S(2)}) %collective-permute-start.49) | collective-permute-done | bytes 294944 | tf_op jit(solution)/shard_map/ppermute | solution.py:439
  343.7 4.1 collective-permute-done.58
  349.9 27.8 %collective-permute-done.50 = bf16[4,1,96,384]{3,2,1,0:T(8,128)(2,1)S(1)} collective-permute-done((bf16[4,1,96,384]{3,2,1,0:T(8,128)(2,1)S(1)}, bf16[4,1,96,384]{3,2,1,0:T(8,128)(2,1)S(1)}, u32[]{:S(2)}, u32[]{:S(2)}) %collective-permute-start.50) | collective-permute-done | bytes 294944 | tf_op jit(solution)/shard_map/ppermute | solution.py:439
  385.0 3.1 collective-permute-done.59
  390.5 12.1 %collective-permute-done.60 = bf16[2,1,96,384]{3,2,1,0:T(8,128)(2,1)S(1)} collective-permute-done((bf16[2,1,96,384]{3,2,1,0:T(8,128)(2,1)S(1)}, bf16[2,1,96,384]{3,2,1,0:T(8,128)(2,1)S(1)}, u32[]{:S(2)}, u32[]{:S(2)}) %collective-permute-start.60) | collective-permute-done | bytes 147488 | tf_op jit(solution)/shard_map/ppermute | solution.py:444
  406.7 12.8 %collective-permute-done.66 = bf16[1,2,96,768]{3,2,1,0:T(8,128)(2,1)S(1)} collective-permute-done((bf16[1,2,96,768]{3,2,1,0:T(8,128)(2,1)S(1)}, bf16[1,2,96,768]{3,2,1,0:T(8,128)(2,1)S(1)}, u32[]{:S(2)}, u32[]{:S(2)}) %collective-permute-start.66) | collective-permute-done | bytes 294944 | tf_op jit(solution)/shard_map/ppermute | solution.py:444
  421.8 3.0 collective-permute-done.67
  431.7 3.6 collective-permute-done.78
  436.2 3.2 collective-permute-done.79
  440.9 2.7 collective-permute-done.80
  456.9 6.7 %attn_step.1 = (f32[3,3,96,192]{3,2,1,0:T(8,128)}, f32[3,3,96,192]{3,2,1,0:T(8,128)}, f32[3,3,96,192]{3,2,1,0:T(8,128)}, f32[3,3,96,192]{3,2,1,0:T(8,128)}, bf16...) custom-call(f32[1,1]{1,0:T(1,128)} %bitcast.66.clip, ...), custom_call_target="tpu_custom_call" | custom-call | flops 11796480 | bytes 9289732 | tf_op jit(solution)/shard_map/attn_step/pallas_call | solution.py:422
  463.6 5.1 %feed_step.1 = (f32[2,96,768]{2,1,0:T(8,128)}, f32[2,96,768]{2,1,0:T(8,128)}, f32[2,96,768]{2,1,0:T(8,128)}, f32[2,96,768]{2,1,0:T(8,128)}, bf16[2,96,768]{2,1,0...) custom-call(f32[1,1]{1,0:T(1,128)} %bitcast.66.clip, ...), custom_call_target="tpu_custom_call" | custom-call | flops 47185920 | bytes 12386308 | tf_op jit(solution)/shard_map/feed_step/pallas_call | solution.py:422
  (460 shorter events, 164.6 us)
Async XLA Ops:
  7.2 447.6 %all-reduce.8.cloned.1.call-start = ((), (), s32[]{:S(2)}) async-start(), calls=%async_computation | async-start | bytes 1007616 | tf_op jit(solution)/shard_map/psum | solution.py:877
  27.3 23.5 %collective-permute-start.21 = (bf16[1,2,96,768]{3,2,1,0:T(8,128)(2,1)S(1)}, bf16[1,2,96,768]{3,2,1,0:T(8,128)(2,1)S(1)}, u32[]{:S(2)}, u32[]{:S(2)}) collective-permute-start(bf16[1,2,96,768]{3,2,1,0:T(8,128)(2,1)S(1)} %pad_maximum_fusion.14), channel_id=1, source_target_pairs={{0,2},{1,3},{2,0},{3,1},{4,6},{5,7},{6,4},{7,5},{8,10},{9,11},{10,... | collective-permute-start | bytes 884744 | tf_op jit(solution)/shard_map/ppermute | solution.py:444
  30.0 24.2 %collective-permute-start.28 = (bf16[1,2,96,768]{3,2,1,0:T(8,128)(2,1)S(1)}, bf16[1,2,96,768]{3,2,1,0:T(8,128)(2,1)S(1)}, u32[]{:S(2)}, u32[]{:S(2)}) collective-permute-start(bf16[1,2,96,768]{3,2,1,0:T(8,128)(2,1)S(1)} %pad_maximum_fusion.15), channel_id=1, source_target_pairs={{0,2},{1,3},{2,0},{3,1},{4,6},{5,7},{6,4},{7,5},{8,10},{9,11},{10,... | collective-permute-start | bytes 884744 | tf_op jit(solution)/shard_map/ppermute | solution.py:444
  30.4 24.3 %collective-permute-start.19 = (bf16[1,2,96,768]{3,2,1,0:T(8,128)(2,1)S(1)}, bf16[1,2,96,768]{3,2,1,0:T(8,128)(2,1)S(1)}, u32[]{:S(2)}, u32[]{:S(2)}) collective-permute-start(bf16[1,2,96,768]{3,2,1,0:T(8,128)(2,1)S(1)} %get-tuple-element.386), channel_id=1, source_target_pairs={{0,16},{4,20},{8,24},{12,28},{16,0},{20,4},{24,8},{28,12},{1,17},{... | collective-permute-start | bytes 884744 | tf_op jit(solution)/shard_map/ppermute | solution.py:439
  57.6 29.2 %collective-permute-start.22 = (bf16[2,2,96,768]{3,2,1,0:T(8,128)(2,1)}, bf16[2,2,96,768]{3,2,1,0:T(8,128)(2,1)}, u32[]{:S(2)}, u32[]{:S(2)}) collective-permute-start(bf16[2,2,96,768]{3,2,1,0:T(8,128)(2,1)} %pad_maximum_fusion.7), channel_id=1, source_target_pairs={{0,1},{1,0},{2,3},{3,2},{4,5},{5,4},{6,7},{7,6},{8,9},{9,8},{10,11... | collective-permute-start | bytes 1769480 | tf_op jit(solution)/shard_map/ppermute | solution.py:444
  57.7 39.6 %collective-permute-start.29 = (bf16[2,2,96,768]{3,2,1,0:T(8,128)(2,1)S(1)}, bf16[2,2,96,768]{3,2,1,0:T(8,128)(2,1)}, u32[]{:S(2)}, u32[]{:S(2)}) collective-permute-start(bf16[2,2,96,768]{3,2,1,0:T(8,128)(2,1)S(1)} %pad_maximum_fusion.8), channel_id=1, source_target_pairs={{0,1},{1,0},{2,3},{3,2},{4,5},{5,4},{6,7},{7,6},{8,9},{9,8},{10,11... | collective-permute-start | bytes 1769480 | tf_op jit(solution)/shard_map/ppermute | solution.py:444
  61.0 36.3 %collective-permute-start.34 = (bf16[1,2,2,96,768]{4,3,2,0,1:T(8,128)(2,1)S(1)}, bf16[1,2,2,96,768]{4,3,2,0,1:T(8,128)(2,1)S(1)}, u32[]{:S(2)}, u32[]{:S(2)}) collective-permute-start(bf16[1,2,2,96,768]{4,3,2,0,1:T(8,128)(2,1)S(1)} %pad_maximum_fusion.6), channel_id=1, source_target_pairs={{0,2},{1,3},{2,0},{3,1},{4,6},{5,7},{6,4},{7,5},{8,10},{9,11},{10,... | collective-permute-start | bytes 1769480 | tf_op jit(solution)/shard_map/ppermute | solution.py:444
  103.4 22.0 %collective-permute-start.33 = (bf16[336,768]{1,0:T(8,128)(2,1)S(1)}, bf16[336,768]{1,0:T(8,128)(2,1)S(1)}, u32[]{:S(2)}, u32[]{:S(2)}) collective-permute-start(bf16[336,768]{1,0:T(8,128)(2,1)S(1)} %bitcast.196), channel_id=1, source_target_pairs={{0,8},{4,12},{8,0},{12,4},{16,24},{20,28},{24,16},{28,20},{1,9},{5... | collective-permute-start | bytes 1548296 | tf_op jit(solution)/shard_map/ppermute | solution.py:439
  104.9 29.2 %collective-permute-start.26 = (bf16[4,2,96,768]{3,2,1,0:T(8,128)(2,1)}, bf16[4,2,96,768]{3,2,1,0:T(8,128)(2,1)}, u32[]{:S(2)}, u32[]{:S(2)}) collective-permute-start(bf16[4,2,96,768]{3,2,1,0:T(8,128)(2,1)} %pad_maximum_fusion.1.refs_0_), channel_id=1, source_target_pairs={{0,16},{4,20},{8,24},{12,28},{16,0},{20,4},{24,8},{28,12},{1,17},{... | collective-permute-start | bytes 3538952 | tf_op jit(solution)/shard_map/ppermute | solution.py:439
  106.5 37.8 %collective-permute-start.25 = (bf16[4,2,96,768]{3,2,1,0:T(8,128)(2,1)}, bf16[4,2,96,768]{3,2,1,0:T(8,128)(2,1)}, u32[]{:S(2)}, u32[]{:S(2)}) collective-permute-start(bf16[4,2,96,768]{3,2,1,0:T(8,128)(2,1)} %pad_maximum_fusion.1.refs_0_), channel_id=1, source_target_pairs={{0,4},{4,0},{8,12},{12,8},{16,20},{20,16},{24,28},{28,24},{1,5},{5... | collective-permute-start | bytes 3538952 | tf_op jit(solution)/shard_map/ppermute | solution.py:439
  106.5 51.6 %collective-permute-start.31 = (bf16[4,2,96,768]{3,2,1,0:T(8,128)(2,1)}, bf16[4,2,96,768]{3,2,1,0:T(8,128)(2,1)}, u32[]{:S(2)}, u32[]{:S(2)}) collective-permute-start(bf16[4,2,96,768]{3,2,1,0:T(8,128)(2,1)} %pad_maximum_fusion.2.refs_0_), channel_id=1, source_target_pairs={{0,16},{4,20},{8,24},{12,28},{16,0},{20,4},{24,8},{28,12},{1,17},{... | collective-permute-start | bytes 3538952 | tf_op jit(solution)/shard_map/ppermute | solution.py:439
  107.1 35.4 %collective-permute-start.35 = (bf16[2,2,2,96,768]{4,3,2,0,1:T(8,128)(2,1)}, bf16[2,2,2,96,768]{4,3,2,0,1:T(8,128)(2,1)}, u32[]{:S(2)}, u32[]{:S(2)}) collective-permute-start(bf16[2,2,2,96,768]{4,3,2,0,1:T(8,128)(2,1)} %pad_maximum_fusion.3), channel_id=1, source_target_pairs={{0,1},{1,0},{2,3},{3,2},{4,5},{5,4},{6,7},{7,6},{8,9},{9,8},{10,11... | collective-permute-start | bytes 3538952 | tf_op jit(solution)/shard_map/ppermute | solution.py:444
  134.1 24.0 %collective-permute-start.27 = (bf16[4,2,96,768]{3,2,1,0:T(8,128)(2,1)}, bf16[4,2,96,768]{3,2,1,0:T(8,128)(2,1)}, u32[]{:S(2)}, u32[]{:S(2)}) collective-permute-start(bf16[4,2,96,768]{3,2,1,0:T(8,128)(2,1)} %collective-permute-done.26.refs_2_), channel_id=1, source_target_pairs={{0,4},{4,0},{8,12},{12,8},{16,20},{20,16},{24,28},{28,24},{1,5},{5... | collective-permute-start | bytes 3538952 | tf_op jit(solution)/shard_map/ppermute | solution.py:439
  139.2 32.7 %collective-permute-start.30 = (bf16[4,2,96,768]{3,2,1,0:T(8,128)(2,1)}, bf16[4,2,96,768]{3,2,1,0:T(8,128)(2,1)}, u32[]{:S(2)}, u32[]{:S(2)}) collective-permute-start(bf16[4,2,96,768]{3,2,1,0:T(8,128)(2,1)} %pad_maximum_fusion.2.refs_0_), channel_id=1, source_target_pairs={{0,4},{4,0},{8,12},{12,8},{16,20},{20,16},{24,28},{28,24},{1,5},{5... | collective-permute-start | bytes 3538952 | tf_op jit(solution)/shard_map/ppermute | solution.py:439
  144.2 38.2 %collective-permute-start.36 = (bf16[4,2,96,768]{3,2,1,0:T(8,128)(2,1)S(1)}, bf16[4,2,96,768]{3,2,1,0:T(8,128)(2,1)S(1)}, u32[]{:S(2)}, u32[]{:S(2)}) collective-permute-start(bf16[4,2,96,768]{3,2,1,0:T(8,128)(2,1)S(1)} %get-tuple-element.363.refs_0_.refs_4_), channel_id=1, source_target_pairs={{0,4},{4,0},{8,12},{12,8},{16,20},{20,16},{24,28},{28,24},{1,5},{5... | collective-permute-start | bytes 3538952 | tf_op jit(solution)/shard_map/ppermute | solution.py:439
  144.3 38.2 %collective-permute-start.37 = (bf16[4,2,96,768]{3,2,1,0:T(8,128)(2,1)S(1)}, bf16[4,2,96,768]{3,2,1,0:T(8,128)(2,1)S(1)}, u32[]{:S(2)}, u32[]{:S(2)}) collective-permute-start(bf16[4,2,96,768]{3,2,1,0:T(8,128)(2,1)S(1)} %get-tuple-element.362.refs_2_.refs_6_), channel_id=1, source_target_pairs={{0,4},{4,0},{8,12},{12,8},{16,20},{20,16},{24,28},{28,24},{1,5},{5... | collective-permute-start | bytes 3538952 | tf_op jit(solution)/shard_map/ppermute | solution.py:439
  200.8 26.0 %collective-permute-start.39 = (bf16[4,2,96,768]{3,2,1,0:T(8,128)(2,1)}, bf16[4,2,96,768]{3,2,1,0:T(8,128)(2,1)S(1)}, u32[]{:S(2)}, u32[]{:S(2)}) collective-permute-start(bf16[4,2,96,768]{3,2,1,0:T(8,128)(2,1)} %get-tuple-element.172), channel_id=1, source_target_pairs={{0,4},{4,0},{8,12},{12,8},{16,20},{20,16},{24,28},{28,24},{1,5},{5... | collective-permute-start | bytes 3538952 | tf_op jit(solution)/shard_map/ppermute | solution.py:439
  201.4 22.8 %collective-permute-start.40 = (bf16[4,2,96,768]{3,2,1,0:T(8,128)(2,1)}, bf16[4,2,96,768]{3,2,1,0:T(8,128)(2,1)S(1)}, u32[]{:S(2)}, u32[]{:S(2)}) collective-permute-start(bf16[4,2,96,768]{3,2,1,0:T(8,128)(2,1)} %get-tuple-element.174), channel_id=1, source_target_pairs={{0,4},{4,0},{8,12},{12,8},{16,20},{20,16},{24,28},{28,24},{1,5},{5... | collective-permute-start | bytes 3538952 | tf_op jit(solution)/shard_map/ppermute | solution.py:439
  220.9 68.9 %collective-permute-start.42 = (bf16[4,2,96,768]{3,2,1,0:T(8,128)(2,1)}, bf16[4,2,96,768]{3,2,1,0:T(8,128)(2,1)}, u32[]{:S(2)}, u32[]{:S(2)}) collective-permute-start(bf16[4,2,96,768]{3,2,1,0:T(8,128)(2,1)} %get-tuple-element.181), channel_id=1, source_target_pairs={{0,4},{4,0},{8,12},{12,8},{16,20},{20,16},{24,28},{28,24},{1,5},{5... | collective-permute-start | bytes 3538952 | tf_op jit(solution)/shard_map/ppermute | solution.py:439
  222.9 52.1 %collective-permute-start.38 = (bf16[336,768]{1,0:T(8,128)(2,1)}, bf16[336,768]{1,0:T(8,128)(2,1)}, u32[]{:S(2)}, u32[]{:S(2)}) collective-permute-start(bf16[336,768]{1,0:T(8,128)(2,1)} %slice.267), channel_id=1, source_target_pairs={{0,8},{4,12},{8,0},{12,4},{16,24},{20,28},{24,16},{28,20},{1,9},{5... | collective-permute-start | bytes 1548296 | tf_op jit(solution)/shard_map/ppermute | solution.py:439
  228.0 41.9 %collective-permute-start.72 = (bf16[2,2,96,768]{3,2,1,0:T(8,128)(2,1)}, bf16[2,2,96,768]{3,2,1,0:T(8,128)(2,1)S(1)}, u32[]{:S(2)}, u32[]{:S(2)}) collective-permute-start(bf16[2,2,96,768]{3,2,1,0:T(8,128)(2,1)} %slice.294), channel_id=1, source_target_pairs={{0,1},{1,0},{2,3},{3,2},{4,5},{5,4},{6,7},{7,6},{8,9},{9,8},{10,11... | collective-permute-start | bytes 1769480 | tf_op jit(solution)/shard_map/ppermute | solution.py:444
  230.5 59.3 %collective-permute-start.68 = (bf16[4,2,96,768]{3,2,1,0:T(8,128)(2,1)}, bf16[4,2,96,768]{3,2,1,0:T(8,128)(2,1)}, u32[]{:S(2)}, u32[]{:S(2)}) collective-permute-start(bf16[4,2,96,768]{3,2,1,0:T(8,128)(2,1)} %add_convert_fusion.4), channel_id=1, source_target_pairs={{0,16},{4,20},{8,24},{12,28},{16,0},{20,4},{24,8},{28,12},{1,17},{... | collective-permute-start | bytes 3538952 | tf_op jit(solution)/shard_map/ppermute | solution.py:439
  241.8 30.4 %collective-permute-start.75 = (bf16[1,2,96,768]{3,2,1,0:T(8,128)(2,1)}, bf16[1,2,96,768]{3,2,1,0:T(8,128)(2,1)}, u32[]{:S(2)}, u32[]{:S(2)}) collective-permute-start(bf16[1,2,96,768]{3,2,1,0:T(8,128)(2,1)} %slice.300), channel_id=1, source_target_pairs={{0,2},{1,3},{2,0},{3,1},{4,6},{5,7},{6,4},{7,5},{8,10},{9,11},{10,... | collective-permute-start | bytes 884744 | tf_op jit(solution)/shard_map/ppermute | solution.py:444
  282.9 38.8 %collective-permute-start.63 = (bf16[4,2,96,768]{3,2,1,0:T(8,128)(2,1)}, bf16[4,2,96,768]{3,2,1,0:T(8,128)(2,1)S(1)}, u32[]{:S(2)}, u32[]{:S(2)}) collective-permute-start(bf16[4,2,96,768]{3,2,1,0:T(8,128)(2,1)} %get-tuple-element.222), channel_id=1, source_target_pairs={{0,4},{4,0},{8,12},{12,8},{16,20},{20,16},{24,28},{28,24},{1,5},{5... | collective-permute-start | bytes 3538952 | tf_op jit(solution)/shard_map/ppermute | solution.py:439
  289.3 34.5 %collective-permute-start.77 = (bf16[96,768]{1,0:T(8,128)(2,1)}, bf16[96,768]{1,0:T(8,128)(2,1)}, u32[]{:S(2)}, u32[]{:S(2)}) collective-permute-start(bf16[96,768]{1,0:T(8,128)(2,1)} %slice_bitcast_fusion.3), channel_id=1, source_target_pairs={{0,8},{4,12},{8,0},{12,4},{16,24},{20,28},{24,16},{28,20},{1,9},{5... | collective-permute-start | bytes 442376 | tf_op jit(solution)/shard_map/ppermute | solution.py:439
  292.8 48.2 %collective-permute-start.69 = (bf16[2,2,96,768]{3,2,1,0:T(8,128)(2,1)}, bf16[2,2,96,768]{3,2,1,0:T(8,128)(2,1)}, u32[]{:S(2)}, u32[]{:S(2)}) collective-permute-start(bf16[2,2,96,768]{3,2,1,0:T(8,128)(2,1)} %slice.288), channel_id=1, source_target_pairs={{0,1},{1,0},{2,3},{3,2},{4,5},{5,4},{6,7},{7,6},{8,9},{9,8},{10,11... | collective-permute-start | bytes 1769480 | tf_op jit(solution)/shard_map/ppermute | solution.py:444
  330.0 50.4 %collective-permute-start.62 = (bf16[4,2,96,768]{3,2,1,0:T(8,128)(2,1)S(1)}, bf16[4,2,96,768]{3,2,1,0:T(8,128)(2,1)S(1)}, u32[]{:S(2)}, u32[]{:S(2)}) collective-permute-start(bf16[4,2,96,768]{3,2,1,0:T(8,128)(2,1)S(1)} %copy-done.52), channel_id=1, source_target_pairs={{0,4},{4,0},{8,12},{12,8},{16,20},{20,16},{24,28},{28,24},{1,5},{5... | collective-permute-start | bytes 3538952 | tf_op jit(solution)/shard_map/ppermute | solution.py:439
  339.5 42.2 %collective-permute-start.64 = (bf16[4,2,96,768]{3,2,1,0:T(8,128)(2,1)S(1)}, bf16[4,2,96,768]{3,2,1,0:T(8,128)(2,1)S(1)}, u32[]{:S(2)}, u32[]{:S(2)}) collective-permute-start(bf16[4,2,96,768]{3,2,1,0:T(8,128)(2,1)S(1)} %add_convert_fusion.2), channel_id=1, source_target_pairs={{0,16},{4,20},{8,24},{12,28},{16,0},{20,4},{24,8},{28,12},{1,17},{... | collective-permute-start | bytes 3538952 | tf_op jit(solution)/shard_map/ppermute | solution.py:439
  341.0 36.7 %collective-permute-start.50 = (bf16[4,1,96,384]{3,2,1,0:T(8,128)(2,1)S(1)}, bf16[4,1,96,384]{3,2,1,0:T(8,128)(2,1)S(1)}, u32[]{:S(2)}, u32[]{:S(2)}) collective-permute-start(bf16[4,1,96,384]{3,2,1,0:T(8,128)(2,1)S(1)} %add_convert_fusion.25), channel_id=1, source_target_pairs={{0,16},{4,20},{8,24},{12,28},{16,0},{20,4},{24,8},{28,12},{1,17},{... | collective-permute-start | bytes 884744 | tf_op jit(solution)/shard_map/ppermute | solution.py:439
  347.8 31.6 %collective-permute-start.70 = (bf16[1,2,96,768]{3,2,1,0:T(8,128)(2,1)S(1)}, bf16[1,2,96,768]{3,2,1,0:T(8,128)(2,1)S(1)}, u32[]{:S(2)}, u32[]{:S(2)}) collective-permute-start(bf16[1,2,96,768]{3,2,1,0:T(8,128)(2,1)S(1)} %slice.290), channel_id=1, source_target_pairs={{0,2},{1,3},{2,0},{3,1},{4,6},{5,7},{6,4},{7,5},{8,10},{9,11},{10,... | collective-permute-start | bytes 884744 | tf_op jit(solution)/shard_map/ppermute | solution.py:444
  349.8 33.9 %collective-permute-start.53 = (bf16[4,1,96,384]{3,2,1,0:T(8,128)(2,1)S(1)}, bf16[4,1,96,384]{3,2,1,0:T(8,128)(2,1)S(1)}, u32[]{:S(2)}, u32[]{:S(2)}) collective-permute-start(bf16[4,1,96,384]{3,2,1,0:T(8,128)(2,1)S(1)} %copy-done.66), channel_id=1, source_target_pairs={{0,4},{4,0},{8,12},{12,8},{16,20},{20,16},{24,28},{28,24},{1,5},{5... | collective-permute-start | bytes 884744 | tf_op jit(solution)/shard_map/ppermute | solution.py:439
  380.4 25.5 %collective-permute-start.71 = (bf16[96,768]{1,0:T(8,128)(2,1)S(1)}, bf16[96,768]{1,0:T(8,128)(2,1)S(1)}, u32[]{:S(2)}, u32[]{:S(2)}) collective-permute-start(bf16[96,768]{1,0:T(8,128)(2,1)S(1)} %slice_bitcast_fusion.5), channel_id=1, source_target_pairs={{0,8},{4,12},{8,0},{12,4},{16,24},{20,28},{24,16},{28,20},{1,9},{5... | collective-permute-start | bytes 442376 | tf_op jit(solution)/shard_map/ppermute | solution.py:439
  (125 other events, 1215.9 us)
Sparse Core Ops, SparseCore 0:
  320.1 46.3 all-reduce.7

commit v3 on v2

v3 whole, which is shorter than its diff:
```python
import functools
import math

import jax
import jax.numpy as jnp
from jax import lax
from jax.experimental import pallas as pl
from jax.experimental.pallas import tpu as pltpu
from jax.sharding import Mesh
from jax.sharding import PartitionSpec as P

HEAD_DIM = 64
STEP = 10

NORM_EPS = 1e-05
CLIP_NORM = 1.0
BETA_FIRST = 0.9
BETA_SECOND = 0.999
ADAM_EPS = 1e-08
WEIGHT_DECAY = 0.01
MATRIX_RATE = 0.12
NORM_RATE = 0.8
AVERAGE_CEILING = 0.999
BF = jnp.bfloat16
F32 = jnp.float32
HIGHEST = lax.Precision.HIGHEST
SCALE = 1.0 / math.sqrt(HEAD_DIM)
DP = ("dq", "stream", "core")
VMEM_LIMIT = 56 * 1024 * 1024
GROUP = 3
MOST_ITEMS = 6


def dot_nn(a, b):
    return lax.dot_general(a, b, (((1,), (0,)), ((), ())), preferred_element_type=F32)


def dot_nt(a, b):
    return lax.dot_general(a, b, (((1,), (1,)), ((), ())), preferred_element_type=F32)


def dot_tn(a, b):
    return lax.dot_general(a, b, (((0,), (0,)), ((), ())), preferred_element_type=F32)


def norm_forward(summed, gain, shift):
    centre = jnp.mean(summed, axis=-1, keepdims=True)
    offset = summed - centre
    spread = jnp.mean(offset * offset, axis=-1, keepdims=True)
    inverse = lax.rsqrt(spread + NORM_EPS)
    normed = offset * inverse
    return normed * gain + shift, normed, inverse


def norm_backward(upstream, gain, normed, inverse):
    scaled = upstream * gain
    first_mean = jnp.mean(scaled, axis=-1, keepdims=True)
    second_mean = jnp.mean(scaled * normed, axis=-1, keepdims=True)
    inward = inverse * (scaled - first_mean - normed * second_mean)
    gain_term = jnp.sum(upstream * normed, axis=0, keepdims=True)
    shift_term = jnp.sum(upstream, axis=0, keepdims=True)
    return inward, gain_term, shift_term


def cut(block, blocks):
    rows = block.shape[0] // blocks
    return [block[i * rows : (i + 1) * rows] for i in range(blocks)]


def stack_rows(parts):
    return jnp.concatenate(parts, axis=0)


def thirds(triple, width):
    return [triple[:, i * width : (i + 1) * width] for i in range(triple.shape[1] // width)]


def lane_head(block):
    return lax.broadcasted_iota(jnp.int32, block.shape, 1) // HEAD_DIM


def spread(block):
    lanes = lane_head(block)
    zero = jnp.zeros_like(block)
    heads = block.shape[1] // HEAD_DIM
    return stack_rows([jnp.where(lanes == h, block, zero) for h in range(heads)])


def gathered(block):
    parts = cut(block, block.shape[1] // HEAD_DIM)
    lanes = lane_head(parts[0])
    out = parts[0]
    for h in range(1, len(parts)):
        out = jnp.where(lanes == h, parts[h], out)
    return out


def item_of(shape, axis, rows):
    place = lax.broadcasted_iota(jnp.int32, shape, axis)
    item = jnp.zeros(shape, jnp.int32)
    for border in range(1, MOST_ITEMS):
        item += (place >= border * rows).astype(jnp.int32)
    return item


def same_item(shape, query_rows, key_rows, heads):
    mask = item_of(shape, 0, query_rows) == item_of(shape, 1, key_rows)
    return stack_rows([mask] * heads)


def attend(query, key, value, mask, blocks):
    pairs = zip(cut(query, blocks), cut(key, blocks))
    scores = stack_rows([jnp.where(mask, dot_nt(spread(q), k) * SCALE, -1e30) for q, k in pairs])
    powered = jnp.exp(scores - jnp.max(scores, axis=-1, keepdims=True))
    probs = (powered * (1.0 / jnp.sum(powered, axis=-1, keepdims=True))).astype(BF)
    mixed = [gathered(dot_nn(p, v)) for p, v in zip(cut(probs, blocks), cut(value, blocks))]
    return probs, stack_rows(mixed).astype(BF)


def attend_back(query, key, value, probs, grad_context, blocks):
    queries, keys, values = cut(query, blocks), cut(key, blocks), cut(value, blocks)
    contexts, weights = [spread(g) for g in cut(grad_context, blocks)], cut(probs, blocks)
    grad_probs = stack_rows([dot_nt(g, v) for g, v in zip(contexts, values)])
    grad_value = stack_rows([dot_tn(p, g) for p, g in zip(weights, contexts)]).astype(BF)
    wide = probs.astype(F32)
    inner = jnp.sum(grad_probs * wide, axis=-1, keepdims=True)
    grad_scores = cut((wide * (grad_probs - inner) * SCALE).astype(BF), blocks)
    grad_query = stack_rows([gathered(dot_nn(s, k)) for s, k in zip(grad_scores, keys)])
    grad_key = stack_rows([dot_tn(s, spread(q)) for s, q in zip(grad_scores, queries)])
    return grad_query.astype(BF), grad_key.astype(BF), grad_value


def load_weight(pieces, weight, column=0):
    row = 0
    for piece in pieces:
        for part in range(piece.shape[1]):
            rows, columns = piece.shape[2:]
            weight[row : row + rows, column : column + columns] = piece[0, part]
            row += rows


def load_halves(pieces, weight):
    middle = len(pieces) // 2
    lower = pl.program_id(0) < pl.num_programs(0) // 2

    @pl.when(lower)
    def _():
        load_weight(pieces[:middle], weight)

    @pl.when(jnp.logical_not(lower))
    def _():
        load_weight(pieces[middle:], weight)


def store_weight(value, pieces):
    row = 0
    for piece in pieces:
        for part in range(piece.shape[1]):
            rows = piece.shape[2]
            piece[0, part] = value[row : row + rows, :].astype(piece.dtype)
            row += rows


def wide_spots(place, piece, shard_rows):
    groups, _, _, streams = piece.shape[:4]
    inner = max(groups // 2, 1)
    row = 0
    for high in range(groups // inner):
        for core in range(2):
            for part in range(streams):
                for sub in range(inner):
                    group = (sub * (groups // inner) + high) ^ place[0, 0]
                    yield row, (group, core ^ place[0, 1], 0, part)
                    row += shard_rows


def load_wide(place, piece, kind, weight):
    rows = piece.shape[5]
    for row, spot in wide_spots(place, piece, rows):
        weight[row : row + rows, :] = piece[spot + (kind,)]


def store_wide(place, value, piece, kind):
    rows = piece.shape[5]
    for row, spot in wide_spots(place, piece, rows):
        piece[spot + (kind,)] = value[row : row + rows, :].astype(piece.dtype)


def partner_order(value):
    dim = value.shape[1]
    eighth = dim // 8
    row = lax.broadcasted_iota(jnp.int32, (dim, dim), 0)
    column = lax.broadcasted_iota(jnp.int32, (dim, dim), 1)
    same = jnp.ones((dim, dim), jnp.bool_)
    for border in range(2 * eighth, dim, 2 * eighth):
        same &= (row >= border) == (column >= border)
    pick = same & (jnp.abs(row - column) == eighth)
    return dot_nn(value, jnp.where(pick, 1.0, 0.0).astype(BF)).astype(BF)


def widen(value, blocks, rows):
    empty = jnp.zeros((rows - value.shape[0] // blocks, value.shape[1]), value.dtype)
    return stack_rows([part for block in cut(value, blocks) for part in (block, empty)])


def cross_forward_kernel(width, blocks, words, regions, stream, lang, vis, norm, *refs):
    first, second, refs = refs[:8], refs[8:16], refs[16:]
    own_one, other_one, lang_n, lang_r, vis_n, vis_r = refs[:6]
    lang_qkv, vis_qkv, lang_ctx, vis_ctx, lang_p, vis_p = refs[6:12]
    weight, lang_acc, vis_acc = refs[12:]
    load_weight(first, weight)
    load_weight(second, weight, first[0].shape[3])
    step = pl.program_id(0)

    @pl.when(step == 0)
    def _():
        lang_acc[...] = lang[...].astype(F32)
        vis_acc[...] = vis[...].astype(F32)

    full = weight[...]
    in_part, out_part = full[:, : 3 * width], full[:, 3 * width :]
    lang_triple = dot_nn(lang[...], in_part).astype(BF)
    vis_triple = dot_nn(vis[...], in_part).astype(BF)
    lang_qkv[0] = lang_triple
    vis_qkv[0] = vis_triple
    lang_query, lang_key, lang_value = thirds(lang_triple, width)
    vis_query, vis_key, vis_value = thirds(vis_triple, width)
    heads = width // HEAD_DIM
    lang_block, vis_block = lang.shape[0] // blocks, vis.shape[0] // blocks
    lang_mask = same_item((lang_block, vis_block), words, regions, heads)
    vis_mask = same_item((vis_block, lang_block), regions, words, heads)
    for query, key, value, probs_ref, ctx_ref, acc, mask in (
        (lang_query, vis_key, vis_value, lang_p, lang_ctx, lang_acc, lang_mask),
        (vis_query, lang_key, lang_value, vis_p, vis_ctx, vis_acc, vis_mask),
    ):
        probs, context = attend(query, key, value, mask, blocks)
        probs_ref[0] = probs
        ctx_ref[0] = context
        acc[...] += dot_nt(context, out_part)

    @pl.when(step == pl.num_programs(0) - 1)
    def _():
        ones = []
        for acc, n_ref, r_ref in ((lang_acc, lang_n, lang_r), (vis_acc, vis_n, vis_r)):
            out, normed, inverse = norm_forward(acc[...], norm[0:1, :], norm[1:2, :])
            ones.append(out.astype(BF))
            n_ref[...] = normed
            r_ref[...] = inverse
        lang_one, vis_one = widen(ones[0], blocks, vis_block), ones[1]
        is_vis = stream[0, 0] == 1
        own_one[...] = jnp.where(is_vis, vis_one, lang_one)
        other_one[...] = partner_order(jnp.where(is_vis, lang_one, vis_one))


def self_forward_kernel(width, blocks, length, own, other, norm, *refs):
    pieces, refs = refs[:8], refs[8:]
    two, n_ref, r_ref, qkv, ctx, probs_ref, weight, acc, rows = refs
    step = pl.program_id(0)
    load_halves(pieces, weight)

    @pl.when(step == 0)
    def _():
        rows[...] = stack_rows([own[...], other[...]])
        acc[...] = rows[...].astype(F32)

    full = weight[...]
    in_part, out_part = full[:, : 3 * width], full[:, 3 * width :]
    triple = dot_nn(rows[...], in_part).astype(BF)
    qkv[0] = triple
    block = rows.shape[0] // blocks
    mask = same_item((block, block), length[0, 0], length[0, 0], width // HEAD_DIM)
    probs, context = attend(*thirds(triple, width), mask, blocks)
    probs_ref[0] = probs
    ctx[0] = context
    acc[...] += dot_nt(context, out_part)

    @pl.when(step == pl.num_programs(0) - 1)
    def _():
        out, normed, inverse = norm_forward(acc[...], norm[0:1, :], norm[1:2, :])
        two[...] = out.astype(BF)
        n_ref[...] = normed
        r_ref[...] = inverse


def feed_kernel(place, rows, normed_two, inverse, cot, norm, piece, *refs):
    three, grads, down_ref, self_gain, self_shift, feed_gain, feed_shift, refs = refs[:7] + (refs[7:],)
    weight_in, weight_out, active, slope, acc, branch, branch_turned, turned = refs
    step, groups = pl.program_id(0), pl.num_programs(0) // 2
    group = lax.rem(step, groups)

    @pl.when(step == 0)
    def _():
        acc[...] = normed_two[...] * norm[0:1, :] + norm[1:2, :]
        turned[...] = rows[...].T

    @pl.when(step < groups)
    def _():
        load_wide(place, piece, 0, weight_in.at[group])
        load_wide(place, piece, 1, weight_out.at[group])
        hidden = dot_nn(rows[...], weight_in[group])
        normal = 0.5 * (1.0 + lax.erf(hidden * 0.7071067811865476))
        slopes = normal + hidden * jnp.exp(-0.5 * hidden * hidden) * 0.3989422804014327
        actives = (hidden * normal).astype(BF)
        active[group] = actives
        slope[group] = slopes.astype(BF)
        acc[...] += dot_nt(actives, weight_out[group])

    @pl.when(step == groups - 1)
    def _():
        gain = norm[2:3, :]
        out, normed, inverse_three = norm_forward(acc[...], gain, norm[3:4, :])
        three[...] = out.astype(BF)
        inward, gain_term, shift_term = norm_backward(
            cot[...].astype(F32), gain, normed, inverse_three
        )
        acc[...] = inward
        branch[...] = inward.astype(BF)
        branch_turned[...] = inward.astype(BF).T
        feed_gain[...] = gain_term
        feed_shift[...] = shift_term

    @pl.when(step >= groups)
    def _():
        store_wide(place, dot_nn(branch_turned[...], active[group]), grads, 1)
        grad_active = dot_nn(branch[...], weight_out[group])
        grad_hidden = (grad_active * slope[group].astype(F32)).astype(BF)
        store_wide(place, dot_nn(turned[...], grad_hidden), grads, 0)
        acc[...] += dot_nt(grad_hidden, weight_in[group])

    @pl.when(step == 2 * groups - 1)
    def _():
        down, gain_term, shift_term = norm_backward(
            acc[...], norm[0:1, :], normed_two[...], inverse[...]
        )
        down_ref[...] = down
        self_gain[...] = gain_term
        self_shift[...] = shift_term


def self_backward_kernel(width, blocks, inward, own, other, qkv, ctx, probs, *refs):
    pieces, grads, refs = refs[:8], refs[8:12], refs[12:]
    down_own, down_other, weight, acc, branch, turned, branch_turned = refs
    load_halves(pieces, weight)
    step = pl.program_id(0)

    @pl.when(step == 0)
    def _():
        acc[...] = inward[...]
        gradient = inward[...].astype(BF)
        branch[...] = gradient
        branch_turned[...] = gradient.T
        turned[...] = stack_rows([own[...], other[...]]).T

    full = weight[...]
    in_part, out_part = full[:, : 3 * width], full[:, 3 * width :]
    grad_context = dot_nn(branch[...], out_part).astype(BF)
    grads_of = attend_back(*thirds(qkv[0], width), probs[0], grad_context, blocks)
    grad_triple = jnp.concatenate(grads_of, axis=1)
    in_grad = dot_nn(turned[...], grad_triple).astype(BF)
    out_grad = dot_nn(branch_turned[...], ctx[0]).astype(BF)
    store_weight(jnp.concatenate([in_grad, out_grad], axis=1), grads)
    acc[...] += dot_nt(grad_triple, in_part)

    @pl.when(step == pl.num_programs(0) - 1)
    def _():
        slot = own.shape[0]
        down_own[...] = acc[:slot].astype(BF)
        down_other[...] = partner_order(acc[slot:].astype(BF))


def cross_backward_kernel(
    width, blocks, stream, own_up, other_up, lang, vis, lang_n, lang_r, vis_n, vis_r, norm, *refs
):
    lang_qkv, vis_qkv, lang_ctx, vis_ctx, lang_p, vis_p = refs[:6]
    first, second, refs = refs[6:14], refs[14:22], refs[22:]
    first_grads, second_grads, refs = refs[:8], refs[8:16], refs[16:]
    lang_out, vis_out, gain_ref, shift_ref = refs[:4]
    weight, lang_acc, vis_acc, lang_branch, vis_branch, turned, branch_turned = refs[4:]
    load_weight(first, weight)
    load_weight(second, weight, first[0].shape[3])
    step = pl.program_id(0)

    @pl.when(step == 0)
    def _():
        is_vis = stream[0, 0] == 1
        own, other = own_up[...].astype(F32), other_up[...].astype(F32)
        lang_block = lang.shape[0] // blocks
        lang_up = cut(jnp.where(is_vis, other, own), blocks)
        lang_up = stack_rows([block[:lang_block] for block in lang_up])
        vis_up = jnp.where(is_vis, own, other)
        gain_total, shift_total = 0.0, 0.0
        for up, n_ref, r_ref, acc, branch in (
            (lang_up, lang_n, lang_r, lang_acc, lang_branch),
            (vis_up, vis_n, vis_r, vis_acc, vis_branch),
        ):
            inward, gain_term, shift_term = norm_backward(
                up, norm[0:1, :], n_ref[...], r_ref[...]
            )
            acc[...] = inward
            branch[...] = inward.astype(BF)
            gain_total += gain_term
            shift_total += shift_term
        gain_ref[...] = gain_total
        shift_ref[...] = shift_total
        turned[...] = stack_rows([lang[...], vis[...]]).T
        branch_turned[...] = stack_rows([lang_branch[...], vis_branch[...]]).T

    full = weight[...]
    in_part, out_part = full[:, : 3 * width], full[:, 3 * width :]
    lang_gc = dot_nn(lang_branch[...], out_part).astype(BF)
    vis_gc = dot_nn(vis_branch[...], out_part).astype(BF)
    lang_query, lang_key, lang_value = thirds(lang_qkv[0], width)
    vis_query, vis_key, vis_value = thirds(vis_qkv[0], width)
    lang_dq, vis_dk, vis_dv = attend_back(
        lang_query, vis_key, vis_value, lang_p[0], lang_gc, blocks
    )
    vis_dq, lang_dk, lang_dv = attend_back(
        vis_query, lang_key, lang_value, vis_p[0], vis_gc, blocks
    )
    lang_grad = jnp.concatenate([lang_dq, lang_dk, lang_dv], axis=1)
    vis_grad = jnp.concatenate([vis_dq, vis_dk, vis_dv], axis=1)
    in_grad = dot_nn(turned[...], stack_rows([lang_grad, vis_grad]))
    out_grad = dot_nn(branch_turned[...], stack_rows([lang_ctx[0], vis_ctx[0]]))
    grad = jnp.concatenate([in_grad.astype(BF), out_grad.astype(BF)], axis=1)
    middle = first[0].shape[3]
    store_weight(grad[:, :middle], first_grads)
    store_weight(grad[:, middle:], second_grads)
    lang_acc[...] += dot_nt(lang_grad, in_part)
    vis_acc[...] += dot_nt(vis_grad, in_part)

    @pl.when(step == pl.num_programs(0) - 1)
    def _():
        lang_out[...] = lang_acc[...].astype(lang_out.dtype)
        vis_out[...] = vis_acc[...].astype(vis_out.dtype)


def store_step(state, clip, outs):
    new = adamw_step(*state, MATRIX_RATE, clip)
    for (ref, place), value in zip(outs, new[:4] + (new[3], new[4])):
        ref[place] = value.astype(ref.dtype)


def step_kernel(width, sums, theirs, home_low, home_high, stream_one, stream_two, feed, *refs):
    ins, outs, feed_in, feed_out, norm_in = (refs[4 * i : 4 * i + 4] for i in range(5))
    refs = refs[20:]
    step = pl.program_id(0)
    total = sums[...] + theirs[...]
    norm_grad = total[:-1]
    squares = jnp.sum(norm_grad * norm_grad, keepdims=True) + total[-1:, 0:1]
    grad_norm = jnp.sqrt(squares)
    clip = CLIP_NORM / jnp.maximum(grad_norm, CLIP_NORM)
    refs[-1][...] = grad_norm
    for place in range(norm_in[0].shape[0]):
        state = [ref[place] for ref in norm_in]
        new = adamw_step(norm_grad[2 * place : 2 * place + 2], *state, NORM_RATE, clip)
        for ref, value in zip(refs[24:29], new):
            ref[place] = value
    home = jnp.concatenate([home_low[...], home_high[...]], axis=1)
    grad = jnp.where(step == 0, home, jnp.where(step == 1, stream_one[...], stream_two[...]))
    for kind in range(3):
        part = grad[:, kind * width : (kind + 1) * width]
        store_step([part] + [ref[0, kind] for ref in ins], clip, [(r, (0, kind)) for r in refs[:6]])
    part = grad[:, 3 * width :].T
    store_step([part] + [ref[0] for ref in outs], clip, [(r, 0) for r in refs[6:12]])
    for stream in range(feed.shape[0]):
        part = feed[stream, 0]
        state = [part] + [ref[stream] for ref in feed_in]
        store_step(state, clip, [(r, stream) for r in refs[12:18]])
        state = [feed[stream, 1]] + [ref[stream] for ref in feed_out]
        store_step(state, clip, [(r, stream) for r in refs[18:24]])


def whole(shape):
    return pl.BlockSpec(shape, lambda m: (0,) * len(shape))


def per_step(shape):
    rest = (0,) * (len(shape) - 1)
    return pl.BlockSpec((1,) + tuple(shape[1:]), lambda m: (m,) + rest)


def part_of(shape, pick):
    rest = (0,) * (len(shape) - 1)
    return pl.BlockSpec((1,) + tuple(shape[1:]), lambda m: (pick(m),) + rest)


def group_of(shape, pick):
    block = (shape[0], shape[1], 1) + tuple(shape[3:])
    return pl.BlockSpec(block, lambda m: (0, 0, pick(m), 0, 0, 0, 0))


def call(kernel, steps, ins, outs, scratch, name, flops):
    spec = {
        "whole": lambda s: whole(s),
        "step": lambda s: per_step(s),
        "early": lambda s: group_of(s, lambda m: jnp.minimum(m, s[2] - 1)),
        "late": lambda s: group_of(s, lambda m: jnp.maximum(m - s[2], 0)),
        "low": lambda s: part_of(s, lambda m: jnp.minimum(m, s[0] - 1)),
        "high": lambda s: part_of(s, lambda m: jnp.maximum(m - s[0], 0)),
        "rows": lambda s: pl.BlockSpec(
            tuple(s[:-2]) + (s[-2] // steps, s[-1]), lambda m: (0,) * (len(s) - 2) + (m, 0)
        ),
        "scalar": lambda s: pl.BlockSpec(memory_space=pltpu.SMEM),
    }
    moved = sum(a.size * a.dtype.itemsize for _, a in ins)
    moved += sum(math.prod(s) * jnp.dtype(t).itemsize for _, s, t in outs)
    return pl.pallas_call(
        kernel,
        grid=(steps,),
        in_specs=[spec[kind](a.shape) for kind, a in ins],
        out_specs=[spec[kind](s) for kind, s, _ in outs],
        out_shape=[jax.ShapeDtypeStruct(s, t) for _, s, t in outs],
        scratch_shapes=[pltpu.VMEM(s, t) for s, t in scratch],
        compiler_params=pltpu.CompilerParams(
            vmem_limit_bytes=VMEM_LIMIT, dimension_semantics=("arbitrary",)
        ),
        cost_estimate=pl.CostEstimate(flops=flops, bytes_accessed=moved, transcendentals=0),
        name=name,
    )(*[a for _, a in ins])


def swap_dp(value, bit):
    axis, place = (("core", 0), ("stream", 0), ("dq", bit - 2))[min(bit, 2)]
    count = lax.axis_size(axis)
    return lax.ppermute(value, axis, [(i, i ^ (1 << place)) for i in range(count)])


def swap_mp(value, bit):
    count = lax.axis_size("mp")
    return lax.ppermute(value, "mp", [(i, i ^ (1 << bit)) for i in range(count)])


def after(value, *others):
    flat, tree = jax.tree.flatten(value)
    kept = lax.optimization_barrier((flat, jax.tree.leaves(others)))[0]
    return jax.tree.unflatten(tree, kept)


def swap_mask(value, axis, mask):
    count = lax.axis_size(axis)
    return lax.ppermute(value, axis, [(i, i ^ mask) for i in range(count)])


def sum_up(value):
    count = lax.axis_size("mp")
    mask = 1
    while mask < count:
        if 2 * mask < count:
            theirs = [swap_mask(value, "mp", mask * k) for k in (1, 2, 3)]
            value = (value + theirs[0]) + (theirs[1] + theirs[2])
            mask *= 4
        else:
            value += swap_mask(value, "mp", mask)
            mask *= 2
    both = ("dq", "stream")
    count = lax.axis_size(both)
    mask = 1
    while mask < count:
        if 2 * mask < count:
            theirs = [swap_mask(value, both, mask * k) for k in (1, 2, 3)]
            value = (value + theirs[0]) + (theirs[1] + theirs[2])
            mask *= 4
        else:
            value += swap_mask(value, both, mask)
            mask *= 2
    return value, swap_dp(value, 0)


def extra_bits():
    return range(3, 2 + int(math.log2(lax.axis_size("dq"))))


def mp_bits():
    return range(int(math.log2(lax.axis_size("mp"))))


def gather_mp(current):
    for bit in reversed(mp_bits()):
        current = jnp.concatenate([current, swap_mp(current, bit)], axis=0)
    return current


def gather_extra(current):
    for bit in extra_bits():
        current = jnp.concatenate([current, swap_dp(current, bit)], axis=2)
    return current


def scatter_mp(current):
    for bit in mp_bits():
        half = current.shape[0] // 2
        current = added(current[:half], swap_mp(current[half:], bit))
    return current


def scatter_extra(current):
    for bit in reversed(extra_bits()):
        half = current.shape[2] // 2
        current = added(current[:, :, :half], swap_dp(current[:, :, half:], bit))
    return current


def added(mine, theirs):
    return (mine.astype(F32) + theirs.astype(F32)).astype(BF)


def grow(found, place, bit):
    for key in list(found):
        new = list(key)
        new[place] = 1
        found[tuple(new)] = swap_dp(found[key], bit)


def shrink(found, place, bit):
    for key in [k for k in found if k[place] == 0]:
        far = list(key)
        far[place] = 1
        found[key] = added(found[key], swap_dp(found.pop(tuple(far)), bit))


def home_list(found):
    return [found[(hi, mid, lo)] for hi in (0, 1) for lo in (0, 1) for mid in (0, 1)]


def stream_list(found):
    return [found[(hi, lo)] for hi in (0, 1) for lo in (0, 1)]


def home_keys(arrays):
    return {(i >> 2, i & 1, (i >> 1) & 1): a for i, a in enumerate(arrays)}


def stream_keys(arrays):
    return {(i >> 1, i & 1): a for i, a in enumerate(arrays)}


def adamw_step(gradient, moment, square, weight, average, rate, clip_scale):
    average_decay = min(AVERAGE_CEILING, (1.0 + STEP) / (10.0 + STEP))
    clipped = gradient * clip_scale
    moment_new = BETA_FIRST * moment + (1.0 - BETA_FIRST) * clipped
    square_new = BETA_SECOND * square + (1.0 - BETA_SECOND) * clipped * clipped
    corrected = moment_new / (1.0 - BETA_FIRST**STEP)
    denominator = jnp.sqrt(square_new / (1.0 - BETA_SECOND**STEP)) + ADAM_EPS
    weight_new = weight - rate * (corrected / denominator + WEIGHT_DECAY * weight)
    average_new = average_decay * average + (1.0 - average_decay) * weight_new
    return (clipped, moment_new, square_new, weight_new, average_new)


def pad_rows(block, rows):
    return jnp.pad(block, ((0, rows - block.shape[0]), (0, 0)))


def local(
    language,
    images,
    counts,
    language_cot,
    vision_cot,
    attn_in_weight,
    attn_in_moment,
    attn_in_square,
    attn_in_average,
    attn_out_weight,
    attn_out_moment,
    attn_out_square,
    attn_out_average,
    ffn_in_weight,
    ffn_in_moment,
    ffn_in_square,
    ffn_in_average,
    ffn_out_weight,
    ffn_out_moment,
    ffn_out_square,
    ffn_out_average,
    norm_weight,
    norm_moment,
    norm_square,
    norm_average,
):
    n_dp, n_mp = lax.axis_size(DP), lax.axis_size("mp")
    me = lax.axis_index(DP)
    stream = (me >> 1) & 1
    is_vis = stream == 1
    own_items, words, dim = language.shape
    regions = images.shape[1]
    blocks = own_items // GROUP
    lang_block, vis_block = (-(-GROUP * rows // 16) * 16 for rows in (words, regions))
    lang_pad, slot = blocks * lang_block, blocks * vis_block
    total = 2 * slot
    shard_rows = attn_in_weight.shape[1]
    width = attn_in_weight.shape[3]
    units = ffn_in_weight.shape[2]
    heads = width // HEAD_DIM
    half = 2 * width
    eighth = dim // 8

    def mine_first(pair):
        return jnp.where(is_vis, pair[1], pair[0]), jnp.where(is_vis, pair[0], pair[1])

    attn_shards = [
        jnp.concatenate(
            [attn_in_weight[b].reshape(shard_rows, 3 * width), attn_out_weight[b].T], axis=1
        ).astype(BF)[None, None]
        for b in range(3)
    ]
    def pair_up(shards, *pins):
        own, other = mine_first(shards)
        return jnp.concatenate([own, swap_dp(after(other, *pins), 1)], axis=1)

    halves = [attn_shards[0][..., c : c + half] for c in (0, half)]
    self_pair = pair_up(attn_shards[1:])
    for bit in reversed(mp_bits()):
        halves = [jnp.concatenate([h, swap_mp(h, bit)], axis=0) for h in halves]
        if bit == mp_bits()[-1]:
            feed_own, feed_other = mine_first(
                [jnp.stack([ffn_in_weight[s].astype(BF), ffn_out_weight[s].T.astype(BF)]) for s in range(2)]
            )
            feed_pair = jnp.stack([feed_own, swap_dp(feed_other, 1)])
            feed_w = lax.all_gather(after(feed_pair, halves), ("dq", "core", "mp"), axis=0)
            feed_w = feed_w.reshape((n_dp // 4, 2, n_mp) + feed_pair.shape)
    first, second = ({(0, 0, 0): gather_extra(h)} for h in halves)

    def gather_step(current, index):
        return jnp.concatenate([current, swap_mp(current, mp_bits()[-1 - index])], axis=0)

    n_bits = len(mp_bits())
    self_low = self_pair
    for index in range(n_bits - 1):
        self_low = gather_step(self_low, index)
    grow(first, 0, 2)
    grow(second, 1, 1)

    place = jnp.arange(dim, dtype=jnp.int32)
    block = place // shard_rows
    sub, high = block % (n_dp // 8), block // (n_dp // 8)
    relative = 8 * sub + 4 * (high >> 2) + ((high >> 1) & 1) + 2 * (high & 1)
    origin = (relative ^ me) * shard_rows + place % shard_rows
    order = (place[:, None] == origin[None, :]).astype(BF)

    def to_order(value):
        return dot_nn(value, order).astype(BF)

    def from_order(value, precision=None):
        return lax.dot_general(
            value, order, (((1,), (1,)), ((), ())), preferred_element_type=F32, precision=precision
        )

    norm_ordered = lax.dot_general(
        norm_weight.reshape(-1, dim),
        order.astype(F32),
        (((1,), (0,)), ((), ())),
        precision=HIGHEST,
        preferred_element_type=F32,
    ).reshape(norm_weight.shape)
    norm_cross = norm_ordered[:, 0]
    norm_self = jnp.where(is_vis, norm_ordered[:, 2], norm_ordered[:, 1])
    norm_feed = jnp.where(is_vis, norm_ordered[:, 4], norm_ordered[:, 3])
    norm_pair = jnp.concatenate([norm_self, norm_feed], axis=0)

    def in_blocks(value, rows, target):
        value = value.reshape(blocks, rows, dim)
        value = jnp.pad(value, ((0, 0), (0, target - rows), (0, 0)))
        return value.reshape(blocks * target, dim)

    def out_of_blocks(value, rows):
        return value.reshape(blocks, -1, dim)[:, :rows].reshape(blocks * rows, dim)

    lang_rows, vis_rows = GROUP * words, GROUP * regions
    first_item = lax.axis_index("mp") * own_items
    bounds = jnp.cumsum(counts[0])
    positions = first_item + jnp.arange(own_items, dtype=jnp.int32)
    item_image = jnp.sum((bounds[None, :] <= positions[:, None]).astype(jnp.int32), axis=1)
    region = jnp.arange(regions, dtype=jnp.int32)
    row_source = (item_image[:, None] * regions + region[None, :]).reshape(blocks, vis_rows) + 1
    row_source = jnp.pad(row_source, ((0, 0), (0, vis_block - vis_rows))).reshape(slot, 1)
    image_count = images.shape[0] * regions
    picker = (row_source == 1 + jnp.arange(image_count, dtype=jnp.int32)[None, :]).astype(BF)
    lang = to_order(in_blocks(language, lang_rows, lang_block))
    image_rows = to_order(images.reshape(-1, dim))
    vis = dot_nn(picker, image_rows).astype(BF)

    lang_cot = in_blocks(language_cot, lang_rows, vis_block)
    vis_cot = in_blocks(vision_cot, vis_rows, vis_block)
    cot_own, cot_other = mine_first((lang_cot, vis_cot))

    length = jnp.where(is_vis, regions, words).astype(jnp.int32).reshape(1, 1)

    first, second = after((first, second), lang, vis)
    grow(first, 1, 1)
    grow(second, 0, 2)
    self_low = {(0, 0): gather_extra(self_low)}
    self_high = {(0, 0): swap_mp(self_low[(0, 0)], 0)}
    grow(first, 2, 0)
    grow(second, 2, 0)
    pieces = lambda arrays: [("step", a) for a in arrays]
    which = stream.astype(jnp.int32).reshape(1, 1)
    ins = [("scalar", which)] + [("whole", a) for a in (lang, vis, norm_cross)]
    outs = [("whole", (slot, dim), BF)] * 2
    for rows in (lang_pad, slot):
        outs += [("whole", (rows, dim), F32), ("whole", (rows, 1), F32)]
    outs += [("step", (n_mp, rows, 3 * width), BF) for rows in (lang_pad, slot)]
    outs += [("step", (n_mp, rows, width), BF) for rows in (lang_pad, slot)]
    outs += [
        ("step", (n_mp, heads * lang_pad, vis_block), BF),
        ("step", (n_mp, heads * slot, lang_block), BF),
    ]
    both = lang_pad + slot
    cross_w = home_list(first) + home_list(second)
    cross_w = after(cross_w, self_low)
    grow(self_low, 0, 2)
    found = call(
        functools.partial(cross_forward_kernel, width, blocks, words, regions),
        n_mp,
        ins + pieces(cross_w),
        outs,
        [((dim, 4 * width), BF), ((lang_pad, dim), F32), ((slot, dim), F32)],
        "cross_forward",
        12 * both * dim * 4 * width * n_mp,
    )
    own_one, other_one, lang_n, lang_r, vis_n, vis_r = found[:6]
    cross_saved = found[6:]

    other_one = swap_dp(other_one, 1)
    self_high, self_low, cot_other = after((self_high, self_low, cot_other), other_one)
    grow(self_high, 0, 2)
    grow(self_low, 1, 0)
    grow(self_high, 1, 0)
    self_pieces = [("low", a) for a in stream_list(self_low)]
    self_pieces += [("high", a) for a in stream_list(self_high)]
    rows_two, normed_two, inverse_two, self_qkv, self_ctx, self_probs = call(
        functools.partial(self_forward_kernel, width, 2 * blocks),
        n_mp,
        [("scalar", length)] + [("whole", a) for a in (own_one, other_one, norm_self)]
        + self_pieces,
        [
            ("whole", (total, dim), BF),
            ("whole", (total, dim), F32),
            ("whole", (total, 1), F32),
            ("step", (n_mp, total, 3 * width), BF),
            ("step", (n_mp, total, width), BF),
            ("step", (n_mp, heads * total, vis_block), BF),
        ],
        [((dim, 4 * width), BF), ((total, dim), F32), ((total, dim), BF)],
        "self_forward",
        12 * total * dim * 4 * width * n_mp,
    )
    cot = to_order(jnp.concatenate([cot_own, swap_dp(cot_other, 1)], axis=0))
    spot = jnp.stack([me >> 2, me & 1]).astype(jnp.int32).reshape(1, 2)

    whole_row = ("whole", (1, dim), F32)
    rows_three, feed_g, inward, self_gain, self_shift, feed_gain, feed_shift = call(
        feed_kernel,
        2 * n_mp,
        [("scalar", spot)]
        + [("whole", a) for a in (rows_two, normed_two, inverse_two, cot, norm_pair)]
        + [("early", feed_w)],
        [("whole", (total, dim), BF), ("late", feed_w.shape, BF), ("whole", (total, dim), F32)]
        + [whole_row] * 4,
        [((n_mp, dim, units), BF)] * 2
        + [((n_mp, total, units), BF)] * 2
        + [((total, dim), F32), ((total, dim), BF), ((dim, total), BF), ((dim, total), BF)],
        "feed",
        24 * total * dim * units * n_mp,
    )

    feed_sum = lax.psum_scatter(
        (feed_g * (1 + 0 * (me < 0)).astype(BF)).reshape((-1,) + feed_pair.shape), ("dq", "core", "mp"), scatter_dimension=0, tiled=True
    )[0]

    def core_step(found, *pins):
        theirs = [swap_dp(found[(hi, 1)], 0) for hi in (0, 1)]
        return [found[(hi, 0)] for hi in (0, 1)], after(theirs, *pins)

    def split(mine, theirs):
        middle = mine.shape[0] // 2
        return added(mine[:middle], theirs[:middle]), added(mine[middle:], theirs[middle:])

    def send_mp(parts, bit):
        return [(keep, swap_mp(far, bit)) for keep, far in parts]

    found = call(
        functools.partial(self_backward_kernel, width, 2 * blocks),
        n_mp,
        [("whole", a) for a in (inward, own_one, other_one)]
        + [("step", a) for a in (self_qkv, self_ctx, self_probs)]
        + self_pieces,
        [("step", (n_mp, 2, eighth, 4 * width), BF)] * 4 + [("whole", (slot, dim), BF)] * 2,
        [((dim, 4 * width), BF), ((total, dim), F32), ((total, dim), BF)] + [((dim, total), BF)] * 2,
        "self_backward",
        20 * total * dim * 4 * width * n_mp,
    )
    self_g = stream_keys(found[:4])
    own_up, other_up = found[4:]
    other_up = swap_dp(other_up, 1)
    self_core = core_step(self_g)
    self_sums = [added(m, t) for m, t in zip(*self_core)]
    own_up = after(own_up, self_sums)
    found = call(
        functools.partial(cross_backward_kernel, width, blocks),
        n_mp,
        [("scalar", which)]
        + [("whole", a) for a in (own_up, other_up, lang, vis)]
        + [("whole", a) for a in (lang_n, lang_r, vis_n, vis_r, norm_cross)]
        + [("step", a) for a in cross_saved]
        + pieces(cross_w),
        [("step", (n_mp, 1, eighth, half), BF)] * 16
        + [
            ("whole", (lang_pad, dim), BF),
            ("whole", (slot, dim), BF),
            ("whole", (1, dim), F32),
            ("whole", (1, dim), F32),
        ],
        [
            ((dim, 4 * width), BF),
            ((lang_pad, dim), F32),
            ((slot, dim), F32),
            ((lang_pad, dim), BF),
            ((slot, dim), BF),
            ((dim, both), BF),
            ((dim, both), BF),
        ],
        "cross_backward",
        20 * both * dim * 4 * width * n_mp,
    )
    first_g, second_g = home_keys(found[:8]), home_keys(found[8:16])
    lang_back, vis_back, cross_gain, cross_shift = found[16:]
    self_far = swap_dp(self_sums[1], 2)
    self_far = after(self_far, lang_back)
    late = after((first_g, second_g, lang_back, vis_back, cross_gain, cross_shift), self_far)
    first_g, second_g, lang_back, vis_back, cross_gain, cross_shift = late
    shrink(first_g, 2, 0)
    shrink(second_g, 2, 0)
    shrink(first_g, 1, 1)
    shrink(second_g, 0, 2)
    self_part = split(self_sums[0], self_far)
    first_g, second_g = after((first_g, second_g), self_part)
    late = after((lang_back, vis_back, cross_gain, cross_shift, rows_three), first_g, second_g)
    lang_back, vis_back, cross_gain, cross_shift, rows_three = late
    shrink(first_g, 0, 2)
    shrink(second_g, 1, 1)
    first_sum, second_sum = scatter_extra(first_g[(0, 0, 0)]), scatter_extra(second_g[(0, 0, 0)])
    homes, pair = [first_sum, second_sum], None
    for bit in range(n_bits):
        homes = [added(*send_mp([(h[: len(h) // 2], h[len(h) // 2 :])], bit)[0]) for h in homes]
        pair = added(*send_mp([self_part], bit)[0])
        self_part = pair[: len(pair) // 2], pair[len(pair) // 2 :]
        if bit == 0:
            theirs = swap_dp(feed_sum[1], 1)
            homes = after(homes, pair, theirs)
            mine, theirs = feed_sum[0].astype(F32), theirs.astype(F32)
            feed_total = [jnp.where(is_vis, theirs, mine), jnp.where(is_vis, mine, theirs)]
    attn_total = [h[0, 0].astype(F32) for h in homes]
    pair = scatter_extra(pair)
    mine, theirs = pair[0, 0].astype(F32), swap_dp(pair[0, 1], 1).astype(F32)
    attn_total += [jnp.where(is_vis, theirs, mine), jnp.where(is_vis, mine, theirs)]

    final = from_order(rows_three).astype(BF)
    final_other = swap_dp(final[slot:], 1)
    language_out = out_of_blocks(jnp.where(is_vis, final_other, final[:slot]), lang_rows)
    vision_out = out_of_blocks(jnp.where(is_vis, final[:slot], final_other), vis_rows)

    language_grad = from_order(out_of_blocks(lang_back, lang_rows)).reshape(language.shape)
    place_mp = lax.axis_index("mp")
    part = -(-image_count // n_mp // 16) * 16
    index = jnp.arange(n_mp, dtype=jnp.int32)
    far = sum(((index >> b) & 1) << (n_bits - 1 - b) for b in range(n_bits))
    rows = ((far ^ place_mp)[:, None] * part + jnp.arange(part, dtype=jnp.int32)[None, :]).reshape(1, -1)
    chooser = (row_source == 1 + rows).astype(BF)
    image_term = lax.dot_general(
        chooser, vis_back, (((0,), (0,)), ((), ())), preferred_element_type=F32
    ).astype(BF)
    image_term = from_order(image_term).astype(BF).reshape(n_mp, part, dim)
    image_term = gather_mp(scatter_mp(image_term))
    for b in range(n_bits):
        shape = (1 << b, 2, -1, part, dim)
        flipped = image_term.reshape(shape)[:, ::-1].reshape(image_term.shape)
        image_term = jnp.where((place_mp >> b) & 1 == 1, flipped, image_term)
    axes = tuple(reversed(range(n_bits))) + (n_bits, n_bits + 1)
    image_term = image_term.reshape((2,) * n_bits + (part, dim)).transpose(axes)
    image_grad = image_term.reshape(-1, dim)[:image_count].astype(F32).reshape(images.shape)

    here = (jnp.arange(2, dtype=jnp.int32) == stream).astype(F32)[:, None, None]
    norm_partial = jnp.concatenate(
        [
            jnp.concatenate([cross_gain, cross_shift], axis=0)[None],
            here * jnp.concatenate([self_gain, self_shift], axis=0)[None],
            here * jnp.concatenate([feed_gain, feed_shift], axis=0)[None],
        ],
        axis=0,
    )
    norm_partial = from_order(norm_partial.reshape(-1, dim), HIGHEST)

    squares = sum(jnp.sum(g * g) for g in attn_total + feed_total)
    sums, their_sums = sum_up(jnp.concatenate([norm_partial, jnp.full((1, dim), squares)], axis=0))
    kinds = [("step", t) for t in (F32, F32, F32, F32, BF, F32)]
    norm_in = [
        jnp.swapaxes(a, 0, 1)
        for a in (norm_moment, norm_square, norm_weight, norm_average)
    ]
    wide_in = [jnp.swapaxes(a, 1, 2) for a in (attn_in_moment, attn_in_square, attn_in_weight, attn_in_average)]
    wide_out = [attn_out_moment, attn_out_square, attn_out_weight, attn_out_average]
    feed_in = [ffn_in_moment, ffn_in_square, ffn_in_weight, ffn_in_average]
    feed_out = [
        jnp.swapaxes(a, 1, 2)
        for a in (ffn_out_moment, ffn_out_square, ffn_out_weight, ffn_out_average)
    ]
    by_rows = "rows" if shard_rows % 48 == 0 else "whole"
    stepped = call(
        functools.partial(step_kernel, width),
        3,
        [("whole", a) for a in [sums, their_sums] + attn_total]
        + [(by_rows, jnp.stack(feed_total))]
        + [("step", a) for a in wide_in + wide_out]
        + [(by_rows, a) for a in feed_in + feed_out]
        + [("whole", a) for a in norm_in],
        [(k, wide_in[0].shape, t) for k, t in kinds]
        + [(k, wide_out[0].shape, t) for k, t in kinds]
        + [(by_rows, feed_in[0].shape, t) for k, t in kinds * 2]
        + [("whole", norm_in[0].shape, F32)] * 5
        + [("whole", (1, 1), F32)],
        [],
        "step",
        20 * 8 * dim * width,
    )
    stepped = [jnp.swapaxes(a, 1, 2) if i < 6 or 18 <= i < 24 else a for i, a in enumerate(stepped)]
    stepped[24:29] = [jnp.swapaxes(a, 0, 1) for a in stepped[24:29]]

    results = [
        language_out.reshape(language.shape),
        vision_out.reshape(vision_cot.shape),
        language_grad,
        image_grad,
    ]
    results += stepped[:-1]
    return tuple(results) + (stepped[-1][0, 0],)


def solution(mesh):
    shape = (mesh.shape["dp"] // 4, 2, 2, mesh.shape["mp"])
    mesh = Mesh(mesh.devices.reshape(shape), DP + ("mp",))
    rows = P(DP + ("mp",), None, None)
    attn_in, attn_out = P(None, DP, None, "mp"), P(None, "mp", DP)
    ffn_in, ffn_out = P(None, DP, "mp"), P(None, "mp", DP)
    in_specs = (rows, P(DP, None, None), P(DP, None), rows, rows)
    in_specs += (attn_in,) * 4 + (attn_out,) * 4 + (ffn_in,) * 4 + (ffn_out,) * 4 + (P(),) * 4
    out_specs = (rows, rows, rows, P(DP, None, None))
    out_specs += (attn_in,) * 6 + (attn_out,) * 6 + (ffn_in,) * 6 + (ffn_out,) * 6 + (P(),) * 6
    return jax.shard_map(local, mesh=mesh, in_specs=in_specs, out_specs=out_specs, check_vma=False)
```

time: 485 us -> 401 us (0.83)
  local copies, waits for them, and re-layouts: 37.4 us -> 10.6 us
  other arithmetic: 42.2 us -> 17.7 us
  starting transfers between devices: 71.2 us -> 60.7 us
  Pallas kernels: 131 us -> 122 us
  waiting for transfers between devices: 158 us -> 152 us
    pallas_call x9 -> x6, Pallas kernels: 131 us -> 122 us  [call(): pl.pallas_call(kernel, grid=(steps,), in_specs=[spec[kind](a.shape) for k...]
    ppermute x59 -> x52, starting transfers between devices: 43 us -> 34.8 us  [the longest x46 26.8 us: swap_dp(): lax.ppermute(value, axis, [(i, i ^ 1 << place) for i in range(count)])]
    concatenate x10 -> x2, other arithmetic: 8.16 us -> 0.09 us  [gather_mp(): current = jnp.concatenate([current, swap_mp(current, bit)], axis=0)]
    convert_element_type x24 -> x19, other arithmetic: 12.4 us -> 6.16 us  [added(): return (mine.astype(F32) + theirs.astype(F32)).astype(BF)]
    another operation x6 -> x2, local copies, waits for them, and re-layouts: 6.33 us -> 0.08 us  [local(): jnp.stack([ffn_in_weight[s].astype(BF), ffn_out_weight[s].T.astype(BF)])]
    select_n x7 -> x2, other arithmetic: 5.17 us -> 0.2 us  [the longest x1 0.14 us: local(): image_term = jnp.where(place_mp >> b & 1 == 1, flipped, image_term)]
    ppermute x59 -> x52, waiting for transfers between devices: 85 us -> 81.3 us  [the longest x46 74.3 us: swap_dp(): lax.ppermute(value, axis, [(i, i ^ 1 << place) for i in range(count)])]
    ppermute x24 -> x16, waiting for transfers between devices: 73.1 us -> 70.5 us  [swap_mp(): return lax.ppermute(value, 'mp', [(i, i ^ 1 << bit) for i in range(count)])]
  transfers between devices with their start and end apart: 84 -> 70, of which waited for: 27 -> 35; matrix products, arithmetic and copies ran while one was open for 18% -> 9% of each run, Pallas kernels for 21% -> 19%
where the time goes in v3:
time: 401 us; the launch traced here: 395 us
  waiting for transfers between devices  152 us (38%)
  Pallas kernels  122 us (30%)
  starting transfers between devices  60.7 us (15%)
  between operations  19.3 us (5%)
  other arithmetic  17.7 us (4%)
  matrix products  12.9 us (3%)
  local copies, waits for them, and re-layouts  10.6 us (3%)
    pallas_call x6, Pallas kernels, call(): pl.pallas_call(kernel, grid=(steps,), in_specs=[spec[kind](a.shape) for k...  122 us
    ppermute x46, waiting for transfers between devices, swap_dp(): lax.ppermute(value, axis, [(i, i ^ 1 << place) for i in range(count)])  74.3 us
    ppermute x16, waiting for transfers between devices, swap_mp(): return lax.ppermute(value, 'mp', [(i, i ^ 1 << bit) for i in range(count)])  70.5 us
    ppermute x46, starting transfers between devices, swap_dp(): lax.ppermute(value, axis, [(i, i ^ 1 << place) for i in range(count)])  26.8 us
    ppermute x16, starting transfers between devices, swap_mp(): return lax.ppermute(value, 'mp', [(i, i ^ 1 << bit) for i in range(count)])  25.8 us
  transfers between devices with their start and end apart: 70, of which 35 were waited for; matrix products, arithmetic and copies ran while one was open for 9% of the time, Pallas kernels for 19%

profile of v3, /device:TPU:0, one launch (start us, length us, event | category | flops | bytes accessed | tf_op | source)
XLA Modules:
  0.0 395.4 jit_solution(59412674386769537)
XLA Ops:
  9.2 4.1 %collective-permute-start.3 = (bf16[1,1,96,384]{3,2,1,0:T(8,128)(2,1)S(1)}, bf16[1,1,96,384]{3,2,1,0:T(8,128)(2,1)S(1)}, u32[]{:S(2)}, u32[]{:S(2)}) collective-permute-start(bf16[1,1,96,384]{3,2,1,0:T(8,128)(2,1)S(1)} %get-tuple-element.350), channel_id=1, source_target_pairs={{0,2},{1,3},{2,0},{3,1},{4,6},{5,7},{6,4},{7,5},{8,10},{9,11},{10,... | collective-permute-start | bytes 221192 | tf_op jit(solution)/shard_map/ppermute | solution.py:530
  15.5 2.7 collective-permute-done.3
  36.4 2.6 collective-permute-start.19
  39.0 7.5 %collective-permute-done.2.refs_4_.refs_10_ = bf16[4,1,96,384]{3,2,1,0:T(8,128)(2,1)S(1)} collective-permute-done((bf16[4,1,96,384]{3,2,1,0:T(8,128)(2,1)S(1)}, bf16[4,1,96,384]{3,2,1,0:T(8,128)(2,1)S(1)}, u32[]{:S(2)}, u32[]{:S(2)}) %collective-permute-start.2) | collective-permute-done | bytes 294944 | tf_op jit(solution)/shard_map/ppermute | solution.py:525
  50.6 15.6 %collective-permute-done.19 = bf16[1,2,96,768]{3,2,1,0:T(8,128)(2,1)S(1)} collective-permute-done((bf16[1,2,96,768]{3,2,1,0:T(8,128)(2,1)S(1)}, bf16[1,2,96,768]{3,2,1,0:T(8,128)(2,1)S(1)}, u32[]{:S(2)}, u32[]{:S(2)}) %collective-permute-start.19) | collective-permute-done | bytes 294944 | tf_op jit(solution)/shard_map/ppermute | solution.py:530
  72.0 15.4 %cross_forward.1 = (bf16[336,768]{1,0:T(8,128)(2,1)}, bf16[336,768]{1,0:T(8,128)(2,1)}, f32[192,768]{1,0:T(8,128)}, f32[192,1]{1,0:T(8,128)}, f32[336,768]{1,0:T...) custom-call(s32[1,1]{1,0:T(1,128)} %bitcast.stream, ...), custom_call_target="tpu_custom_call" | custom-call | flops 14948499456 | bytes 12468292 | tf_op jit(solution)/shard_map/cross_forward/pallas_call | solution.py:507
  87.8 19.8 %collective-permute-done.21.refs_4_ = bf16[2,2,96,768]{3,2,1,0:T(8,128)(2,1)S(1)} collective-permute-done((bf16[2,2,96,768]{3,2,1,0:T(8,128)(2,1)S(1)}, bf16[2,2,96,768]{3,2,1,0:T(8,128)(2,1)S(1)}, u32[]{:S(2)}, u32[]{:S(2)}) %collective-permute-start.21) | collective-permute-done | bytes 589856 | tf_op jit(solution)/shard_map/ppermute | solution.py:530
  108.4 15.1 %collective-permute-done.26.refs_6_ = bf16[2,2,96,768]{3,2,1,0:T(8,128)(2,1)S(1)} collective-permute-done((bf16[2,2,96,768]{3,2,1,0:T(8,128)(2,1)S(1)}, bf16[2,2,96,768]{3,2,1,0:T(8,128)(2,1)S(1)}, u32[]{:S(2)}, u32[]{:S(2)}) %collective-permute-start.26) | collective-permute-done | bytes 589856 | tf_op jit(solution)/shard_map/ppermute | solution.py:525
  124.8 3.0 fusion.10.cot
  127.9 14.4 %self_forward.1 = (bf16[672,768]{1,0:T(8,128)(2,1)}, f32[672,768]{1,0:T(8,128)}, f32[672,1]{1,0:T(8,128)}, bf16[4,672,576]{2,1,0:T(8,128)(2,1)}, bf16[4,672,192]...) custom-call(s32[1,1]{1,0:T(1,128)} %bitcast.4.length, bf16[336,768]{1,0:T(8,128)(2,1)} %get-tuple-element.195.own, ...), custom_call_target="tpu_custom_call" | custom-call | flops 19025362944 | bytes 14791300 | tf_op jit(solution)/shard_map/self_forward/pallas_call | solution.py:507
  142.4 33.5 %feed.1 = (bf16[672,768]{1,0:T(8,128)(2,1)}, bf16[2,2,4,2,2,96,768]{6,5,4,3,2,1,0:T(8,128)(2,1)}, f32[672,768]{1,0:T(8,128)}, f32[1,768]{1,0:T(1,128)}, f32[1,76...) custom-call(s32[1,2]{1,0:T(1,128)} %add_bitcast_fusion.place, bf16[672,768]{1,0:T(8,128)(2,1)} %get-tuple-element.200.rows, ...), custom_call_target="tpu_custom_call" | custom-call | flops 38050725888 | bytes 26126984 | tf_op jit(solution)/shard_map/feed/pallas_call | solution.py:507
  175.9 25.0 %self_backward.1 = (bf16[4,2,96,768]{3,2,1,0:T(8,128)(2,1)}, bf16[4,2,96,768]{3,2,1,0:T(8,128)(2,1)}, bf16[4,2,96,768]{3,2,1,0:T(8,128)(2,1)}, bf16[4,2,96,768]{...) custom-call(f32[672,768]{1,0:T(8,128)} %get-tuple-element.205.inward, ...), custom_call_target="tpu_custom_call" | custom-call | flops 31708938240 | bytes 19501056 | tf_op jit(solution)/shard_map/self_backward/pallas_call | solution.py:507
  208.4 7.7 %collective-permute-done.32.other_up = bf16[336,768]{1,0:T(8,128)(2,1)S(1)} collective-permute-done((bf16[336,768]{1,0:T(8,128)(2,1)}, bf16[336,768]{1,0:T(8,128)(2,1)S(1)}, u32[]{:S(2)}, u32[]{:S(2)}) %collective-permute-start.32) | collective-permute-done | bytes 516128 | tf_op jit(solution)/shard_map/ppermute | solution.py:525
  216.9 21.7 %cross_backward.1 = (bf16[4,1,96,384]{3,2,1,0:T(8,128)(2,1)}, bf16[4,1,96,384]{3,2,1,0:T(8,128)(2,1)}, bf16[4,1,96,384]{3,2,1,0:T(8,128)(2,1)}, bf16[4,1,96,384]...) custom-call(s32[1,1]{1,0:T(1,128)} %bitcast.stream, ...), custom_call_target="tpu_custom_call" | custom-call | flops 24914165760 | bytes 18004036 | tf_op jit(solution)/shard_map/cross_backward/pallas_call | solution.py:507
  238.6 12.1 %collective-permute-done.33 = bf16[4,2,96,768]{3,2,1,0:T(8,128)(2,1)S(1)} collective-permute-done((bf16[4,2,96,768]{3,2,1,0:T(8,128)(2,1)S(1)}, bf16[4,2,96,768]{3,2,1,0:T(8,128)(2,1)S(1)}, u32[]{:S(2)}, u32[]{:S(2)}) %collective-permute-start.33) | collective-permute-done | bytes 1179680 | tf_op jit(solution)/shard_map/ppermute | solution.py:525
  256.5 9.2 %collective-permute-done.45 = bf16[4,1,96,384]{3,2,1,0:T(8,128)(2,1)S(1)} collective-permute-done((bf16[4,1,96,384]{3,2,1,0:T(8,128)(2,1)S(1)}, bf16[4,1,96,384]{3,2,1,0:T(8,128)(2,1)S(1)}, u32[]{:S(2)}, u32[]{:S(2)}) %collective-permute-start.45) | collective-permute-done | bytes 294944 | tf_op jit(solution)/shard_map/ppermute | solution.py:525
  268.0 3.7 collective-permute-done.42
  274.9 5.5 %collective-permute-done.36 = bf16[4,1,96,384]{3,2,1,0:T(8,128)(2,1)S(1)} collective-permute-done((bf16[4,1,96,384]{3,2,1,0:T(8,128)(2,1)S(1)}, bf16[4,1,96,384]{3,2,1,0:T(8,128)(2,1)S(1)}, u32[]{:S(2)}, u32[]{:S(2)}) %collective-permute-start.36) | collective-permute-done | bytes 294944 | tf_op jit(solution)/shard_map/ppermute | solution.py:525
  283.7 2.3 collective-permute-start.59
  286.0 2.3 fusion.12
  298.5 11.4 %collective-permute-done.47 = bf16[2,96,768]{2,1,0:T(8,128)(2,1)S(1)} collective-permute-done((bf16[2,96,768]{2,1,0:T(8,128)(2,1)}, bf16[2,96,768]{2,1,0:T(8,128)(2,1)S(1)}, u32[]{:S(2)}, u32[]{:S(2)}) %collective-permute-start.47) | collective-permute-done | bytes 294944 | tf_op jit(solution)/shard_map/ppermute | solution.py:530
  310.0 2.3 collective-permute-start.48
  313.9 2.4 collective-permute-done.48
  316.3 3.5 collective-permute-start.49
  321.4 5.2 %collective-permute-done.49 = bf16[1,96,768]{2,1,0:T(8,128)(2,1)S(1)} collective-permute-done((bf16[1,96,768]{2,1,0:T(8,128)(2,1)S(1)}, bf16[1,96,768]{2,1,0:T(8,128)(2,1)S(1)}, u32[]{:S(2)}, u32[]{:S(2)}) %collective-permute-start.49) | collective-permute-done | bytes 147488 | tf_op jit(solution)/shard_map/ppermute | solution.py:530
  328.9 5.3 %collective-permute-done.50 = bf16[2,96,768]{2,1,0:T(8,128)(2,1)S(1)} collective-permute-done((bf16[2,96,768]{2,1,0:T(8,128)(2,1)S(1)}, bf16[2,96,768]{2,1,0:T(8,128)(2,1)S(1)}, u32[]{:S(2)}, u32[]{:S(2)}) %collective-permute-start.50) | collective-permute-done | bytes 294944 | tf_op jit(solution)/shard_map/ppermute | solution.py:530
  338.1 4.6 %collective-permute-done.56 = bf16[2,96,768]{2,1,0:T(8,128)(2,1)S(1)} collective-permute-done((bf16[2,96,768]{2,1,0:T(8,128)(2,1)S(1)}, bf16[2,96,768]{2,1,0:T(8,128)(2,1)S(1)}, u32[]{:S(2)}, u32[]{:S(2)}) %collective-permute-start.56) | collective-permute-done | bytes 294944 | tf_op jit(solution)/shard_map/ppermute | solution.py:525
  342.7 4.6 %collective-permute-start.58 = (bf16[1,1,96,384]{3,2,1,0:T(8,128)(2,1)S(1)}, bf16[1,1,96,384]{3,2,1,0:T(8,128)(2,1)S(1)}, u32[]{:S(2)}, u32[]{:S(2)}) collective-permute-start(bf16[1,1,96,384]{3,2,1,0:T(8,128)(2,1)S(1)} %slice.193), channel_id=1, source_target_pairs={{0,2},{1,3},{2,0},{3,1},{4,6},{5,7},{6,4},{7,5},{8,10},{9,11},{10,... | collective-permute-start | bytes 221192 | tf_op jit(solution)/shard_map/ppermute | solution.py:530
  348.3 3.4 collective-permute-done.58
  358.7 2.6 collective-permute-start.62
  364.8 2.4 collective-permute-done.63
  376.1 12.3 %step.1 = (f32[3,3,96,192]{3,2,1,0:T(8,128)}, f32[3,3,96,192]{3,2,1,0:T(8,128)}, f32[3,3,96,192]{3,2,1,0:T(8,128)}, f32[3,3,96,192]{3,2,1,0:T(8,128)}, bf16[3,3,...) custom-call(f32[11,768]{1,0:T(8,128)} %copy-done.21, ...), custom_call_target="tpu_custom_call" | custom-call | flops 23592960 | bytes 22020100 | tf_op jit(solution)/shard_map/step/pallas_call | solution.py:507
  (342 shorter events, 93.0 us)
Async XLA Ops:
  7.2 135.1 %all-gather.3.cloned.1.call-start = ((), (), s32[]{:S(2)}) async-start(), calls=%async_computation.2 | async-start | bytes 10027008 | tf_op jit(solution)/shard_map/all_gather | solution.py:719
  23.0 311.4 %reduce-scatter.2.cloned.1.call-start = ((), (), s32[]{:S(2)}) async-start(), calls=%async_computation.1 | async-start | bytes 10027008 | tf_op jit(solution)/shard_map/reduce_scatter | solution.py:866
  23.8 12.6 %collective-permute-start.18 = (bf16[1,1,96,768]{3,2,1,0:T(8,128)(2,1)S(1)}, bf16[1,1,96,768]{3,2,1,0:T(8,128)(2,1)S(1)}, u32[]{:S(2)}, u32[]{:S(2)}) collective-permute-start(bf16[1,1,96,768]{3,2,1,0:T(8,128)(2,1)S(1)} %get-tuple-element.338), channel_id=1, source_target_pairs={{0,8},{8,0},{1,9},{9,1},{2,10},{10,2},{3,11},{11,3},{4,12},{12,4},... | collective-permute-start | bytes 442376 | tf_op jit(solution)/shard_map/ppermute | solution.py:525
  33.5 13.1 %collective-permute-start.2 = (bf16[4,1,96,384]{3,2,1,0:T(8,128)(2,1)S(1)}, bf16[4,1,96,384]{3,2,1,0:T(8,128)(2,1)S(1)}, u32[]{:S(2)}, u32[]{:S(2)}) collective-permute-start(bf16[4,1,96,384]{3,2,1,0:T(8,128)(2,1)S(1)} %pad_maximum_fusion.4.refs_0_.refs_6_), channel_id=1, source_target_pairs={{0,16},{16,0},{1,17},{17,1},{2,18},{18,2},{3,19},{19,3},{4,20},{20... | collective-permute-start | bytes 884744 | tf_op jit(solution)/shard_map/ppermute | solution.py:525
  36.4 29.8 %collective-permute-start.19 = (bf16[1,2,96,768]{3,2,1,0:T(8,128)(2,1)S(1)}, bf16[1,2,96,768]{3,2,1,0:T(8,128)(2,1)S(1)}, u32[]{:S(2)}, u32[]{:S(2)}) collective-permute-start(bf16[1,2,96,768]{3,2,1,0:T(8,128)(2,1)S(1)} %pad_maximum_fusion.6), channel_id=1, source_target_pairs={{0,2},{1,3},{2,0},{3,1},{4,6},{5,7},{6,4},{7,5},{8,10},{9,11},{10,... | collective-permute-start | bytes 884744 | tf_op jit(solution)/shard_map/ppermute | solution.py:530
  46.6 19.6 %collective-permute-start.9 = (bf16[4,1,96,384]{3,2,1,0:T(8,128)(2,1)S(1)}, bf16[4,1,96,384]{3,2,1,0:T(8,128)(2,1)S(1)}, u32[]{:S(2)}, u32[]{:S(2)}) collective-permute-start(bf16[4,1,96,384]{3,2,1,0:T(8,128)(2,1)S(1)} %collective-permute-done.2.refs_4_.refs_10_), channel_id=1, source_target_pairs={{0,8},{8,0},{1,9},{9,1},{2,10},{10,2},{3,11},{11,3},{4,12},{12,4},... | collective-permute-start | bytes 884744 | tf_op jit(solution)/shard_map/ppermute | solution.py:525
  47.0 19.7 %collective-permute-start.14 = (bf16[4,1,96,384]{3,2,1,0:T(8,128)(2,1)S(1)}, bf16[4,1,96,384]{3,2,1,0:T(8,128)(2,1)}, u32[]{:S(2)}, u32[]{:S(2)}) collective-permute-start(bf16[4,1,96,384]{3,2,1,0:T(8,128)(2,1)S(1)} %pad_maximum_fusion.5.refs_8_.refs_14_), channel_id=1, source_target_pairs={{0,16},{16,0},{1,17},{17,1},{2,18},{18,2},{3,19},{19,3},{4,20},{20... | collective-permute-start | bytes 884744 | tf_op jit(solution)/shard_map/ppermute | solution.py:525
  48.0 19.6 %collective-permute-start.15 = (bf16[4,1,96,384]{3,2,1,0:T(8,128)(2,1)S(1)}, bf16[4,1,96,384]{3,2,1,0:T(8,128)(2,1)}, u32[]{:S(2)}, u32[]{:S(2)}) collective-permute-start(bf16[4,1,96,384]{3,2,1,0:T(8,128)(2,1)S(1)} %collective-permute-done.5.refs_9_.refs_15_), channel_id=1, source_target_pairs={{0,16},{16,0},{1,17},{17,1},{2,18},{18,2},{3,19},{19,3},{4,20},{20... | collective-permute-start | bytes 884744 | tf_op jit(solution)/shard_map/ppermute | solution.py:525
  49.0 19.1 %collective-permute-start.6 = (bf16[4,1,96,384]{3,2,1,0:T(8,128)(2,1)S(1)}, bf16[4,1,96,384]{3,2,1,0:T(8,128)(2,1)}, u32[]{:S(2)}, u32[]{:S(2)}) collective-permute-start(bf16[4,1,96,384]{3,2,1,0:T(8,128)(2,1)S(1)} %pad_maximum_fusion.4.refs_0_.refs_6_), channel_id=1, source_target_pairs={{0,8},{8,0},{1,9},{9,1},{2,10},{10,2},{3,11},{11,3},{4,12},{12,4},... | collective-permute-start | bytes 884744 | tf_op jit(solution)/shard_map/ppermute | solution.py:525
  70.1 37.5 %collective-permute-start.21 = (bf16[2,2,96,768]{3,2,1,0:T(8,128)(2,1)S(1)}, bf16[2,2,96,768]{3,2,1,0:T(8,128)(2,1)S(1)}, u32[]{:S(2)}, u32[]{:S(2)}) collective-permute-start(bf16[2,2,96,768]{3,2,1,0:T(8,128)(2,1)S(1)} %pad_maximum_fusion.1.refs_0_), channel_id=1, source_target_pairs={{0,1},{1,0},{2,3},{3,2},{4,5},{5,4},{6,7},{7,6},{8,9},{9,8},{10,11... | collective-permute-start | bytes 1769480 | tf_op jit(solution)/shard_map/ppermute | solution.py:530
  70.2 37.4 %collective-permute-start.22 = (bf16[2,2,96,768]{3,2,1,0:T(8,128)(2,1)S(1)}, bf16[2,2,96,768]{3,2,1,0:T(8,128)(2,1)}, u32[]{:S(2)}, u32[]{:S(2)}) collective-permute-start(bf16[2,2,96,768]{3,2,1,0:T(8,128)(2,1)S(1)} %pad_maximum_fusion.1.refs_0_), channel_id=1, source_target_pairs={{0,16},{16,0},{1,17},{17,1},{2,18},{18,2},{3,19},{19,3},{4,20},{20... | collective-permute-start | bytes 1769480 | tf_op jit(solution)/shard_map/ppermute | solution.py:525
  87.3 20.2 %collective-permute-start.20 = (bf16[336,768]{1,0:T(8,128)(2,1)}, bf16[336,768]{1,0:T(8,128)(2,1)}, u32[]{:S(2)}, u32[]{:S(2)}) collective-permute-start(bf16[336,768]{1,0:T(8,128)(2,1)} %get-tuple-element.196), channel_id=1, source_target_pairs={{0,8},{8,0},{1,9},{9,1},{2,10},{10,2},{3,11},{11,3},{4,12},{12,4},... | collective-permute-start | bytes 1548296 | tf_op jit(solution)/shard_map/ppermute | solution.py:525
  107.6 15.9 %collective-permute-start.26 = (bf16[2,2,96,768]{3,2,1,0:T(8,128)(2,1)S(1)}, bf16[2,2,96,768]{3,2,1,0:T(8,128)(2,1)S(1)}, u32[]{:S(2)}, u32[]{:S(2)}) collective-permute-start(bf16[2,2,96,768]{3,2,1,0:T(8,128)(2,1)S(1)} %collective-permute-done.21.refs_4_), channel_id=1, source_target_pairs={{0,16},{16,0},{1,17},{17,1},{2,18},{18,2},{3,19},{19,3},{4,20},{20... | collective-permute-start | bytes 1769480 | tf_op jit(solution)/shard_map/ppermute | solution.py:525
  107.7 17.1 %collective-permute-start.28 = (bf16[336,768]{1,0:T(8,128)(2,1)S(1)}, bf16[336,768]{1,0:T(8,128)(2,1)}, u32[]{:S(2)}, u32[]{:S(2)}) collective-permute-start(bf16[336,768]{1,0:T(8,128)(2,1)S(1)} %bitcast.195), channel_id=1, source_target_pairs={{0,8},{8,0},{1,9},{9,1},{2,10},{10,2},{3,11},{11,3},{4,12},{12,4},... | collective-permute-start | bytes 1548296 | tf_op jit(solution)/shard_map/ppermute | solution.py:525
  107.7 20.1 %collective-permute-start.25 = (bf16[2,2,96,768]{3,2,1,0:T(8,128)(2,1)S(1)}, bf16[2,2,96,768]{3,2,1,0:T(8,128)(2,1)}, u32[]{:S(2)}, u32[]{:S(2)}) collective-permute-start(bf16[2,2,96,768]{3,2,1,0:T(8,128)(2,1)S(1)} %collective-permute-done.21.refs_4_), channel_id=1, source_target_pairs={{0,4},{4,0},{1,5},{5,1},{2,6},{6,2},{3,7},{7,3},{8,12},{12,8},{9,1... | collective-permute-start | bytes 1769480 | tf_op jit(solution)/shard_map/ppermute | solution.py:525
  107.8 20.0 %collective-permute-start.23 = (bf16[2,2,96,768]{3,2,1,0:T(8,128)(2,1)S(1)}, bf16[2,2,96,768]{3,2,1,0:T(8,128)(2,1)}, u32[]{:S(2)}, u32[]{:S(2)}) collective-permute-start(bf16[2,2,96,768]{3,2,1,0:T(8,128)(2,1)S(1)} %pad_maximum_fusion.1.refs_0_), channel_id=1, source_target_pairs={{0,4},{4,0},{1,5},{5,1},{2,6},{6,2},{3,7},{7,3},{8,12},{12,8},{9,1... | collective-permute-start | bytes 1769480 | tf_op jit(solution)/shard_map/ppermute | solution.py:525
  108.3 19.5 %collective-permute-start.24 = (bf16[2,2,96,768]{3,2,1,0:T(8,128)(2,1)}, bf16[2,2,96,768]{3,2,1,0:T(8,128)(2,1)}, u32[]{:S(2)}, u32[]{:S(2)}) collective-permute-start(bf16[2,2,96,768]{3,2,1,0:T(8,128)(2,1)} %collective-permute-done.22.refs_2_), channel_id=1, source_target_pairs={{0,4},{4,0},{1,5},{5,1},{2,6},{6,2},{3,7},{7,3},{8,12},{12,8},{9,1... | collective-permute-start | bytes 1769480 | tf_op jit(solution)/shard_map/ppermute | solution.py:525
  201.8 14.3 %collective-permute-start.32 = (bf16[336,768]{1,0:T(8,128)(2,1)}, bf16[336,768]{1,0:T(8,128)(2,1)S(1)}, u32[]{:S(2)}, u32[]{:S(2)}) collective-permute-start(bf16[336,768]{1,0:T(8,128)(2,1)} %get-tuple-element.217), channel_id=1, source_target_pairs={{0,8},{8,0},{1,9},{9,1},{2,10},{10,2},{3,11},{11,3},{4,12},{12,4},... | collective-permute-start | bytes 1548296 | tf_op jit(solution)/shard_map/ppermute | solution.py:525
  207.9 42.8 %collective-permute-start.33 = (bf16[4,2,96,768]{3,2,1,0:T(8,128)(2,1)S(1)}, bf16[4,2,96,768]{3,2,1,0:T(8,128)(2,1)S(1)}, u32[]{:S(2)}, u32[]{:S(2)}) collective-permute-start(bf16[4,2,96,768]{3,2,1,0:T(8,128)(2,1)S(1)} %add_convert_fusion), channel_id=1, source_target_pairs={{0,16},{16,0},{1,17},{17,1},{2,18},{18,2},{3,19},{19,3},{4,20},{20... | collective-permute-start | bytes 3538952 | tf_op jit(solution)/shard_map/ppermute | solution.py:525
  251.5 29.0 %collective-permute-start.55 = (bf16[2,2,96,768]{3,2,1,0:T(8,128)(2,1)S(1)}, bf16[2,2,96,768]{3,2,1,0:T(8,128)(2,1)S(1)}, u32[]{:S(2)}, u32[]{:S(2)}) collective-permute-start(bf16[2,2,96,768]{3,2,1,0:T(8,128)(2,1)S(1)} %add_convert_fusion.3), channel_id=1, source_target_pairs={{0,1},{1,0},{2,3},{3,2},{4,5},{5,4},{6,7},{7,6},{8,9},{9,8},{10,11... | collective-permute-start | bytes 1769480 | tf_op jit(solution)/shard_map/ppermute | solution.py:530
  251.7 16.2 %collective-permute-start.40 = (bf16[4,1,96,384]{3,2,1,0:T(8,128)(2,1)S(1)}, bf16[4,1,96,384]{3,2,1,0:T(8,128)(2,1)S(1)}, u32[]{:S(2)}, u32[]{:S(2)}) collective-permute-start(bf16[4,1,96,384]{3,2,1,0:T(8,128)(2,1)S(1)} %copy-done.46), channel_id=1, source_target_pairs={{0,4},{4,0},{1,5},{5,1},{2,6},{6,2},{3,7},{7,3},{8,12},{12,8},{9,1... | collective-permute-start | bytes 884744 | tf_op jit(solution)/shard_map/ppermute | solution.py:525
  254.1 11.6 %collective-permute-start.45 = (bf16[4,1,96,384]{3,2,1,0:T(8,128)(2,1)S(1)}, bf16[4,1,96,384]{3,2,1,0:T(8,128)(2,1)S(1)}, u32[]{:S(2)}, u32[]{:S(2)}) collective-permute-start(bf16[4,1,96,384]{3,2,1,0:T(8,128)(2,1)S(1)} %add_convert_fusion.9), channel_id=1, source_target_pairs={{0,16},{16,0},{1,17},{17,1},{2,18},{18,2},{3,19},{19,3},{4,20},{20... | collective-permute-start | bytes 884744 | tf_op jit(solution)/shard_map/ppermute | solution.py:525
  254.5 17.1 %collective-permute-start.42 = (bf16[4,1,96,384]{3,2,1,0:T(8,128)(2,1)S(1)}, bf16[4,1,96,384]{3,2,1,0:T(8,128)(2,1)S(1)}, u32[]{:S(2)}, u32[]{:S(2)}) collective-permute-start(bf16[4,1,96,384]{3,2,1,0:T(8,128)(2,1)S(1)} %add_convert_fusion.12), channel_id=1, source_target_pairs={{0,16},{16,0},{1,17},{17,1},{2,18},{18,2},{3,19},{19,3},{4,20},{20... | collective-permute-start | bytes 884744 | tf_op jit(solution)/shard_map/ppermute | solution.py:525
  256.4 16.9 %collective-permute-start.37 = (bf16[4,1,96,384]{3,2,1,0:T(8,128)(2,1)S(1)}, bf16[4,1,96,384]{3,2,1,0:T(8,128)(2,1)S(1)}, u32[]{:S(2)}, u32[]{:S(2)}) collective-permute-start(bf16[4,1,96,384]{3,2,1,0:T(8,128)(2,1)S(1)} %copy-done.45), channel_id=1, source_target_pairs={{0,4},{4,0},{1,5},{5,1},{2,6},{6,2},{3,7},{7,3},{8,12},{12,8},{9,1... | collective-permute-start | bytes 884744 | tf_op jit(solution)/shard_map/ppermute | solution.py:525
  280.7 14.4 %collective-permute-start.53 = (bf16[4,1,96,384]{3,2,1,0:T(8,128)(2,1)}, bf16[4,1,96,384]{3,2,1,0:T(8,128)(2,1)}, u32[]{:S(2)}, u32[]{:S(2)}) collective-permute-start(bf16[4,1,96,384]{3,2,1,0:T(8,128)(2,1)} %add_convert_fusion.8), channel_id=1, source_target_pairs={{0,8},{8,0},{1,9},{9,1},{2,10},{10,2},{3,11},{11,3},{4,12},{12,4},... | collective-permute-start | bytes 884744 | tf_op jit(solution)/shard_map/ppermute | solution.py:525
  282.3 14.5 %collective-permute-start.51 = (bf16[4,1,96,384]{3,2,1,0:T(8,128)(2,1)}, bf16[4,1,96,384]{3,2,1,0:T(8,128)(2,1)S(1)}, u32[]{:S(2)}, u32[]{:S(2)}) collective-permute-start(bf16[4,1,96,384]{3,2,1,0:T(8,128)(2,1)} %add_convert_fusion.14), channel_id=1, source_target_pairs={{0,16},{16,0},{1,17},{17,1},{2,18},{18,2},{3,19},{19,3},{4,20},{20... | collective-permute-start | bytes 884744 | tf_op jit(solution)/shard_map/ppermute | solution.py:525
  283.7 28.6 %collective-permute-start.59 = (bf16[1,2,96,768]{3,2,1,0:T(8,128)(2,1)}, bf16[1,2,96,768]{3,2,1,0:T(8,128)(2,1)S(1)}, u32[]{:S(2)}, u32[]{:S(2)}) collective-permute-start(bf16[1,2,96,768]{3,2,1,0:T(8,128)(2,1)} %slice.233), channel_id=1, source_target_pairs={{0,2},{1,3},{2,0},{3,1},{4,6},{5,7},{6,4},{7,5},{8,10},{9,11},{10,... | collective-permute-start | bytes 884744 | tf_op jit(solution)/shard_map/ppermute | solution.py:530
  289.1 20.8 %collective-permute-start.47 = (bf16[2,96,768]{2,1,0:T(8,128)(2,1)}, bf16[2,96,768]{2,1,0:T(8,128)(2,1)S(1)}, u32[]{:S(2)}, u32[]{:S(2)}) collective-permute-start(bf16[2,96,768]{2,1,0:T(8,128)(2,1)} %bitcast.45), channel_id=1, source_target_pairs={{0,1},{1,0},{2,3},{3,2},{4,5},{5,4},{6,7},{7,6},{8,9},{9,8},{10,11... | collective-permute-start | bytes 884744 | tf_op jit(solution)/shard_map/ppermute | solution.py:530
  294.4 32.8 %collective-permute-start.46 = (bf16[336,768]{1,0:T(8,128)(2,1)S(1)}, bf16[336,768]{1,0:T(8,128)(2,1)S(1)}, u32[]{:S(2)}, u32[]{:S(2)}) collective-permute-start(bf16[336,768]{1,0:T(8,128)(2,1)S(1)} %slice.217), channel_id=1, source_target_pairs={{0,8},{8,0},{1,9},{9,1},{2,10},{10,2},{3,11},{11,3},{4,12},{12,4},... | collective-permute-start | bytes 1548296 | tf_op jit(solution)/shard_map/ppermute | solution.py:525
  296.2 25.1 %collective-permute-start.54 = (bf16[2,1,96,384]{3,2,1,0:T(8,128)(2,1)S(1)}, bf16[2,1,96,384]{3,2,1,0:T(8,128)(2,1)S(1)}, u32[]{:S(2)}, u32[]{:S(2)}) collective-permute-start(bf16[2,1,96,384]{3,2,1,0:T(8,128)(2,1)S(1)} %slice.230), channel_id=1, source_target_pairs={{0,1},{1,0},{2,3},{3,2},{4,5},{5,4},{6,7},{7,6},{8,9},{9,8},{10,11... | collective-permute-start | bytes 442376 | tf_op jit(solution)/shard_map/ppermute | solution.py:530
  296.9 30.2 %collective-permute-start.52 = (bf16[2,1,96,384]{3,2,1,0:T(8,128)(2,1)S(1)}, bf16[2,1,96,384]{3,2,1,0:T(8,128)(2,1)S(1)}, u32[]{:S(2)}, u32[]{:S(2)}) collective-permute-start(bf16[2,1,96,384]{3,2,1,0:T(8,128)(2,1)S(1)} %slice.228), channel_id=1, source_target_pairs={{0,1},{1,0},{2,3},{3,2},{4,5},{5,4},{6,7},{7,6},{8,9},{9,8},{10,11... | collective-permute-start | bytes 442376 | tf_op jit(solution)/shard_map/ppermute | solution.py:530
  316.3 10.3 %collective-permute-start.49 = (bf16[1,96,768]{2,1,0:T(8,128)(2,1)S(1)}, bf16[1,96,768]{2,1,0:T(8,128)(2,1)S(1)}, u32[]{:S(2)}, u32[]{:S(2)}) collective-permute-start(bf16[1,96,768]{2,1,0:T(8,128)(2,1)S(1)} %add_convert_fusion.22), channel_id=1, source_target_pairs={{0,2},{1,3},{2,0},{3,1},{4,6},{5,7},{6,4},{7,5},{8,10},{9,11},{10,... | collective-permute-start | bytes 442376 | tf_op jit(solution)/shard_map/ppermute | solution.py:530
  (90 other events, 776.4 us)
Sparse Core Ops, SparseCore 0:
  23.1 109.7 all-gather.2
  176.0 133.8 reduce-scatter.1

commit v4 on v3

--- a/solution.py
+++ b/solution.py
@@ -152,13 +152,14 @@
         load_weight(pieces[middle:], weight)
 
 
-def store_weight(value, pieces):
-    row = 0
-    for piece in pieces:
-        for part in range(piece.shape[1]):
-            rows = piece.shape[2]
-            piece[0, part] = value[row : row + rows, :].astype(piece.dtype)
-            row += rows
+def store_pair(value, near, far, by_group=False):
+    rows = near.shape[3]
+    for high in range(2):
+        for core, piece in enumerate((near, far)):
+            for mid in range(2):
+                row = (4 * high + 2 * core + mid) * rows
+                spot = (high, 0, mid) if by_group else (high, mid, 0)
+                piece[spot] = value[row : row + rows, :].astype(piece.dtype)
 
 
 def wide_spots(place, piece, shard_rows):
@@ -252,17 +253,8 @@
         other_one[...] = partner_order(jnp.where(is_vis, lang_one, vis_one))
 
 
-def self_forward_kernel(width, blocks, length, own, other, norm, *refs):
-    pieces, refs = refs[:8], refs[8:]
-    two, n_ref, r_ref, qkv, ctx, probs_ref, weight, acc, rows = refs
-    step = pl.program_id(0)
-    load_halves(pieces, weight)
-
-    @pl.when(step == 0)
-    def _():
-        rows[...] = stack_rows([own[...], other[...]])
-        acc[...] = rows[...].astype(F32)
-
+def self_forward_step(width, blocks, length, rows, pieces, weight, qkv, ctx, probs_ref):
+    load_weight(pieces, weight)
     full = weight[...]
     in_part, out_part = full[:, : 3 * width], full[:, 3 * width :]
     triple = dot_nn(rows[...], in_part).astype(BF)
@@ -272,7 +264,31 @@
     probs, context = attend(*thirds(triple, width), mask, blocks)
     probs_ref[0] = probs
     ctx[0] = context
-    acc[...] += dot_nt(context, out_part)
+    return dot_nt(context, out_part)
+
+
+def self_first_kernel(width, blocks, length, own, other, *refs):
+    pieces, (acc, qkv, ctx, probs, weight, rows) = refs[:4], refs[4:]
+
+    @pl.when(pl.program_id(0) == 0)
+    def _():
+        rows[...] = stack_rows([own[...], other[...]])
+        acc[...] = rows[...].astype(F32)
+
+    acc[...] += self_forward_step(width, blocks, length, rows, pieces, weight, qkv, ctx, probs)
+
+
+def self_second_kernel(width, blocks, length, own, other, norm, summed, *refs):
+    pieces, refs = refs[:4], refs[7:]
+    two, n_ref, r_ref, qkv, ctx, probs, weight, acc, rows = refs
+    step = pl.program_id(0)
+
+    @pl.when(step == 0)
+    def _():
+        rows[...] = stack_rows([own[...], other[...]])
+        acc[...] = summed[...]
+
+    acc[...] += self_forward_step(width, blocks, length, rows, pieces, weight, qkv, ctx, probs)
 
     @pl.when(step == pl.num_programs(0) - 1)
     def _():
@@ -338,7 +354,7 @@
 
 
 def self_backward_kernel(width, blocks, inward, own, other, qkv, ctx, probs, *refs):
-    pieces, grads, refs = refs[:8], refs[8:12], refs[12:]
+    pieces, near, far, refs = refs[:8], refs[8], refs[9], refs[10:]
     down_own, down_other, weight, acc, branch, turned, branch_turned = refs
     load_halves(pieces, weight)
     step = pl.program_id(0)
@@ -358,7 +374,7 @@
     grad_triple = jnp.concatenate(grads_of, axis=1)
     in_grad = dot_nn(turned[...], grad_triple).astype(BF)
     out_grad = dot_nn(branch_turned[...], ctx[0]).astype(BF)
-    store_weight(jnp.concatenate([in_grad, out_grad], axis=1), grads)
+    store_pair(jnp.concatenate([in_grad, out_grad], axis=1), near, far, True)
     acc[...] += dot_nt(grad_triple, in_part)
 
     @pl.when(step == pl.num_programs(0) - 1)
@@ -369,13 +385,27 @@
 
 
 def cross_backward_kernel(
-    width, blocks, stream, own_up, other_up, lang, vis, lang_n, lang_r, vis_n, vis_r, norm, *refs
+    width,
+    blocks,
+    stream,
+    own_up,
+    other_up,
+    lang,
+    vis,
+    lang_n,
+    lang_r,
+    vis_n,
+    vis_r,
+    norm,
+    order,
+    source,
+    targets,
+    *refs,
 ):
     lang_qkv, vis_qkv, lang_ctx, vis_ctx, lang_p, vis_p = refs[:6]
     first, second, refs = refs[6:14], refs[14:22], refs[22:]
-    first_grads, second_grads, refs = refs[:8], refs[8:16], refs[16:]
-    lang_out, vis_out, gain_ref, shift_ref = refs[:4]
-    weight, lang_acc, vis_acc, lang_branch, vis_branch, turned, branch_turned = refs[4:]
+    near, far, lang_out, image_out, gain_ref, shift_ref = refs[:6]
+    weight, lang_acc, vis_acc, lang_branch, vis_branch, turned, branch_turned = refs[6:]
     load_weight(first, weight)
     load_weight(second, weight, first[0].shape[3])
     step = pl.program_id(0)
@@ -422,16 +452,16 @@
     in_grad = dot_nn(turned[...], stack_rows([lang_grad, vis_grad]))
     out_grad = dot_nn(branch_turned[...], stack_rows([lang_ctx[0], vis_ctx[0]]))
     grad = jnp.concatenate([in_grad.astype(BF), out_grad.astype(BF)], axis=1)
-    middle = first[0].shape[3]
-    store_weight(grad[:, :middle], first_grads)
-    store_weight(grad[:, middle:], second_grads)
+    store_pair(grad, near, far)
     lang_acc[...] += dot_nt(lang_grad, in_part)
     vis_acc[...] += dot_nt(vis_grad, in_part)
 
     @pl.when(step == pl.num_programs(0) - 1)
     def _():
-        lang_out[...] = lang_acc[...].astype(lang_out.dtype)
-        vis_out[...] = vis_acc[...].astype(vis_out.dtype)
+        lang_out[...] = dot_nt(lang_acc[...].astype(BF), order[...])
+        chooser = jnp.where(source[...] == targets[...], 1.0, 0.0).astype(BF)
+        image = dot_tn(chooser, vis_acc[...].astype(BF)).astype(BF)
+        image_out[...] = dot_nt(image, order[...]).astype(BF)
 
 
 def store_step(state, clip, outs):
@@ -440,7 +470,24 @@
         ref[place] = value.astype(ref.dtype)
 
 
-def step_kernel(width, sums, theirs, home_low, home_high, stream_one, stream_two, feed, *refs):
+def prepare_kernel(norms, kept, sent, self_low, self_theirs, feed_sum, feed_theirs, sums):
+    home = kept[...].astype(F32) + sent[...].astype(F32)
+    squares = jnp.sum(home * home, keepdims=True)[0]
+    for value in (self_low[0], self_theirs[...]):
+        wide = value.astype(F32)
+        squares += jnp.sum(wide * wide, keepdims=True)
+    for kind in range(feed_theirs.shape[0]):
+        for value in (feed_sum[0, kind], feed_theirs[kind]):
+            wide = value.astype(F32)
+            squares += jnp.sum(wide * wide, keepdims=True)
+    count = norms.shape[0]
+    sums[:count, :] = norms[...]
+    sums[count:, :] = jnp.broadcast_to(squares, (1, norms.shape[1]))
+
+
+def step_kernel(
+    width, stream, sums, theirs, kept, sent, self_low, self_theirs, feed_sum, feed_theirs, *refs
+):
     ins, outs, feed_in, feed_out, norm_in = (refs[4 * i : 4 * i + 4] for i in range(5))
     refs = refs[20:]
     step = pl.program_id(0)
@@ -455,19 +502,24 @@
         new = adamw_step(norm_grad[2 * place : 2 * place + 2], *state, NORM_RATE, clip)
         for ref, value in zip(refs[24:29], new):
             ref[place] = value
-    home = jnp.concatenate([home_low[...], home_high[...]], axis=1)
-    grad = jnp.where(step == 0, home, jnp.where(step == 1, stream_one[...], stream_two[...]))
+    is_vis = stream[0, 0] == 1
+
+    def by_stream(mine, other):
+        mine, other = mine.astype(F32), other.astype(F32)
+        return jnp.where(is_vis, other, mine), jnp.where(is_vis, mine, other)
+
+    home = kept[0].astype(F32) + sent[0].astype(F32)
+    one, two = by_stream(self_low[0], self_theirs[...])
+    grad = jnp.where(step == 0, home, jnp.where(step == 1, one, two))
     for kind in range(3):
         part = grad[:, kind * width : (kind + 1) * width]
         store_step([part] + [ref[0, kind] for ref in ins], clip, [(r, (0, kind)) for r in refs[:6]])
     part = grad[:, 3 * width :].T
     store_step([part] + [ref[0] for ref in outs], clip, [(r, 0) for r in refs[6:12]])
-    for stream in range(feed.shape[0]):
-        part = feed[stream, 0]
-        state = [part] + [ref[stream] for ref in feed_in]
-        store_step(state, clip, [(r, stream) for r in refs[12:18]])
-        state = [feed[stream, 1]] + [ref[stream] for ref in feed_out]
-        store_step(state, clip, [(r, stream) for r in refs[18:24]])
+    for kind, state_in, first in ((0, feed_in, 12), (1, feed_out, 18)):
+        for place, part in enumerate(by_stream(feed_sum[0, kind], feed_theirs[kind])):
+            state = [part] + [ref[place] for ref in state_in]
+            store_step(state, clip, [(r, place) for r in refs[first : first + 6]])
 
 
 def whole(shape):
@@ -489,7 +541,7 @@
     return pl.BlockSpec(block, lambda m: (0, 0, pick(m), 0, 0, 0, 0))
 
 
-def call(kernel, steps, ins, outs, scratch, name, flops):
+def call(kernel, steps, ins, outs, scratch, name, flops, aliases=()):
     spec = {
         "whole": lambda s: whole(s),
         "step": lambda s: per_step(s),
@@ -500,6 +552,14 @@
         "rows": lambda s: pl.BlockSpec(
             tuple(s[:-2]) + (s[-2] // steps, s[-1]), lambda m: (0,) * (len(s) - 2) + (m, 0)
         ),
+        "pair": lambda s: pl.BlockSpec(
+            tuple(s[:2]) + (1,) + tuple(s[3:]), lambda m: (0, 0, m, 0, 0)
+        ),
+        "groups": lambda s: pl.BlockSpec(
+            (s[0], 1) + tuple(s[2:]), lambda m: (0, m, 0, 0, 0)
+        ),
+        "upper": lambda s: part_of(s, lambda m: m + s[0] // 2),
+        "kept": lambda s: pl.BlockSpec(memory_space=pl.ANY),
         "scalar": lambda s: pl.BlockSpec(memory_space=pltpu.SMEM),
     }
     moved = sum(a.size * a.dtype.itemsize for _, a in ins)
@@ -511,6 +571,7 @@
         out_specs=[spec[kind](s) for kind, s, _ in outs],
         out_shape=[jax.ShapeDtypeStruct(s, t) for _, s, t in outs],
         scratch_shapes=[pltpu.VMEM(s, t) for s, t in scratch],
+        input_output_aliases=dict(aliases),
         compiler_params=pltpu.CompilerParams(
             vmem_limit_bytes=VMEM_LIMIT, dimension_semantics=("arbitrary",)
         ),
@@ -534,6 +595,10 @@
     flat, tree = jax.tree.flatten(value)
     kept = lax.optimization_barrier((flat, jax.tree.leaves(others)))[0]
     return jax.tree.unflatten(tree, kept)
+
+
+def together(*values):
+    return lax.optimization_barrier(values)
 
 
 def swap_mask(value, axis, mask):
@@ -595,8 +660,8 @@
 
 def scatter_extra(current):
     for bit in reversed(extra_bits()):
-        half = current.shape[2] // 2
-        current = added(current[:, :, :half], swap_dp(current[:, :, half:], bit))
+        low, high = jnp.split(current, 2, axis=-2)
+        current = added(low, swap_dp(high, bit))
     return current
 
 
@@ -824,27 +889,42 @@
     self_high, self_low, cot_other = after((self_high, self_low, cot_other), other_one)
     grow(self_high, 0, 2)
     grow(self_low, 1, 0)
+    half_groups = n_mp // 2
+    saved = [
+        (n_mp, total, 3 * width),
+        (n_mp, total, width),
+        (n_mp, heads * total, vis_block),
+    ]
+    first_half = call(
+        functools.partial(self_first_kernel, width, 2 * blocks),
+        half_groups,
+        [("scalar", length)]
+        + [("whole", a) for a in (own_one, other_one)]
+        + [("step", a) for a in stream_list(self_low)],
+        [("whole", (total, dim), F32)] + [("step", a, BF) for a in saved],
+        [((dim, 4 * width), BF), ((total, dim), BF)],
+        "self_first",
+        6 * total * dim * 4 * width * n_mp,
+    )
+    self_high, cot_theirs = after((self_high, swap_dp(cot_other, 1)), first_half[0])
     grow(self_high, 1, 0)
     self_pieces = [("low", a) for a in stream_list(self_low)]
     self_pieces += [("high", a) for a in stream_list(self_high)]
     rows_two, normed_two, inverse_two, self_qkv, self_ctx, self_probs = call(
-        functools.partial(self_forward_kernel, width, 2 * blocks),
-        n_mp,
-        [("scalar", length)] + [("whole", a) for a in (own_one, other_one, norm_self)]
-        + self_pieces,
-        [
-            ("whole", (total, dim), BF),
-            ("whole", (total, dim), F32),
-            ("whole", (total, 1), F32),
-            ("step", (n_mp, total, 3 * width), BF),
-            ("step", (n_mp, total, width), BF),
-            ("step", (n_mp, heads * total, vis_block), BF),
-        ],
+        functools.partial(self_second_kernel, width, 2 * blocks),
+        half_groups,
+        [("scalar", length)]
+        + [("whole", a) for a in (own_one, other_one, norm_self, first_half[0])]
+        + [("step", a) for a in stream_list(self_high)]
+        + [("kept", a) for a in first_half[1:]],
+        [("whole", (total, dim), BF), ("whole", (total, dim), F32), ("whole", (total, 1), F32)]
+        + [("upper", a, BF) for a in saved],
         [((dim, 4 * width), BF), ((total, dim), F32), ((total, dim), BF)],
-        "self_forward",
-        12 * total * dim * 4 * width * n_mp,
+        "self_second",
+        6 * total * dim * 4 * width * n_mp,
+        [(9 + i, 3 + i) for i in range(3)],
     )
-    cot = to_order(jnp.concatenate([cot_own, swap_dp(cot_other, 1)], axis=0))
+    cot = to_order(jnp.concatenate([cot_own, cot_theirs], axis=0))
     spot = jnp.stack([me >> 2, me & 1]).astype(jnp.int32).reshape(1, 2)
 
     whole_row = ("whole", (1, dim), F32)
@@ -884,29 +964,35 @@
         [("whole", a) for a in (inward, own_one, other_one)]
         + [("step", a) for a in (self_qkv, self_ctx, self_probs)]
         + self_pieces,
-        [("step", (n_mp, 2, eighth, 4 * width), BF)] * 4 + [("whole", (slot, dim), BF)] * 2,
+        [("groups", (2, n_mp, 2, eighth, 4 * width), BF)] * 2 + [("whole", (slot, dim), BF)] * 2,
         [((dim, 4 * width), BF), ((total, dim), F32), ((total, dim), BF)] + [((dim, total), BF)] * 2,
         "self_backward",
         20 * total * dim * 4 * width * n_mp,
     )
-    self_g = stream_keys(found[:4])
-    own_up, other_up = found[4:]
+    self_near, self_far = found[:2]
+    own_up, other_up = found[2:]
     other_up = swap_dp(other_up, 1)
-    self_core = core_step(self_g)
-    self_sums = [added(m, t) for m, t in zip(*self_core)]
+    self_far = swap_dp(self_far, 0)
+    self_sums = [scatter_extra(added(self_near[hi], self_far[hi])) for hi in (0, 1)]
     own_up = after(own_up, self_sums)
+    place_mp = lax.axis_index("mp")
+    part = -(-image_count // n_mp // 16) * 16
+    index = jnp.arange(n_mp, dtype=jnp.int32)
+    far = sum(((index >> b) & 1) << (n_bits - 1 - b) for b in range(n_bits))
+    rows = ((far ^ place_mp)[:, None] * part + jnp.arange(part, dtype=jnp.int32)[None, :]).reshape(1, -1)
     found = call(
         functools.partial(cross_backward_kernel, width, blocks),
         n_mp,
         [("scalar", which)]
         + [("whole", a) for a in (own_up, other_up, lang, vis)]
         + [("whole", a) for a in (lang_n, lang_r, vis_n, vis_r, norm_cross)]
+        + [("whole", a) for a in (order, row_source, 1 + rows)]
         + [("step", a) for a in cross_saved]
         + pieces(cross_w),
-        [("step", (n_mp, 1, eighth, half), BF)] * 16
+        [("pair", (2, 2, n_mp, eighth, 4 * width), BF)] * 2
         + [
-            ("whole", (lang_pad, dim), BF),
-            ("whole", (slot, dim), BF),
+            ("whole", (lang_pad, dim), F32),
+            ("whole", (n_mp * part, dim), BF),
             ("whole", (1, dim), F32),
             ("whole", (1, dim), F32),
         ],
@@ -922,63 +1008,67 @@
         "cross_backward",
         20 * both * dim * 4 * width * n_mp,
     )
-    first_g, second_g = home_keys(found[:8]), home_keys(found[8:16])
-    lang_back, vis_back, cross_gain, cross_shift = found[16:]
-    self_far = swap_dp(self_sums[1], 2)
-    self_far = after(self_far, lang_back)
-    late = after((first_g, second_g, lang_back, vis_back, cross_gain, cross_shift), self_far)
-    first_g, second_g, lang_back, vis_back, cross_gain, cross_shift = late
-    shrink(first_g, 2, 0)
-    shrink(second_g, 2, 0)
-    shrink(first_g, 1, 1)
-    shrink(second_g, 0, 2)
-    self_part = split(self_sums[0], self_far)
-    first_g, second_g = after((first_g, second_g), self_part)
-    late = after((lang_back, vis_back, cross_gain, cross_shift, rows_three), first_g, second_g)
-    lang_back, vis_back, cross_gain, cross_shift, rows_three = late
-    shrink(first_g, 0, 2)
-    shrink(second_g, 1, 1)
-    first_sum, second_sum = scatter_extra(first_g[(0, 0, 0)]), scatter_extra(second_g[(0, 0, 0)])
-    homes, pair = [first_sum, second_sum], None
-    for bit in range(n_bits):
-        homes = [added(*send_mp([(h[: len(h) // 2], h[len(h) // 2 :])], bit)[0]) for h in homes]
-        pair = added(*send_mp([self_part], bit)[0])
-        self_part = pair[: len(pair) // 2], pair[len(pair) // 2 :]
-        if bit == 0:
-            theirs = swap_dp(feed_sum[1], 1)
-            homes = after(homes, pair, theirs)
-            mine, theirs = feed_sum[0].astype(F32), theirs.astype(F32)
-            feed_total = [jnp.where(is_vis, theirs, mine), jnp.where(is_vis, mine, theirs)]
-    attn_total = [h[0, 0].astype(F32) for h in homes]
-    pair = scatter_extra(pair)
-    mine, theirs = pair[0, 0].astype(F32), swap_dp(pair[0, 1], 1).astype(F32)
-    attn_total += [jnp.where(is_vis, theirs, mine), jnp.where(is_vis, mine, theirs)]
+    near, far, lang_back, image_term, cross_gain, cross_shift = found
+
+    def parts(value):
+        middle = value.shape[0] // 2
+        return value[:middle], value[middle:]
+
+    def total_of(*terms):
+        return functools.reduce(jnp.add, [t.astype(F32) for t in terms]).astype(BF)
+
+    self_kept = self_sums[0]
+    self_far = swap_dp(self_sums[1][1:], 2)
+    late = together(near, far, lang_back, image_term, self_far)
+    near, far, lang_back, image_term, self_far = late
+    far = swap_dp(far, 0)
+    self_sent = total_of(self_kept[2:], self_far[1:])
+    left, right = (slice(c, c + half) for c in (0, half))
+    first = [added(near[:, mid, ..., left], far[:, mid, ..., left]) for mid in (0, 1)]
+    second = [added(near[hi, ..., right], far[hi, ..., right]) for hi in (0, 1)]
+    first, second, self_sent, lang_back = together(first, second, self_sent, lang_back)
+
+    first_far, second_far, self_sent = swap_dp(first[1], 1), swap_dp(second[1], 2), swap_mp(self_sent, 0)
+    late = together(first, second, first_far, second_far, self_sent, rows_three, image_term)
+    first, second, first_far, second_far, self_sent, rows_three, image_term = late
+    first = [added(first[0][i], first_far[i]) for i in (0, 1)]
+    second = [added(second[0][i], second_far[i]) for i in (0, 1)]
+    first, second, self_sent = together(first, second, self_sent)
+    self_one = total_of(self_kept[1], self_far[0], self_sent[1])
+
+    first_far, second_far = swap_dp(first[1], 2), swap_dp(second[1], 1)
+    self_ones = [swap_mp(self_one[1:], 1)]
+    self_near = swap_dp(self_sums[1][:1], 2)
+    late = together(first[0], second[0], first_far, second_far, self_ones, self_near, image_term)
+    first, second, first_far, second_far, self_ones, self_near, image_term = late
+    home = jnp.concatenate([added(first, first_far), added(second, second_far)], axis=-1)
+    home = scatter_extra(home)
+    self_low = total_of(self_kept[0], self_near[0], self_sent[0])
+
+    kept, sent = parts(home)
+    sent = swap_mp(sent, 0)
+    self_ones = [swap_mp(after(self_one[:1], home), 1)] + self_ones
+    image_kept, image_sent = parts(image_term.reshape(n_mp, part, dim))
+    image_sent = swap_mp(image_sent, 0)
+    late = together(kept, sent, self_low, self_ones, image_kept, image_sent)
+    kept, sent, self_low, self_ones, image_kept, image_sent = late
+    self_low = added(self_low, jnp.concatenate(self_ones, axis=0))
+    home, image_term = added(kept, sent), added(image_kept, image_sent)
+
+    kept, sent = parts(home)
+    sent, theirs, feed_theirs = swap_mp(sent, 1), swap_dp(self_low[1], 1), swap_dp(feed_sum[1], 1)
+    image_kept, image_sent = parts(image_term)
+    image_sent = swap_mp(image_sent, 1)
+    late = together(kept, sent, self_low, theirs, feed_theirs, image_kept, image_sent)
+    kept, sent, self_low, theirs, feed_theirs, image_kept, image_sent = late
+    image_term = added(image_kept, image_sent)
 
     final = from_order(rows_three).astype(BF)
-    final_other = swap_dp(final[slot:], 1)
+    final_other = after(swap_dp(final[slot:], 1), kept)
     language_out = out_of_blocks(jnp.where(is_vis, final_other, final[:slot]), lang_rows)
     vision_out = out_of_blocks(jnp.where(is_vis, final[:slot], final_other), vis_rows)
 
-    language_grad = from_order(out_of_blocks(lang_back, lang_rows)).reshape(language.shape)
-    place_mp = lax.axis_index("mp")
-    part = -(-image_count // n_mp // 16) * 16
-    index = jnp.arange(n_mp, dtype=jnp.int32)
-    far = sum(((index >> b) & 1) << (n_bits - 1 - b) for b in range(n_bits))
-    rows = ((far ^ place_mp)[:, None] * part + jnp.arange(part, dtype=jnp.int32)[None, :]).reshape(1, -1)
-    chooser = (row_source == 1 + rows).astype(BF)
-    image_term = lax.dot_general(
-        chooser, vis_back, (((0,), (0,)), ((), ())), preferred_element_type=F32
-    ).astype(BF)
-    image_term = from_order(image_term).astype(BF).reshape(n_mp, part, dim)
-    image_term = gather_mp(scatter_mp(image_term))
-    for b in range(n_bits):
-        shape = (1 << b, 2, -1, part, dim)
-        flipped = image_term.reshape(shape)[:, ::-1].reshape(image_term.shape)
-        image_term = jnp.where((place_mp >> b) & 1 == 1, flipped, image_term)
-    axes = tuple(reversed(range(n_bits))) + (n_bits, n_bits + 1)
-    image_term = image_term.reshape((2,) * n_bits + (part, dim)).transpose(axes)
-    image_grad = image_term.reshape(-1, dim)[:image_count].astype(F32).reshape(images.shape)
-
+    language_grad = out_of_blocks(lang_back, lang_rows).reshape(language.shape)
     here = (jnp.arange(2, dtype=jnp.int32) == stream).astype(F32)[:, None, None]
     norm_partial = jnp.concatenate(
         [
@@ -990,8 +1080,28 @@
     )
     norm_partial = from_order(norm_partial.reshape(-1, dim), HIGHEST)
 
-    squares = sum(jnp.sum(g * g) for g in attn_total + feed_total)
-    sums, their_sums = sum_up(jnp.concatenate([norm_partial, jnp.full((1, dim), squares)], axis=0))
+    totals = [kept, sent, self_low, theirs]
+    sums = call(
+        prepare_kernel,
+        1,
+        [("whole", a) for a in [norm_partial] + totals + [feed_sum, feed_theirs]],
+        [("whole", (norm_partial.shape[0] + 1, dim), F32)],
+        [],
+        "prepare",
+        8 * dim * width,
+    )[0]
+    sums, their_sums = sum_up(sums)
+    image_term = after(image_term, kept)
+    for bit in reversed(mp_bits()):
+        image_term = jnp.concatenate([image_term, swap_mp(image_term, bit)], axis=0)
+    for b in range(n_bits):
+        shape = (1 << b, 2, -1, part, dim)
+        flipped = image_term.reshape(shape)[:, ::-1].reshape(image_term.shape)
+        image_term = jnp.where((place_mp >> b) & 1 == 1, flipped, image_term)
+    axes = tuple(reversed(range(n_bits))) + (n_bits, n_bits + 1)
+    image_term = image_term.reshape((2,) * n_bits + (part, dim)).transpose(axes)
+    image_grad = image_term.reshape(-1, dim)[:image_count].astype(F32).reshape(images.shape)
+
     kinds = [("step", t) for t in (F32, F32, F32, F32, BF, F32)]
     norm_in = [
         jnp.swapaxes(a, 0, 1)
@@ -1008,8 +1118,9 @@
     stepped = call(
         functools.partial(step_kernel, width),
         3,
-        [("whole", a) for a in [sums, their_sums] + attn_total]
-        + [(by_rows, jnp.stack(feed_total))]
+        [("scalar", which)]
+        + [("whole", a) for a in [sums, their_sums] + totals]
+        + [(by_rows, feed_sum), (by_rows, feed_theirs)]
         + [("step", a) for a in wide_in + wide_out]
         + [(by_rows, a) for a in feed_in + feed_out]
         + [("whole", a) for a in norm_in],

time: 401 us -> 379 us (0.945)
  waiting for transfers between devices: 152 us -> 128 us
  starting transfers between devices: 60.7 us -> 49.8 us
  Pallas kernels: 122 us -> 131 us
  local copies, waits for them, and re-layouts: 10.6 us -> 17.5 us
  other arithmetic: 17.7 us -> 22 us
  between operations: 19.3 us -> 15.2 us
    ppermute x46 -> x37, waiting for transfers between devices: 74.3 us -> 40.6 us  [swap_dp(): lax.ppermute(value, axis, [(i, i ^ 1 << place) for i in range(count)])]
    ppermute x16 -> x15, waiting for transfers between devices: 70.5 us -> 81.8 us  [swap_mp(): return lax.ppermute(value, 'mp', [(i, i ^ 1 << bit) for i in range(count)])]
    pallas_call x6 -> x8, Pallas kernels: 122 us -> 131 us  [call(): pl.pallas_call(kernel, grid=(steps,), in_specs=[spec[kind](a.shape) for k...]
    ppermute x46 -> x37, starting transfers between devices: 26.8 us -> 21.2 us  [swap_dp(): lax.ppermute(value, axis, [(i, i ^ 1 << place) for i in range(count)])]
    ppermute x16 -> x15, starting transfers between devices: 25.8 us -> 20.6 us  [swap_mp(): return lax.ppermute(value, 'mp', [(i, i ^ 1 << bit) for i in range(count)])]
    convert_element_type x19 -> x11, other arithmetic: 6.16 us -> 9.16 us  [added(): return (mine.astype(F32) + theirs.astype(F32)).astype(BF)]
  transfers between devices with their start and end apart: 70 -> 60, of which waited for: 35 -> 29; matrix products, arithmetic and copies ran while one was open for 9% -> 11% of each run, Pallas kernels for 19% -> 26%
where the time goes in v4:
time: 379 us; the launch traced here: 372 us
  Pallas kernels  131 us (35%)
  waiting for transfers between devices  128 us (34%)
  starting transfers between devices  49.8 us (13%)
  other arithmetic  22 us (6%)
  local copies, waits for them, and re-layouts  17.5 us (5%)
  between operations  15.2 us (4%)
  matrix products  9.61 us (3%)
    pallas_call x8, Pallas kernels, call(): pl.pallas_call(kernel, grid=(steps,), in_specs=[spec[kind](a.shape) for k...  131 us
    ppermute x15, waiting for transfers between devices, swap_mp(): return lax.ppermute(value, 'mp', [(i, i ^ 1 << bit) for i in range(count)])  81.8 us
    ppermute x37, waiting for transfers between devices, swap_dp(): lax.ppermute(value, axis, [(i, i ^ 1 << place) for i in range(count)])  40.6 us
    ppermute x37, starting transfers between devices, swap_dp(): lax.ppermute(value, axis, [(i, i ^ 1 << place) for i in range(count)])  21.2 us
    ppermute x15, starting transfers between devices, swap_mp(): return lax.ppermute(value, 'mp', [(i, i ^ 1 << bit) for i in range(count)])  20.6 us
    convert_element_type x11, other arithmetic, added(): return (mine.astype(F32) + theirs.astype(F32)).astype(BF)  9.16 us
    ppermute x6, starting transfers between devices, swap_mask(): return lax.ppermute(value, axis, [(i, i ^ mask) for i in range(count)])  7.94 us
  transfers between devices with their start and end apart: 60, of which 29 were waited for; matrix products, arithmetic and copies ran while one was open for 11% of the time, Pallas kernels for 26%

profile of v4, /device:TPU:0, one launch (start us, length us, event | category | flops | bytes accessed | tf_op | source)
XLA Modules:
  0.0 372.4 jit_solution(6141807183946500651)
XLA Ops:
  9.2 4.1 %collective-permute-start.3 = (bf16[1,1,96,384]{3,2,1,0:T(8,128)(2,1)S(1)}, bf16[1,1,96,384]{3,2,1,0:T(8,128)(2,1)S(1)}, u32[]{:S(2)}, u32[]{:S(2)}) collective-permute-start(bf16[1,1,96,384]{3,2,1,0:T(8,128)(2,1)S(1)} %get-tuple-element.360), channel_id=1, source_target_pairs={{0,2},{1,3},{2,0},{3,1},{4,6},{5,7},{6,4},{7,5},{8,10},{9,11},{10,... | collective-permute-start | bytes 221192 | tf_op jit(solution)/shard_map/ppermute | solution.py:591
  15.5 2.7 collective-permute-done.3
  18.2 2.2 collective-permute-done
  36.4 2.6 collective-permute-start.19
  39.1 7.5 %collective-permute-done.2.refs_4_.refs_10_ = bf16[4,1,96,384]{3,2,1,0:T(8,128)(2,1)S(1)} collective-permute-done((bf16[4,1,96,384]{3,2,1,0:T(8,128)(2,1)S(1)}, bf16[4,1,96,384]{3,2,1,0:T(8,128)(2,1)S(1)}, u32[]{:S(2)}, u32[]{:S(2)}) %collective-permute-start.2) | collective-permute-done | bytes 294944 | tf_op jit(solution)/shard_map/ppermute | solution.py:586
  50.6 15.6 %collective-permute-done.19 = bf16[1,2,96,768]{3,2,1,0:T(8,128)(2,1)S(1)} collective-permute-done((bf16[1,2,96,768]{3,2,1,0:T(8,128)(2,1)S(1)}, bf16[1,2,96,768]{3,2,1,0:T(8,128)(2,1)S(1)}, u32[]{:S(2)}, u32[]{:S(2)}) %collective-permute-start.19) | collective-permute-done | bytes 294944 | tf_op jit(solution)/shard_map/ppermute | solution.py:591
  71.9 15.4 %cross_forward.1 = (bf16[336,768]{1,0:T(8,128)(2,1)}, bf16[336,768]{1,0:T(8,128)(2,1)}, f32[192,768]{1,0:T(8,128)}, f32[192,1]{1,0:T(8,128)}, f32[336,768]{1,0:T...) custom-call(s32[1,1]{1,0:T(1,128)} %bitcast.stream, ...), custom_call_target="tpu_custom_call" | custom-call | flops 14948499456 | bytes 12468292 | tf_op jit(solution)/shard_map/cross_forward/pallas_call | solution.py:567
  87.7 19.9 %collective-permute-done.21.refs_0_.refs_4_ = bf16[2,2,96,768]{3,2,1,0:T(8,128)(2,1)S(1)} collective-permute-done((bf16[2,2,96,768]{3,2,1,0:T(8,128)(2,1)S(1)}, bf16[2,2,96,768]{3,2,1,0:T(8,128)(2,1)S(1)}, u32[]{:S(2)}, u32[]{:S(2)}) %collective-permute-start.21) | collective-permute-done | bytes 589856 | tf_op jit(solution)/shard_map/ppermute | solution.py:591
  111.0 8.2 %self_first.1 = (f32[672,768]{1,0:T(8,128)}, bf16[4,672,576]{2,1,0:T(8,128)(2,1)}, bf16[4,672,192]{2,1,0:T(8,128)(2,1)}, bf16[4,2016,112]{2,1,0:T(8,128)(2,1)}) custom-call(s32[1,1]{1,0:T(1,128)} %bitcast.4.length, bf16[336,768]{1,0:T(8,128)(2,1)} %get-tuple-element.198.own, bf16[336,768]{1,0:T(8,128)(2,1)} %collective-permute-done.20.other, ...), custom_call_target="tpu_custom_call" | custom-call | flops 9512681472 | bytes 11390980 | tf_op jit(solution)/shard_map/self_first/pallas_call | solution.py:567
  119.1 3.0 collective-permute-done.26
  128.5 10.0 %self_second.1 = (bf16[672,768]{1,0:T(8,128)(2,1)}, f32[672,768]{1,0:T(8,128)}, f32[672,1]{1,0:T(8,128)}, bf16[4,672,576]{2,1,0:T(8,128)(2,1)}, bf16[4,672,192]{...) custom-call(s32[1,1]{1,0:T(1,128)} %bitcast.4.length, ...), custom_call_target="tpu_custom_call", output_to_operand_aliasing={{3}: (9, {}), {4}: (10, {}), {5}: (11, {})} | custom-call | flops 9512681472 | bytes 20431492 | tf_op jit(solution)/shard_map/self_second/pallas_call | solution.py:567
  138.5 33.6 %feed.1 = (bf16[672,768]{1,0:T(8,128)(2,1)}, bf16[2,2,4,2,2,96,768]{6,5,4,3,2,1,0:T(8,128)(2,1)}, f32[672,768]{1,0:T(8,128)}, f32[1,768]{1,0:T(1,128)}, f32[1,76...) custom-call(s32[1,2]{1,0:T(1,128)} %add_bitcast_fusion.place, bf16[672,768]{1,0:T(8,128)(2,1)} %get-tuple-element.210.rows, ...), custom_call_target="tpu_custom_call" | custom-call | flops 38050725888 | bytes 26126984 | tf_op jit(solution)/shard_map/feed/pallas_call | solution.py:567
  172.2 25.4 %self_backward.1 = (bf16[2,4,2,96,768]{4,3,2,1,0:T(8,128)(2,1)}, bf16[2,4,2,96,768]{4,3,2,1,0:T(8,128)(2,1)}, bf16[336,768]{1,0:T(8,128)(2,1)}, bf16[336,768]{1,0:T(8,128)(2,1)}) custom-call(f32[672,768]{1,0:T(8,128)} %get-tuple-element.215.inward, bf16[336,768]{1,0:T(8,128)(2,1)} %get-tuple-element.198.own, bf16[336,768]{1,0:T(8,128)(2,1)} %collective-permute-done.20.other, ...), custom_call_target="tpu_custom_call" | custom-call | flops 31708938240 | bytes 19501056 | tf_op jit(solution)/shard_map/self_backward/pallas_call | solution.py:567
  203.7 3.0 add_convert_fusion
  207.4 7.5 %collective-permute-done.30.other_up = bf16[336,768]{1,0:T(8,128)(2,1)S(1)} collective-permute-done((bf16[336,768]{1,0:T(8,128)(2,1)}, bf16[336,768]{1,0:T(8,128)(2,1)S(1)}, u32[]{:S(2)}, u32[]{:S(2)}) %collective-permute-start.30) | collective-permute-done | bytes 516128 | tf_op jit(solution)/shard_map/ppermute | solution.py:586
  215.8 23.4 %cross_backward.1 = (bf16[2,2,4,96,768]{4,3,2,1,0:T(8,128)(2,1)}, bf16[2,2,4,96,768]{4,3,2,1,0:T(8,128)(2,1)}, f32[192,768]{1,0:T(8,128)}, bf16[384,768]{1,0:T(8...) custom-call(s32[1,1]{1,0:T(1,128)} %bitcast.stream, bf16[336,768]{1,0:T(8,128)(2,1)} %get-tuple-element.219.own_up, ...), custom_call_target="tpu_custom_call" | custom-call | flops 24914165760 | bytes 19555204 | tf_op jit(solution)/shard_map/cross_backward/pallas_call | solution.py:567
  240.2 3.8 %collective-permute-done.33 = bf16[2,2,4,96,768]{4,3,2,1,0:T(8,128)(2,1)S(1)} collective-permute-done((bf16[2,2,4,96,768]{4,3,2,1,0:T(8,128)(2,1)}, bf16[2,2,4,96,768]{4,3,2,1,0:T(8,128)(2,1)S(1)}, u32[]{:S(2)}, u32[]{:S(2)}) %collective-permute-start.33) | collective-permute-done | bytes 2359328 | tf_op jit(solution)/shard_map/ppermute | solution.py:586
  253.6 9.5 %collective-permute-done.34 = bf16[2,4,96,384]{3,2,1,0:T(8,128)(2,1)} collective-permute-done((bf16[2,4,96,384]{3,2,1,0:T(8,128)(2,1)}, bf16[2,4,96,384]{3,2,1,0:T(8,128)(2,1)}, u32[]{:S(2)}, u32[]{:S(2)}) %collective-permute-start.34) | collective-permute-done | bytes 589856 | tf_op jit(solution)/shard_map/ppermute | solution.py:586
  264.2 2.4 fusion.35
  270.2 3.6 collective-permute-start.40
  274.5 17.7 %collective-permute-done.40 = bf16[1,96,768]{2,1,0:T(8,128)(2,1)S(1)} collective-permute-done((bf16[1,96,768]{2,1,0:T(8,128)(2,1)S(1)}, bf16[1,96,768]{2,1,0:T(8,128)(2,1)S(1)}, u32[]{:S(2)}, u32[]{:S(2)}) %collective-permute-start.40) | collective-permute-done | bytes 147488 | tf_op jit(solution)/shard_map/ppermute | solution.py:591
  292.5 2.1 collective-permute-start.44
  297.7 3.0 collective-permute-done.43
  300.6 6.4 %collective-permute-done.42 = bf16[2,96,768]{2,1,0:T(8,128)(2,1)S(1)} collective-permute-done((bf16[2,96,768]{2,1,0:T(8,128)(2,1)S(1)}, bf16[2,96,768]{2,1,0:T(8,128)(2,1)S(1)}, u32[]{:S(2)}, u32[]{:S(2)}) %collective-permute-start.42) | collective-permute-done | bytes 294944 | tf_op jit(solution)/shard_map/ppermute | solution.py:591
  307.0 6.1 %collective-permute-done.44 = bf16[2,96,768]{2,1,0:T(8,128)(2,1)S(1)} collective-permute-done((bf16[2,96,768]{2,1,0:T(8,128)(2,1)S(1)}, bf16[2,96,768]{2,1,0:T(8,128)(2,1)S(1)}, u32[]{:S(2)}, u32[]{:S(2)}) %collective-permute-start.44) | collective-permute-done | bytes 294944 | tf_op jit(solution)/shard_map/ppermute | solution.py:591
  317.5 2.9 collective-permute-start.45
  320.4 2.6 fusion.norms
  325.3 3.1 collective-permute-done.45.sent
  329.2 2.4 prepare.1
  331.6 2.8 collective-permute-start.52
  337.8 3.3 collective-permute-done.53
  351.4 12.3 %step.1 = (f32[3,3,96,192]{3,2,1,0:T(8,128)}, f32[3,3,96,192]{3,2,1,0:T(8,128)}, f32[3,3,96,192]{3,2,1,0:T(8,128)}, f32[3,3,96,192]{3,2,1,0:T(8,128)}, bf16[3,3,...) custom-call(s32[1,1]{1,0:T(1,128)} %bitcast.stream, ...), custom_call_target="tpu_custom_call" | custom-call | flops 23592960 | bytes 21577736 | tf_op jit(solution)/shard_map/step/pallas_call | solution.py:567
  (301 shorter events, 89.3 us)
Async XLA Ops:
  7.2 131.3 %all-gather.3.cloned.1.call-start = ((), (), s32[]{:S(2)}) async-start(), calls=%async_computation.2 | async-start | bytes 10027008 | tf_op jit(solution)/shard_map/all_gather | solution.py:784
  23.0 292.2 %reduce-scatter.2.cloned.1.call-start = ((), (), s32[]{:S(2)}) async-start(), calls=%async_computation.1 | async-start | bytes 10027008 | tf_op jit(solution)/shard_map/reduce_scatter | solution.py:946
  23.8 12.6 %collective-permute-start.18 = (bf16[1,1,96,768]{3,2,1,0:T(8,128)(2,1)S(1)}, bf16[1,1,96,768]{3,2,1,0:T(8,128)(2,1)S(1)}, u32[]{:S(2)}, u32[]{:S(2)}) collective-permute-start(bf16[1,1,96,768]{3,2,1,0:T(8,128)(2,1)S(1)} %get-tuple-element.342), channel_id=1, source_target_pairs={{0,8},{8,0},{1,9},{9,1},{2,10},{10,2},{3,11},{11,3},{4,12},{12,4},... | collective-permute-start | bytes 442376 | tf_op jit(solution)/shard_map/ppermute | solution.py:586
  33.5 13.1 %collective-permute-start.2 = (bf16[4,1,96,384]{3,2,1,0:T(8,128)(2,1)S(1)}, bf16[4,1,96,384]{3,2,1,0:T(8,128)(2,1)S(1)}, u32[]{:S(2)}, u32[]{:S(2)}) collective-permute-start(bf16[4,1,96,384]{3,2,1,0:T(8,128)(2,1)S(1)} %pad_maximum_fusion.3.refs_0_.refs_6_), channel_id=1, source_target_pairs={{0,16},{16,0},{1,17},{17,1},{2,18},{18,2},{3,19},{19,3},{4,20},{20... | collective-permute-start | bytes 884744 | tf_op jit(solution)/shard_map/ppermute | solution.py:586
  36.4 29.8 %collective-permute-start.19 = (bf16[1,2,96,768]{3,2,1,0:T(8,128)(2,1)S(1)}, bf16[1,2,96,768]{3,2,1,0:T(8,128)(2,1)S(1)}, u32[]{:S(2)}, u32[]{:S(2)}) collective-permute-start(bf16[1,2,96,768]{3,2,1,0:T(8,128)(2,1)S(1)} %pad_maximum_fusion.5), channel_id=1, source_target_pairs={{0,2},{1,3},{2,0},{3,1},{4,6},{5,7},{6,4},{7,5},{8,10},{9,11},{10,... | collective-permute-start | bytes 884744 | tf_op jit(solution)/shard_map/ppermute | solution.py:591
  46.6 19.6 %collective-permute-start.9 = (bf16[4,1,96,384]{3,2,1,0:T(8,128)(2,1)S(1)}, bf16[4,1,96,384]{3,2,1,0:T(8,128)(2,1)}, u32[]{:S(2)}, u32[]{:S(2)}) collective-permute-start(bf16[4,1,96,384]{3,2,1,0:T(8,128)(2,1)S(1)} %collective-permute-done.2.refs_4_.refs_10_), channel_id=1, source_target_pairs={{0,8},{8,0},{1,9},{9,1},{2,10},{10,2},{3,11},{11,3},{4,12},{12,4},... | collective-permute-start | bytes 884744 | tf_op jit(solution)/shard_map/ppermute | solution.py:586
  47.0 19.7 %collective-permute-start.14 = (bf16[4,1,96,384]{3,2,1,0:T(8,128)(2,1)S(1)}, bf16[4,1,96,384]{3,2,1,0:T(8,128)(2,1)}, u32[]{:S(2)}, u32[]{:S(2)}) collective-permute-start(bf16[4,1,96,384]{3,2,1,0:T(8,128)(2,1)S(1)} %pad_maximum_fusion.4.refs_8_.refs_14_), channel_id=1, source_target_pairs={{0,16},{16,0},{1,17},{17,1},{2,18},{18,2},{3,19},{19,3},{4,20},{20... | collective-permute-start | bytes 884744 | tf_op jit(solution)/shard_map/ppermute | solution.py:586
  48.0 19.6 %collective-permute-start.15 = (bf16[4,1,96,384]{3,2,1,0:T(8,128)(2,1)S(1)}, bf16[4,1,96,384]{3,2,1,0:T(8,128)(2,1)}, u32[]{:S(2)}, u32[]{:S(2)}) collective-permute-start(bf16[4,1,96,384]{3,2,1,0:T(8,128)(2,1)S(1)} %collective-permute-done.5.refs_9_.refs_15_), channel_id=1, source_target_pairs={{0,16},{16,0},{1,17},{17,1},{2,18},{18,2},{3,19},{19,3},{4,20},{20... | collective-permute-start | bytes 884744 | tf_op jit(solution)/shard_map/ppermute | solution.py:586
  49.1 19.1 %collective-permute-start.6 = (bf16[4,1,96,384]{3,2,1,0:T(8,128)(2,1)S(1)}, bf16[4,1,96,384]{3,2,1,0:T(8,128)(2,1)}, u32[]{:S(2)}, u32[]{:S(2)}) collective-permute-start(bf16[4,1,96,384]{3,2,1,0:T(8,128)(2,1)S(1)} %pad_maximum_fusion.3.refs_0_.refs_6_), channel_id=1, source_target_pairs={{0,8},{8,0},{1,9},{9,1},{2,10},{10,2},{3,11},{11,3},{4,12},{12,4},... | collective-permute-start | bytes 884744 | tf_op jit(solution)/shard_map/ppermute | solution.py:586
  70.1 37.6 %collective-permute-start.21 = (bf16[2,2,96,768]{3,2,1,0:T(8,128)(2,1)S(1)}, bf16[2,2,96,768]{3,2,1,0:T(8,128)(2,1)S(1)}, u32[]{:S(2)}, u32[]{:S(2)}) collective-permute-start(bf16[2,2,96,768]{3,2,1,0:T(8,128)(2,1)S(1)} %pad_maximum_fusion.1.refs_0_), channel_id=1, source_target_pairs={{0,1},{1,0},{2,3},{3,2},{4,5},{5,4},{6,7},{7,6},{8,9},{9,8},{10,11... | collective-permute-start | bytes 1769480 | tf_op jit(solution)/shard_map/ppermute | solution.py:591
  70.2 37.5 %collective-permute-start.22 = (bf16[2,2,96,768]{3,2,1,0:T(8,128)(2,1)S(1)}, bf16[2,2,96,768]{3,2,1,0:T(8,128)(2,1)}, u32[]{:S(2)}, u32[]{:S(2)}) collective-permute-start(bf16[2,2,96,768]{3,2,1,0:T(8,128)(2,1)S(1)} %pad_maximum_fusion.1.refs_0_), channel_id=1, source_target_pairs={{0,16},{16,0},{1,17},{17,1},{2,18},{18,2},{3,19},{19,3},{4,20},{20... | collective-permute-start | bytes 1769480 | tf_op jit(solution)/shard_map/ppermute | solution.py:586
  87.3 20.4 %collective-permute-start.20 = (bf16[336,768]{1,0:T(8,128)(2,1)}, bf16[336,768]{1,0:T(8,128)(2,1)}, u32[]{:S(2)}, u32[]{:S(2)}) collective-permute-start(bf16[336,768]{1,0:T(8,128)(2,1)} %get-tuple-element.199), channel_id=1, source_target_pairs={{0,8},{8,0},{1,9},{9,1},{2,10},{10,2},{3,11},{11,3},{4,12},{12,4},... | collective-permute-start | bytes 1548296 | tf_op jit(solution)/shard_map/ppermute | solution.py:586
  108.3 15.4 %collective-permute-start.25 = (bf16[2,2,96,768]{3,2,1,0:T(8,128)(2,1)S(1)}, bf16[2,2,96,768]{3,2,1,0:T(8,128)(2,1)S(1)}, u32[]{:S(2)}, u32[]{:S(2)}) collective-permute-start(bf16[2,2,96,768]{3,2,1,0:T(8,128)(2,1)S(1)} %collective-permute-done.21.refs_0_.refs_4_), channel_id=1, source_target_pairs={{0,16},{16,0},{1,17},{17,1},{2,18},{18,2},{3,19},{19,3},{4,20},{20... | collective-permute-start | bytes 1769480 | tf_op jit(solution)/shard_map/ppermute | solution.py:586
  108.4 13.8 %collective-permute-start.26 = (bf16[336,768]{1,0:T(8,128)(2,1)S(1)}, bf16[336,768]{1,0:T(8,128)(2,1)S(1)}, u32[]{:S(2)}, u32[]{:S(2)}) collective-permute-start(bf16[336,768]{1,0:T(8,128)(2,1)S(1)} %bitcast.200), channel_id=1, source_target_pairs={{0,8},{8,0},{1,9},{9,1},{2,10},{10,2},{3,11},{11,3},{4,12},{12,4},... | collective-permute-start | bytes 1548296 | tf_op jit(solution)/shard_map/ppermute | solution.py:586
  200.6 14.4 %collective-permute-start.30 = (bf16[336,768]{1,0:T(8,128)(2,1)}, bf16[336,768]{1,0:T(8,128)(2,1)S(1)}, u32[]{:S(2)}, u32[]{:S(2)}) collective-permute-start(bf16[336,768]{1,0:T(8,128)(2,1)} %get-tuple-element.220), channel_id=1, source_target_pairs={{0,8},{8,0},{1,9},{9,1},{2,10},{10,2},{3,11},{11,3},{4,12},{12,4},... | collective-permute-start | bytes 1548296 | tf_op jit(solution)/shard_map/ppermute | solution.py:586
  206.9 32.3 %collective-permute-start.32 = (bf16[3,2,96,768]{3,2,1,0:T(8,128)(2,1)S(1)}, bf16[3,2,96,768]{3,2,1,0:T(8,128)(2,1)S(1)}, u32[]{:S(2)}, u32[]{:S(2)}) collective-permute-start(bf16[3,2,96,768]{3,2,1,0:T(8,128)(2,1)S(1)} %slice_bitcast_fusion), channel_id=1, source_target_pairs={{0,16},{16,0},{1,17},{17,1},{2,18},{18,2},{3,19},{19,3},{4,20},{20... | collective-permute-start | bytes 2654216 | tf_op jit(solution)/shard_map/ppermute | solution.py:586
  247.4 15.7 %collective-permute-start.34 = (bf16[2,4,96,384]{3,2,1,0:T(8,128)(2,1)}, bf16[2,4,96,384]{3,2,1,0:T(8,128)(2,1)}, u32[]{:S(2)}, u32[]{:S(2)}) collective-permute-start(bf16[2,4,96,384]{3,2,1,0:T(8,128)(2,1)} %fusion.24), channel_id=1, source_target_pairs={{0,8},{8,0},{1,9},{9,1},{2,10},{10,2},{3,11},{11,3},{4,12},{12,4},... | collective-permute-start | bytes 1769480 | tf_op jit(solution)/shard_map/ppermute | solution.py:586
  247.7 16.5 %collective-permute-start.35 = (bf16[2,4,96,384]{3,2,1,0:T(8,128)(2,1)}, bf16[2,4,96,384]{3,2,1,0:T(8,128)(2,1)}, u32[]{:S(2)}, u32[]{:S(2)}) collective-permute-start(bf16[2,4,96,384]{3,2,1,0:T(8,128)(2,1)} %get-tuple-element.244), channel_id=1, source_target_pairs={{0,16},{16,0},{1,17},{17,1},{2,18},{18,2},{3,19},{19,3},{4,20},{20... | collective-permute-start | bytes 1769480 | tf_op jit(solution)/shard_map/ppermute | solution.py:586
  247.7 16.5 %collective-permute-start.36 = (bf16[2,2,96,768]{3,2,1,0:T(8,128)(2,1)}, bf16[2,2,96,768]{3,2,1,0:T(8,128)(2,1)}, u32[]{:S(2)}, u32[]{:S(2)}) collective-permute-start(bf16[2,2,96,768]{3,2,1,0:T(8,128)(2,1)} %fusion.11), channel_id=1, source_target_pairs={{0,1},{1,0},{2,3},{3,2},{4,5},{5,4},{6,7},{7,6},{8,9},{9,8},{10,11... | collective-permute-start | bytes 1769480 | tf_op jit(solution)/shard_map/ppermute | solution.py:591
  251.9 22.6 %collective-permute-start.41 = (bf16[1,2,96,768]{3,2,1,0:T(8,128)(2,1)}, bf16[1,2,96,768]{3,2,1,0:T(8,128)(2,1)}, u32[]{:S(2)}, u32[]{:S(2)}) collective-permute-start(bf16[1,2,96,768]{3,2,1,0:T(8,128)(2,1)} %slice_bitcast_fusion.5), channel_id=1, source_target_pairs={{0,16},{16,0},{1,17},{17,1},{2,18},{18,2},{3,19},{19,3},{4,20},{20... | collective-permute-start | bytes 884744 | tf_op jit(solution)/shard_map/ppermute | solution.py:586
  266.6 25.5 %collective-permute-start.38 = (bf16[4,96,384]{2,1,0:T(8,128)(2,1)}, bf16[4,96,384]{2,1,0:T(8,128)(2,1)S(1)}, u32[]{:S(2)}, u32[]{:S(2)}) collective-permute-start(bf16[4,96,384]{2,1,0:T(8,128)(2,1)} %get-tuple-element.256), channel_id=1, source_target_pairs={{0,16},{16,0},{1,17},{17,1},{2,18},{18,2},{3,19},{19,3},{4,20},{20... | collective-permute-start | bytes 884744 | tf_op jit(solution)/shard_map/ppermute | solution.py:586
  267.2 24.9 %collective-permute-start.39 = (bf16[4,96,384]{2,1,0:T(8,128)(2,1)}, bf16[4,96,384]{2,1,0:T(8,128)(2,1)S(1)}, u32[]{:S(2)}, u32[]{:S(2)}) collective-permute-start(bf16[4,96,384]{2,1,0:T(8,128)(2,1)} %get-tuple-element.257), channel_id=1, source_target_pairs={{0,8},{8,0},{1,9},{9,1},{2,10},{10,2},{3,11},{11,3},{4,12},{12,4},... | collective-permute-start | bytes 884744 | tf_op jit(solution)/shard_map/ppermute | solution.py:586
  270.2 21.9 %collective-permute-start.40 = (bf16[1,96,768]{2,1,0:T(8,128)(2,1)S(1)}, bf16[1,96,768]{2,1,0:T(8,128)(2,1)S(1)}, u32[]{:S(2)}, u32[]{:S(2)}) collective-permute-start(bf16[1,96,768]{2,1,0:T(8,128)(2,1)S(1)} %get-tuple-element.348), channel_id=1, source_target_pairs={{0,2},{1,3},{2,0},{3,1},{4,6},{5,7},{6,4},{7,5},{8,10},{9,11},{10,... | collective-permute-start | bytes 442376 | tf_op jit(solution)/shard_map/ppermute | solution.py:591
  274.4 26.2 %collective-permute-start.43 = (bf16[1,96,768]{2,1,0:T(8,128)(2,1)S(1)}, bf16[1,96,768]{2,1,0:T(8,128)(2,1)S(1)}, u32[]{:S(2)}, u32[]{:S(2)}) collective-permute-start(bf16[1,96,768]{2,1,0:T(8,128)(2,1)S(1)} %get-tuple-element.265), channel_id=1, source_target_pairs={{0,2},{1,3},{2,0},{3,1},{4,6},{5,7},{6,4},{7,5},{8,10},{9,11},{10,... | collective-permute-start | bytes 442376 | tf_op jit(solution)/shard_map/ppermute | solution.py:591
  292.3 14.7 %collective-permute-start.42 = (bf16[2,96,768]{2,1,0:T(8,128)(2,1)S(1)}, bf16[2,96,768]{2,1,0:T(8,128)(2,1)S(1)}, u32[]{:S(2)}, u32[]{:S(2)}) collective-permute-start(bf16[2,96,768]{2,1,0:T(8,128)(2,1)S(1)} %get-tuple-element.336), channel_id=1, source_target_pairs={{0,1},{1,0},{2,3},{3,2},{4,5},{5,4},{6,7},{7,6},{8,9},{9,8},{10,11... | collective-permute-start | bytes 884744 | tf_op jit(solution)/shard_map/ppermute | solution.py:591
  292.5 20.7 %collective-permute-start.44 = (bf16[2,96,768]{2,1,0:T(8,128)(2,1)S(1)}, bf16[2,96,768]{2,1,0:T(8,128)(2,1)S(1)}, u32[]{:S(2)}, u32[]{:S(2)}) collective-permute-start(bf16[2,96,768]{2,1,0:T(8,128)(2,1)S(1)} %bitcast.202), channel_id=1, source_target_pairs={{0,1},{1,0},{2,3},{3,2},{4,5},{5,4},{6,7},{7,6},{8,9},{9,8},{10,11... | collective-permute-start | bytes 884744 | tf_op jit(solution)/shard_map/ppermute | solution.py:591
  296.4 39.7 %collective-permute-start.37 = (bf16[336,768]{1,0:T(8,128)(2,1)}, bf16[336,768]{1,0:T(8,128)(2,1)}, u32[]{:S(2)}, u32[]{:S(2)}) collective-permute-start(bf16[336,768]{1,0:T(8,128)(2,1)} %slice.321), channel_id=1, source_target_pairs={{0,8},{8,0},{1,9},{9,1},{2,10},{10,2},{3,11},{11,3},{4,12},{12,4},... | collective-permute-start | bytes 1548296 | tf_op jit(solution)/shard_map/ppermute | solution.py:586
  313.3 12.0 %collective-permute-start.48 = (bf16[1,96,768]{2,1,0:T(8,128)(2,1)S(1)}, bf16[1,96,768]{2,1,0:T(8,128)(2,1)S(1)}, u32[]{:S(2)}, u32[]{:S(2)}) collective-permute-start(bf16[1,96,768]{2,1,0:T(8,128)(2,1)S(1)} %get-tuple-element.343), channel_id=1, source_target_pairs={{0,2},{1,3},{2,0},{3,1},{4,6},{5,7},{6,4},{7,5},{8,10},{9,11},{10,... | collective-permute-start | bytes 442376 | tf_op jit(solution)/shard_map/ppermute | solution.py:591
  313.5 11.8 %collective-permute-start.46 = (bf16[96,768]{1,0:T(8,128)(2,1)S(1)}, bf16[96,768]{1,0:T(8,128)(2,1)S(1)}, u32[]{:S(2)}, u32[]{:S(2)}) collective-permute-start(bf16[96,768]{1,0:T(8,128)(2,1)S(1)} %slice_bitcast_fusion.7), channel_id=1, source_target_pairs={{0,8},{8,0},{1,9},{9,1},{2,10},{10,2},{3,11},{11,3},{4,12},{12,4},... | collective-permute-start | bytes 442376 | tf_op jit(solution)/shard_map/ppermute | solution.py:586
  316.2 12.2 %collective-permute-start.47 = (bf16[2,96,768]{2,1,0:T(8,128)(2,1)S(1)}, bf16[2,96,768]{2,1,0:T(8,128)(2,1)S(1)}, u32[]{:S(2)}, u32[]{:S(2)}) collective-permute-start(bf16[2,96,768]{2,1,0:T(8,128)(2,1)S(1)} %slice_bitcast_fusion.3), channel_id=1, source_target_pairs={{0,8},{8,0},{1,9},{9,1},{2,10},{10,2},{3,11},{11,3},{4,12},{12,4},... | collective-permute-start | bytes 884744 | tf_op jit(solution)/shard_map/ppermute | solution.py:586
  317.5 10.9 %collective-permute-start.45 = (bf16[1,96,768]{2,1,0:T(8,128)(2,1)}, bf16[1,96,768]{2,1,0:T(8,128)(2,1)S(1)}, u32[]{:S(2)}, u32[]{:S(2)}) collective-permute-start(bf16[1,96,768]{2,1,0:T(8,128)(2,1)} %get-tuple-element.345), channel_id=1, source_target_pairs={{0,2},{1,3},{2,0},{3,1},{4,6},{5,7},{6,4},{7,5},{8,10},{9,11},{10,... | collective-permute-start | bytes 442376 | tf_op jit(solution)/shard_map/ppermute | solution.py:591
  346.3 17.4 %collective-permute-start.50 = (bf16[2,96,768]{2,1,0:T(8,128)(2,1)S(1)}, bf16[2,96,768]{2,1,0:T(8,128)(2,1)S(1)}, u32[]{:S(2)}, u32[]{:S(2)}) collective-permute-start(bf16[2,96,768]{2,1,0:T(8,128)(2,1)S(1)} %pad_maximum_fusion.6), channel_id=1, source_target_pairs={{0,1},{1,0},{2,3},{3,2},{4,5},{5,4},{6,7},{7,6},{8,9},{9,8},{10,11... | collective-permute-start | bytes 884744 | tf_op jit(solution)/shard_map/ppermute | solution.py:591
  (74 other events, 572.9 us)
Sparse Core Ops, SparseCore 0:
  23.2 107.2 all-gather.2
  172.3 130.1 reduce-scatter.1

commit v5 on v4

--- a/solution.py
+++ b/solution.py
@@ -353,35 +353,57 @@
         self_shift[...] = shift_term
 
 
-def self_backward_kernel(width, blocks, inward, own, other, qkv, ctx, probs, *refs):
-    pieces, near, far, refs = refs[:8], refs[8], refs[9], refs[10:]
-    down_own, down_other, weight, acc, branch, turned, branch_turned = refs
+def self_other_kernel(width, blocks, inward, qkv, probs, *refs):
+    pieces, (triple_ref, down, weight, acc, branch) = refs[:8], refs[8:]
     load_halves(pieces, weight)
     step = pl.program_id(0)
 
     @pl.when(step == 0)
     def _():
         acc[...] = inward[...]
-        gradient = inward[...].astype(BF)
-        branch[...] = gradient
-        branch_turned[...] = gradient.T
-        turned[...] = stack_rows([own[...], other[...]]).T
+        branch[...] = inward[...].astype(BF)
 
     full = weight[...]
     in_part, out_part = full[:, : 3 * width], full[:, 3 * width :]
     grad_context = dot_nn(branch[...], out_part).astype(BF)
     grads_of = attend_back(*thirds(qkv[0], width), probs[0], grad_context, blocks)
     grad_triple = jnp.concatenate(grads_of, axis=1)
-    in_grad = dot_nn(turned[...], grad_triple).astype(BF)
+    triple_ref[0] = grad_triple
+    acc[...] += dot_nt(grad_triple, in_part)
+
+    @pl.when(step == pl.num_programs(0) - 1)
+    def _():
+        down[...] = partner_order(acc[...].astype(BF))
+
+
+def self_own_kernel(width, blocks, inward, own, other, qkv, ctx, probs, other_triple, *refs):
+    pieces, near, far, refs = refs[:8], refs[8], refs[9], refs[10:]
+    down, weight, acc, branch, turned, branch_turned = refs
+    load_halves(pieces, weight)
+    step = pl.program_id(0)
+
+    @pl.when(step == 0)
+    def _():
+        slot = own.shape[0]
+        acc[...] = inward[:slot, :]
+        gradient = inward[...].astype(BF)
+        branch[...] = gradient[:slot]
+        branch_turned[...] = gradient.T
+        turned[...] = stack_rows([own[...], other[...]]).T
+
+    full = weight[...]
+    in_part, out_part = full[:, : 3 * width], full[:, 3 * width :]
+    grad_context = dot_nn(branch[...], out_part).astype(BF)
+    grads_of = attend_back(*thirds(qkv[0], width), probs[0], grad_context, blocks)
+    grad_triple = jnp.concatenate(grads_of, axis=1)
+    in_grad = dot_nn(turned[...], stack_rows([grad_triple, other_triple[0]])).astype(BF)
     out_grad = dot_nn(branch_turned[...], ctx[0]).astype(BF)
     store_pair(jnp.concatenate([in_grad, out_grad], axis=1), near, far, True)
     acc[...] += dot_nt(grad_triple, in_part)
 
     @pl.when(step == pl.num_programs(0) - 1)
     def _():
-        slot = own.shape[0]
-        down_own[...] = acc[:slot].astype(BF)
-        down_other[...] = partner_order(acc[slot:].astype(BF))
+        down[...] = acc[...].astype(BF)
 
 
 def cross_backward_kernel(
@@ -559,6 +581,9 @@
             (s[0], 1) + tuple(s[2:]), lambda m: (0, m, 0, 0, 0)
         ),
         "upper": lambda s: part_of(s, lambda m: m + s[0] // 2),
+        "own": lambda s: pl.BlockSpec((1, s[1] // 2, s[2]), lambda m: (m, 0, 0)),
+        "other": lambda s: pl.BlockSpec((1, s[1] // 2, s[2]), lambda m: (m, 1, 0)),
+        "other_rows": lambda s: pl.BlockSpec((s[0] // 2, s[1]), lambda m: (1, 0)),
         "kept": lambda s: pl.BlockSpec(memory_space=pl.ANY),
         "scalar": lambda s: pl.BlockSpec(memory_space=pltpu.SMEM),
     }
@@ -958,20 +983,28 @@
     def send_mp(parts, bit):
         return [(keep, swap_mp(far, bit)) for keep, far in parts]
 
-    found = call(
-        functools.partial(self_backward_kernel, width, 2 * blocks),
+    other_triple, other_up = call(
+        functools.partial(self_other_kernel, width, blocks),
+        n_mp,
+        [("other_rows", inward), ("other", self_qkv), ("other", self_probs)] + self_pieces,
+        [("step", (n_mp, slot, 3 * width), BF), ("whole", (slot, dim), BF)],
+        [((dim, 4 * width), BF), ((slot, dim), F32), ((slot, dim), BF)],
+        "self_other",
+        2 * total * dim * 4 * width * n_mp,
+    )
+    other_up = swap_dp(other_up, 1)
+    self_near, self_far, own_up = call(
+        functools.partial(self_own_kernel, width, blocks),
         n_mp,
         [("whole", a) for a in (inward, own_one, other_one)]
-        + [("step", a) for a in (self_qkv, self_ctx, self_probs)]
+        + [("own", self_qkv), ("step", self_ctx), ("own", self_probs), ("step", other_triple)]
         + self_pieces,
-        [("groups", (2, n_mp, 2, eighth, 4 * width), BF)] * 2 + [("whole", (slot, dim), BF)] * 2,
-        [((dim, 4 * width), BF), ((total, dim), F32), ((total, dim), BF)] + [((dim, total), BF)] * 2,
-        "self_backward",
-        20 * total * dim * 4 * width * n_mp,
+        [("groups", (2, n_mp, 2, eighth, 4 * width), BF)] * 2 + [("whole", (slot, dim), BF)],
+        [((dim, 4 * width), BF), ((slot, dim), F32), ((slot, dim), BF)] + [((dim, total), BF)] * 2,
+        "self_own",
+        2 * total * dim * 4 * width * n_mp,
     )
-    self_near, self_far = found[:2]
-    own_up, other_up = found[2:]
-    other_up = swap_dp(other_up, 1)
+    self_near, self_far, own_up, other_up = together(self_near, self_far, own_up, other_up)
     self_far = swap_dp(self_far, 0)
     self_sums = [scatter_extra(added(self_near[hi], self_far[hi])) for hi in (0, 1)]
     own_up = after(own_up, self_sums)
@@ -1006,7 +1039,7 @@
             ((dim, both), BF),
         ],
         "cross_backward",
-        20 * both * dim * 4 * width * n_mp,
+        6 * both * dim * 4 * width * n_mp,
     )
     near, far, lang_back, image_term, cross_gain, cross_shift = found
 
@@ -1019,8 +1052,8 @@
 
     self_kept = self_sums[0]
     self_far = swap_dp(self_sums[1][1:], 2)
-    late = together(near, far, lang_back, image_term, self_far)
-    near, far, lang_back, image_term, self_far = late
+    late = together(near, far, lang_back, image_term, self_far, cross_gain, cross_shift)
+    near, far, lang_back, image_term, self_far, cross_gain, cross_shift = late
     far = swap_dp(far, 0)
     self_sent = total_of(self_kept[2:], self_far[1:])
     left, right = (slice(c, c + half) for c in (0, half))
@@ -1036,39 +1069,6 @@
     first, second, self_sent = together(first, second, self_sent)
     self_one = total_of(self_kept[1], self_far[0], self_sent[1])
 
-    first_far, second_far = swap_dp(first[1], 2), swap_dp(second[1], 1)
-    self_ones = [swap_mp(self_one[1:], 1)]
-    self_near = swap_dp(self_sums[1][:1], 2)
-    late = together(first[0], second[0], first_far, second_far, self_ones, self_near, image_term)
-    first, second, first_far, second_far, self_ones, self_near, image_term = late
-    home = jnp.concatenate([added(first, first_far), added(second, second_far)], axis=-1)
-    home = scatter_extra(home)
-    self_low = total_of(self_kept[0], self_near[0], self_sent[0])
-
-    kept, sent = parts(home)
-    sent = swap_mp(sent, 0)
-    self_ones = [swap_mp(after(self_one[:1], home), 1)] + self_ones
-    image_kept, image_sent = parts(image_term.reshape(n_mp, part, dim))
-    image_sent = swap_mp(image_sent, 0)
-    late = together(kept, sent, self_low, self_ones, image_kept, image_sent)
-    kept, sent, self_low, self_ones, image_kept, image_sent = late
-    self_low = added(self_low, jnp.concatenate(self_ones, axis=0))
-    home, image_term = added(kept, sent), added(image_kept, image_sent)
-
-    kept, sent = parts(home)
-    sent, theirs, feed_theirs = swap_mp(sent, 1), swap_dp(self_low[1], 1), swap_dp(feed_sum[1], 1)
-    image_kept, image_sent = parts(image_term)
-    image_sent = swap_mp(image_sent, 1)
-    late = together(kept, sent, self_low, theirs, feed_theirs, image_kept, image_sent)
-    kept, sent, self_low, theirs, feed_theirs, image_kept, image_sent = late
-    image_term = added(image_kept, image_sent)
-
-    final = from_order(rows_three).astype(BF)
-    final_other = after(swap_dp(final[slot:], 1), kept)
-    language_out = out_of_blocks(jnp.where(is_vis, final_other, final[:slot]), lang_rows)
-    vision_out = out_of_blocks(jnp.where(is_vis, final[:slot], final_other), vis_rows)
-
-    language_grad = out_of_blocks(lang_back, lang_rows).reshape(language.shape)
     here = (jnp.arange(2, dtype=jnp.int32) == stream).astype(F32)[:, None, None]
     norm_partial = jnp.concatenate(
         [
@@ -1080,6 +1080,41 @@
     )
     norm_partial = from_order(norm_partial.reshape(-1, dim), HIGHEST)
 
+    final = from_order(rows_three).astype(BF)
+
+    first_far, second_far = swap_dp(first[1], 2), swap_dp(second[1], 1)
+    self_ones = [swap_mp(self_one[1:], 1)]
+    self_near = swap_dp(self_sums[1][:1], 2)
+    extras = image_term, norm_partial, final
+    late = together(first[0], second[0], first_far, second_far, self_ones, self_near, extras)
+    first, second, first_far, second_far, self_ones, self_near, extras = late
+    image_term, norm_partial, final = extras
+    home = jnp.concatenate([added(first, first_far), added(second, second_far)], axis=-1)
+    home = scatter_extra(home)
+    self_low = total_of(self_kept[0], self_near[0], self_sent[0])
+
+    kept, sent = parts(home)
+    sent = swap_mp(sent, 0)
+    self_ones = [swap_mp(after(self_one[:1], home), 1)] + self_ones
+    final_other = swap_dp(final[slot:], 1)
+    late = together(kept, sent, self_low, self_ones, image_term, final_other)
+    kept, sent, self_low, self_ones, image_term, final_other = late
+    self_low = added(self_low, jnp.concatenate(self_ones, axis=0))
+    home = added(kept, sent)
+
+    kept, sent = parts(home)
+    sent, theirs, feed_theirs = swap_mp(sent, 1), swap_dp(self_low[1], 1), swap_dp(feed_sum[1], 1)
+    image_kept, image_sent = parts(image_term.reshape(n_mp, part, dim))
+    image_sent = swap_mp(image_sent, 0)
+    late = together(kept, sent, self_low, theirs, feed_theirs, image_kept, image_sent)
+    kept, sent, self_low, theirs, feed_theirs, image_kept, image_sent = late
+    image_term = added(image_kept, image_sent)
+
+    final_other = after(final_other, kept)
+    language_out = out_of_blocks(jnp.where(is_vis, final_other, final[:slot]), lang_rows)
+    vision_out = out_of_blocks(jnp.where(is_vis, final[:slot], final_other), vis_rows)
+
+    language_grad = out_of_blocks(lang_back, lang_rows).reshape(language.shape)
     totals = [kept, sent, self_low, theirs]
     sums = call(
         prepare_kernel,
@@ -1092,6 +1127,9 @@
     )[0]
     sums, their_sums = sum_up(sums)
     image_term = after(image_term, kept)
+    for bit in range(1, n_bits):
+        kept_part, sent_part = parts(image_term)
+        image_term = added(kept_part, swap_mp(sent_part, bit))
     for bit in reversed(mp_bits()):
         image_term = jnp.concatenate([image_term, swap_mp(image_term, bit)], axis=0)
     for b in range(n_bits):

time: 379 us -> 367 us (0.968)
  waiting for transfers between devices: 128 us -> 113 us
  Pallas kernels: 131 us -> 136 us
    ppermute x15, waiting for transfers between devices: 81.8 us -> 69.1 us  [swap_mp(): return lax.ppermute(value, 'mp', [(i, i ^ 1 << bit) for i in range(count)])]
    pallas_call x8 -> x9, Pallas kernels: 131 us -> 136 us  [call(): pl.pallas_call(kernel, grid=(steps,), in_specs=[spec[kind](a.shape) for k...]
  transfers between devices with their start and end apart: 60 -> 60, of which waited for: 29 -> 28; matrix products, arithmetic and copies ran while one was open for 11% -> 10% of each run, Pallas kernels for 26% -> 28%
where the time goes in v5:
time: 367 us; the launch traced here: 361 us
  Pallas kernels  136 us (37%)
  waiting for transfers between devices  113 us (31%)
  starting transfers between devices  50.3 us (14%)
  other arithmetic  21.1 us (6%)
  local copies, waits for them, and re-layouts  15.8 us (4%)
  between operations  15.5 us (4%)
  matrix products  9.64 us (3%)
    pallas_call x9, Pallas kernels, call(): pl.pallas_call(kernel, grid=(steps,), in_specs=[spec[kind](a.shape) for k...  136 us
    ppermute x15, waiting for transfers between devices, swap_mp(): return lax.ppermute(value, 'mp', [(i, i ^ 1 << bit) for i in range(count)])  69.1 us
    ppermute x37, waiting for transfers between devices, swap_dp(): lax.ppermute(value, axis, [(i, i ^ 1 << place) for i in range(count)])  37 us
    ppermute x37, starting transfers between devices, swap_dp(): lax.ppermute(value, axis, [(i, i ^ 1 << place) for i in range(count)])  23.4 us
    ppermute x15, starting transfers between devices, swap_mp(): return lax.ppermute(value, 'mp', [(i, i ^ 1 << bit) for i in range(count)])  18.9 us
    convert_element_type x11, other arithmetic, added(): return (mine.astype(F32) + theirs.astype(F32)).astype(BF)  8.8 us
    ppermute x6, starting transfers between devices, swap_mask(): return lax.ppermute(value, axis, [(i, i ^ mask) for i in range(count)])  7.94 us
  transfers between devices with their start and end apart: 60, of which 28 were waited for; matrix products, arithmetic and copies ran while one was open for 10% of the time, Pallas kernels for 28%

profile of v5, /device:TPU:0, one launch (start us, length us, event | category | flops | bytes accessed | tf_op | source)
XLA Modules:
  0.0 361.3 jit_solution(10566871408673083994)
XLA Ops:
  9.2 4.1 %collective-permute-start.3 = (bf16[1,1,96,384]{3,2,1,0:T(8,128)(2,1)S(1)}, bf16[1,1,96,384]{3,2,1,0:T(8,128)(2,1)S(1)}, u32[]{:S(2)}, u32[]{:S(2)}) collective-permute-start(bf16[1,1,96,384]{3,2,1,0:T(8,128)(2,1)S(1)} %get-tuple-element.376), channel_id=1, source_target_pairs={{0,2},{1,3},{2,0},{3,1},{4,6},{5,7},{6,4},{7,5},{8,10},{9,11},{10,... | collective-permute-start | bytes 221192 | tf_op jit(solution)/shard_map/ppermute | solution.py:616
  15.5 2.7 collective-permute-done.3
  18.2 2.2 collective-permute-done
  36.4 2.6 collective-permute-start.19
  39.1 7.5 %collective-permute-done.2.refs_4_.refs_10_ = bf16[4,1,96,384]{3,2,1,0:T(8,128)(2,1)S(1)} collective-permute-done((bf16[4,1,96,384]{3,2,1,0:T(8,128)(2,1)S(1)}, bf16[4,1,96,384]{3,2,1,0:T(8,128)(2,1)S(1)}, u32[]{:S(2)}, u32[]{:S(2)}) %collective-permute-start.2) | collective-permute-done | bytes 294944 | tf_op jit(solution)/shard_map/ppermute | solution.py:611
  50.6 15.6 %collective-permute-done.19 = bf16[1,2,96,768]{3,2,1,0:T(8,128)(2,1)S(1)} collective-permute-done((bf16[1,2,96,768]{3,2,1,0:T(8,128)(2,1)S(1)}, bf16[1,2,96,768]{3,2,1,0:T(8,128)(2,1)S(1)}, u32[]{:S(2)}, u32[]{:S(2)}) %collective-permute-start.19) | collective-permute-done | bytes 294944 | tf_op jit(solution)/shard_map/ppermute | solution.py:616
  72.0 15.5 %cross_forward.1 = (bf16[336,768]{1,0:T(8,128)(2,1)}, bf16[336,768]{1,0:T(8,128)(2,1)}, f32[192,768]{1,0:T(8,128)}, f32[192,1]{1,0:T(8,128)}, f32[336,768]{1,0:T...) custom-call(s32[1,1]{1,0:T(1,128)} %bitcast.stream, ...), custom_call_target="tpu_custom_call" | custom-call | flops 14948499456 | bytes 12468292 | tf_op jit(solution)/shard_map/cross_forward/pallas_call | solution.py:592
  88.6 18.9 %collective-permute-done.21.refs_0_.refs_4_ = bf16[2,2,96,768]{3,2,1,0:T(8,128)(2,1)S(1)} collective-permute-done((bf16[2,2,96,768]{3,2,1,0:T(8,128)(2,1)S(1)}, bf16[2,2,96,768]{3,2,1,0:T(8,128)(2,1)S(1)}, u32[]{:S(2)}, u32[]{:S(2)}) %collective-permute-start.21) | collective-permute-done | bytes 589856 | tf_op jit(solution)/shard_map/ppermute | solution.py:616
  111.2 8.2 %self_first.1 = (f32[672,768]{1,0:T(8,128)}, bf16[4,672,576]{2,1,0:T(8,128)(2,1)}, bf16[4,672,192]{2,1,0:T(8,128)(2,1)}, bf16[4,2016,112]{2,1,0:T(8,128)(2,1)}) custom-call(s32[1,1]{1,0:T(1,128)} %bitcast.4.length, bf16[336,768]{1,0:T(8,128)(2,1)} %get-tuple-element.207.own, bf16[336,768]{1,0:T(8,128)(2,1)} %collective-permute-done.20.other, ...), custom_call_target="tpu_custom_call" | custom-call | flops 9512681472 | bytes 11390980 | tf_op jit(solution)/shard_map/self_first/pallas_call | solution.py:592
  119.5 2.5 collective-permute-done.26
  125.3 2.1 fusion.7.cot
  128.4 10.0 %self_second.1 = (bf16[672,768]{1,0:T(8,128)(2,1)}, f32[672,768]{1,0:T(8,128)}, f32[672,1]{1,0:T(8,128)}, bf16[4,672,576]{2,1,0:T(8,128)(2,1)}, bf16[4,672,192]{...) custom-call(s32[1,1]{1,0:T(1,128)} %bitcast.4.length, ...), custom_call_target="tpu_custom_call", output_to_operand_aliasing={{3}: (9, {}), {4}: (10, {}), {5}: (11, {})} | custom-call | flops 9512681472 | bytes 20431492 | tf_op jit(solution)/shard_map/self_second/pallas_call | solution.py:592
  138.4 33.5 %feed.1 = (bf16[672,768]{1,0:T(8,128)(2,1)}, bf16[2,2,4,2,2,96,768]{6,5,4,3,2,1,0:T(8,128)(2,1)}, f32[672,768]{1,0:T(8,128)}, f32[1,768]{1,0:T(1,128)}, f32[1,76...) custom-call(s32[1,2]{1,0:T(1,128)} %add_bitcast_fusion.place, bf16[672,768]{1,0:T(8,128)(2,1)} %get-tuple-element.219.rows, ...), custom_call_target="tpu_custom_call" | custom-call | flops 38050725888 | bytes 26126984 | tf_op jit(solution)/shard_map/feed/pallas_call | solution.py:592
  171.9 11.6 %self_other.1 = (bf16[4,336,576]{2,1,0:T(8,128)(2,1)}, bf16[336,768]{1,0:T(8,128)(2,1)}) custom-call(f32[672,768]{1,0:T(8,128)} %get-tuple-element.224.inward, bf16[4,672,576]{2,1,0:T(8,128)(2,1)} %get-tuple-element.225.qkv, bf16[4,2016,112]{2,1,0:T(8,128)(2,1)} %get-tuple-element.227.probs, bf16[2,2,96,768]{3,2,1,0:T(8,128)(2,1)} %copy-done, ...), custom_call_target="tpu_custom_call" | custom-call | flops 3170893824 | bytes 13750272 | tf_op jit(solution)/shard_map/self_other/pallas_call | solution.py:592
  183.8 18.9 %self_own.1 = (bf16[2,4,2,96,768]{4,3,2,1,0:T(8,128)(2,1)}, bf16[2,4,2,96,768]{4,3,2,1,0:T(8,128)(2,1)}, bf16[336,768]{1,0:T(8,128)(2,1)}) custom-call(f32[672,768]{1,0:T(8,128)} %get-tuple-element.224.inward, bf16[336,768]{1,0:T(8,128)(2,1)} %get-tuple-element.207.own, bf16[336,768]{1,0:T(8,128)(2,1)} %collective-permute-done.20.other, ...), custom_call_target="tpu_custom_call" | custom-call | flops 3170893824 | bytes 20533248 | tf_op jit(solution)/shard_map/self_own/pallas_call | solution.py:592
  205.1 3.2 collective-permute-done.31
  208.3 2.3 add_convert_fusion
  212.6 23.4 %cross_backward.1 = (bf16[2,2,4,96,768]{4,3,2,1,0:T(8,128)(2,1)}, bf16[2,2,4,96,768]{4,3,2,1,0:T(8,128)(2,1)}, f32[192,768]{1,0:T(8,128)}, bf16[384,768]{1,0:T(8...) custom-call(s32[1,1]{1,0:T(1,128)} %bitcast.stream, bf16[336,768]{1,0:T(8,128)(2,1)} %get-tuple-element.233.own_up, ...), custom_call_target="tpu_custom_call" | custom-call | flops 7474249728 | bytes 19555204 | tf_op jit(solution)/shard_map/cross_backward/pallas_call | solution.py:592
  237.2 3.6 %collective-permute-done.33 = bf16[2,2,4,96,768]{4,3,2,1,0:T(8,128)(2,1)S(1)} collective-permute-done((bf16[2,2,4,96,768]{4,3,2,1,0:T(8,128)(2,1)}, bf16[2,2,4,96,768]{4,3,2,1,0:T(8,128)(2,1)S(1)}, u32[]{:S(2)}, u32[]{:S(2)}) %collective-permute-start.33) | collective-permute-done | bytes 2359328 | tf_op jit(solution)/shard_map/ppermute | solution.py:611
  251.6 2.6 fusion.1.norms
  254.2 5.7 %collective-permute-done.34 = bf16[2,4,96,384]{3,2,1,0:T(8,128)(2,1)} collective-permute-done((bf16[2,4,96,384]{3,2,1,0:T(8,128)(2,1)}, bf16[2,4,96,384]{3,2,1,0:T(8,128)(2,1)}, u32[]{:S(2)}, u32[]{:S(2)}) %collective-permute-start.34) | collective-permute-done | bytes 589856 | tf_op jit(solution)/shard_map/ppermute | solution.py:611
  259.9 3.2 collective-permute-done.35
  270.5 5.1 %collective-permute-done.40 = bf16[1,2,96,768]{3,2,1,0:T(8,128)(2,1)} collective-permute-done((bf16[1,2,96,768]{3,2,1,0:T(8,128)(2,1)S(1)}, bf16[1,2,96,768]{3,2,1,0:T(8,128)(2,1)}, u32[]{:S(2)}, u32[]{:S(2)}) %collective-permute-start.40) | collective-permute-done | bytes 294944 | tf_op jit(solution)/shard_map/ppermute | solution.py:611
  275.7 9.7 %collective-permute-done.39 = bf16[1,96,768]{2,1,0:T(8,128)(2,1)S(1)} collective-permute-done((bf16[1,96,768]{2,1,0:T(8,128)(2,1)S(1)}, bf16[1,96,768]{2,1,0:T(8,128)(2,1)S(1)}, u32[]{:S(2)}, u32[]{:S(2)}) %collective-permute-start.39) | collective-permute-done | bytes 147488 | tf_op jit(solution)/shard_map/ppermute | solution.py:616
  290.4 4.9 %collective-permute-done.42 = bf16[1,96,768]{2,1,0:T(8,128)(2,1)S(1)} collective-permute-done((bf16[1,96,768]{2,1,0:T(8,128)(2,1)S(1)}, bf16[1,96,768]{2,1,0:T(8,128)(2,1)S(1)}, u32[]{:S(2)}, u32[]{:S(2)}) %collective-permute-start.42) | collective-permute-done | bytes 147488 | tf_op jit(solution)/shard_map/ppermute | solution.py:616
  295.3 3.1 collective-permute-done.41
  305.4 7.3 %collective-permute-done.44.sent = bf16[1,96,768]{2,1,0:T(8,128)(2,1)S(1)} collective-permute-done((bf16[1,96,768]{2,1,0:T(8,128)(2,1)S(1)}, bf16[1,96,768]{2,1,0:T(8,128)(2,1)S(1)}, u32[]{:S(2)}, u32[]{:S(2)}) %collective-permute-start.44) | collective-permute-done | bytes 147488 | tf_op jit(solution)/shard_map/ppermute | solution.py:616
  316.1 2.5 prepare.1
  320.6 2.3 collective-permute-start.53
  324.6 4.9 %collective-permute-done.52 = f32[11,768]{1,0:T(8,128)S(1)} collective-permute-done((f32[11,768]{1,0:T(8,128)}, f32[11,768]{1,0:T(8,128)S(1)}, u32[]{:S(2)}, u32[]{:S(2)}) %collective-permute-start.52) | collective-permute-done | bytes 33824 | tf_op jit(solution)/shard_map/ppermute | solution.py:631
  335.6 2.1 collective-permute-done.56
  340.1 12.3 %step.1 = (f32[3,3,96,192]{3,2,1,0:T(8,128)}, f32[3,3,96,192]{3,2,1,0:T(8,128)}, f32[3,3,96,192]{3,2,1,0:T(8,128)}, f32[3,3,96,192]{3,2,1,0:T(8,128)}, bf16[3,3,...) custom-call(s32[1,1]{1,0:T(1,128)} %bitcast.stream, ...), custom_call_target="tpu_custom_call" | custom-call | flops 23592960 | bytes 21577736 | tf_op jit(solution)/shard_map/step/pallas_call | solution.py:592
  (308 shorter events, 91.9 us)
Async XLA Ops:
  7.2 131.1 %all-gather.3.cloned.1.call-start = ((), (), s32[]{:S(2)}) async-start(), calls=%async_computation.2 | async-start | bytes 10027008 | tf_op jit(solution)/shard_map/all_gather | solution.py:809
  23.0 277.8 %reduce-scatter.2.cloned.1.call-start = ((), (), s32[]{:S(2)}) async-start(), calls=%async_computation.1 | async-start | bytes 10027008 | tf_op jit(solution)/shard_map/reduce_scatter | solution.py:971
  23.8 12.6 %collective-permute-start.18 = (bf16[1,1,96,768]{3,2,1,0:T(8,128)(2,1)S(1)}, bf16[1,1,96,768]{3,2,1,0:T(8,128)(2,1)S(1)}, u32[]{:S(2)}, u32[]{:S(2)}) collective-permute-start(bf16[1,1,96,768]{3,2,1,0:T(8,128)(2,1)S(1)} %get-tuple-element.360), channel_id=1, source_target_pairs={{0,8},{8,0},{1,9},{9,1},{2,10},{10,2},{3,11},{11,3},{4,12},{12,4},... | collective-permute-start | bytes 442376 | tf_op jit(solution)/shard_map/ppermute | solution.py:611
  33.5 13.1 %collective-permute-start.2 = (bf16[4,1,96,384]{3,2,1,0:T(8,128)(2,1)S(1)}, bf16[4,1,96,384]{3,2,1,0:T(8,128)(2,1)S(1)}, u32[]{:S(2)}, u32[]{:S(2)}) collective-permute-start(bf16[4,1,96,384]{3,2,1,0:T(8,128)(2,1)S(1)} %pad_maximum_fusion.4.refs_0_.refs_6_), channel_id=1, source_target_pairs={{0,16},{16,0},{1,17},{17,1},{2,18},{18,2},{3,19},{19,3},{4,20},{20... | collective-permute-start | bytes 884744 | tf_op jit(solution)/shard_map/ppermute | solution.py:611
  36.4 29.8 %collective-permute-start.19 = (bf16[1,2,96,768]{3,2,1,0:T(8,128)(2,1)S(1)}, bf16[1,2,96,768]{3,2,1,0:T(8,128)(2,1)S(1)}, u32[]{:S(2)}, u32[]{:S(2)}) collective-permute-start(bf16[1,2,96,768]{3,2,1,0:T(8,128)(2,1)S(1)} %pad_maximum_fusion.6), channel_id=1, source_target_pairs={{0,2},{1,3},{2,0},{3,1},{4,6},{5,7},{6,4},{7,5},{8,10},{9,11},{10,... | collective-permute-start | bytes 884744 | tf_op jit(solution)/shard_map/ppermute | solution.py:616
  46.6 19.6 %collective-permute-start.9 = (bf16[4,1,96,384]{3,2,1,0:T(8,128)(2,1)S(1)}, bf16[4,1,96,384]{3,2,1,0:T(8,128)(2,1)S(1)}, u32[]{:S(2)}, u32[]{:S(2)}) collective-permute-start(bf16[4,1,96,384]{3,2,1,0:T(8,128)(2,1)S(1)} %collective-permute-done.2.refs_4_.refs_10_), channel_id=1, source_target_pairs={{0,8},{8,0},{1,9},{9,1},{2,10},{10,2},{3,11},{11,3},{4,12},{12,4},... | collective-permute-start | bytes 884744 | tf_op jit(solution)/shard_map/ppermute | solution.py:611
  47.0 19.7 %collective-permute-start.14 = (bf16[4,1,96,384]{3,2,1,0:T(8,128)(2,1)S(1)}, bf16[4,1,96,384]{3,2,1,0:T(8,128)(2,1)S(1)}, u32[]{:S(2)}, u32[]{:S(2)}) collective-permute-start(bf16[4,1,96,384]{3,2,1,0:T(8,128)(2,1)S(1)} %pad_maximum_fusion.5.refs_8_.refs_14_), channel_id=1, source_target_pairs={{0,16},{16,0},{1,17},{17,1},{2,18},{18,2},{3,19},{19,3},{4,20},{20... | collective-permute-start | bytes 884744 | tf_op jit(solution)/shard_map/ppermute | solution.py:611
  48.0 19.6 %collective-permute-start.15 = (bf16[4,1,96,384]{3,2,1,0:T(8,128)(2,1)S(1)}, bf16[4,1,96,384]{3,2,1,0:T(8,128)(2,1)}, u32[]{:S(2)}, u32[]{:S(2)}) collective-permute-start(bf16[4,1,96,384]{3,2,1,0:T(8,128)(2,1)S(1)} %collective-permute-done.5.refs_9_.refs_15_), channel_id=1, source_target_pairs={{0,16},{16,0},{1,17},{17,1},{2,18},{18,2},{3,19},{19,3},{4,20},{20... | collective-permute-start | bytes 884744 | tf_op jit(solution)/shard_map/ppermute | solution.py:611
  49.1 19.1 %collective-permute-start.6 = (bf16[4,1,96,384]{3,2,1,0:T(8,128)(2,1)S(1)}, bf16[4,1,96,384]{3,2,1,0:T(8,128)(2,1)}, u32[]{:S(2)}, u32[]{:S(2)}) collective-permute-start(bf16[4,1,96,384]{3,2,1,0:T(8,128)(2,1)S(1)} %pad_maximum_fusion.4.refs_0_.refs_6_), channel_id=1, source_target_pairs={{0,8},{8,0},{1,9},{9,1},{2,10},{10,2},{3,11},{11,3},{4,12},{12,4},... | collective-permute-start | bytes 884744 | tf_op jit(solution)/shard_map/ppermute | solution.py:611
  69.9 37.6 %collective-permute-start.21 = (bf16[2,2,96,768]{3,2,1,0:T(8,128)(2,1)S(1)}, bf16[2,2,96,768]{3,2,1,0:T(8,128)(2,1)S(1)}, u32[]{:S(2)}, u32[]{:S(2)}) collective-permute-start(bf16[2,2,96,768]{3,2,1,0:T(8,128)(2,1)S(1)} %pad_maximum_fusion.1.refs_0_), channel_id=1, source_target_pairs={{0,1},{1,0},{2,3},{3,2},{4,5},{5,4},{6,7},{7,6},{8,9},{9,8},{10,11... | collective-permute-start | bytes 1769480 | tf_op jit(solution)/shard_map/ppermute | solution.py:616
  70.0 37.5 %collective-permute-start.22 = (bf16[2,2,96,768]{3,2,1,0:T(8,128)(2,1)S(1)}, bf16[2,2,96,768]{3,2,1,0:T(8,128)(2,1)S(1)}, u32[]{:S(2)}, u32[]{:S(2)}) collective-permute-start(bf16[2,2,96,768]{3,2,1,0:T(8,128)(2,1)S(1)} %pad_maximum_fusion.1.refs_0_), channel_id=1, source_target_pairs={{0,16},{16,0},{1,17},{17,1},{2,18},{18,2},{3,19},{19,3},{4,20},{20... | collective-permute-start | bytes 1769480 | tf_op jit(solution)/shard_map/ppermute | solution.py:611
  87.4 20.1 %collective-permute-start.20 = (bf16[336,768]{1,0:T(8,128)(2,1)}, bf16[336,768]{1,0:T(8,128)(2,1)}, u32[]{:S(2)}, u32[]{:S(2)}) collective-permute-start(bf16[336,768]{1,0:T(8,128)(2,1)} %get-tuple-element.208), channel_id=1, source_target_pairs={{0,8},{8,0},{1,9},{9,1},{2,10},{10,2},{3,11},{11,3},{4,12},{12,4},... | collective-permute-start | bytes 1548296 | tf_op jit(solution)/shard_map/ppermute | solution.py:611
  108.1 15.4 %collective-permute-start.25 = (bf16[2,2,96,768]{3,2,1,0:T(8,128)(2,1)S(1)}, bf16[2,2,96,768]{3,2,1,0:T(8,128)(2,1)S(1)}, u32[]{:S(2)}, u32[]{:S(2)}) collective-permute-start(bf16[2,2,96,768]{3,2,1,0:T(8,128)(2,1)S(1)} %collective-permute-done.21.refs_0_.refs_4_), channel_id=1, source_target_pairs={{0,16},{16,0},{1,17},{17,1},{2,18},{18,2},{3,19},{19,3},{4,20},{20... | collective-permute-start | bytes 1769480 | tf_op jit(solution)/shard_map/ppermute | solution.py:611
  108.2 13.8 %collective-permute-start.26 = (bf16[336,768]{1,0:T(8,128)(2,1)S(1)}, bf16[336,768]{1,0:T(8,128)(2,1)S(1)}, u32[]{:S(2)}, u32[]{:S(2)}) collective-permute-start(bf16[336,768]{1,0:T(8,128)(2,1)S(1)} %bitcast.200), channel_id=1, source_target_pairs={{0,8},{8,0},{1,9},{9,1},{2,10},{10,2},{3,11},{11,3},{4,12},{12,4},... | collective-permute-start | bytes 1548296 | tf_op jit(solution)/shard_map/ppermute | solution.py:611
  183.6 19.1 %collective-permute-start.30 = (bf16[336,768]{1,0:T(8,128)(2,1)}, bf16[336,768]{1,0:T(8,128)(2,1)S(1)}, u32[]{:S(2)}, u32[]{:S(2)}) collective-permute-start(bf16[336,768]{1,0:T(8,128)(2,1)} %get-tuple-element.232), channel_id=1, source_target_pairs={{0,8},{8,0},{1,9},{9,1},{2,10},{10,2},{3,11},{11,3},{4,12},{12,4},... | collective-permute-start | bytes 1548296 | tf_op jit(solution)/shard_map/ppermute | solution.py:611
  210.7 25.3 %collective-permute-start.32 = (bf16[3,2,96,768]{3,2,1,0:T(8,128)(2,1)S(1)}, bf16[3,2,96,768]{3,2,1,0:T(8,128)(2,1)S(1)}, u32[]{:S(2)}, u32[]{:S(2)}) collective-permute-start(bf16[3,2,96,768]{3,2,1,0:T(8,128)(2,1)S(1)} %slice_bitcast_fusion), channel_id=1, source_target_pairs={{0,16},{16,0},{1,17},{17,1},{2,18},{18,2},{3,19},{19,3},{4,20},{20... | collective-permute-start | bytes 2654216 | tf_op jit(solution)/shard_map/ppermute | solution.py:611
  244.2 15.7 %collective-permute-start.34 = (bf16[2,4,96,384]{3,2,1,0:T(8,128)(2,1)}, bf16[2,4,96,384]{3,2,1,0:T(8,128)(2,1)}, u32[]{:S(2)}, u32[]{:S(2)}) collective-permute-start(bf16[2,4,96,384]{3,2,1,0:T(8,128)(2,1)} %fusion.24), channel_id=1, source_target_pairs={{0,8},{8,0},{1,9},{9,1},{2,10},{10,2},{3,11},{11,3},{4,12},{12,4},... | collective-permute-start | bytes 1769480 | tf_op jit(solution)/shard_map/ppermute | solution.py:611
  245.9 17.2 %collective-permute-start.35 = (bf16[2,4,96,384]{3,2,1,0:T(8,128)(2,1)}, bf16[2,4,96,384]{3,2,1,0:T(8,128)(2,1)}, u32[]{:S(2)}, u32[]{:S(2)}) collective-permute-start(bf16[2,4,96,384]{3,2,1,0:T(8,128)(2,1)} %get-tuple-element.260), channel_id=1, source_target_pairs={{0,16},{16,0},{1,17},{17,1},{2,18},{18,2},{3,19},{19,3},{4,20},{20... | collective-permute-start | bytes 1769480 | tf_op jit(solution)/shard_map/ppermute | solution.py:611
  247.7 16.5 %collective-permute-start.36 = (bf16[2,2,96,768]{3,2,1,0:T(8,128)(2,1)}, bf16[2,2,96,768]{3,2,1,0:T(8,128)(2,1)}, u32[]{:S(2)}, u32[]{:S(2)}) collective-permute-start(bf16[2,2,96,768]{3,2,1,0:T(8,128)(2,1)} %fusion.11), channel_id=1, source_target_pairs={{0,1},{1,0},{2,3},{3,2},{4,5},{5,4},{6,7},{7,6},{8,9},{9,8},{10,11... | collective-permute-start | bytes 1769480 | tf_op jit(solution)/shard_map/ppermute | solution.py:616
  249.2 26.5 %collective-permute-start.40 = (bf16[1,2,96,768]{3,2,1,0:T(8,128)(2,1)S(1)}, bf16[1,2,96,768]{3,2,1,0:T(8,128)(2,1)}, u32[]{:S(2)}, u32[]{:S(2)}) collective-permute-start(bf16[1,2,96,768]{3,2,1,0:T(8,128)(2,1)S(1)} %slice_bitcast_fusion.5), channel_id=1, source_target_pairs={{0,16},{16,0},{1,17},{17,1},{2,18},{18,2},{3,19},{19,3},{4,20},{20... | collective-permute-start | bytes 884744 | tf_op jit(solution)/shard_map/ppermute | solution.py:611
  265.8 19.6 %collective-permute-start.37 = (bf16[4,96,384]{2,1,0:T(8,128)(2,1)S(1)}, bf16[4,96,384]{2,1,0:T(8,128)(2,1)S(1)}, u32[]{:S(2)}, u32[]{:S(2)}) collective-permute-start(bf16[4,96,384]{2,1,0:T(8,128)(2,1)S(1)} %get-tuple-element.271), channel_id=1, source_target_pairs={{0,16},{16,0},{1,17},{17,1},{2,18},{18,2},{3,19},{19,3},{4,20},{20... | collective-permute-start | bytes 884744 | tf_op jit(solution)/shard_map/ppermute | solution.py:611
  266.9 18.4 %collective-permute-start.38 = (bf16[4,96,384]{2,1,0:T(8,128)(2,1)S(1)}, bf16[4,96,384]{2,1,0:T(8,128)(2,1)S(1)}, u32[]{:S(2)}, u32[]{:S(2)}) collective-permute-start(bf16[4,96,384]{2,1,0:T(8,128)(2,1)S(1)} %get-tuple-element.272), channel_id=1, source_target_pairs={{0,8},{8,0},{1,9},{9,1},{2,10},{10,2},{3,11},{11,3},{4,12},{12,4},... | collective-permute-start | bytes 884744 | tf_op jit(solution)/shard_map/ppermute | solution.py:611
  268.0 17.3 %collective-permute-start.39 = (bf16[1,96,768]{2,1,0:T(8,128)(2,1)S(1)}, bf16[1,96,768]{2,1,0:T(8,128)(2,1)S(1)}, u32[]{:S(2)}, u32[]{:S(2)}) collective-permute-start(bf16[1,96,768]{2,1,0:T(8,128)(2,1)S(1)} %get-tuple-element.364), channel_id=1, source_target_pairs={{0,2},{1,3},{2,0},{3,1},{4,6},{5,7},{6,4},{7,5},{8,10},{9,11},{10,... | collective-permute-start | bytes 442376 | tf_op jit(solution)/shard_map/ppermute | solution.py:616
  285.4 13.0 %collective-permute-start.43 = (bf16[336,768]{1,0:T(8,128)(2,1)S(1)}, bf16[336,768]{1,0:T(8,128)(2,1)S(1)}, u32[]{:S(2)}, u32[]{:S(2)}) collective-permute-start(bf16[336,768]{1,0:T(8,128)(2,1)S(1)} %slice.280), channel_id=1, source_target_pairs={{0,8},{8,0},{1,9},{9,1},{2,10},{10,2},{3,11},{11,3},{4,12},{12,4},... | collective-permute-start | bytes 1548296 | tf_op jit(solution)/shard_map/ppermute | solution.py:611
  287.2 11.2 %collective-permute-start.41 = (bf16[2,96,768]{2,1,0:T(8,128)(2,1)S(1)}, bf16[2,96,768]{2,1,0:T(8,128)(2,1)S(1)}, u32[]{:S(2)}, u32[]{:S(2)}) collective-permute-start(bf16[2,96,768]{2,1,0:T(8,128)(2,1)S(1)} %get-tuple-element.354), channel_id=1, source_target_pairs={{0,1},{1,0},{2,3},{3,2},{4,5},{5,4},{6,7},{7,6},{8,9},{9,8},{10,11... | collective-permute-start | bytes 884744 | tf_op jit(solution)/shard_map/ppermute | solution.py:616
  300.7 11.9 %collective-permute-start.47 = (bf16[2,96,768]{2,1,0:T(8,128)(2,1)}, bf16[2,96,768]{2,1,0:T(8,128)(2,1)}, u32[]{:S(2)}, u32[]{:S(2)}) collective-permute-start(bf16[2,96,768]{2,1,0:T(8,128)(2,1)} %bitcast.61), channel_id=1, source_target_pairs={{0,1},{1,0},{2,3},{3,2},{4,5},{5,4},{6,7},{7,6},{8,9},{9,8},{10,11... | collective-permute-start | bytes 884744 | tf_op jit(solution)/shard_map/ppermute | solution.py:616
  301.8 10.9 %collective-permute-start.46 = (bf16[2,96,768]{2,1,0:T(8,128)(2,1)S(1)}, bf16[2,96,768]{2,1,0:T(8,128)(2,1)S(1)}, u32[]{:S(2)}, u32[]{:S(2)}) collective-permute-start(bf16[2,96,768]{2,1,0:T(8,128)(2,1)S(1)} %slice_bitcast_fusion.3), channel_id=1, source_target_pairs={{0,8},{8,0},{1,9},{9,1},{2,10},{10,2},{3,11},{11,3},{4,12},{12,4},... | collective-permute-start | bytes 884744 | tf_op jit(solution)/shard_map/ppermute | solution.py:611
  303.4 9.3 %collective-permute-start.44 = (bf16[1,96,768]{2,1,0:T(8,128)(2,1)S(1)}, bf16[1,96,768]{2,1,0:T(8,128)(2,1)S(1)}, u32[]{:S(2)}, u32[]{:S(2)}) collective-permute-start(bf16[1,96,768]{2,1,0:T(8,128)(2,1)S(1)} %get-tuple-element.361), channel_id=1, source_target_pairs={{0,2},{1,3},{2,0},{3,1},{4,6},{5,7},{6,4},{7,5},{8,10},{9,11},{10,... | collective-permute-start | bytes 442376 | tf_op jit(solution)/shard_map/ppermute | solution.py:616
  313.9 10.6 %collective-permute-start.48 = (bf16[1,96,768]{2,1,0:T(8,128)(2,1)S(1)}, bf16[1,96,768]{2,1,0:T(8,128)(2,1)S(1)}, u32[]{:S(2)}, u32[]{:S(2)}) collective-permute-start(bf16[1,96,768]{2,1,0:T(8,128)(2,1)S(1)} %slice.294), channel_id=1, source_target_pairs={{0,2},{1,3},{2,0},{3,1},{4,6},{5,7},{6,4},{7,5},{8,10},{9,11},{10,... | collective-permute-start | bytes 442376 | tf_op jit(solution)/shard_map/ppermute | solution.py:616
  319.4 10.1 %collective-permute-start.52 = (f32[11,768]{1,0:T(8,128)}, f32[11,768]{1,0:T(8,128)S(1)}, u32[]{:S(2)}, u32[]{:S(2)}) collective-permute-start(f32[11,768]{1,0:T(8,128)} %prepare.1), channel_id=1, source_target_pairs={{0,2},{1,3},{2,0},{3,1},{4,6},{5,7},{6,4},{7,5},{8,10},{9,11},{10,... | collective-permute-start | bytes 101384 | tf_op jit(solution)/shard_map/ppermute | solution.py:631
  324.5 9.3 %collective-permute-start.49 = (bf16[1,96,768]{2,1,0:T(8,128)(2,1)S(1)}, bf16[1,96,768]{2,1,0:T(8,128)(2,1)S(1)}, u32[]{:S(2)}, u32[]{:S(2)}) collective-permute-start(bf16[1,96,768]{2,1,0:T(8,128)(2,1)S(1)} %add_convert_fusion.15), channel_id=1, source_target_pairs={{0,2},{1,3},{2,0},{3,1},{4,6},{5,7},{6,4},{7,5},{8,10},{9,11},{10,... | collective-permute-start | bytes 442376 | tf_op jit(solution)/shard_map/ppermute | solution.py:616
  333.9 18.5 %collective-permute-start.50 = (bf16[2,96,768]{2,1,0:T(8,128)(2,1)S(1)}, bf16[2,96,768]{2,1,0:T(8,128)(2,1)S(1)}, u32[]{:S(2)}, u32[]{:S(2)}) collective-permute-start(bf16[2,96,768]{2,1,0:T(8,128)(2,1)S(1)} %pad_maximum_fusion.7), channel_id=1, source_target_pairs={{0,1},{1,0},{2,3},{3,2},{4,5},{5,4},{6,7},{7,6},{8,9},{9,8},{10,11... | collective-permute-start | bytes 884744 | tf_op jit(solution)/shard_map/ppermute | solution.py:616
  (78 other events, 680.8 us)
Sparse Core Ops, SparseCore 0:
  23.2 107.2 all-gather.2
  172.1 119.7 reduce-scatter.1

commit v6 on v5

--- a/solution.py
+++ b/solution.py
@@ -513,17 +513,22 @@
     ins, outs, feed_in, feed_out, norm_in = (refs[4 * i : 4 * i + 4] for i in range(5))
     refs = refs[20:]
     step = pl.program_id(0)
-    total = sums[...] + theirs[...]
-    norm_grad = total[:-1]
-    squares = jnp.sum(norm_grad * norm_grad, keepdims=True) + total[-1:, 0:1]
-    grad_norm = jnp.sqrt(squares)
-    clip = CLIP_NORM / jnp.maximum(grad_norm, CLIP_NORM)
-    refs[-1][...] = grad_norm
-    for place in range(norm_in[0].shape[0]):
-        state = [ref[place] for ref in norm_in]
-        new = adamw_step(norm_grad[2 * place : 2 * place + 2], *state, NORM_RATE, clip)
-        for ref, value in zip(refs[24:29], new):
-            ref[place] = value
+    @pl.when(step == 0)
+    def _():
+        total = sums[...] + theirs[...]
+        norm_grad = total[:-1]
+        squares = jnp.sum(norm_grad * norm_grad, keepdims=True) + total[-1:, 0:1]
+        grad_norm = jnp.sqrt(squares)
+        clip = CLIP_NORM / jnp.maximum(grad_norm, CLIP_NORM)
+        refs[-2][...] = grad_norm
+        refs[-1][...] = clip
+        for place in range(norm_in[0].shape[0]):
+            state = [ref[place] for ref in norm_in]
+            new = adamw_step(norm_grad[2 * place : 2 * place + 2], *state, NORM_RATE, clip)
+            for ref, value in zip(refs[24:29], new):
+                ref[place] = value
+
+    clip = refs[-1][...]
     is_vis = stream[0, 0] == 1
 
     def by_stream(mine, other):
@@ -1083,11 +1088,10 @@
     final = from_order(rows_three).astype(BF)
 
     first_far, second_far = swap_dp(first[1], 2), swap_dp(second[1], 1)
-    self_ones = [swap_mp(self_one[1:], 1)]
     self_near = swap_dp(self_sums[1][:1], 2)
     extras = image_term, norm_partial, final
-    late = together(first[0], second[0], first_far, second_far, self_ones, self_near, extras)
-    first, second, first_far, second_far, self_ones, self_near, extras = late
+    late = together(first[0], second[0], first_far, second_far, self_near, extras)
+    first, second, first_far, second_far, self_near, extras = late
     image_term, norm_partial, final = extras
     home = jnp.concatenate([added(first, first_far), added(second, second_far)], axis=-1)
     home = scatter_extra(home)
@@ -1095,11 +1099,11 @@
 
     kept, sent = parts(home)
     sent = swap_mp(sent, 0)
-    self_ones = [swap_mp(after(self_one[:1], home), 1)] + self_ones
+    self_ones = swap_mp(self_one, 1)
     final_other = swap_dp(final[slot:], 1)
     late = together(kept, sent, self_low, self_ones, image_term, final_other)
     kept, sent, self_low, self_ones, image_term, final_other = late
-    self_low = added(self_low, jnp.concatenate(self_ones, axis=0))
+    self_low = added(self_low, self_ones)
     home = added(kept, sent)
 
     kept, sent = parts(home)
@@ -1167,7 +1171,7 @@
         + [(by_rows, feed_in[0].shape, t) for k, t in kinds * 2]
         + [("whole", norm_in[0].shape, F32)] * 5
         + [("whole", (1, 1), F32)],
-        [],
+        [((1, 1), F32)],
         "step",
         20 * 8 * dim * width,
     )

time: 367 us -> 367 us (level)
  waiting for transfers between devices: 113 us -> 117 us
    ppermute x37, waiting for transfers between devices: 37 us -> 46.6 us  [swap_dp(): lax.ppermute(value, axis, [(i, i ^ 1 << place) for i in range(count)])]
    ppermute x15 -> x14, waiting for transfers between devices: 69.1 us -> 64.1 us  [swap_mp(): return lax.ppermute(value, 'mp', [(i, i ^ 1 << bit) for i in range(count)])]
    ppermute x15 -> x14, starting transfers between devices: 18.9 us -> 17.5 us  [swap_mp(): return lax.ppermute(value, 'mp', [(i, i ^ 1 << bit) for i in range(count)])]
  transfers between devices with their start and end apart: 60 -> 59, of which waited for: 28 -> 28; matrix products, arithmetic and copies ran while one was open for 10% -> 10% of each run, Pallas kernels for 28% -> 28%
where the time goes in v6:
time: 367 us; the launch traced here: 361 us
  Pallas kernels  135 us (37%)
  waiting for transfers between devices  117 us (32%)
  starting transfers between devices  47.6 us (13%)
  other arithmetic  19.7 us (5%)
  local copies, waits for them, and re-layouts  17.7 us (5%)
  between operations  15.5 us (4%)
  matrix products  8.83 us (2%)
    pallas_call x9, Pallas kernels, call(): pl.pallas_call(kernel, grid=(steps,), in_specs=[spec[kind](a.shape) for k...  135 us
    ppermute x14, waiting for transfers between devices, swap_mp(): return lax.ppermute(value, 'mp', [(i, i ^ 1 << bit) for i in range(count)])  64.1 us
    ppermute x37, waiting for transfers between devices, swap_dp(): lax.ppermute(value, axis, [(i, i ^ 1 << place) for i in range(count)])  46.6 us
    ppermute x37, starting transfers between devices, swap_dp(): lax.ppermute(value, axis, [(i, i ^ 1 << place) for i in range(count)])  22.2 us
    ppermute x14, starting transfers between devices, swap_mp(): return lax.ppermute(value, 'mp', [(i, i ^ 1 << bit) for i in range(count)])  17.5 us
    convert_element_type x11, other arithmetic, added(): return (mine.astype(F32) + theirs.astype(F32)).astype(BF)  8.81 us
    ppermute x6, starting transfers between devices, swap_mask(): return lax.ppermute(value, axis, [(i, i ^ mask) for i in range(count)])  7.93 us
  transfers between devices with their start and end apart: 59, of which 28 were waited for; matrix products, arithmetic and copies ran while one was open for 10% of the time, Pallas kernels for 28%

profile of v6, /device:TPU:0, one launch (start us, length us, event | category | flops | bytes accessed | tf_op | source)
XLA Modules:
  0.0 361.2 jit_solution(18223915986172149196)
XLA Ops:
  9.2 4.1 %collective-permute-start.3 = (bf16[1,1,96,384]{3,2,1,0:T(8,128)(2,1)S(1)}, bf16[1,1,96,384]{3,2,1,0:T(8,128)(2,1)S(1)}, u32[]{:S(2)}, u32[]{:S(2)}) collective-permute-start(bf16[1,1,96,384]{3,2,1,0:T(8,128)(2,1)S(1)} %get-tuple-element.370), channel_id=1, source_target_pairs={{0,2},{1,3},{2,0},{3,1},{4,6},{5,7},{6,4},{7,5},{8,10},{9,11},{10,... | collective-permute-start | bytes 221192 | tf_op jit(solution)/shard_map/ppermute | solution.py:621
  15.5 2.7 collective-permute-done.3
  18.2 2.2 collective-permute-done
  28.5 1.9 convolution_convert_fusion.vis
  36.5 2.6 collective-permute-start.19
  39.1 7.5 %collective-permute-done.2.refs_4_.refs_10_ = bf16[4,1,96,384]{3,2,1,0:T(8,128)(2,1)S(1)} collective-permute-done((bf16[4,1,96,384]{3,2,1,0:T(8,128)(2,1)S(1)}, bf16[4,1,96,384]{3,2,1,0:T(8,128)(2,1)S(1)}, u32[]{:S(2)}, u32[]{:S(2)}) %collective-permute-start.2) | collective-permute-done | bytes 294944 | tf_op jit(solution)/shard_map/ppermute | solution.py:616
  50.6 15.6 %collective-permute-done.19 = bf16[1,2,96,768]{3,2,1,0:T(8,128)(2,1)S(1)} collective-permute-done((bf16[1,2,96,768]{3,2,1,0:T(8,128)(2,1)S(1)}, bf16[1,2,96,768]{3,2,1,0:T(8,128)(2,1)S(1)}, u32[]{:S(2)}, u32[]{:S(2)}) %collective-permute-start.19) | collective-permute-done | bytes 294944 | tf_op jit(solution)/shard_map/ppermute | solution.py:621
  72.0 15.5 %cross_forward.1 = (bf16[336,768]{1,0:T(8,128)(2,1)}, bf16[336,768]{1,0:T(8,128)(2,1)}, f32[192,768]{1,0:T(8,128)}, f32[192,1]{1,0:T(8,128)}, f32[336,768]{1,0:T...) custom-call(s32[1,1]{1,0:T(1,128)} %bitcast.stream, ...), custom_call_target="tpu_custom_call" | custom-call | flops 14948499456 | bytes 12468292 | tf_op jit(solution)/shard_map/cross_forward/pallas_call | solution.py:597
  89.8 17.8 %collective-permute-done.21.refs_0_.refs_4_ = bf16[2,2,96,768]{3,2,1,0:T(8,128)(2,1)S(1)} collective-permute-done((bf16[2,2,96,768]{3,2,1,0:T(8,128)(2,1)S(1)}, bf16[2,2,96,768]{3,2,1,0:T(8,128)(2,1)S(1)}, u32[]{:S(2)}, u32[]{:S(2)}) %collective-permute-start.21) | collective-permute-done | bytes 589856 | tf_op jit(solution)/shard_map/ppermute | solution.py:621
  112.1 7.9 %self_first.1 = (f32[672,768]{1,0:T(8,128)}, bf16[4,672,576]{2,1,0:T(8,128)(2,1)}, bf16[4,672,192]{2,1,0:T(8,128)(2,1)}, bf16[4,2016,112]{2,1,0:T(8,128)(2,1)}) custom-call(s32[1,1]{1,0:T(1,128)} %bitcast.4.length, bf16[336,768]{1,0:T(8,128)(2,1)} %get-tuple-element.204.own, bf16[336,768]{1,0:T(8,128)(2,1)} %copy-done.23, bf16[2,2,96,768]{3,2,1,0:T(8,128)(2,1)} %copy-done, ...), custom_call_target="tpu_custom_call" | custom-call | flops 9512681472 | bytes 11390980 | tf_op jit(solution)/shard_map/self_first/pallas_call | solution.py:597
  119.9 3.0 collective-permute-done.26
  126.0 2.1 fusion.7.cot
  129.1 9.9 %self_second.1 = (bf16[672,768]{1,0:T(8,128)(2,1)}, f32[672,768]{1,0:T(8,128)}, f32[672,1]{1,0:T(8,128)}, bf16[4,672,576]{2,1,0:T(8,128)(2,1)}, bf16[4,672,192]{...) custom-call(s32[1,1]{1,0:T(1,128)} %bitcast.4.length, ...), custom_call_target="tpu_custom_call", output_to_operand_aliasing={{3}: (9, {}), {4}: (10, {}), {5}: (11, {})} | custom-call | flops 9512681472 | bytes 20431492 | tf_op jit(solution)/shard_map/self_second/pallas_call | solution.py:597
  139.0 33.4 %feed.1 = (bf16[672,768]{1,0:T(8,128)(2,1)}, bf16[2,2,4,2,2,96,768]{6,5,4,3,2,1,0:T(8,128)(2,1)}, f32[672,768]{1,0:T(8,128)}, f32[1,768]{1,0:T(1,128)}, f32[1,76...) custom-call(s32[1,2]{1,0:T(1,128)} %add_bitcast_fusion.place, bf16[672,768]{1,0:T(8,128)(2,1)} %get-tuple-element.216.rows, ...), custom_call_target="tpu_custom_call" | custom-call | flops 38050725888 | bytes 26126984 | tf_op jit(solution)/shard_map/feed/pallas_call | solution.py:597
  172.4 11.6 %self_other.1 = (bf16[4,336,576]{2,1,0:T(8,128)(2,1)}, bf16[336,768]{1,0:T(8,128)(2,1)}) custom-call(f32[672,768]{1,0:T(8,128)} %get-tuple-element.221.inward, bf16[4,672,576]{2,1,0:T(8,128)(2,1)} %get-tuple-element.222.qkv, bf16[4,2016,112]{2,1,0:T(8,128)(2,1)} %get-tuple-element.224.probs, bf16[2,2,96,768]{3,2,1,0:T(8,128)(2,1)} %copy-done, ...), custom_call_target="tpu_custom_call" | custom-call | flops 3170893824 | bytes 13750272 | tf_op jit(solution)/shard_map/self_other/pallas_call | solution.py:597
  184.2 18.9 %self_own.1 = (bf16[2,4,2,96,768]{4,3,2,1,0:T(8,128)(2,1)}, bf16[2,4,2,96,768]{4,3,2,1,0:T(8,128)(2,1)}, bf16[336,768]{1,0:T(8,128)(2,1)}) custom-call(f32[672,768]{1,0:T(8,128)} %get-tuple-element.221.inward, bf16[336,768]{1,0:T(8,128)(2,1)} %get-tuple-element.204.own, bf16[336,768]{1,0:T(8,128)(2,1)} %copy-done.23, ...), custom_call_target="tpu_custom_call" | custom-call | flops 3170893824 | bytes 20533248 | tf_op jit(solution)/shard_map/self_own/pallas_call | solution.py:597
  205.5 3.1 collective-permute-done.31
  208.6 2.3 add_convert_fusion
  213.3 23.3 %cross_backward.1 = (bf16[2,2,4,96,768]{4,3,2,1,0:T(8,128)(2,1)}, bf16[2,2,4,96,768]{4,3,2,1,0:T(8,128)(2,1)}, f32[192,768]{1,0:T(8,128)}, bf16[384,768]{1,0:T(8...) custom-call(s32[1,1]{1,0:T(1,128)} %bitcast.stream, bf16[336,768]{1,0:T(8,128)(2,1)} %get-tuple-element.230.own_up, ...), custom_call_target="tpu_custom_call" | custom-call | flops 7474249728 | bytes 19555204 | tf_op jit(solution)/shard_map/cross_backward/pallas_call | solution.py:597
  237.8 3.7 %collective-permute-done.33 = bf16[2,2,4,96,768]{4,3,2,1,0:T(8,128)(2,1)S(1)} collective-permute-done((bf16[2,2,4,96,768]{4,3,2,1,0:T(8,128)(2,1)}, bf16[2,2,4,96,768]{4,3,2,1,0:T(8,128)(2,1)S(1)}, u32[]{:S(2)}, u32[]{:S(2)}) %collective-permute-start.33) | collective-permute-done | bytes 2359328 | tf_op jit(solution)/shard_map/ppermute | solution.py:616
  241.5 2.1 fusion.24
  250.4 10.2 %collective-permute-done.34 = bf16[2,4,96,384]{3,2,1,0:T(8,128)(2,1)} collective-permute-done((bf16[2,4,96,384]{3,2,1,0:T(8,128)(2,1)}, bf16[2,4,96,384]{3,2,1,0:T(8,128)(2,1)}, u32[]{:S(2)}, u32[]{:S(2)}) %collective-permute-start.34) | collective-permute-done | bytes 589856 | tf_op jit(solution)/shard_map/ppermute | solution.py:616
  260.6 3.5 collective-permute-done.35
  264.1 3.1 collective-permute-done.36
  271.8 3.9 %collective-permute-done.39 = bf16[1,2,96,768]{3,2,1,0:T(8,128)(2,1)} collective-permute-done((bf16[1,2,96,768]{3,2,1,0:T(8,128)(2,1)}, bf16[1,2,96,768]{3,2,1,0:T(8,128)(2,1)}, u32[]{:S(2)}, u32[]{:S(2)}) %collective-permute-start.39) | collective-permute-done | bytes 294944 | tf_op jit(solution)/shard_map/ppermute | solution.py:616
  275.7 5.7 %collective-permute-done.37 = bf16[4,96,384]{2,1,0:T(8,128)(2,1)S(1)} collective-permute-done((bf16[4,96,384]{2,1,0:T(8,128)(2,1)S(1)}, bf16[4,96,384]{2,1,0:T(8,128)(2,1)S(1)}, u32[]{:S(2)}, u32[]{:S(2)}) %collective-permute-start.37) | collective-permute-done | bytes 294944 | tf_op jit(solution)/shard_map/ppermute | solution.py:616
  287.2 12.3 %collective-permute-done.41 = bf16[2,96,768]{2,1,0:T(8,128)(2,1)S(1)} collective-permute-done((bf16[2,96,768]{2,1,0:T(8,128)(2,1)S(1)}, bf16[2,96,768]{2,1,0:T(8,128)(2,1)S(1)}, u32[]{:S(2)}, u32[]{:S(2)}) %collective-permute-start.41) | collective-permute-done | bytes 294944 | tf_op jit(solution)/shard_map/ppermute | solution.py:621
  307.4 5.7 %collective-permute-done.43.sent = bf16[1,96,768]{2,1,0:T(8,128)(2,1)S(1)} collective-permute-done((bf16[1,96,768]{2,1,0:T(8,128)(2,1)S(1)}, bf16[1,96,768]{2,1,0:T(8,128)(2,1)S(1)}, u32[]{:S(2)}, u32[]{:S(2)}) %collective-permute-start.43) | collective-permute-done | bytes 147488 | tf_op jit(solution)/shard_map/ppermute | solution.py:621
  317.9 2.5 prepare.1
  325.7 6.0 %collective-permute-done.51 = f32[11,768]{1,0:T(8,128)S(1)} collective-permute-done((f32[11,768]{1,0:T(8,128)}, f32[11,768]{1,0:T(8,128)S(1)}, u32[]{:S(2)}, u32[]{:S(2)}) %collective-permute-start.51) | collective-permute-done | bytes 33824 | tf_op jit(solution)/shard_map/ppermute | solution.py:636
  332.6 3.4 collective-permute-start.55
  340.6 11.6 %step.1 = (f32[3,3,96,192]{3,2,1,0:T(8,128)}, f32[3,3,96,192]{3,2,1,0:T(8,128)}, f32[3,3,96,192]{3,2,1,0:T(8,128)}, f32[3,3,96,192]{3,2,1,0:T(8,128)}, bf16[3,3,...) custom-call(s32[1,1]{1,0:T(1,128)} %bitcast.stream, ...), custom_call_target="tpu_custom_call" | custom-call | flops 23592960 | bytes 21577736 | tf_op jit(solution)/shard_map/step/pallas_call | solution.py:597
  (316 shorter events, 86.7 us)
Async XLA Ops:
  7.2 131.7 %all-gather.3.cloned.1.call-start = ((), (), s32[]{:S(2)}) async-start(), calls=%async_computation.2 | async-start | bytes 10027008 | tf_op jit(solution)/shard_map/all_gather | solution.py:814
  9.2 9.0 %collective-permute-start.3 = (bf16[1,1,96,384]{3,2,1,0:T(8,128)(2,1)S(1)}, bf16[1,1,96,384]{3,2,1,0:T(8,128)(2,1)S(1)}, u32[]{:S(2)}, u32[]{:S(2)}) collective-permute-start(bf16[1,1,96,384]{3,2,1,0:T(8,128)(2,1)S(1)} %get-tuple-element.370), channel_id=1, source_target_pairs={{0,2},{1,3},{2,0},{3,1},{4,6},{5,7},{6,4},{7,5},{8,10},{9,11},{10,... | collective-permute-start | bytes 221192 | tf_op jit(solution)/shard_map/ppermute | solution.py:621
  23.0 279.7 %reduce-scatter.2.cloned.1.call-start = ((), (), s32[]{:S(2)}) async-start(), calls=%async_computation.1 | async-start | bytes 10027008 | tf_op jit(solution)/shard_map/reduce_scatter | solution.py:976
  23.8 12.6 %collective-permute-start.18 = (bf16[1,1,96,768]{3,2,1,0:T(8,128)(2,1)S(1)}, bf16[1,1,96,768]{3,2,1,0:T(8,128)(2,1)S(1)}, u32[]{:S(2)}, u32[]{:S(2)}) collective-permute-start(bf16[1,1,96,768]{3,2,1,0:T(8,128)(2,1)S(1)} %get-tuple-element.356), channel_id=1, source_target_pairs={{0,8},{8,0},{1,9},{9,1},{2,10},{10,2},{3,11},{11,3},{4,12},{12,4},... | collective-permute-start | bytes 442376 | tf_op jit(solution)/shard_map/ppermute | solution.py:616
  33.5 13.1 %collective-permute-start.2 = (bf16[4,1,96,384]{3,2,1,0:T(8,128)(2,1)S(1)}, bf16[4,1,96,384]{3,2,1,0:T(8,128)(2,1)S(1)}, u32[]{:S(2)}, u32[]{:S(2)}) collective-permute-start(bf16[4,1,96,384]{3,2,1,0:T(8,128)(2,1)S(1)} %pad_maximum_fusion.4.refs_0_.refs_6_), channel_id=1, source_target_pairs={{0,16},{16,0},{1,17},{17,1},{2,18},{18,2},{3,19},{19,3},{4,20},{20... | collective-permute-start | bytes 884744 | tf_op jit(solution)/shard_map/ppermute | solution.py:616
  36.5 29.8 %collective-permute-start.19 = (bf16[1,2,96,768]{3,2,1,0:T(8,128)(2,1)S(1)}, bf16[1,2,96,768]{3,2,1,0:T(8,128)(2,1)S(1)}, u32[]{:S(2)}, u32[]{:S(2)}) collective-permute-start(bf16[1,2,96,768]{3,2,1,0:T(8,128)(2,1)S(1)} %pad_maximum_fusion.6), channel_id=1, source_target_pairs={{0,2},{1,3},{2,0},{3,1},{4,6},{5,7},{6,4},{7,5},{8,10},{9,11},{10,... | collective-permute-start | bytes 884744 | tf_op jit(solution)/shard_map/ppermute | solution.py:621
  46.6 19.6 %collective-permute-start.9 = (bf16[4,1,96,384]{3,2,1,0:T(8,128)(2,1)S(1)}, bf16[4,1,96,384]{3,2,1,0:T(8,128)(2,1)S(1)}, u32[]{:S(2)}, u32[]{:S(2)}) collective-permute-start(bf16[4,1,96,384]{3,2,1,0:T(8,128)(2,1)S(1)} %collective-permute-done.2.refs_4_.refs_10_), channel_id=1, source_target_pairs={{0,8},{8,0},{1,9},{9,1},{2,10},{10,2},{3,11},{11,3},{4,12},{12,4},... | collective-permute-start | bytes 884744 | tf_op jit(solution)/shard_map/ppermute | solution.py:616
  47.0 19.7 %collective-permute-start.14 = (bf16[4,1,96,384]{3,2,1,0:T(8,128)(2,1)S(1)}, bf16[4,1,96,384]{3,2,1,0:T(8,128)(2,1)}, u32[]{:S(2)}, u32[]{:S(2)}) collective-permute-start(bf16[4,1,96,384]{3,2,1,0:T(8,128)(2,1)S(1)} %pad_maximum_fusion.5.refs_8_.refs_14_), channel_id=1, source_target_pairs={{0,16},{16,0},{1,17},{17,1},{2,18},{18,2},{3,19},{19,3},{4,20},{20... | collective-permute-start | bytes 884744 | tf_op jit(solution)/shard_map/ppermute | solution.py:616
  48.0 19.6 %collective-permute-start.15 = (bf16[4,1,96,384]{3,2,1,0:T(8,128)(2,1)S(1)}, bf16[4,1,96,384]{3,2,1,0:T(8,128)(2,1)}, u32[]{:S(2)}, u32[]{:S(2)}) collective-permute-start(bf16[4,1,96,384]{3,2,1,0:T(8,128)(2,1)S(1)} %collective-permute-done.5.refs_9_.refs_15_), channel_id=1, source_target_pairs={{0,16},{16,0},{1,17},{17,1},{2,18},{18,2},{3,19},{19,3},{4,20},{20... | collective-permute-start | bytes 884744 | tf_op jit(solution)/shard_map/ppermute | solution.py:616
  49.1 19.1 %collective-permute-start.6 = (bf16[4,1,96,384]{3,2,1,0:T(8,128)(2,1)S(1)}, bf16[4,1,96,384]{3,2,1,0:T(8,128)(2,1)}, u32[]{:S(2)}, u32[]{:S(2)}) collective-permute-start(bf16[4,1,96,384]{3,2,1,0:T(8,128)(2,1)S(1)} %pad_maximum_fusion.4.refs_0_.refs_6_), channel_id=1, source_target_pairs={{0,8},{8,0},{1,9},{9,1},{2,10},{10,2},{3,11},{11,3},{4,12},{12,4},... | collective-permute-start | bytes 884744 | tf_op jit(solution)/shard_map/ppermute | solution.py:616
  70.0 37.6 %collective-permute-start.21 = (bf16[2,2,96,768]{3,2,1,0:T(8,128)(2,1)S(1)}, bf16[2,2,96,768]{3,2,1,0:T(8,128)(2,1)S(1)}, u32[]{:S(2)}, u32[]{:S(2)}) collective-permute-start(bf16[2,2,96,768]{3,2,1,0:T(8,128)(2,1)S(1)} %pad_maximum_fusion.refs_0_), channel_id=1, source_target_pairs={{0,1},{1,0},{2,3},{3,2},{4,5},{5,4},{6,7},{7,6},{8,9},{9,8},{10,11... | collective-permute-start | bytes 1769480 | tf_op jit(solution)/shard_map/ppermute | solution.py:621
  70.1 37.5 %collective-permute-start.22 = (bf16[2,2,96,768]{3,2,1,0:T(8,128)(2,1)S(1)}, bf16[2,2,96,768]{3,2,1,0:T(8,128)(2,1)S(1)}, u32[]{:S(2)}, u32[]{:S(2)}) collective-permute-start(bf16[2,2,96,768]{3,2,1,0:T(8,128)(2,1)S(1)} %pad_maximum_fusion.refs_0_), channel_id=1, source_target_pairs={{0,16},{16,0},{1,17},{17,1},{2,18},{18,2},{3,19},{19,3},{4,20},{20... | collective-permute-start | bytes 1769480 | tf_op jit(solution)/shard_map/ppermute | solution.py:616
  87.4 20.1 %collective-permute-start.20 = (bf16[336,768]{1,0:T(8,128)(2,1)}, bf16[336,768]{1,0:T(8,128)(2,1)S(1)}, u32[]{:S(2)}, u32[]{:S(2)}) collective-permute-start(bf16[336,768]{1,0:T(8,128)(2,1)} %get-tuple-element.205), channel_id=1, source_target_pairs={{0,8},{8,0},{1,9},{9,1},{2,10},{10,2},{3,11},{11,3},{4,12},{12,4},... | collective-permute-start | bytes 1548296 | tf_op jit(solution)/shard_map/ppermute | solution.py:616
  108.9 15.3 %collective-permute-start.25 = (bf16[2,2,96,768]{3,2,1,0:T(8,128)(2,1)S(1)}, bf16[2,2,96,768]{3,2,1,0:T(8,128)(2,1)S(1)}, u32[]{:S(2)}, u32[]{:S(2)}) collective-permute-start(bf16[2,2,96,768]{3,2,1,0:T(8,128)(2,1)S(1)} %collective-permute-done.21.refs_0_.refs_4_), channel_id=1, source_target_pairs={{0,16},{16,0},{1,17},{17,1},{2,18},{18,2},{3,19},{19,3},{4,20},{20... | collective-permute-start | bytes 1769480 | tf_op jit(solution)/shard_map/ppermute | solution.py:616
  109.0 13.9 %collective-permute-start.26 = (bf16[336,768]{1,0:T(8,128)(2,1)}, bf16[336,768]{1,0:T(8,128)(2,1)S(1)}, u32[]{:S(2)}, u32[]{:S(2)}) collective-permute-start(bf16[336,768]{1,0:T(8,128)(2,1)} %bitcast.198), channel_id=1, source_target_pairs={{0,8},{8,0},{1,9},{9,1},{2,10},{10,2},{3,11},{11,3},{4,12},{12,4},... | collective-permute-start | bytes 1548296 | tf_op jit(solution)/shard_map/ppermute | solution.py:616
  184.1 19.0 %collective-permute-start.30 = (bf16[336,768]{1,0:T(8,128)(2,1)}, bf16[336,768]{1,0:T(8,128)(2,1)S(1)}, u32[]{:S(2)}, u32[]{:S(2)}) collective-permute-start(bf16[336,768]{1,0:T(8,128)(2,1)} %get-tuple-element.229), channel_id=1, source_target_pairs={{0,8},{8,0},{1,9},{9,1},{2,10},{10,2},{3,11},{11,3},{4,12},{12,4},... | collective-permute-start | bytes 1548296 | tf_op jit(solution)/shard_map/ppermute | solution.py:616
  211.0 25.7 %collective-permute-start.32 = (bf16[3,2,96,768]{3,2,1,0:T(8,128)(2,1)S(1)}, bf16[3,2,96,768]{3,2,1,0:T(8,128)(2,1)S(1)}, u32[]{:S(2)}, u32[]{:S(2)}) collective-permute-start(bf16[3,2,96,768]{3,2,1,0:T(8,128)(2,1)S(1)} %slice_bitcast_fusion), channel_id=1, source_target_pairs={{0,16},{16,0},{1,17},{17,1},{2,18},{18,2},{3,19},{19,3},{4,20},{20... | collective-permute-start | bytes 2654216 | tf_op jit(solution)/shard_map/ppermute | solution.py:616
  245.0 15.7 %collective-permute-start.34 = (bf16[2,4,96,384]{3,2,1,0:T(8,128)(2,1)}, bf16[2,4,96,384]{3,2,1,0:T(8,128)(2,1)}, u32[]{:S(2)}, u32[]{:S(2)}) collective-permute-start(bf16[2,4,96,384]{3,2,1,0:T(8,128)(2,1)} %fusion.24), channel_id=1, source_target_pairs={{0,8},{8,0},{1,9},{9,1},{2,10},{10,2},{3,11},{11,3},{4,12},{12,4},... | collective-permute-start | bytes 1769480 | tf_op jit(solution)/shard_map/ppermute | solution.py:616
  246.6 17.5 %collective-permute-start.35 = (bf16[2,4,96,384]{3,2,1,0:T(8,128)(2,1)}, bf16[2,4,96,384]{3,2,1,0:T(8,128)(2,1)}, u32[]{:S(2)}, u32[]{:S(2)}) collective-permute-start(bf16[2,4,96,384]{3,2,1,0:T(8,128)(2,1)} %get-tuple-element.257), channel_id=1, source_target_pairs={{0,16},{16,0},{1,17},{17,1},{2,18},{18,2},{3,19},{19,3},{4,20},{20... | collective-permute-start | bytes 1769480 | tf_op jit(solution)/shard_map/ppermute | solution.py:616
  248.2 19.1 %collective-permute-start.36 = (bf16[2,2,96,768]{3,2,1,0:T(8,128)(2,1)}, bf16[2,2,96,768]{3,2,1,0:T(8,128)(2,1)}, u32[]{:S(2)}, u32[]{:S(2)}) collective-permute-start(bf16[2,2,96,768]{3,2,1,0:T(8,128)(2,1)} %fusion.11), channel_id=1, source_target_pairs={{0,1},{1,0},{2,3},{3,2},{4,5},{5,4},{6,7},{7,6},{8,9},{9,8},{10,11... | collective-permute-start | bytes 1769480 | tf_op jit(solution)/shard_map/ppermute | solution.py:621
  249.9 25.8 %collective-permute-start.39 = (bf16[1,2,96,768]{3,2,1,0:T(8,128)(2,1)}, bf16[1,2,96,768]{3,2,1,0:T(8,128)(2,1)}, u32[]{:S(2)}, u32[]{:S(2)}) collective-permute-start(bf16[1,2,96,768]{3,2,1,0:T(8,128)(2,1)} %slice_bitcast_fusion.6), channel_id=1, source_target_pairs={{0,16},{16,0},{1,17},{17,1},{2,18},{18,2},{3,19},{19,3},{4,20},{20... | collective-permute-start | bytes 884744 | tf_op jit(solution)/shard_map/ppermute | solution.py:616
  268.9 12.6 %collective-permute-start.37 = (bf16[4,96,384]{2,1,0:T(8,128)(2,1)S(1)}, bf16[4,96,384]{2,1,0:T(8,128)(2,1)S(1)}, u32[]{:S(2)}, u32[]{:S(2)}) collective-permute-start(bf16[4,96,384]{2,1,0:T(8,128)(2,1)S(1)} %get-tuple-element.268), channel_id=1, source_target_pairs={{0,16},{16,0},{1,17},{17,1},{2,18},{18,2},{3,19},{19,3},{4,20},{20... | collective-permute-start | bytes 884744 | tf_op jit(solution)/shard_map/ppermute | solution.py:616
  268.9 12.5 %collective-permute-start.38 = (bf16[4,96,384]{2,1,0:T(8,128)(2,1)S(1)}, bf16[4,96,384]{2,1,0:T(8,128)(2,1)S(1)}, u32[]{:S(2)}, u32[]{:S(2)}) collective-permute-start(bf16[4,96,384]{2,1,0:T(8,128)(2,1)S(1)} %get-tuple-element.269), channel_id=1, source_target_pairs={{0,8},{8,0},{1,9},{9,1},{2,10},{10,2},{3,11},{11,3},{4,12},{12,4},... | collective-permute-start | bytes 884744 | tf_op jit(solution)/shard_map/ppermute | solution.py:616
  282.8 16.7 %collective-permute-start.41 = (bf16[2,96,768]{2,1,0:T(8,128)(2,1)S(1)}, bf16[2,96,768]{2,1,0:T(8,128)(2,1)S(1)}, u32[]{:S(2)}, u32[]{:S(2)}) collective-permute-start(bf16[2,96,768]{2,1,0:T(8,128)(2,1)S(1)} %get-tuple-element.338), channel_id=1, source_target_pairs={{0,2},{1,3},{2,0},{3,1},{4,6},{5,7},{6,4},{7,5},{8,10},{9,11},{10,... | collective-permute-start | bytes 884744 | tf_op jit(solution)/shard_map/ppermute | solution.py:621
  284.5 15.8 %collective-permute-start.42 = (bf16[336,768]{1,0:T(8,128)(2,1)S(1)}, bf16[336,768]{1,0:T(8,128)(2,1)S(1)}, u32[]{:S(2)}, u32[]{:S(2)}) collective-permute-start(bf16[336,768]{1,0:T(8,128)(2,1)S(1)} %slice.264), channel_id=1, source_target_pairs={{0,8},{8,0},{1,9},{9,1},{2,10},{10,2},{3,11},{11,3},{4,12},{12,4},... | collective-permute-start | bytes 1548296 | tf_op jit(solution)/shard_map/ppermute | solution.py:616
  286.2 14.0 %collective-permute-start.40 = (bf16[2,96,768]{2,1,0:T(8,128)(2,1)S(1)}, bf16[2,96,768]{2,1,0:T(8,128)(2,1)S(1)}, u32[]{:S(2)}, u32[]{:S(2)}) collective-permute-start(bf16[2,96,768]{2,1,0:T(8,128)(2,1)S(1)} %get-tuple-element.350), channel_id=1, source_target_pairs={{0,1},{1,0},{2,3},{3,2},{4,5},{5,4},{6,7},{7,6},{8,9},{9,8},{10,11... | collective-permute-start | bytes 884744 | tf_op jit(solution)/shard_map/ppermute | solution.py:621
  302.6 11.9 %collective-permute-start.46 = (bf16[2,96,768]{2,1,0:T(8,128)(2,1)}, bf16[2,96,768]{2,1,0:T(8,128)(2,1)}, u32[]{:S(2)}, u32[]{:S(2)}) collective-permute-start(bf16[2,96,768]{2,1,0:T(8,128)(2,1)} %bitcast.60), channel_id=1, source_target_pairs={{0,1},{1,0},{2,3},{3,2},{4,5},{5,4},{6,7},{7,6},{8,9},{9,8},{10,11... | collective-permute-start | bytes 884744 | tf_op jit(solution)/shard_map/ppermute | solution.py:621
  303.7 10.8 %collective-permute-start.45 = (bf16[2,96,768]{2,1,0:T(8,128)(2,1)S(1)}, bf16[2,96,768]{2,1,0:T(8,128)(2,1)S(1)}, u32[]{:S(2)}, u32[]{:S(2)}) collective-permute-start(bf16[2,96,768]{2,1,0:T(8,128)(2,1)S(1)} %slice_bitcast_fusion.3), channel_id=1, source_target_pairs={{0,8},{8,0},{1,9},{9,1},{2,10},{10,2},{3,11},{11,3},{4,12},{12,4},... | collective-permute-start | bytes 884744 | tf_op jit(solution)/shard_map/ppermute | solution.py:616
  315.7 9.7 %collective-permute-start.47 = (bf16[1,96,768]{2,1,0:T(8,128)(2,1)S(1)}, bf16[1,96,768]{2,1,0:T(8,128)(2,1)S(1)}, u32[]{:S(2)}, u32[]{:S(2)}) collective-permute-start(bf16[1,96,768]{2,1,0:T(8,128)(2,1)S(1)} %slice.278), channel_id=1, source_target_pairs={{0,2},{1,3},{2,0},{3,1},{4,6},{5,7},{6,4},{7,5},{8,10},{9,11},{10,... | collective-permute-start | bytes 442376 | tf_op jit(solution)/shard_map/ppermute | solution.py:621
  322.2 9.5 %collective-permute-start.51 = (f32[11,768]{1,0:T(8,128)}, f32[11,768]{1,0:T(8,128)S(1)}, u32[]{:S(2)}, u32[]{:S(2)}) collective-permute-start(f32[11,768]{1,0:T(8,128)} %prepare.1), channel_id=1, source_target_pairs={{0,2},{1,3},{2,0},{3,1},{4,6},{5,7},{6,4},{7,5},{8,10},{9,11},{10,... | collective-permute-start | bytes 101384 | tf_op jit(solution)/shard_map/ppermute | solution.py:636
  325.4 10.6 %collective-permute-start.48 = (bf16[1,96,768]{2,1,0:T(8,128)(2,1)S(1)}, bf16[1,96,768]{2,1,0:T(8,128)(2,1)S(1)}, u32[]{:S(2)}, u32[]{:S(2)}) collective-permute-start(bf16[1,96,768]{2,1,0:T(8,128)(2,1)S(1)} %add_convert_fusion.15), channel_id=1, source_target_pairs={{0,2},{1,3},{2,0},{3,1},{4,6},{5,7},{6,4},{7,5},{8,10},{9,11},{10,... | collective-permute-start | bytes 442376 | tf_op jit(solution)/shard_map/ppermute | solution.py:621
  336.0 16.2 %collective-permute-start.49 = (bf16[2,96,768]{2,1,0:T(8,128)(2,1)S(1)}, bf16[2,96,768]{2,1,0:T(8,128)(2,1)S(1)}, u32[]{:S(2)}, u32[]{:S(2)}) collective-permute-start(bf16[2,96,768]{2,1,0:T(8,128)(2,1)S(1)} %pad_maximum_fusion.7), channel_id=1, source_target_pairs={{0,1},{1,0},{2,3},{3,2},{4,5},{5,4},{6,7},{7,6},{8,9},{9,8},{10,11... | collective-permute-start | bytes 884744 | tf_op jit(solution)/shard_map/ppermute | solution.py:621
  (83 other events, 739.6 us)
Sparse Core Ops, SparseCore 0:
  23.2 106.5 all-gather.2
  172.5 116.1 reduce-scatter.1
